TPU v7x, 512 devices: a whole 4x8x8 slice. The times are simulated.
512 devices in a mesh: img: 32 (over y, z_lo, core), txt: 16 (over z_hi, x).
Axes of the slice: x: 4, y: 8, z: 8 (z_hi: 4, z_lo: 2; z = z_hi * 2 + z_lo), core: 2. Of those that a mesh axis runs over, the one named last changes fastest.
Arguments:
- image_emb: float32 [8192, 1152], P(('img', 'txt')), may hold values from -30 to 30
- text_emb: float32 [8192, 1152], P(('img', 'txt')), may hold values from -30 to 30
Outputs:
- loss: float32 [], replicated
- image_grad: float32 [8192, 1152], P(('img', 'txt'))
- text_grad: float32 [8192, 1152], P(('img', 'txt'))
All inputs are finite; a program needn't handle non-finite values.
Results may differ from a plain program's by a relative error of at most 0.0003.
Values sent between devices are 32-bit elements; how exact they have to be, the bound alone decides.
No kernel may reach another device: no remote copies, remote signals or barrier semaphores. Data moves between devices by JAX's collectives and lax.ppermute only.
A program may use at most 64 MiB of HBM per device.

v0:
```python
import jax
import jax.numpy as jnp
from jax import lax
from jax.sharding import PartitionSpec as P

LOGIT_MULT = 16.0
LOGIT_SHIFT = -10.0
EPSILON = 1e-06


def normalize(values):
    length = jnp.sqrt(jnp.sum(values * values, axis=1, keepdims=True) + EPSILON)
    return (values / length, length)


def project_back(unit, direction, length):
    inner = jnp.sum(unit * direction, axis=1, keepdims=True)
    return (direction - unit * inner) / length


def full_dot(left, right):
    return jnp.dot(left, right, precision=lax.Precision.HIGHEST, preferred_element_type=jnp.float32)


def on_device(image_emb, text_emb):
    row_count, feature_count = image_emb.shape
    img_count = lax.axis_size("img")
    txt_count = lax.axis_size("txt")
    pair_count = row_count * img_count * txt_count
    logit_mult = LOGIT_MULT
    image_unit, image_norm = normalize(image_emb)
    text_unit, text_norm = normalize(text_emb)
    img_place = lax.axis_index("img")
    txt_place = lax.axis_index("txt")
    image_block = lax.all_gather(image_unit, "txt", axis=0, tiled=True)
    image_index = img_place * (txt_count * row_count) + jnp.arange(
        txt_count * row_count, dtype=jnp.int32
    )
    text_block = lax.all_gather(text_unit, "img", axis=0, tiled=True)
    local_index = jnp.arange(text_block.shape[0], dtype=jnp.int32)
    text_index = (
        local_index // row_count * txt_count + txt_place
    ) * row_count + local_index % row_count
    logits = logit_mult * full_dot(image_block, text_block.T) + LOGIT_SHIFT
    target = jnp.where(image_index[:, None] == text_index[None, :], 1.0, -1.0).astype(jnp.float32)
    loss_part = jnp.sum(jax.nn.softplus(-target * logits))
    slope = -target * jax.nn.sigmoid(-target * logits) / pair_count
    slope, loss_local = (slope, loss_part)
    image_term = logit_mult * full_dot(slope, text_block)
    text_term = logit_mult * full_dot(slope.T, image_block)
    text_dir = lax.psum_scatter(text_term, "img", scatter_dimension=0, tiled=True)
    image_dir = lax.psum_scatter(image_term, "txt", scatter_dimension=0, tiled=True)
    grand_total = lax.psum(loss_local, ("img", "txt"))
    loss = grand_total / pair_count
    return (
        loss,
        project_back(image_unit, image_dir, image_norm),
        project_back(text_unit, text_dir, text_norm),
    )


def solution(mesh):
    return jax.shard_map(
        on_device,
        mesh=mesh,
        in_specs=(P(("img", "txt"), None), P(("img", "txt"), None)),
        out_specs=(P(), P(("img", "txt"), None), P(("img", "txt"), None)),
        check_vma=False,
    )
```

profile of v0, /device:TPU:1, one launch (start us, length us, event | category | flops | bytes accessed | tf_op | source)
XLA Modules:
  0.0 375.7 jit_solution(8630747046760421794)
XLA Ops:
  7.2 0.0 all-gather.3.cloned.1.call-start
  7.2 1.0 multiply_reduce_fusion.3
  8.2 1.6 broadcast_divide_fusion.1
  9.8 0.0 all-gather.3.cloned.1.call-update
  9.9 0.0 all-gather.5.cloned.1.call-start
  9.9 1.0 multiply_reduce_fusion.2
  10.9 1.6 broadcast_divide_fusion
  12.5 0.0 all-gather.5.cloned.1.call-update
  12.5 0.0 reduce-scatter.3.cloned.1.call-start
  12.6 63.5 %all-gather.3.cloned.1.call-done = f32[256,1152]{1,0:T(8,128)} async-done(((f32[16,1152]{1,0:T(8,128)}), f32[256,1152]{1,0:T(8,128)}) %all-gather.3.cloned.1.call-update) | async-done | bytes 1179664 | tf_op jit(solution)/shard_map/all_gather | solution.py:35
  76.2 69.5 %all-gather.5.cloned.1.call-done = f32[512,1152]{1,0:T(8,128)} async-done(((f32[16,1152]{1,0:T(8,128)}), f32[512,1152]{1,0:T(8,128)}) %all-gather.5.cloned.1.call-update) | async-done | bytes 2359312 | tf_op jit(solution)/shard_map/all_gather | solution.py:39
  145.6 5.5 %fusion.2 = (f32[]{:T(128)}, f32[256,512]{1,0:T(8,128)S(1)}) fusion(f32[256,1152]{1,0:T(8,128)} %all-gather.3.cloned.1.call-done, f32[512,1152]{1,0:T(8,128)} %all-gather.5.cloned.1.call-done, s32[512]{0:T(512)S(1)} %fusion.10, s32[256]{0:T(256)S(1)} %iota_add_fusion), kind=kOutput, calls=%fused_computation.6 | convolution fusion | flops 1813643264 | bytes 4066308 | tf_op jit(solution)/shard_map/dot_general | solution.py:22
  151.1 3.4 convolution_multiply_fusion.1
  154.5 0.0 reduce-scatter.3.cloned.1.call-update
  154.6 0.0 reduce-scatter.5.cloned.1.call-start
  154.6 3.9 %convolution_multiply_fusion = f32[512,1152]{1,0:T(8,128)} fusion(f32[256,1152]{1,0:T(8,128)S(1)} %copy-done.1, f32[256,512]{1,0:T(8,128)S(1)} %get-tuple-element.4, s32[512]{0:T(512)S(1)} %fusion.10, s32[256]{0:T(256)S(1)} %iota_add_fusion), kind=kOutput, calls=%fused_computation | convolution fusion | flops 1813577728 | bytes 4066304 | tf_op jit(solution)/shard_map/dot_general | solution.py:22
  158.5 0.0 reduce-scatter.5.cloned.1.call-update
  158.5 99.8 %psum.7 = f32[]{:T(128)} all-reduce(f32[]{:T(128)} %get-tuple-element.3), channel_id=1, replica_groups=mesh['img'=32,'txt'=16] {'img','txt'}, use_global_device_ids=true, to_apply=%region_3.4 | all-reduce | flops 1 | bytes 8 | tf_op jit(solution)/shard_map/psum | solution.py:53
  259.0 0.0 reduce-scatter.3.cloned.1.call-done
  259.1 1.1 multiply_reduce_fusion.1
  260.2 1.6 subtract_divide_fusion.1
  261.8 103.6 %reduce-scatter.5.cloned.1.call-done = f32[16,1152]{1,0:T(8,128)} async-done(((f32[512,1152]{1,0:T(8,128)}), f32[16,1152]{1,0:T(8,128)}) %reduce-scatter.5.cloned.1.call-update) | async-done | bytes 73744 | tf_op jit(solution)/shard_map/reduce_scatter | solution.py:51
  365.3 1.1 multiply_reduce_fusion
  366.4 1.6 subtract_divide_fusion
  (12 shorter events, 0.0 us)
Async XLA Ops:
  7.2 69.0 %all-gather.3.cloned.1.call-start = ((), (), s32[]{:S(2)}) async-start(), calls=%async_computation.2 | async-start | bytes 1253376 | tf_op jit(solution)/shard_map/all_gather | solution.py:35
  9.9 135.8 %all-gather.5.cloned.1.call-start = ((), (), s32[]{:S(2)}) async-start(), calls=%async_computation.3 | async-start | bytes 2433024 | tf_op jit(solution)/shard_map/all_gather | solution.py:39
  12.5 246.5 %reduce-scatter.3.cloned.1.call-start = ((), (), s32[]{:S(2)}) async-start(), calls=%async_computation.4 | async-start | bytes 1253376 | tf_op jit(solution)/shard_map/reduce_scatter | solution.py:52
  145.6 5.5 %copy-start = (f32[512,1152]{1,0:T(8,128)S(1)}, f32[512,1152]{1,0:T(8,128)}, u32[]{:S(2)}) copy-start(f32[512,1152]{1,0:T(8,128)} %all-gather.5.cloned.1.call-done) | copy-start | bytes 7077892
  151.1 3.5 copy-start.1
  154.6 104.5 %copy-start.2 = (f32[16,1152]{1,0:T(8,128)S(1)}, f32[16,1152]{1,0:T(8,128)}, u32[]{:S(2)}) copy-start(f32[16,1152]{1,0:T(8,128)} %param.2) | copy-start | bytes 221188
  154.6 210.8 %reduce-scatter.5.cloned.1.call-start = ((), (), s32[]{:S(2)}) async-start(), calls=%async_computation.5 | async-start | bytes 2433024 | tf_op jit(solution)/shard_map/reduce_scatter | solution.py:51
  158.5 206.8 %copy-start.3 = (f32[16,1152]{1,0:T(8,128)S(1)}, f32[16,1152]{1,0:T(8,128)}, u32[]{:S(2)}) copy-start(f32[16,1152]{1,0:T(8,128)} %param.3) | copy-start | bytes 221188
Sparse Core Ops, SparseCore 0:
  11.6 64.5 all-gather.2
  78.9 66.6 all-gather.4
  154.7 90.1 reduce-scatter.2
  247.5 117.7 reduce-scatter.4
where the time goes:
time: 378 us; the launch traced here: 376 us
  waiting for transfers between devices  237 us (63%)
  blocking collectives  99.8 us (26%)
  between operations  15.6 us (4%)
  matrix products  12.8 us (3%)
  other arithmetic  10.6 us (3%)
    reduce_scatter x1, waiting for transfers between devices, on_device(): lax.psum_scatter(text_term, 'img', scatter_dimension=0, tiled=True)  104 us
    psum x1, blocking collectives, on_device(): grand_total = lax.psum(loss_local, ('img', 'txt'))  99.8 us
    all_gather x1, waiting for transfers between devices, on_device(): text_block = lax.all_gather(text_unit, 'img', axis=0, tiled=True)  69.5 us
    all_gather x1, waiting for transfers between devices, on_device(): image_block = lax.all_gather(image_unit, 'txt', axis=0, tiled=True)  63.5 us
    dot_general x3, matrix products, full_dot(): jnp.dot(left, right, precision=lax.Precision.HIGHEST, preferred_element_t...  12.8 us
  transfers between devices with their start and end apart: 4, of which 3 were waited for; matrix products, arithmetic and copies ran while one was open for 2% of the time, Pallas kernels for 0%

commit v1 on v0

v1 whole, which is shorter than its diff:
```python
import jax
import jax.numpy as jnp
from jax import lax
from jax.sharding import Mesh, PartitionSpec as P

LOGIT_MULT = 16.0
LOGIT_SHIFT = -10.0
EPSILON = 1e-06

AXES = ("y", "zl", "c", "zh", "x")
SIZES = (8, 2, 2, 4, 4)
LANES = 128


def normalize(values):
    length = jnp.sqrt(jnp.sum(values * values, axis=1, keepdims=True) + EPSILON)
    return (values / length, length)


def project_back(unit, direction, length):
    inner = jnp.sum(unit * direction, axis=1, keepdims=True)
    return (direction - unit * inner) / length


def full_dot(left, right):
    return jnp.dot(left, right, precision=lax.Precision.HIGHEST, preferred_element_type=jnp.float32)


def shifted(values, axis, step):
    count = lax.axis_size(axis)
    return lax.ppermute(values, axis, [(i, (i + step) % count) for i in range(count)])


def exchange(values, axes):
    return lax.all_to_all(values, axes, 0, 0, tiled=True)


def on_device(image_emb, text_emb):
    rows, features = image_emb.shape
    y_count = lax.axis_size("y")
    pair_count = rows * lax.axis_size(AXES)
    text_unit, text_norm = normalize(text_emb)
    image_unit, image_norm = normalize(image_emb)

    text_y = exchange(jnp.tile(text_unit, (y_count, 1)), "y")
    image_z = jnp.concatenate([image_unit] + [shifted(image_unit, "zh", k) for k in range(1, 4)])
    image_block = jnp.concatenate([image_z] + [shifted(image_z, "x", k) for k in range(1, 4)])
    text_z = jnp.concatenate([text_y, shifted(text_y, "zl", 1)])
    text_block = jnp.concatenate([text_z, shifted(text_z, "c", 1)])

    own = lax.axis_index("y") * rows
    image_index = jnp.arange(image_block.shape[0], dtype=jnp.int32)
    text_index = jnp.arange(text_block.shape[0], dtype=jnp.int32) - own
    matched = (image_index[:, None] == text_index[None, :]) & (image_index[:, None] < rows)
    target = jnp.where(matched, 1.0, -1.0).astype(jnp.float32)
    logits = LOGIT_MULT * full_dot(image_block, text_block.T) + LOGIT_SHIFT
    loss_part = jnp.sum(jax.nn.softplus(-target * logits))
    slope = -target * jax.nn.sigmoid(-target * logits) / pair_count

    group = ("zl", "c", "zh", "x")
    losses = exchange(jnp.full((lax.axis_size(group), LANES), loss_part), group)
    loss_group = jnp.sum(losses[:, 0])

    text_term = LOGIT_MULT * full_dot(slope.T, image_block)
    image_term = LOGIT_MULT * full_dot(slope, text_block)

    half = text_term.shape[0] // 2
    text_c = text_term[:half] + shifted(text_term[half:], "c", 1)
    quarter = half // 2
    text_zl = text_c[:quarter] + shifted(text_c[quarter:], "zl", 1)

    parts = image_term.reshape(4, -1, features)
    image_x = parts[0] + sum(shifted(parts[k], "x", -k) for k in range(1, 4))
    parts = image_x.reshape(4, -1, features)
    image_dir = parts[0] + sum(shifted(parts[k], "zh", -k) for k in range(1, 4))

    packed = text_zl.reshape(y_count, rows * features // LANES, LANES)
    packed = jnp.concatenate([packed, jnp.full((y_count, 8, LANES), loss_group)], axis=1)
    packed = jnp.sum(exchange(packed, "y"), axis=0)
    text_dir = packed[:-8].reshape(rows, features)
    loss = packed[-1, 0] / pair_count
    return (
        loss,
        project_back(image_unit, image_dir, image_norm),
        project_back(text_unit, text_dir, text_norm),
    )


def solution(mesh):
    split = Mesh(mesh.devices.reshape(SIZES), AXES)
    return jax.shard_map(
        on_device,
        mesh=split,
        in_specs=(P(AXES, None), P(AXES, None)),
        out_specs=(P(), P(AXES, None), P(AXES, None)),
        check_vma=False,
    )
```

time: 378 us -> 164 us (0.43)
  waiting for transfers between devices: 237 us -> 48 us
  blocking collectives: 99.8 us -> 0 us
  starting transfers between devices: 0.16 us -> 84.2 us
  between operations: 15.6 us -> 2.89 us
  local copies, waits for them, and re-layouts: 0.02 us -> 6.58 us
    all_gather x2 -> x0, waiting for transfers between devices: 133 us -> none  [the longest x1 69.5 us: on_device(): text_block = lax.all_gather(text_unit, 'img', axis=0, tiled=True)]
    reduce_scatter x2 -> x0, waiting for transfers between devices: 104 us -> none  [the longest x1 104 us: on_device(): lax.psum_scatter(text_term, 'img', scatter_dimension=0, tiled=True)]
    psum x1 -> x0, blocking collectives: 99.8 us -> none  [on_device(): grand_total = lax.psum(loss_local, ('img', 'txt'))]
    ppermute x0 -> x16, starting transfers between devices: none -> 68.1 us  [shifted(): lax.ppermute(values, axis, [(i, (i + step) % count) for i in range(count)])]
    ppermute x0 -> x16, waiting for transfers between devices: none -> 31.3 us  [shifted(): lax.ppermute(values, axis, [(i, (i + step) % count) for i in range(count)])]
    all_to_all x0 -> x3, waiting for transfers between devices: none -> 16.7 us  [exchange(): return lax.all_to_all(values, axes, 0, 0, tiled=True)]
    all_to_all x0 -> x3, starting transfers between devices: none -> 16.2 us  [exchange(): return lax.all_to_all(values, axes, 0, 0, tiled=True)]
  transfers between devices with their start and end apart: 4 -> 19, of which waited for: 3 -> 9; matrix products, arithmetic and copies ran while one was open for 2% -> 7% of each run, Pallas kernels for 0% -> 0%
where the time goes in v1:
time: 164 us; the launch traced here: 161 us
  starting transfers between devices  84.2 us (51%)
  waiting for transfers between devices  48 us (29%)
  matrix products  11.2 us (7%)
  other arithmetic  8.27 us (5%)
  local copies, waits for them, and re-layouts  6.58 us (4%)
  between operations  2.89 us (2%)
    ppermute x16, starting transfers between devices, shifted(): lax.ppermute(values, axis, [(i, (i + step) % count) for i in range(count)])  68.1 us
    ppermute x16, waiting for transfers between devices, shifted(): lax.ppermute(values, axis, [(i, (i + step) % count) for i in range(count)])  31.3 us
    all_to_all x3, waiting for transfers between devices, exchange(): return lax.all_to_all(values, axes, 0, 0, tiled=True)  16.7 us
    all_to_all x3, starting transfers between devices, exchange(): return lax.all_to_all(values, axes, 0, 0, tiled=True)  16.2 us
    dot_general x3, matrix products, full_dot(): jnp.dot(left, right, precision=lax.Precision.HIGHEST, preferred_element_t...  11.2 us
  transfers between devices with their start and end apart: 19, of which 9 were waited for; matrix products, arithmetic and copies ran while one was open for 7% of the time, Pallas kernels for 0%

profile of v1, /device:TPU:1, one launch (start us, length us, event | category | flops | bytes accessed | tf_op | source)
XLA Modules:
  0.0 161.2 jit_solution(12999805929784314473)
XLA Ops:
  3.5 7.7 %all-to-all-start = ((f32[8,16,1152]{2,1,0:T(8,128)}), f32[8,16,1152]{2,1,0:T(8,128)S(1)}, u32[]{:S(2)}, u32[]{:S(2)}) async-start(f32[8,16,1152]{2,1,0:T(8,128)} %tile.2), calls=%async_computation | async-start | bytes 1179648 | tf_op jit(solution)/shard_map/all_to_all | solution.py:35
  11.3 16.3 %all-to-all-done = f32[8,16,1152]{2,1,0:T(8,128)S(1)} async-done(((f32[8,16,1152]{2,1,0:T(8,128)}), f32[8,16,1152]{2,1,0:T(8,128)S(1)}, u32[]{:S(2)}, u32[]{:S(2)}) %all-to-all-start) | async-done | bytes 589856 | tf_op jit(solution)/shard_map/all_to_all | solution.py:35
  27.6 6.9 %collective-permute-start.6 = (f32[128,1152]{1,0:T(8,128)S(1)}, f32[128,1152]{1,0:T(8,128)S(1)}, u32[]{:S(2)}, u32[]{:S(2)}) collective-permute-start(f32[128,1152]{1,0:T(8,128)S(1)} %bitcast.5), channel_id=1, source_target_pairs={{0,32},{32,0},{1,33},{33,1},{2,34},{34,2},{3,35},{35,3},{4,36},{36... | collective-permute-start | bytes 1769480 | tf_op jit(solution)/shard_map/ppermute | solution.py:31
  34.6 9.8 %collective-permute-start.2 = (f32[16,1152]{1,0:T(8,128)S(1)}, f32[16,1152]{1,0:T(8,128)S(1)}, u32[]{:S(2)}, u32[]{:S(2)}) collective-permute-start(f32[16,1152]{1,0:T(8,128)S(1)} %get-tuple-element.6), channel_id=1, source_target_pairs={{0,12},{4,0},{8,4},{12,8},{1,13},{5,1},{9,5},{13,9},{2,14},{6,2},{... | collective-permute-start | bytes 221192 | tf_op jit(solution)/shard_map/ppermute | solution.py:31
  46.3 4.2 %collective-permute-start = (f32[16,1152]{1,0:T(8,128)S(1)}, f32[16,1152]{1,0:T(8,128)S(1)}, u32[]{:S(2)}, u32[]{:S(2)}) collective-permute-start(f32[16,1152]{1,0:T(8,128)S(1)} %get-tuple-element.6), channel_id=1, source_target_pairs={{0,4},{4,8},{8,12},{12,0},{1,5},{5,9},{9,13},{13,1},{2,6},{6,10},{... | collective-permute-start | bytes 221192 | tf_op jit(solution)/shard_map/ppermute | solution.py:31
  50.6 6.1 %collective-permute-done.1 = f32[16,1152]{1,0:T(8,128)S(1)} collective-permute-done((f32[16,1152]{1,0:T(8,128)S(1)}, f32[16,1152]{1,0:T(8,128)S(1)}, u32[]{:S(2)}, u32[]{:S(2)}) %collective-permute-start.1) | collective-permute-done | bytes 73760 | tf_op jit(solution)/shard_map/ppermute | solution.py:31
  56.7 4.7 %collective-permute-done = f32[16,1152]{1,0:T(8,128)S(1)} collective-permute-done((f32[16,1152]{1,0:T(8,128)S(1)}, f32[16,1152]{1,0:T(8,128)S(1)}, u32[]{:S(2)}, u32[]{:S(2)}) %collective-permute-start) | collective-permute-done | bytes 73760 | tf_op jit(solution)/shard_map/ppermute | solution.py:31
  61.4 4.4 %collective-permute-start.5 = (f32[64,1152]{1,0:T(8,128)S(1)}, f32[64,1152]{1,0:T(8,128)S(1)}, u32[]{:S(2)}, u32[]{:S(2)}) collective-permute-start(f32[64,1152]{1,0:T(8,128)S(1)} %pad_maximum_fusion.10), channel_id=1, source_target_pairs={{0,3},{1,0},{2,1},{3,2},{4,7},{5,4},{6,5},{7,6},{8,11},{9,8},{10,9... | collective-permute-start | bytes 884744 | tf_op jit(solution)/shard_map/ppermute | solution.py:31
  65.8 2.4 %collective-permute-start.4 = (f32[64,1152]{1,0:T(8,128)S(1)}, f32[64,1152]{1,0:T(8,128)S(1)}, u32[]{:S(2)}, u32[]{:S(2)}) collective-permute-start(f32[64,1152]{1,0:T(8,128)S(1)} %pad_maximum_fusion.10), channel_id=1, source_target_pairs={{0,2},{1,3},{2,0},{3,1},{4,6},{5,7},{6,4},{7,5},{8,10},{9,11},{10,... | collective-permute-start | bytes 884744 | tf_op jit(solution)/shard_map/ppermute | solution.py:31
  68.3 2.5 %collective-permute-start.3 = (f32[64,1152]{1,0:T(8,128)S(1)}, f32[64,1152]{1,0:T(8,128)S(1)}, u32[]{:S(2)}, u32[]{:S(2)}) collective-permute-start(f32[64,1152]{1,0:T(8,128)S(1)} %pad_maximum_fusion.10), channel_id=1, source_target_pairs={{0,1},{1,2},{2,3},{3,0},{4,5},{5,6},{6,7},{7,4},{8,9},{9,10},{10,1... | collective-permute-start | bytes 884744 | tf_op jit(solution)/shard_map/ppermute | solution.py:31
  70.9 4.3 %collective-permute-start.7 = (f32[256,1152]{1,0:T(8,128)S(1)}, f32[256,1152]{1,0:T(8,128)S(1)}, u32[]{:S(2)}, u32[]{:S(2)}) collective-permute-start(f32[256,1152]{1,0:T(8,128)S(1)} %pad_maximum_fusion.9), channel_id=1, source_target_pairs={{0,16},{16,0},{1,17},{17,1},{2,18},{18,2},{3,19},{19,3},{4,20},{20... | collective-permute-start | bytes 3538952 | tf_op jit(solution)/shard_map/ppermute | solution.py:31
  75.2 8.9 %collective-permute-done.3 = f32[64,1152]{1,0:T(8,128)S(1)} collective-permute-done((f32[64,1152]{1,0:T(8,128)S(1)}, f32[64,1152]{1,0:T(8,128)S(1)}, u32[]{:S(2)}, u32[]{:S(2)}) %collective-permute-start.3) | collective-permute-done | bytes 294944 | tf_op jit(solution)/shard_map/ppermute | solution.py:31
  84.3 3.3 %fusion.4 = (f32[]{:T(128)}, f32[256,512]{1,0:T(8,128)S(1)}) fusion(f32[256,1152]{1,0:T(8,128)S(1)} %constant_dynamic-update-slice_fusion, f32[256,1152]{1,0:T(8,128)S(1)} %collective-permute-done.7, f32[128,1152]{1,0:T(8,128)S(1)} %collective-permute-done.6, f32[128,1152]{1,0:T(8,128)S(1)} %bitcast.7, pred[256]{0:T(512)(128)(4,1)S(1)} %iota_compare_fusion.1, ...), kind=kOutput, calls=%fused_computation.11 | convolution fusion | flops 1814953984 | bytes 4065540 | tf_op jit(solution)/shard_map/dot_general | solution.py:26
  87.6 3.9 %convolution_multiply_fusion = f32[512,1152]{1,0:T(8,128)S(1)} fusion(f32[256,1152]{1,0:T(8,128)} %copy-done.7, f32[256,512]{1,0:T(8,128)S(1)} %get-tuple-element.14, s32[512]{0:T(512)S(1)} %iota_subtract_fusion, pred[256]{0:T(512)(128)(4,1)S(1)} %iota_compare_fusion.1), kind=kOutput, calls=%fused_computation | convolution fusion | flops 1813708800 | bytes 4065536 | tf_op jit(solution)/shard_map/dot_general | solution.py:26
  92.7 2.7 %collective-permute-start.8 = (f32[256,1152]{1,0:T(8,128)}, f32[256,1152]{1,0:T(8,128)}, u32[]{:S(2)}, u32[]{:S(2)}) collective-permute-start(f32[256,1152]{1,0:T(8,128)} %slice.69), channel_id=1, source_target_pairs={{0,16},{16,0},{1,17},{17,1},{2,18},{18,2},{3,19},{19,3},{4,20},{20... | collective-permute-start | bytes 3538952 | tf_op jit(solution)/shard_map/ppermute | solution.py:31
  96.7 5.0 %all-to-all-start.1 = ((f32[64,1,128]{2,1,0:T(1,128)}), f32[64,1,128]{2,1,0:T(1,128)}, u32[]{:S(2)}, u32[]{:S(2)}) async-start(f32[64,1,128]{2,1,0:T(1,128)} %broadcast_in_dim.12), calls=%async_computation.1 | async-start | bytes 65536 | tf_op jit(solution)/shard_map/all_to_all | solution.py:35
  101.7 3.9 %convolution_multiply_fusion.1 = f32[256,1152]{1,0:T(8,128)S(1)} fusion(f32[256,1152]{1,0:T(8,128)} %copy-done.8, f32[128,1152]{1,0:T(8,128)S(1)} %copy-done.5, f32[128,1152]{1,0:T(8,128)S(1)} %bitcast.8, f32[256,512]{1,0:T(8,128)} %copy-done.9, s32[512]{0:T(512)S(1)} %iota_subtract_fusion, pred[256]{0:T(512)(128)(4,1)S(1)} %iota_compare_fusion.1), kind=kOutput, calls=%fused_computation.1 | convolution fusion | flops 1814593536 | bytes 4065536 | tf_op jit(solution)/shard_map/dot_general | solution.py:26
  106.7 4.6 %collective-permute-start.11 = (f32[64,1152]{1,0:T(8,128)}, f32[64,1152]{1,0:T(8,128)}, u32[]{:S(2)}, u32[]{:S(2)}) collective-permute-start(f32[64,1152]{1,0:T(8,128)} %get-tuple-element.7), channel_id=1, source_target_pairs={{0,2},{1,3},{2,0},{3,1},{4,6},{5,7},{6,4},{7,5},{8,10},{9,11},{10,... | collective-permute-start | bytes 884744 | tf_op jit(solution)/shard_map/ppermute | solution.py:31
  113.5 4.3 %collective-permute-start.10 = (f32[64,1152]{1,0:T(8,128)}, f32[64,1152]{1,0:T(8,128)}, u32[]{:S(2)}, u32[]{:S(2)}) collective-permute-start(f32[64,1152]{1,0:T(8,128)} %get-tuple-element.9), channel_id=1, source_target_pairs={{0,3},{1,0},{2,1},{3,2},{4,7},{5,4},{6,5},{7,6},{8,11},{9,8},{10,9... | collective-permute-start | bytes 884744 | tf_op jit(solution)/shard_map/ppermute | solution.py:31
  119.3 3.3 %collective-permute-start.9 = (f32[128,1152]{1,0:T(8,128)S(1)}, f32[128,1152]{1,0:T(8,128)S(1)}, u32[]{:S(2)}, u32[]{:S(2)}) collective-permute-start(f32[128,1152]{1,0:T(8,128)S(1)} %slice.71), channel_id=1, source_target_pairs={{0,32},{32,0},{1,33},{33,1},{2,34},{34,2},{3,35},{35,3},{4,36},{36... | collective-permute-start | bytes 1769480 | tf_op jit(solution)/shard_map/ppermute | solution.py:31
  126.9 8.0 %collective-permute-done.9 = f32[128,1152]{1,0:T(8,128)S(1)} collective-permute-done((f32[128,1152]{1,0:T(8,128)S(1)}, f32[128,1152]{1,0:T(8,128)S(1)}, u32[]{:S(2)}, u32[]{:S(2)}) %collective-permute-start.9) | collective-permute-done | bytes 589856 | tf_op jit(solution)/shard_map/ppermute | solution.py:31
  136.6 3.5 %all-to-all-start.2 = ((f32[8,152,128]{2,1,0:T(8,128)}), f32[8,152,128]{2,1,0:T(8,128)S(1)}, u32[]{:S(2)}, u32[]{:S(2)}) async-start(f32[8,152,128]{2,1,0:T(8,128)} %concatenate.21), calls=%async_computation.2 | async-start | bytes 1245184 | tf_op jit(solution)/shard_map/all_to_all | solution.py:35
  140.1 7.1 %collective-permute-start.14 = (f32[16,1152]{1,0:T(8,128)S(1)}, f32[16,1152]{1,0:T(8,128)S(1)}, u32[]{:S(2)}, u32[]{:S(2)}) collective-permute-start(f32[16,1152]{1,0:T(8,128)S(1)} %get-tuple-element.10), channel_id=1, source_target_pairs={{0,8},{4,12},{8,0},{12,4},{1,9},{5,13},{9,1},{13,5},{2,10},{6,14},... | collective-permute-start | bytes 221192 | tf_op jit(solution)/shard_map/ppermute | solution.py:31
  149.4 5.2 %collective-permute-start.13 = (f32[16,1152]{1,0:T(8,128)S(1)}, f32[16,1152]{1,0:T(8,128)S(1)}, u32[]{:S(2)}, u32[]{:S(2)}) collective-permute-start(f32[16,1152]{1,0:T(8,128)S(1)} %get-tuple-element.12), channel_id=1, source_target_pairs={{0,12},{4,0},{8,4},{12,8},{1,13},{5,1},{9,5},{13,9},{2,14},{6,2},{... | collective-permute-start | bytes 221192 | tf_op jit(solution)/shard_map/ppermute | solution.py:31
  (73 shorter events, 25.3 us)
Async XLA Ops:
  3.5 24.1 %all-to-all-start = ((f32[8,16,1152]{2,1,0:T(8,128)}), f32[8,16,1152]{2,1,0:T(8,128)S(1)}, u32[]{:S(2)}, u32[]{:S(2)}) async-start(f32[8,16,1152]{2,1,0:T(8,128)} %tile.2), calls=%async_computation | async-start | bytes 1179648 | tf_op jit(solution)/shard_map/all_to_all | solution.py:35
  27.6 43.1 %collective-permute-start.6 = (f32[128,1152]{1,0:T(8,128)S(1)}, f32[128,1152]{1,0:T(8,128)S(1)}, u32[]{:S(2)}, u32[]{:S(2)}) collective-permute-start(f32[128,1152]{1,0:T(8,128)S(1)} %bitcast.5), channel_id=1, source_target_pairs={{0,32},{32,0},{1,33},{33,1},{2,34},{34,2},{3,35},{35,3},{4,36},{36... | collective-permute-start | bytes 1769480 | tf_op jit(solution)/shard_map/ppermute | solution.py:31
  34.6 36.3 %copy-start = (f32[16,1152]{1,0:T(8,128)}, f32[16,1152]{1,0:T(8,128)S(1)}, u32[]{:S(2)}) copy-start(f32[16,1152]{1,0:T(8,128)S(1)} %get-tuple-element.6) | copy-start | bytes 221188
  34.6 16.0 %collective-permute-start.2 = (f32[16,1152]{1,0:T(8,128)S(1)}, f32[16,1152]{1,0:T(8,128)S(1)}, u32[]{:S(2)}, u32[]{:S(2)}) collective-permute-start(f32[16,1152]{1,0:T(8,128)S(1)} %get-tuple-element.6), channel_id=1, source_target_pairs={{0,12},{4,0},{8,4},{12,8},{1,13},{5,1},{9,5},{13,9},{2,14},{6,2},{... | collective-permute-start | bytes 221192 | tf_op jit(solution)/shard_map/ppermute | solution.py:31
  44.4 12.3 %collective-permute-start.1 = (f32[16,1152]{1,0:T(8,128)S(1)}, f32[16,1152]{1,0:T(8,128)S(1)}, u32[]{:S(2)}, u32[]{:S(2)}) collective-permute-start(f32[16,1152]{1,0:T(8,128)S(1)} %get-tuple-element.6), channel_id=1, source_target_pairs={{0,8},{4,12},{8,0},{12,4},{1,9},{5,13},{9,1},{13,5},{2,10},{6,14},... | collective-permute-start | bytes 221192 | tf_op jit(solution)/shard_map/ppermute | solution.py:31
  46.3 15.1 %collective-permute-start = (f32[16,1152]{1,0:T(8,128)S(1)}, f32[16,1152]{1,0:T(8,128)S(1)}, u32[]{:S(2)}, u32[]{:S(2)}) collective-permute-start(f32[16,1152]{1,0:T(8,128)S(1)} %get-tuple-element.6), channel_id=1, source_target_pairs={{0,4},{4,8},{8,12},{12,0},{1,5},{5,9},{9,13},{13,1},{2,6},{6,10},{... | collective-permute-start | bytes 221192 | tf_op jit(solution)/shard_map/ppermute | solution.py:31
  61.4 22.8 %collective-permute-start.5 = (f32[64,1152]{1,0:T(8,128)S(1)}, f32[64,1152]{1,0:T(8,128)S(1)}, u32[]{:S(2)}, u32[]{:S(2)}) collective-permute-start(f32[64,1152]{1,0:T(8,128)S(1)} %pad_maximum_fusion.10), channel_id=1, source_target_pairs={{0,3},{1,0},{2,1},{3,2},{4,7},{5,4},{6,5},{7,6},{8,11},{9,8},{10,9... | collective-permute-start | bytes 884744 | tf_op jit(solution)/shard_map/ppermute | solution.py:31
  65.8 18.3 %collective-permute-start.4 = (f32[64,1152]{1,0:T(8,128)S(1)}, f32[64,1152]{1,0:T(8,128)S(1)}, u32[]{:S(2)}, u32[]{:S(2)}) collective-permute-start(f32[64,1152]{1,0:T(8,128)S(1)} %pad_maximum_fusion.10), channel_id=1, source_target_pairs={{0,2},{1,3},{2,0},{3,1},{4,6},{5,7},{6,4},{7,5},{8,10},{9,11},{10,... | collective-permute-start | bytes 884744 | tf_op jit(solution)/shard_map/ppermute | solution.py:31
  68.3 15.9 %collective-permute-start.3 = (f32[64,1152]{1,0:T(8,128)S(1)}, f32[64,1152]{1,0:T(8,128)S(1)}, u32[]{:S(2)}, u32[]{:S(2)}) collective-permute-start(f32[64,1152]{1,0:T(8,128)S(1)} %pad_maximum_fusion.10), channel_id=1, source_target_pairs={{0,1},{1,2},{2,3},{3,0},{4,5},{5,6},{6,7},{7,4},{8,9},{9,10},{10,1... | collective-permute-start | bytes 884744 | tf_op jit(solution)/shard_map/ppermute | solution.py:31
  70.8 13.5 %copy-start.4 = (f32[128,1152]{1,0:T(8,128)}, f32[128,1152]{1,0:T(8,128)S(1)}, u32[]{:S(2)}) copy-start(f32[128,1152]{1,0:T(8,128)S(1)} %collective-permute-done.6) | copy-start | bytes 1769476
  70.9 13.3 %collective-permute-start.7 = (f32[256,1152]{1,0:T(8,128)S(1)}, f32[256,1152]{1,0:T(8,128)S(1)}, u32[]{:S(2)}, u32[]{:S(2)}) collective-permute-start(f32[256,1152]{1,0:T(8,128)S(1)} %pad_maximum_fusion.9), channel_id=1, source_target_pairs={{0,16},{16,0},{1,17},{17,1},{2,18},{18,2},{3,19},{19,3},{4,20},{20... | collective-permute-start | bytes 3538952 | tf_op jit(solution)/shard_map/ppermute | solution.py:31
  92.7 25.1 %collective-permute-start.8 = (f32[256,1152]{1,0:T(8,128)}, f32[256,1152]{1,0:T(8,128)}, u32[]{:S(2)}, u32[]{:S(2)}) collective-permute-start(f32[256,1152]{1,0:T(8,128)} %slice.69), channel_id=1, source_target_pairs={{0,16},{16,0},{1,17},{17,1},{2,18},{18,2},{3,19},{19,3},{4,20},{20... | collective-permute-start | bytes 3538952 | tf_op jit(solution)/shard_map/ppermute | solution.py:31
  96.7 25.9 %all-to-all-start.1 = ((f32[64,1,128]{2,1,0:T(1,128)}), f32[64,1,128]{2,1,0:T(1,128)}, u32[]{:S(2)}, u32[]{:S(2)}) async-start(f32[64,1,128]{2,1,0:T(1,128)} %broadcast_in_dim.12), calls=%async_computation.1 | async-start | bytes 65536 | tf_op jit(solution)/shard_map/all_to_all | solution.py:35
  105.6 13.6 %copy-start.3 = (f32[256,1152]{1,0:T(8,128)}, f32[256,1152]{1,0:T(8,128)S(1)}, u32[]{:S(2)}) copy-start(f32[256,1152]{1,0:T(8,128)S(1)} %convolution_multiply_fusion.1) | copy-start | bytes 3538948
  106.7 17.3 %collective-permute-start.11 = (f32[64,1152]{1,0:T(8,128)}, f32[64,1152]{1,0:T(8,128)}, u32[]{:S(2)}, u32[]{:S(2)}) collective-permute-start(f32[64,1152]{1,0:T(8,128)} %get-tuple-element.7), channel_id=1, source_target_pairs={{0,2},{1,3},{2,0},{3,1},{4,6},{5,7},{6,4},{7,5},{8,10},{9,11},{10,... | collective-permute-start | bytes 884744 | tf_op jit(solution)/shard_map/ppermute | solution.py:31
  111.3 14.3 %collective-permute-start.12 = (f32[64,1152]{1,0:T(8,128)}, f32[64,1152]{1,0:T(8,128)}, u32[]{:S(2)}, u32[]{:S(2)}) collective-permute-start(f32[64,1152]{1,0:T(8,128)} %get-tuple-element.8), channel_id=1, source_target_pairs={{0,1},{1,2},{2,3},{3,0},{4,5},{5,6},{6,7},{7,4},{8,9},{9,10},{10,1... | collective-permute-start | bytes 884744 | tf_op jit(solution)/shard_map/ppermute | solution.py:31
  113.5 12.1 %collective-permute-start.10 = (f32[64,1152]{1,0:T(8,128)}, f32[64,1152]{1,0:T(8,128)}, u32[]{:S(2)}, u32[]{:S(2)}) collective-permute-start(f32[64,1152]{1,0:T(8,128)} %get-tuple-element.9), channel_id=1, source_target_pairs={{0,3},{1,0},{2,1},{3,2},{4,7},{5,4},{6,5},{7,6},{8,11},{9,8},{10,9... | collective-permute-start | bytes 884744 | tf_op jit(solution)/shard_map/ppermute | solution.py:31
  119.3 15.6 %collective-permute-start.9 = (f32[128,1152]{1,0:T(8,128)S(1)}, f32[128,1152]{1,0:T(8,128)S(1)}, u32[]{:S(2)}, u32[]{:S(2)}) collective-permute-start(f32[128,1152]{1,0:T(8,128)S(1)} %slice.71), channel_id=1, source_target_pairs={{0,32},{32,0},{1,33},{33,1},{2,34},{34,2},{3,35},{35,3},{4,36},{36... | collective-permute-start | bytes 1769480 | tf_op jit(solution)/shard_map/ppermute | solution.py:31
  135.0 21.7 %copy-start.1 = (f32[16,1152]{1,0:T(8,128)S(1)}, f32[16,1152]{1,0:T(8,128)}, u32[]{:S(2)}) copy-start(f32[16,1152]{1,0:T(8,128)} %copy-done) | copy-start | bytes 221188
  136.6 21.3 %all-to-all-start.2 = ((f32[8,152,128]{2,1,0:T(8,128)}), f32[8,152,128]{2,1,0:T(8,128)S(1)}, u32[]{:S(2)}, u32[]{:S(2)}) async-start(f32[8,152,128]{2,1,0:T(8,128)} %concatenate.21), calls=%async_computation.2 | async-start | bytes 1245184 | tf_op jit(solution)/shard_map/all_to_all | solution.py:35
  140.1 18.4 %copy-start.2 = (f32[16,1152]{1,0:T(8,128)S(1)}, f32[16,1152]{1,0:T(8,128)}, u32[]{:S(2)}) copy-start(f32[16,1152]{1,0:T(8,128)} %param.3) | copy-start | bytes 221188
  140.1 14.5 %collective-permute-start.14 = (f32[16,1152]{1,0:T(8,128)S(1)}, f32[16,1152]{1,0:T(8,128)S(1)}, u32[]{:S(2)}, u32[]{:S(2)}) collective-permute-start(f32[16,1152]{1,0:T(8,128)S(1)} %get-tuple-element.10), channel_id=1, source_target_pairs={{0,8},{4,12},{8,0},{12,4},{1,9},{5,13},{9,1},{13,5},{2,10},{6,14},... | collective-permute-start | bytes 221192 | tf_op jit(solution)/shard_map/ppermute | solution.py:31
  147.2 7.7 %collective-permute-start.15 = (f32[16,1152]{1,0:T(8,128)S(1)}, f32[16,1152]{1,0:T(8,128)S(1)}, u32[]{:S(2)}, u32[]{:S(2)}) collective-permute-start(f32[16,1152]{1,0:T(8,128)S(1)} %get-tuple-element.11), channel_id=1, source_target_pairs={{0,4},{4,8},{8,12},{12,0},{1,5},{5,9},{9,13},{13,1},{2,6},{6,10},{... | collective-permute-start | bytes 221192 | tf_op jit(solution)/shard_map/ppermute | solution.py:31
  149.4 7.2 %collective-permute-start.13 = (f32[16,1152]{1,0:T(8,128)S(1)}, f32[16,1152]{1,0:T(8,128)S(1)}, u32[]{:S(2)}, u32[]{:S(2)}) collective-permute-start(f32[16,1152]{1,0:T(8,128)S(1)} %get-tuple-element.12), channel_id=1, source_target_pairs={{0,12},{4,0},{8,4},{12,8},{1,13},{5,1},{9,5},{13,9},{2,14},{6,2},{... | collective-permute-start | bytes 221192 | tf_op jit(solution)/shard_map/ppermute | solution.py:31
  (5 other events, 35.3 us)

commit v2 on v0

v2 whole, which is shorter than its diff:
```python
import jax
import jax.numpy as jnp
from jax import lax
from jax.experimental import pallas as pl
from jax.experimental.pallas import tpu as pltpu
from jax.sharding import Mesh, PartitionSpec as P

LOGIT_MULT = 16.0
LOGIT_SHIFT = -10.0
EPSILON = 1e-06

AXES = ("y", "zl", "c", "zh", "x")
SIZES = (8, 2, 2, 4, 4)
NY, NZH, NX = 8, 4, 4
ROWS, FEATURES, LANES = 16, 1152, 128
COLS = FEATURES // LANES
PACK = COLS * ROWS
PAIRS = 8192
F32, BF16 = jnp.float32, jnp.bfloat16

VMEM = pl.BlockSpec(memory_space=pltpu.VMEM)
ANY = pl.BlockSpec(memory_space=pl.ANY)
SMEM = pl.BlockSpec(memory_space=pltpu.SMEM)


def shape(*dims):
    return jax.ShapeDtypeStruct(dims, F32)


def call(kernel, ins, outs, in_specs=None, out_specs=None, flops=0, **kw):
    moved = 4 * sum(a.size for a in list(ins) + list(outs))
    return pl.pallas_call(
        kernel,
        out_shape=outs,
        in_specs=in_specs or [VMEM] * len(ins),
        out_specs=out_specs or [VMEM] * len(outs),
        cost_estimate=pl.CostEstimate(flops=flops, bytes_accessed=moved, transcendentals=0),
        compiler_params=pltpu.CompilerParams(vmem_limit_bytes=40 * 2**20),
        **kw,
    )(*ins)


def shifted(values, axis, step):
    count = lax.axis_size(axis)
    return lax.ppermute(values, axis, [(i, (i + step) % count) for i in range(count)])


def exchange(values, axes):
    return lax.all_to_all(values, axes, 0, 0, tiled=True)


def normalize(values):
    length = jnp.sqrt(jnp.sum(values * values, axis=1, keepdims=True) + EPSILON)
    return values / length, length


def project_back(unit, direction, length):
    inner = jnp.sum(unit * direction, axis=1, keepdims=True)
    return (direction - unit * inner) / length


def halves(values):
    high = values.astype(BF16)
    return high, (values - high.astype(F32)).astype(BF16)


def dot3(left, right, dims):
    def dot(a, b):
        return lax.dot_general(a, b, (dims, ((), ())), preferred_element_type=F32)

    return dot(left[1], right[0]) + dot(left[0], right[1]) + dot(left[0], right[0])


def normalize_kernel(image_ref, text_ref, image_out, text_out):
    image_out[...] = normalize(image_ref[...])[0]
    text_unit = normalize(text_ref[...])[0]
    for y in range(NY):
        text_out[pl.ds(y * ROWS, ROWS), :] = text_unit


def spread_kernel(z0, z1, z2, z3, text_ref, image_out, text_out):
    for x in range(NX):
        for k, part in enumerate((z0, z1, z2, z3)):
            image_out[pl.ds((x * NZH + k) * ROWS, ROWS), :] = part[...]


def logits_kernel(place, image_ref, a_ref, b_ref, c_ref, d_ref, slope_out, other_out, loss_out):
    image = halves(image_ref[...])
    quarter = a_ref.shape[0]
    count = image_ref.shape[0]
    row = lax.broadcasted_iota(jnp.int32, (count, quarter), 0) - place[0]
    column = lax.broadcasted_iota(jnp.int32, (count, quarter), 1) - place[1]
    matched = (row == column) & (row >= 0) & (row < ROWS)
    total = jnp.zeros((), F32)
    for k, ref in enumerate((c_ref, d_ref, a_ref, b_ref)):
        logits = LOGIT_MULT * dot3(image, halves(ref[...]), ((1,), (1,))) + LOGIT_SHIFT
        if ref is a_ref:
            logits = jnp.where(matched, -logits, logits)
        small = jnp.exp(-jnp.abs(logits))
        total += jnp.sum(jnp.maximum(logits, 0.0) + jnp.log1p(small))
        slope = jnp.where(logits >= 0.0, 1.0, small) / (1.0 + small) * (LOGIT_MULT / PAIRS)
        if ref is a_ref:
            slope = jnp.where(matched, -slope, slope)
        slope_out[:, pl.ds((k + 2) % 4 * quarter, quarter)] = slope
        if k < 2:
            other_out[pl.ds(k * quarter, quarter), :] = dot3(halves(slope), image, ((0,), (0,)))
    loss_out[...] = jnp.full(loss_out.shape, total)


def image_kernel(slope_ref, a_ref, b_ref, c_ref, d_ref, out):
    quarter = a_ref.shape[0]
    total = None
    for k, ref in enumerate((a_ref, b_ref, c_ref, d_ref)):
        slope = slope_ref[:, pl.ds(k * quarter, quarter)]
        term = dot3(halves(slope), halves(ref[...]), ((1,), (0,)))
        total = term if total is None else total + term
    out[...] = total


def text_kernel(slope_ref, image_ref, other_ref, keep_out, send_out):
    image = halves(image_ref[...])
    quarter = keep_out.shape[0]
    for k, out in ((1, send_out), (0, keep_out)):
        rows = pl.ds(k * quarter, quarter)
        out[...] = dot3(halves(slope_ref[:, rows]), image, ((0,), (0,))) + other_ref[rows, :]


def join_kernel(image_ref, keep_ref, received_ref, losses_ref, packed_out, *zs):
    count = image_ref.shape[0] // NX
    for k, out in enumerate(zs):
        rows = [pl.ds(x * count + k * ROWS, ROWS) for x in range(NX)]
        out[...] = (image_ref[rows[0], :] + image_ref[rows[1], :]) + (image_ref[rows[2], :] + image_ref[rows[3], :])
    loss = jnp.sum(losses_ref[:, 0:1])
    for y in range(NY):
        rows = pl.ds(y * ROWS, ROWS)
        for k in range(COLS):
            lanes = pl.ds(k * LANES, LANES)
            packed_out[y, pl.ds(k * ROWS, ROWS), :] = keep_ref[rows, lanes] + received_ref[rows, lanes]
        packed_out[y, pl.ds(PACK, 8), :] = jnp.full((8, LANES), loss)


def image_grad_kernel(emb_ref, z0, z1, z2, z3, out):
    unit, length = normalize(emb_ref[...])
    out[...] = project_back(unit, (z0[...] + z1[...]) + (z2[...] + z3[...]), length)


def text_grad_kernel(emb_ref, packed_ref, out, loss_out):
    unit, length = normalize(emb_ref[...])
    total = packed_ref[0]
    for y in range(1, NY):
        total = total + packed_ref[y]
    direction = jnp.concatenate([total[k * ROWS : (k + 1) * ROWS] for k in range(COLS)], axis=1)
    out[...] = project_back(unit, direction, length)
    loss_out[...] = total[PACK:] / PAIRS


def on_device(image_emb, text_emb):
    rows, features = image_emb.shape
    image_unit, text_tiled = call(
        normalize_kernel, (image_emb, text_emb), [shape(rows, features), shape(NY * rows, features)]
    )
    text_y = exchange(text_tiled, "y")
    zs = [image_unit] + [shifted(image_unit, "zh", k) for k in range(1, NZH)]
    image_tiled, text_a = call(
        spread_kernel,
        (*zs, text_y),
        [shape(NX * NZH * rows, features), shape(*text_y.shape)],
        in_specs=[VMEM] * 4 + [ANY],
        out_specs=[VMEM, ANY],
        input_output_aliases={4: 1},
    )
    image = exchange(image_tiled, "x")
    text_b = shifted(text_a, "zl", 1)
    text_c = shifted(text_a, "c", 1)
    text_d = shifted(text_b, "c", 1)

    place = jnp.stack([lax.axis_index("x") * (NZH * rows), lax.axis_index("y") * rows]).astype(jnp.int32)
    count, quarter = image.shape[0], text_a.shape[0]
    product = 2 * count * quarter * features * 3
    slope, other, loss = call(
        logits_kernel,
        (place, image, text_a, text_b, text_c, text_d),
        [shape(count, 4 * quarter), shape(2 * quarter, features), shape(64, LANES)],
        in_specs=[SMEM] + [VMEM] * 5,
        flops=6 * product,
    )
    received = shifted(other, "c", 1)
    losses = exchange(loss, ("zl", "c", "zh", "x"))
    (image_term,) = call(
        image_kernel, (slope, text_a, text_b, text_c, text_d), [shape(count, features)], flops=4 * product
    )
    image_x = exchange(image_term, "x")
    keep, send = call(
        text_kernel, (slope, image, received), [shape(quarter, features)] * 2, flops=2 * product
    )
    received = shifted(send, "zl", 1)
    packed, *zs = call(
        join_kernel,
        (image_x, keep, received, losses),
        [shape(NY, PACK + 8, LANES)] + [shape(rows, features)] * NZH,
    )
    packed = exchange(packed, "y")
    zs = [zs[0]] + [shifted(zs[k], "zh", -k) for k in range(1, NZH)]
    (image_grad,) = call(image_grad_kernel, (image_emb, *zs), [shape(rows, features)])
    text_grad, loss = call(text_grad_kernel, (text_emb, packed), [shape(rows, features), shape(8, LANES)])
    return loss[0, 0], image_grad, text_grad


def solution(mesh):
    split = Mesh(mesh.devices.reshape(SIZES), AXES)
    return jax.shard_map(
        on_device,
        mesh=split,
        in_specs=(P(AXES, None), P(AXES, None)),
        out_specs=(P(), P(AXES, None), P(AXES, None)),
        check_vma=False,
    )
```

time: 378 us -> 135 us (0.36)
  waiting for transfers between devices: 237 us -> 40.3 us
  blocking collectives: 99.8 us -> 0 us
  starting transfers between devices: 0.16 us -> 72 us
  between operations: 15.6 us -> 0.81 us
  Pallas kernels: 0 us -> 14.1 us
  matrix products: 12.8 us -> 0 us
  other arithmetic: 10.6 us -> 0.08 us
  local copies, waits for them, and re-layouts: 0.02 us -> 6.25 us
    all_gather x2 -> x0, waiting for transfers between devices: 133 us -> none  [the longest x1 69.5 us: on_device(): text_block = lax.all_gather(text_unit, 'img', axis=0, tiled=True)]
    reduce_scatter x2 -> x0, waiting for transfers between devices: 104 us -> none  [the longest x1 104 us: on_device(): lax.psum_scatter(text_term, 'img', scatter_dimension=0, tiled=True)]
    psum x1 -> x0, blocking collectives: 99.8 us -> none  [on_device(): grand_total = lax.psum(loss_local, ('img', 'txt'))]
    ppermute x0 -> x11, starting transfers between devices: none -> 44.9 us  [shifted(): lax.ppermute(values, axis, [(i, (i + step) % count) for i in range(count)])]
    all_to_all x0 -> x5, starting transfers between devices: none -> 27.1 us  [exchange(): return lax.all_to_all(values, axes, 0, 0, tiled=True)]
    all_to_all x0 -> x5, waiting for transfers between devices: none -> 21 us  [exchange(): return lax.all_to_all(values, axes, 0, 0, tiled=True)]
    ppermute x0 -> x11, waiting for transfers between devices: none -> 19.3 us  [shifted(): lax.ppermute(values, axis, [(i, (i + step) % count) for i in range(count)])]
    pallas_call x0 -> x8, Pallas kernels: none -> 14.1 us  [call(): pl.pallas_call(kernel, out_shape=outs, in_specs=in_specs or [VMEM] * len(...]
  transfers between devices with their start and end apart: 4 -> 16, of which waited for: 3 -> 10; matrix products, arithmetic and copies ran while one was open for 2% -> 0% of each run, Pallas kernels for 0% -> 4%
where the time goes in v2:
time: 135 us; the launch traced here: 134 us
  starting transfers between devices  72 us (53%)
  waiting for transfers between devices  40.3 us (30%)
  Pallas kernels  14.1 us (10%)
  local copies, waits for them, and re-layouts  6.25 us (5%)
    ppermute x11, starting transfers between devices, shifted(): lax.ppermute(values, axis, [(i, (i + step) % count) for i in range(count)])  44.9 us
    all_to_all x5, starting transfers between devices, exchange(): return lax.all_to_all(values, axes, 0, 0, tiled=True)  27.1 us
    all_to_all x5, waiting for transfers between devices, exchange(): return lax.all_to_all(values, axes, 0, 0, tiled=True)  21 us
    ppermute x11, waiting for transfers between devices, shifted(): lax.ppermute(values, axis, [(i, (i + step) % count) for i in range(count)])  19.3 us
    pallas_call x8, Pallas kernels, call(): pl.pallas_call(kernel, out_shape=outs, in_specs=in_specs or [VMEM] * len(...  14.1 us
    unnamed x16, local copies, waits for them, and re-layouts  5.74 us
  transfers between devices with their start and end apart: 16, of which 10 were waited for; matrix products, arithmetic and copies ran while one was open for 0% of the time, Pallas kernels for 4%

profile of v2, /device:TPU:1, one launch (start us, length us, event | category | flops | bytes accessed | tf_op | source)
XLA Modules:
  0.0 133.5 jit_solution(8845892260579555237)
XLA Ops:
  3.4 7.7 %all-to-all-start = ((f32[8,16,1152]{2,1,0:T(8,128)}), f32[8,16,1152]{2,1,0:T(8,128)S(1)}, u32[]{:S(2)}, u32[]{:S(2)}) async-start(f32[8,16,1152]{2,1,0:T(8,128)} %bitcast.2), calls=%async_computation | async-start | bytes 1179648 | tf_op jit(solution)/shard_map/all_to_all | solution.py:49
  11.0 10.6 %collective-permute-start.2 = (f32[16,1152]{1,0:T(8,128)S(1)}, f32[16,1152]{1,0:T(8,128)S(1)}, u32[]{:S(2)}, u32[]{:S(2)}) collective-permute-start(f32[16,1152]{1,0:T(8,128)S(1)} %get-tuple-element.19.z0), channel_id=1, source_target_pairs={{0,12},{4,0},{8,4},{12,8},{1,13},{5,1},{9,5},{13,9},{2,14},{6,2},{... | collective-permute-start | bytes 221192 | tf_op jit(solution)/shard_map/ppermute | solution.py:45
  23.6 4.2 %collective-permute-start = (f32[16,1152]{1,0:T(8,128)S(1)}, f32[16,1152]{1,0:T(8,128)S(1)}, u32[]{:S(2)}, u32[]{:S(2)}) collective-permute-start(f32[16,1152]{1,0:T(8,128)S(1)} %get-tuple-element.19.z0), channel_id=1, source_target_pairs={{0,4},{4,8},{8,12},{12,0},{1,5},{5,9},{9,13},{13,1},{2,6},{6,10},{... | collective-permute-start | bytes 221192 | tf_op jit(solution)/shard_map/ppermute | solution.py:45
  27.9 3.6 %collective-permute-done.1.z2 = f32[16,1152]{1,0:T(8,128)S(1)} collective-permute-done((f32[16,1152]{1,0:T(8,128)S(1)}, f32[16,1152]{1,0:T(8,128)S(1)}, u32[]{:S(2)}, u32[]{:S(2)}) %collective-permute-start.1) | collective-permute-done | bytes 73760 | tf_op jit(solution)/shard_map/ppermute | solution.py:45
  32.7 6.2 %collective-permute-start.3 = (f32[128,1152]{1,0:T(8,128)S(1)}, f32[128,1152]{1,0:T(8,128)S(1)}, u32[]{:S(2)}, u32[]{:S(2)}) collective-permute-start(f32[128,1152]{1,0:T(8,128)S(1)} %get-tuple-element.22.a_ref), channel_id=1, source_target_pairs={{0,32},{32,0},{1,33},{33,1},{2,34},{34,2},{3,35},{35,3},{4,36},{36... | collective-permute-start | bytes 1769480 | tf_op jit(solution)/shard_map/ppermute | solution.py:45
  38.9 4.0 %all-to-all-start.1 = ((f32[4,64,1152]{2,1,0:T(8,128)}), f32[4,64,1152]{2,1,0:T(8,128)S(1)}, u32[]{:S(2)}, u32[]{:S(2)}) async-start(f32[4,64,1152]{2,1,0:T(8,128)} %bitcast.4), calls=%async_computation.1 | async-start | bytes 2359296 | tf_op jit(solution)/shard_map/all_to_all | solution.py:49
  43.0 3.1 %collective-permute-start.4 = (f32[128,1152]{1,0:T(8,128)S(1)}, f32[128,1152]{1,0:T(8,128)S(1)}, u32[]{:S(2)}, u32[]{:S(2)}) collective-permute-start(f32[128,1152]{1,0:T(8,128)S(1)} %get-tuple-element.22.a_ref), channel_id=1, source_target_pairs={{0,16},{16,0},{1,17},{17,1},{2,18},{18,2},{3,19},{19,3},{4,20},{20... | collective-permute-start | bytes 1769480 | tf_op jit(solution)/shard_map/ppermute | solution.py:45
  46.0 6.0 %collective-permute-done.3.b_ref = f32[128,1152]{1,0:T(8,128)S(1)} collective-permute-done((f32[128,1152]{1,0:T(8,128)S(1)}, f32[128,1152]{1,0:T(8,128)S(1)}, u32[]{:S(2)}, u32[]{:S(2)}) %collective-permute-start.3) | collective-permute-done | bytes 589856 | tf_op jit(solution)/shard_map/ppermute | solution.py:45
  52.0 3.0 %collective-permute-start.5 = (f32[128,1152]{1,0:T(8,128)S(1)}, f32[128,1152]{1,0:T(8,128)S(1)}, u32[]{:S(2)}, u32[]{:S(2)}) collective-permute-start(f32[128,1152]{1,0:T(8,128)S(1)} %collective-permute-done.3.b_ref), channel_id=1, source_target_pairs={{0,16},{16,0},{1,17},{17,1},{2,18},{18,2},{3,19},{19,3},{4,20},{20... | collective-permute-start | bytes 1769480 | tf_op jit(solution)/shard_map/ppermute | solution.py:45
  55.2 3.1 %all-to-all-done.1 = f32[4,64,1152]{2,1,0:T(8,128)S(1)} async-done(((f32[4,64,1152]{2,1,0:T(8,128)}), f32[4,64,1152]{2,1,0:T(8,128)S(1)}, u32[]{:S(2)}, u32[]{:S(2)}) %all-to-all-start.1) | async-done | bytes 1179680 | tf_op jit(solution)/shard_map/all_to_all | solution.py:49
  60.2 4.7 %shard_map.51 = (f32[256,512]{1,0:T(8,128)S(1)}, f32[256,1152]{1,0:T(8,128)}, f32[64,128]{1,0:T(8,128)}) custom-call(s32[2]{0:T(128)S(1)} %pad_add_fusion.place, f32[256,1152]{1,0:T(8,128)S(1)} %bitcast.14, f32[128,1152]{1,0:T(8,128)S(1)} %get-tuple-element.22.a_ref, f32[128,1152]{1,0:T(8,128)S(1)} %collective-permute-done.3.b_ref, ...), custom_call_target="tpu_custom_call" | custom-call | flops 1358954496 | bytes 5275656 | tf_op jit(solution)/shard_map/pallas_call | solution.py:32
  65.0 4.0 %collective-permute-start.6 = (f32[256,1152]{1,0:T(8,128)}, f32[256,1152]{1,0:T(8,128)}, u32[]{:S(2)}, u32[]{:S(2)}) collective-permute-start(f32[256,1152]{1,0:T(8,128)} %get-tuple-element.24), channel_id=1, source_target_pairs={{0,16},{16,0},{1,17},{17,1},{2,18},{18,2},{3,19},{19,3},{4,20},{20... | collective-permute-start | bytes 3538952 | tf_op jit(solution)/shard_map/ppermute | solution.py:45
  68.9 7.2 %all-to-all-start.3 = ((f32[64,1,128]{2,1,0:T(1,128)}), f32[64,1,128]{2,1,0:T(1,128)S(1)}, u32[]{:S(2)}, u32[]{:S(2)}) async-start(f32[64,1,128]{2,1,0:T(1,128)} %bitcast.9), calls=%async_computation.3 | async-start | bytes 65536 | tf_op jit(solution)/shard_map/all_to_all | solution.py:49
  80.3 5.2 %all-to-all-done.3 = f32[64,1,128]{2,1,0:T(1,128)S(1)} async-done(((f32[64,1,128]{2,1,0:T(1,128)}), f32[64,1,128]{2,1,0:T(1,128)S(1)}, u32[]{:S(2)}, u32[]{:S(2)}) %all-to-all-start.3) | async-done | bytes 32800 | tf_op jit(solution)/shard_map/all_to_all | solution.py:49
  85.5 3.5 %all-to-all-start.2 = ((f32[4,64,1152]{2,1,0:T(8,128)}), f32[4,64,1152]{2,1,0:T(8,128)S(1)}, u32[]{:S(2)}, u32[]{:S(2)}) async-start(f32[4,64,1152]{2,1,0:T(8,128)} %bitcast.17), calls=%async_computation.2 | async-start | bytes 2359296 | tf_op jit(solution)/shard_map/all_to_all | solution.py:49
  89.0 2.6 %shard_map.53 = (f32[128,1152]{1,0:T(8,128)S(1)}, f32[128,1152]{1,0:T(8,128)}) custom-call(f32[256,512]{1,0:T(8,128)S(1)} %get-tuple-element.23.slope_ref, f32[256,1152]{1,0:T(8,128)S(1)} %bitcast.15, f32[256,1152]{1,0:T(8,128)} %collective-permute-done.6.other_ref), custom_call_target="tpu_custom_call" | custom-call | flops 452984832 | bytes 4063232 | tf_op jit(solution)/shard_map/pallas_call | solution.py:32
  91.6 2.3 %collective-permute-start.7 = (f32[128,1152]{1,0:T(8,128)}, f32[128,1152]{1,0:T(8,128)S(1)}, u32[]{:S(2)}, u32[]{:S(2)}) collective-permute-start(f32[128,1152]{1,0:T(8,128)} %get-tuple-element.26), channel_id=1, source_target_pairs={{0,32},{32,0},{1,33},{33,1},{2,34},{34,2},{3,35},{35,3},{4,36},{36... | collective-permute-start | bytes 1769480 | tf_op jit(solution)/shard_map/ppermute | solution.py:45
  94.0 11.0 %all-to-all-done.2 = f32[4,64,1152]{2,1,0:T(8,128)S(1)} async-done(((f32[4,64,1152]{2,1,0:T(8,128)}), f32[4,64,1152]{2,1,0:T(8,128)S(1)}, u32[]{:S(2)}, u32[]{:S(2)}) %all-to-all-start.2) | async-done | bytes 1179680 | tf_op jit(solution)/shard_map/all_to_all | solution.py:49
  105.0 3.1 %collective-permute-done.7.received_ref = f32[128,1152]{1,0:T(8,128)S(1)} collective-permute-done((f32[128,1152]{1,0:T(8,128)}, f32[128,1152]{1,0:T(8,128)S(1)}, u32[]{:S(2)}, u32[]{:S(2)}) %collective-permute-start.7) | collective-permute-done | bytes 589856 | tf_op jit(solution)/shard_map/ppermute | solution.py:45
  109.0 4.7 %all-to-all-start.4 = ((f32[8,152,128]{2,1,0:T(8,128)}), f32[8,152,128]{2,1,0:T(8,128)S(1)}, u32[]{:S(2)}, u32[]{:S(2)}) async-start(f32[8,152,128]{2,1,0:T(8,128)} %get-tuple-element.28), calls=%async_computation.4 | async-start | bytes 1245184 | tf_op jit(solution)/shard_map/all_to_all | solution.py:49
  113.7 2.1 %collective-permute-start.8 = (f32[16,1152]{1,0:T(8,128)S(1)}, f32[16,1152]{1,0:T(8,128)S(1)}, u32[]{:S(2)}, u32[]{:S(2)}) collective-permute-start(f32[16,1152]{1,0:T(8,128)S(1)} %get-tuple-element.31), channel_id=1, source_target_pairs={{0,12},{4,0},{8,4},{12,8},{1,13},{5,1},{9,5},{13,9},{2,14},{6,2},{... | collective-permute-start | bytes 221192 | tf_op jit(solution)/shard_map/ppermute | solution.py:45
  115.9 5.4 %collective-permute-start.9 = (f32[16,1152]{1,0:T(8,128)S(1)}, f32[16,1152]{1,0:T(8,128)S(1)}, u32[]{:S(2)}, u32[]{:S(2)}) collective-permute-start(f32[16,1152]{1,0:T(8,128)S(1)} %get-tuple-element.32), channel_id=1, source_target_pairs={{0,8},{4,12},{8,0},{12,4},{1,9},{5,13},{9,1},{13,5},{2,10},{6,14},... | collective-permute-start | bytes 221192 | tf_op jit(solution)/shard_map/ppermute | solution.py:45
  123.2 2.5 %collective-permute-done.9.z2 = f32[16,1152]{1,0:T(8,128)S(1)} collective-permute-done((f32[16,1152]{1,0:T(8,128)S(1)}, f32[16,1152]{1,0:T(8,128)S(1)}, u32[]{:S(2)}, u32[]{:S(2)}) %collective-permute-start.9) | collective-permute-done | bytes 73760 | tf_op jit(solution)/shard_map/ppermute | solution.py:45
  125.7 4.0 %collective-permute-done.10.z3 = f32[16,1152]{1,0:T(8,128)S(1)} collective-permute-done((f32[16,1152]{1,0:T(8,128)S(1)}, f32[16,1152]{1,0:T(8,128)S(1)}, u32[]{:S(2)}, u32[]{:S(2)}) %collective-permute-start.10) | collective-permute-done | bytes 73760 | tf_op jit(solution)/shard_map/ppermute | solution.py:45
  (34 shorter events, 18.7 us)
Async XLA Ops:
  0.6 0.9 copy-start.4
  1.5 0.9 copy-start.6
  3.4 28.2 %all-to-all-start = ((f32[8,16,1152]{2,1,0:T(8,128)}), f32[8,16,1152]{2,1,0:T(8,128)S(1)}, u32[]{:S(2)}, u32[]{:S(2)}) async-start(f32[8,16,1152]{2,1,0:T(8,128)} %bitcast.2), calls=%async_computation | async-start | bytes 1179648 | tf_op jit(solution)/shard_map/all_to_all | solution.py:49
  11.0 16.8 %collective-permute-start.2 = (f32[16,1152]{1,0:T(8,128)S(1)}, f32[16,1152]{1,0:T(8,128)S(1)}, u32[]{:S(2)}, u32[]{:S(2)}) collective-permute-start(f32[16,1152]{1,0:T(8,128)S(1)} %get-tuple-element.19.z0), channel_id=1, source_target_pairs={{0,12},{4,0},{8,4},{12,8},{1,13},{5,1},{9,5},{13,9},{2,14},{6,2},{... | collective-permute-start | bytes 221192 | tf_op jit(solution)/shard_map/ppermute | solution.py:45
  21.7 9.8 %collective-permute-start.1 = (f32[16,1152]{1,0:T(8,128)S(1)}, f32[16,1152]{1,0:T(8,128)S(1)}, u32[]{:S(2)}, u32[]{:S(2)}) collective-permute-start(f32[16,1152]{1,0:T(8,128)S(1)} %get-tuple-element.19.z0), channel_id=1, source_target_pairs={{0,8},{4,12},{8,0},{12,4},{1,9},{5,13},{9,1},{13,5},{2,10},{6,14},... | collective-permute-start | bytes 221192 | tf_op jit(solution)/shard_map/ppermute | solution.py:45
  23.6 8.0 %collective-permute-start = (f32[16,1152]{1,0:T(8,128)S(1)}, f32[16,1152]{1,0:T(8,128)S(1)}, u32[]{:S(2)}, u32[]{:S(2)}) collective-permute-start(f32[16,1152]{1,0:T(8,128)S(1)} %get-tuple-element.19.z0), channel_id=1, source_target_pairs={{0,4},{4,8},{8,12},{12,0},{1,5},{5,9},{9,13},{13,1},{2,6},{6,10},{... | collective-permute-start | bytes 221192 | tf_op jit(solution)/shard_map/ppermute | solution.py:45
  32.7 19.3 %collective-permute-start.3 = (f32[128,1152]{1,0:T(8,128)S(1)}, f32[128,1152]{1,0:T(8,128)S(1)}, u32[]{:S(2)}, u32[]{:S(2)}) collective-permute-start(f32[128,1152]{1,0:T(8,128)S(1)} %get-tuple-element.22.a_ref), channel_id=1, source_target_pairs={{0,32},{32,0},{1,33},{33,1},{2,34},{34,2},{3,35},{35,3},{4,36},{36... | collective-permute-start | bytes 1769480 | tf_op jit(solution)/shard_map/ppermute | solution.py:45
  38.9 19.4 %all-to-all-start.1 = ((f32[4,64,1152]{2,1,0:T(8,128)}), f32[4,64,1152]{2,1,0:T(8,128)S(1)}, u32[]{:S(2)}, u32[]{:S(2)}) async-start(f32[4,64,1152]{2,1,0:T(8,128)} %bitcast.4), calls=%async_computation.1 | async-start | bytes 2359296 | tf_op jit(solution)/shard_map/all_to_all | solution.py:49
  43.0 12.2 %collective-permute-start.4 = (f32[128,1152]{1,0:T(8,128)S(1)}, f32[128,1152]{1,0:T(8,128)S(1)}, u32[]{:S(2)}, u32[]{:S(2)}) collective-permute-start(f32[128,1152]{1,0:T(8,128)S(1)} %get-tuple-element.22.a_ref), channel_id=1, source_target_pairs={{0,16},{16,0},{1,17},{17,1},{2,18},{18,2},{3,19},{19,3},{4,20},{20... | collective-permute-start | bytes 1769480 | tf_op jit(solution)/shard_map/ppermute | solution.py:45
  52.0 6.3 %collective-permute-start.5 = (f32[128,1152]{1,0:T(8,128)S(1)}, f32[128,1152]{1,0:T(8,128)S(1)}, u32[]{:S(2)}, u32[]{:S(2)}) collective-permute-start(f32[128,1152]{1,0:T(8,128)S(1)} %collective-permute-done.3.b_ref), channel_id=1, source_target_pairs={{0,16},{16,0},{1,17},{17,1},{2,18},{18,2},{3,19},{19,3},{4,20},{20... | collective-permute-start | bytes 1769480 | tf_op jit(solution)/shard_map/ppermute | solution.py:45
  58.3 0.8 copy-start.1
  59.2 1.1 copy-start.2
  65.0 24.0 %collective-permute-start.6 = (f32[256,1152]{1,0:T(8,128)}, f32[256,1152]{1,0:T(8,128)}, u32[]{:S(2)}, u32[]{:S(2)}) collective-permute-start(f32[256,1152]{1,0:T(8,128)} %get-tuple-element.24), channel_id=1, source_target_pairs={{0,16},{16,0},{1,17},{17,1},{2,18},{18,2},{3,19},{19,3},{4,20},{20... | collective-permute-start | bytes 3538952 | tf_op jit(solution)/shard_map/ppermute | solution.py:45
  68.9 16.5 %all-to-all-start.3 = ((f32[64,1,128]{2,1,0:T(1,128)}), f32[64,1,128]{2,1,0:T(1,128)S(1)}, u32[]{:S(2)}, u32[]{:S(2)}) async-start(f32[64,1,128]{2,1,0:T(1,128)} %bitcast.9), calls=%async_computation.3 | async-start | bytes 65536 | tf_op jit(solution)/shard_map/all_to_all | solution.py:49
  76.2 1.1 copy-start.3
  79.3 1.0 copy-start
  85.5 19.5 %all-to-all-start.2 = ((f32[4,64,1152]{2,1,0:T(8,128)}), f32[4,64,1152]{2,1,0:T(8,128)S(1)}, u32[]{:S(2)}, u32[]{:S(2)}) async-start(f32[4,64,1152]{2,1,0:T(8,128)} %bitcast.17), calls=%async_computation.2 | async-start | bytes 2359296 | tf_op jit(solution)/shard_map/all_to_all | solution.py:49
  91.6 16.4 %collective-permute-start.7 = (f32[128,1152]{1,0:T(8,128)}, f32[128,1152]{1,0:T(8,128)S(1)}, u32[]{:S(2)}, u32[]{:S(2)}) collective-permute-start(f32[128,1152]{1,0:T(8,128)} %get-tuple-element.26), channel_id=1, source_target_pairs={{0,32},{32,0},{1,33},{33,1},{2,34},{34,2},{3,35},{35,3},{4,36},{36... | collective-permute-start | bytes 1769480 | tf_op jit(solution)/shard_map/ppermute | solution.py:45
  109.0 20.6 %copy-start.5 = (f32[16,1152]{1,0:T(8,128)S(1)}, f32[16,1152]{1,0:T(8,128)}, u32[]{:S(2)}) copy-start(f32[16,1152]{1,0:T(8,128)} %emb_ref.3) | copy-start | bytes 221188
  109.0 23.2 %copy-start.7 = (f32[16,1152]{1,0:T(8,128)S(1)}, f32[16,1152]{1,0:T(8,128)}, u32[]{:S(2)}) copy-start(f32[16,1152]{1,0:T(8,128)} %emb_ref.2) | copy-start | bytes 221188
  109.0 23.1 %all-to-all-start.4 = ((f32[8,152,128]{2,1,0:T(8,128)}), f32[8,152,128]{2,1,0:T(8,128)S(1)}, u32[]{:S(2)}, u32[]{:S(2)}) async-start(f32[8,152,128]{2,1,0:T(8,128)} %get-tuple-element.28), calls=%async_computation.4 | async-start | bytes 1245184 | tf_op jit(solution)/shard_map/all_to_all | solution.py:49
  113.7 9.4 %collective-permute-start.8 = (f32[16,1152]{1,0:T(8,128)S(1)}, f32[16,1152]{1,0:T(8,128)S(1)}, u32[]{:S(2)}, u32[]{:S(2)}) collective-permute-start(f32[16,1152]{1,0:T(8,128)S(1)} %get-tuple-element.31), channel_id=1, source_target_pairs={{0,12},{4,0},{8,4},{12,8},{1,13},{5,1},{9,5},{13,9},{2,14},{6,2},{... | collective-permute-start | bytes 221192 | tf_op jit(solution)/shard_map/ppermute | solution.py:45
  115.9 9.8 %collective-permute-start.9 = (f32[16,1152]{1,0:T(8,128)S(1)}, f32[16,1152]{1,0:T(8,128)S(1)}, u32[]{:S(2)}, u32[]{:S(2)}) collective-permute-start(f32[16,1152]{1,0:T(8,128)S(1)} %get-tuple-element.32), channel_id=1, source_target_pairs={{0,8},{4,12},{8,0},{12,4},{1,9},{5,13},{9,1},{13,5},{2,10},{6,14},... | collective-permute-start | bytes 221192 | tf_op jit(solution)/shard_map/ppermute | solution.py:45
  121.2 8.4 %collective-permute-start.10 = (f32[16,1152]{1,0:T(8,128)S(1)}, f32[16,1152]{1,0:T(8,128)S(1)}, u32[]{:S(2)}, u32[]{:S(2)}) collective-permute-start(f32[16,1152]{1,0:T(8,128)S(1)} %get-tuple-element.33), channel_id=1, source_target_pairs={{0,4},{4,8},{8,12},{12,0},{1,5},{5,9},{9,13},{13,1},{2,6},{6,10},{... | collective-permute-start | bytes 221192 | tf_op jit(solution)/shard_map/ppermute | solution.py:45

commit v3 on v2

v3 whole, which is shorter than its diff:
```python
import jax
import jax.numpy as jnp
from jax import lax
from jax.experimental import pallas as pl
from jax.experimental.pallas import tpu as pltpu
from jax.sharding import Mesh, PartitionSpec as P

LOGIT_MULT = 16.0
LOGIT_SHIFT = -10.0
EPSILON = 1e-06

AXES = ("y", "zl", "c", "zh", "x")
SIZES = (8, 2, 2, 4, 4)
NY, NZH, NX = 8, 4, 4
ROWS, FEATURES, LANES = 16, 1152, 128
COLS = FEATURES // LANES
PACK = COLS * ROWS
PAIRS = 8192
F32, BF16 = jnp.float32, jnp.bfloat16

VMEM = pl.BlockSpec(memory_space=pltpu.VMEM)
ANY = pl.BlockSpec(memory_space=pl.ANY)
SMEM = pl.BlockSpec(memory_space=pltpu.SMEM)


def shape(*dims):
    return jax.ShapeDtypeStruct(dims, F32)


def call(kernel, ins, outs, in_specs=None, out_specs=None, flops=0, **kw):
    moved = 4 * sum(a.size for a in list(ins) + list(outs))
    return pl.pallas_call(
        kernel,
        out_shape=outs,
        in_specs=in_specs or [VMEM] * len(ins),
        out_specs=out_specs or [VMEM] * len(outs),
        cost_estimate=pl.CostEstimate(flops=flops, bytes_accessed=moved, transcendentals=0),
        compiler_params=pltpu.CompilerParams(vmem_limit_bytes=24 * 2**20),
        **kw,
    )(*ins)


def exchange(values, axes):
    return lax.all_to_all(values, axes, 0, 0, tiled=True)


def turned(values, axis, step):
    count = lax.axis_size(axis)
    pairs = [(c * count + i, c * count + (i + (1 - 2 * c) * step) % count) for c in range(2) for i in range(count)]
    return lax.ppermute(values, ("c", axis), pairs)


def planes(values, step):
    pairs = []
    for c in range(2):
        for z in range(2 * NZH):
            to = (z + (1 - 2 * c) * step) % (2 * NZH)
            pairs.append((((z % 2) * 2 + c) * NZH + z // 2, ((to % 2) * 2 + c) * NZH + to // 2))
    return lax.ppermute(values, ("zl", "c", "zh"), pairs)


def other_core(values):
    return lax.ppermute(values, "c", [(0, 1), (1, 0)])


def ring_gather(values, axis):
    back = turned(values, axis, 1)
    ahead = turned(values, axis, -1)
    return values, back, ahead, turned(back, axis, 1)


def normalize(values):
    length = jnp.sqrt(jnp.sum(values * values, axis=1, keepdims=True) + EPSILON)
    return values / length, length


def project_back(unit, direction, length):
    inner = jnp.sum(unit * direction, axis=1, keepdims=True)
    return (direction - unit * inner) / length


def halves(values):
    high = values.astype(BF16)
    return high, (values - high.astype(F32)).astype(BF16)


def dot3(left, right, dims):
    def dot(a, b):
        return lax.dot_general(a, b, (dims, ((), ())), preferred_element_type=F32)

    return dot(left[1], right[0]) + dot(left[0], right[1]) + dot(left[0], right[0])


def normalize_kernel(image_ref, text_ref, image_out, text_out):
    image_out[...] = normalize(image_ref[...])[0]
    text_unit = normalize(text_ref[...])[0]
    for y in range(NY):
        text_out[pl.ds(y * ROWS, ROWS), :] = text_unit


def stack_kernel(*refs):
    for k, part in enumerate(refs[:-1]):
        refs[-1][pl.ds(k * ROWS, ROWS), :] = part[...]


def tie_kernel(*refs):
    pass


def stacked(*refs):
    return jnp.concatenate([ref[...] for ref in refs], axis=0)


def logits_kernel(place, i0, i1, i2, i3, a_ref, b_ref, c_ref, d_ref, slope_out, other_out, loss_out):
    image = halves(stacked(i0, i1, i2, i3))
    quarter = a_ref.shape[0]
    count = NX * i0.shape[0]
    row = lax.broadcasted_iota(jnp.int32, (count, quarter), 0)
    column = lax.broadcasted_iota(jnp.int32, (count, quarter), 1) - place[0]
    matched = (row == column) & (row < ROWS)
    total = jnp.zeros((), F32)
    for k, ref in enumerate((c_ref, d_ref, a_ref, b_ref)):
        logits = LOGIT_MULT * dot3(image, halves(ref[...]), ((1,), (1,))) + LOGIT_SHIFT
        if ref is a_ref:
            logits = jnp.where(matched, -logits, logits)
        small = jnp.exp(-jnp.abs(logits))
        total += jnp.sum(jnp.maximum(logits, 0.0) + jnp.log1p(small))
        slope = jnp.where(logits >= 0.0, 1.0, small) / (1.0 + small) * (LOGIT_MULT / PAIRS)
        if ref is a_ref:
            slope = jnp.where(matched, -slope, slope)
        slope_out[:, pl.ds((k + 2) % 4 * quarter, quarter)] = slope
        if k < 2:
            other_out[pl.ds(k * quarter, quarter), :] = dot3(halves(slope), image, ((0,), (0,)))
    loss_out[...] = jnp.full(loss_out.shape, total)


def image_kernel(slope_ref, a_ref, b_ref, c_ref, d_ref, *outs):
    quarter = a_ref.shape[0]
    total = None
    for k, ref in enumerate((a_ref, b_ref, c_ref, d_ref)):
        slope = slope_ref[:, pl.ds(k * quarter, quarter)]
        term = dot3(halves(slope), halves(ref[...]), ((1,), (0,)))
        total = term if total is None else total + term
    rows = total.shape[0] // NX
    for k, out in enumerate(outs):
        out[...] = total[k * rows : (k + 1) * rows]


def text_kernel(slope_ref, i0, i1, i2, i3, other_ref, keep_out, send_out):
    image = halves(stacked(i0, i1, i2, i3))
    quarter = keep_out.shape[0]
    for k, out in ((1, send_out), (0, keep_out)):
        rows = pl.ds(k * quarter, quarter)
        out[...] = dot3(halves(slope_ref[:, rows]), image, ((0,), (0,))) + other_ref[rows, :]


def add_kernel(left, right, out):
    out[...] = left[...] + right[...]


def join_kernel(x0, x1, x2, keep_ref, received_ref, losses_ref, packed_out, *zs):
    for k, out in enumerate(zs):
        rows = pl.ds(k * ROWS, ROWS)
        out[...] = x0[rows, :] + (x1[rows, :] + x2[rows, :])
    loss = jnp.sum(losses_ref[:, 0:1])
    for y in range(NY):
        rows = pl.ds(y * ROWS, ROWS)
        for k in range(COLS):
            lanes = pl.ds(k * LANES, LANES)
            packed_out[y, pl.ds(k * ROWS, ROWS), :] = keep_ref[rows, lanes] + received_ref[rows, lanes]
        packed_out[y, pl.ds(PACK, 8), :] = jnp.full((8, LANES), loss)


def image_grad_kernel(emb_ref, z0, z1, z2, out):
    unit, length = normalize(emb_ref[...])
    out[...] = project_back(unit, z0[...] + (z1[...] + z2[...]), length)


def text_grad_kernel(emb_ref, packed_ref, out, loss_out):
    unit, length = normalize(emb_ref[...])
    total = packed_ref[0]
    for y in range(1, NY):
        total = total + packed_ref[y]
    direction = jnp.concatenate([total[k * ROWS : (k + 1) * ROWS] for k in range(COLS)], axis=1)
    out[...] = project_back(unit, direction, length)
    loss_out[...] = total[PACK:] / PAIRS


def on_device(image_emb, text_emb):
    rows, features = image_emb.shape
    image_unit, text_tiled = call(
        normalize_kernel, (image_emb, text_emb), [shape(rows, features), shape(NY * rows, features)]
    )
    text_y = exchange(text_tiled, "y")
    (image_z,) = call(stack_kernel, ring_gather(image_unit, "zh"), [shape(NZH * rows, features)])
    images = ring_gather(image_z, "x")
    (text_a,) = call(
        tie_kernel, (text_y, image_z), [shape(*text_y.shape)], [ANY] * 2, [ANY], input_output_aliases={0: 0}
    )
    text_b = planes(text_a, -1)
    text_c = other_core(text_a)
    text_d = other_core(text_b)
    texts = (text_a, text_b, text_c, text_d)

    place = (lax.axis_index("y") * rows).astype(jnp.int32).reshape(1)
    part, quarter = image_z.shape[0], text_a.shape[0]
    product = 2 * NX * part * quarter * features * 3
    slope, other, loss = call(
        logits_kernel,
        (place, *images, *texts),
        [shape(NX * part, 4 * quarter), shape(2 * quarter, features), shape(64, LANES)],
        in_specs=[SMEM] + [VMEM] * 8,
        flops=6 * product,
    )
    received = other_core(other)
    xs = call(image_kernel, (slope, *texts), [shape(part, features)] * NX, flops=4 * product)
    relay = turned(xs[3], "x", -1)
    ahead = turned(xs[2], "x", 1)
    keep, send = call(
        text_kernel, (slope, *images, received), [shape(quarter, features)] * 2, flops=2 * product
    )
    received = planes(send, 1)
    (relay,) = call(add_kernel, (xs[1], relay), [shape(part, features)])
    back = turned(relay, "x", -1)
    losses = exchange(loss, ("zl", "c", "zh", "x"))
    packed, *zs = call(
        join_kernel,
        (xs[0], back, ahead, keep, received, losses),
        [shape(NY, PACK + 8, LANES)] + [shape(rows, features)] * NZH,
    )
    packed = exchange(packed, "y")
    relay = turned(zs[3], "zh", -1)
    ahead = turned(zs[2], "zh", 1)
    (relay,) = call(add_kernel, (zs[1], relay), [shape(rows, features)])
    back = turned(relay, "zh", -1)
    (image_grad,) = call(image_grad_kernel, (image_emb, zs[0], back, ahead), [shape(rows, features)])
    text_grad, loss = call(text_grad_kernel, (text_emb, packed), [shape(rows, features), shape(8, LANES)])
    return loss[0, 0], image_grad, text_grad


def solution(mesh):
    split = Mesh(mesh.devices.reshape(SIZES), AXES)
    return jax.shard_map(
        on_device,
        mesh=split,
        in_specs=(P(AXES, None), P(AXES, None)),
        out_specs=(P(), P(AXES, None), P(AXES, None)),
        check_vma=False,
    )
```

time: 135 us -> 131 us (0.970)
  waiting for transfers between devices: 40.3 us -> 17.9 us
  blocking collectives: 0 us -> 14.3 us
  starting transfers between devices: 72 us -> 85.2 us
  Pallas kernels: 14.1 us -> 10 us
  local copies, waits for them, and re-layouts: 6.25 us -> 2.28 us
    ppermute x11 -> x17, starting transfers between devices: 44.9 us -> 71.4 us  [the longest x12 46.6 us: turned(): return lax.ppermute(values, ('c', axis), pairs)]
    all_to_all x5 -> x2, waiting for transfers between devices: 21 us -> 4.3 us  [exchange(): return lax.all_to_all(values, axes, 0, 0, tiled=True)]
    all_to_all x0 -> x1, blocking collectives: none -> 14.3 us  [exchange(): return lax.all_to_all(values, axes, 0, 0, tiled=True)]
    all_to_all x5 -> x2, starting transfers between devices: 27.1 us -> 13.8 us  [exchange(): return lax.all_to_all(values, axes, 0, 0, tiled=True)]
    ppermute x11 -> x17, waiting for transfers between devices: 19.3 us -> 13.6 us  [the longest x12 12.1 us: turned(): return lax.ppermute(values, ('c', axis), pairs)]
    pallas_call x8 -> x11, Pallas kernels: 14.1 us -> 10 us  [call(): pl.pallas_call(kernel, out_shape=outs, in_specs=in_specs or [VMEM] * len(...]
    unnamed x16 -> x8, local copies, waits for them, and re-layouts: 5.74 us -> 1.77 us
  transfers between devices with their start and end apart: 16 -> 19, of which waited for: 10 -> 9; matrix products, arithmetic and copies ran while one was open for 0% -> 0% of each run, Pallas kernels for 4% -> 3%
where the time goes in v3:
time: 131 us
  starting transfers between devices  85.2 us (65%)
  waiting for transfers between devices  17.9 us (14%)
  blocking collectives  14.3 us (11%)
  Pallas kernels  10 us (8%)
  local copies, waits for them, and re-layouts  2.28 us (2%)
    ppermute x12, starting transfers between devices, turned(): return lax.ppermute(values, ('c', axis), pairs)  46.6 us
    ppermute x3, starting transfers between devices, other_core(): return lax.ppermute(values, 'c', [(0, 1), (1, 0)])  15.5 us
    all_to_all x1, blocking collectives, exchange(): return lax.all_to_all(values, axes, 0, 0, tiled=True)  14.3 us
    all_to_all x2, starting transfers between devices, exchange(): return lax.all_to_all(values, axes, 0, 0, tiled=True)  13.8 us
    ppermute x12, waiting for transfers between devices, turned(): return lax.ppermute(values, ('c', axis), pairs)  12.1 us
    pallas_call x11, Pallas kernels, call(): pl.pallas_call(kernel, out_shape=outs, in_specs=in_specs or [VMEM] * len(...  10 us
    ppermute x2, starting transfers between devices, planes(): return lax.ppermute(values, ('zl', 'c', 'zh'), pairs)  9.31 us
    all_to_all x2, waiting for transfers between devices, exchange(): return lax.all_to_all(values, axes, 0, 0, tiled=True)  4.3 us
  transfers between devices with their start and end apart: 19, of which 9 were waited for; matrix products, arithmetic and copies ran while one was open for 0% of the time, Pallas kernels for 3%

profile of v3, /device:TPU:1, one launch (start us, length us, event | category | flops | bytes accessed | tf_op | source)
XLA Modules:
  0.0 130.6 jit_solution(12039442188206176969)
XLA Ops:
  3.4 7.7 %all-to-all-start = ((f32[8,16,1152]{2,1,0:T(8,128)}), f32[8,16,1152]{2,1,0:T(8,128)S(1)}, u32[]{:S(2)}, u32[]{:S(2)}) async-start(f32[8,16,1152]{2,1,0:T(8,128)} %bitcast.1), calls=%async_computation | async-start | bytes 1179648 | tf_op jit(solution)/shard_map/all_to_all | solution.py:44
  11.0 10.6 %collective-permute-start = (f32[16,1152]{1,0:T(8,128)S(1)}, f32[16,1152]{1,0:T(8,128)S(1)}, u32[]{:S(2)}, u32[]{:S(2)}) collective-permute-start(f32[16,1152]{1,0:T(8,128)S(1)} %get-tuple-element.21.refs_0_), channel_id=1, source_target_pairs={{0,4},{4,8},{8,12},{12,0},{16,28},{20,16},{24,20},{28,24},{1,5},{5... | collective-permute-start | bytes 221192 | tf_op jit(solution)/shard_map/ppermute | solution.py:50
  21.7 1.9 %collective-permute-start.1 = (f32[16,1152]{1,0:T(8,128)S(1)}, f32[16,1152]{1,0:T(8,128)S(1)}, u32[]{:S(2)}, u32[]{:S(2)}) collective-permute-start(f32[16,1152]{1,0:T(8,128)S(1)} %get-tuple-element.21.refs_0_), channel_id=1, source_target_pairs={{0,12},{4,0},{8,4},{12,8},{16,20},{20,24},{24,28},{28,16},{1,13},{... | collective-permute-start | bytes 221192 | tf_op jit(solution)/shard_map/ppermute | solution.py:50
  23.6 5.5 %collective-permute-start.2 = (f32[16,1152]{1,0:T(8,128)S(1)}, f32[16,1152]{1,0:T(8,128)S(1)}, u32[]{:S(2)}, u32[]{:S(2)}) collective-permute-start(f32[16,1152]{1,0:T(8,128)S(1)} %collective-permute-done.refs_1_), channel_id=1, source_target_pairs={{0,4},{4,8},{8,12},{12,0},{16,28},{20,16},{24,20},{28,24},{1,5},{5... | collective-permute-start | bytes 221192 | tf_op jit(solution)/shard_map/ppermute | solution.py:50
  30.5 4.0 %collective-permute-start.6 = (f32[128,1152]{1,0:T(8,128)S(1)}, f32[128,1152]{1,0:T(8,128)S(1)}, u32[]{:S(2)}, u32[]{:S(2)}) collective-permute-start(f32[128,1152]{1,0:T(8,128)S(1)} %shard_map.51.a_ref), channel_id=1, source_target_pairs={{0,44},{32,0},{4,32},{36,4},{8,36},{40,8},{12,40},{44,12},{16,48},... | collective-permute-start | bytes 1769480 | tf_op jit(solution)/shard_map/ppermute | solution.py:59
  34.5 4.4 %collective-permute-start.3 = (f32[64,1152]{1,0:T(8,128)S(1)}, f32[64,1152]{1,0:T(8,128)S(1)}, u32[]{:S(2)}, u32[]{:S(2)}) collective-permute-start(f32[64,1152]{1,0:T(8,128)S(1)} %shard_map.50.refs_1_.i0), channel_id=1, source_target_pairs={{0,1},{1,2},{2,3},{3,0},{16,19},{17,16},{18,17},{19,18},{4,5},{5,6... | collective-permute-start | bytes 884744 | tf_op jit(solution)/shard_map/ppermute | solution.py:50
  38.9 8.2 %collective-permute-start.7 = (f32[128,1152]{1,0:T(8,128)S(1)}, f32[128,1152]{1,0:T(8,128)S(1)}, u32[]{:S(2)}, u32[]{:S(2)}) collective-permute-start(f32[128,1152]{1,0:T(8,128)S(1)} %shard_map.51.a_ref), channel_id=1, source_target_pairs={{0,16},{16,0},{1,17},{17,1},{2,18},{18,2},{3,19},{19,3},{4,20},{20... | collective-permute-start | bytes 1769480 | tf_op jit(solution)/shard_map/ppermute | solution.py:63
  48.6 2.5 %collective-permute-start.8 = (f32[128,1152]{1,0:T(8,128)S(1)}, f32[128,1152]{1,0:T(8,128)S(1)}, u32[]{:S(2)}, u32[]{:S(2)}) collective-permute-start(f32[128,1152]{1,0:T(8,128)S(1)} %collective-permute-done.6.b_ref), channel_id=1, source_target_pairs={{0,16},{16,0},{1,17},{17,1},{2,18},{18,2},{3,19},{19,3},{4,20},{20... | collective-permute-start | bytes 1769480 | tf_op jit(solution)/shard_map/ppermute | solution.py:63
  51.1 3.1 %collective-permute-start.4 = (f32[64,1152]{1,0:T(8,128)S(1)}, f32[64,1152]{1,0:T(8,128)S(1)}, u32[]{:S(2)}, u32[]{:S(2)}) collective-permute-start(f32[64,1152]{1,0:T(8,128)S(1)} %shard_map.50.refs_1_.i0), channel_id=1, source_target_pairs={{0,3},{1,0},{2,1},{3,2},{16,17},{17,18},{18,19},{19,16},{4,7},{5,4... | collective-permute-start | bytes 884744 | tf_op jit(solution)/shard_map/ppermute | solution.py:50
  54.2 3.4 %collective-permute-start.5 = (f32[64,1152]{1,0:T(8,128)S(1)}, f32[64,1152]{1,0:T(8,128)S(1)}, u32[]{:S(2)}, u32[]{:S(2)}) collective-permute-start(f32[64,1152]{1,0:T(8,128)S(1)} %collective-permute-done.3.i1), channel_id=1, source_target_pairs={{0,1},{1,2},{2,3},{3,0},{16,19},{17,16},{18,17},{19,18},{4,5},{5,6... | collective-permute-start | bytes 884744 | tf_op jit(solution)/shard_map/ppermute | solution.py:50
  57.6 2.2 %collective-permute-done.4.i2 = f32[64,1152]{1,0:T(8,128)S(1)} collective-permute-done((f32[64,1152]{1,0:T(8,128)S(1)}, f32[64,1152]{1,0:T(8,128)S(1)}, u32[]{:S(2)}, u32[]{:S(2)}) %collective-permute-start.4) | collective-permute-done | bytes 294944 | tf_op jit(solution)/shard_map/ppermute | solution.py:50
  59.8 3.0 %collective-permute-done.5.i3 = f32[64,1152]{1,0:T(8,128)S(1)} collective-permute-done((f32[64,1152]{1,0:T(8,128)S(1)}, f32[64,1152]{1,0:T(8,128)S(1)}, u32[]{:S(2)}, u32[]{:S(2)}) %collective-permute-start.5) | collective-permute-done | bytes 294944 | tf_op jit(solution)/shard_map/ppermute | solution.py:50
  62.8 3.6 %shard_map.52 = (f32[256,512]{1,0:T(8,128)S(1)}, f32[256,1152]{1,0:T(8,128)S(1)}, f32[64,128]{1,0:T(8,128)S(1)}) custom-call(s32[1]{0:T(128)} %bitcast.place, f32[64,1152]{1,0:T(8,128)S(1)} %shard_map.50.refs_1_.i0, f32[64,1152]{1,0:T(8,128)S(1)} %collective-permute-done.3.i1, f32[64,1152]{1,0:T(8,128)S(1)} %collective-permute-done.4.i2, ...), custom_call_target="tpu_custom_call" | custom-call | flops 1358954496 | bytes 5275652 | tf_op jit(solution)/shard_map/pallas_call | solution.py:32
  66.4 4.8 %collective-permute-start.12 = (f32[256,1152]{1,0:T(8,128)S(1)}, f32[256,1152]{1,0:T(8,128)S(1)}, u32[]{:S(2)}, u32[]{:S(2)}) collective-permute-start(f32[256,1152]{1,0:T(8,128)S(1)} %get-tuple-element.28), channel_id=1, source_target_pairs={{0,16},{16,0},{1,17},{17,1},{2,18},{18,2},{3,19},{19,3},{4,20},{20... | collective-permute-start | bytes 3538952 | tf_op jit(solution)/shard_map/ppermute | solution.py:63
  71.1 2.0 %shard_map.53 = (f32[64,1152]{1,0:T(8,128)S(1)}, f32[64,1152]{1,0:T(8,128)S(1)}, f32[64,1152]{1,0:T(8,128)S(1)}, f32[64,1152]{1,0:T(8,128)S(1)}) custom-call(f32[256,512]{1,0:T(8,128)S(1)} %get-tuple-element.23.slope_ref, f32[128,1152]{1,0:T(8,128)S(1)} %shard_map.51.a_ref, f32[128,1152]{1,0:T(8,128)S(1)} %collective-permute-done.6.b_ref, ...), custom_call_target="tpu_custom_call" | custom-call | flops 905969664 | bytes 4063232 | tf_op jit(solution)/shard_map/pallas_call | solution.py:32
  75.8 5.3 %collective-permute-start.13 = (f32[128,1152]{1,0:T(8,128)S(1)}, f32[128,1152]{1,0:T(8,128)S(1)}, u32[]{:S(2)}, u32[]{:S(2)}) collective-permute-start(f32[128,1152]{1,0:T(8,128)S(1)} %get-tuple-element.30), channel_id=1, source_target_pairs={{0,32},{32,4},{4,36},{36,8},{8,40},{40,12},{12,44},{44,0},{16,60},... | collective-permute-start | bytes 1769480 | tf_op jit(solution)/shard_map/ppermute | solution.py:59
  81.2 4.6 %collective-permute-start.11 = (f32[64,1152]{1,0:T(8,128)S(1)}, f32[64,1152]{1,0:T(8,128)S(1)}, u32[]{:S(2)}, u32[]{:S(2)}) collective-permute-start(f32[64,1152]{1,0:T(8,128)S(1)} %get-tuple-element.27), channel_id=1, source_target_pairs={{0,1},{1,2},{2,3},{3,0},{16,19},{17,16},{18,17},{19,18},{4,5},{5,6... | collective-permute-start | bytes 884744 | tf_op jit(solution)/shard_map/ppermute | solution.py:50
  87.7 14.3 %all_to_all.27 = f32[64,1,128]{2,1,0:T(1,128)S(1)} all-to-all(f32[64,1,128]{2,1,0:T(1,128)S(1)} %bitcast.10), channel_id=1, replica_groups=mesh['y'=8,'zl'=2,'c'=2,'zh'=4,'x'=4] {'zl','c','zh','x'}, dimensions={0} | all-to-all | bytes 65536 | tf_op jit(solution)/shard_map/all_to_all | solution.py:44
  103.1 6.1 %all-to-all-start.2 = ((f32[8,152,128]{2,1,0:T(8,128)}), f32[8,152,128]{2,1,0:T(8,128)S(1)}, u32[]{:S(2)}, u32[]{:S(2)}) async-start(f32[8,152,128]{2,1,0:T(8,128)} %get-tuple-element.32), calls=%async_computation.2 | async-start | bytes 1245184 | tf_op jit(solution)/shard_map/all_to_all | solution.py:44
  109.2 2.3 %collective-permute-start.14 = (f32[16,1152]{1,0:T(8,128)S(1)}, f32[16,1152]{1,0:T(8,128)S(1)}, u32[]{:S(2)}, u32[]{:S(2)}) collective-permute-start(f32[16,1152]{1,0:T(8,128)S(1)} %get-tuple-element.36), channel_id=1, source_target_pairs={{0,12},{4,0},{8,4},{12,8},{16,20},{20,24},{24,28},{28,16},{1,13},{... | collective-permute-start | bytes 221192 | tf_op jit(solution)/shard_map/ppermute | solution.py:50
  111.5 5.1 %collective-permute-start.16 = (f32[16,1152]{1,0:T(8,128)S(1)}, f32[16,1152]{1,0:T(8,128)S(1)}, u32[]{:S(2)}, u32[]{:S(2)}) collective-permute-start(f32[16,1152]{1,0:T(8,128)S(1)} %get-tuple-element.37), channel_id=1, source_target_pairs={{0,4},{4,8},{8,12},{12,0},{16,28},{20,16},{24,20},{28,24},{1,5},{5... | collective-permute-start | bytes 221192 | tf_op jit(solution)/shard_map/ppermute | solution.py:50
  116.9 1.9 %collective-permute-start.15 = (f32[16,1152]{1,0:T(8,128)S(1)}, f32[16,1152]{1,0:T(8,128)S(1)}, u32[]{:S(2)}, u32[]{:S(2)}) collective-permute-start(f32[16,1152]{1,0:T(8,128)S(1)} %shard_map.58), channel_id=1, source_target_pairs={{0,12},{4,0},{8,4},{12,8},{16,20},{20,24},{24,28},{28,16},{1,13},{... | collective-permute-start | bytes 221192 | tf_op jit(solution)/shard_map/ppermute | solution.py:50
  119.2 5.0 %collective-permute-done.15.z1 = f32[16,1152]{1,0:T(8,128)S(1)} collective-permute-done((f32[16,1152]{1,0:T(8,128)S(1)}, f32[16,1152]{1,0:T(8,128)S(1)}, u32[]{:S(2)}, u32[]{:S(2)}) %collective-permute-start.15) | collective-permute-done | bytes 73760 | tf_op jit(solution)/shard_map/ppermute | solution.py:50
  124.9 4.3 %all-to-all-done.2.packed_ref = f32[8,152,128]{2,1,0:T(8,128)S(1)} async-done(((f32[8,152,128]{2,1,0:T(8,128)}), f32[8,152,128]{2,1,0:T(8,128)S(1)}, u32[]{:S(2)}, u32[]{:S(2)}) %all-to-all-start.2) | async-done | bytes 622624 | tf_op jit(solution)/shard_map/all_to_all | solution.py:44
  (35 shorter events, 14.1 us)
Async XLA Ops:
  0.6 0.9 copy-start
  1.5 0.9 copy-start.2
  3.4 27.1 %all-to-all-start = ((f32[8,16,1152]{2,1,0:T(8,128)}), f32[8,16,1152]{2,1,0:T(8,128)S(1)}, u32[]{:S(2)}, u32[]{:S(2)}) async-start(f32[8,16,1152]{2,1,0:T(8,128)} %bitcast.1), calls=%async_computation | async-start | bytes 1179648 | tf_op jit(solution)/shard_map/all_to_all | solution.py:44
  11.0 12.6 %collective-permute-start = (f32[16,1152]{1,0:T(8,128)S(1)}, f32[16,1152]{1,0:T(8,128)S(1)}, u32[]{:S(2)}, u32[]{:S(2)}) collective-permute-start(f32[16,1152]{1,0:T(8,128)S(1)} %get-tuple-element.21.refs_0_), channel_id=1, source_target_pairs={{0,4},{4,8},{8,12},{12,0},{16,28},{20,16},{24,20},{28,24},{1,5},{5... | collective-permute-start | bytes 221192 | tf_op jit(solution)/shard_map/ppermute | solution.py:50
  21.7 8.7 %collective-permute-start.1 = (f32[16,1152]{1,0:T(8,128)S(1)}, f32[16,1152]{1,0:T(8,128)S(1)}, u32[]{:S(2)}, u32[]{:S(2)}) collective-permute-start(f32[16,1152]{1,0:T(8,128)S(1)} %get-tuple-element.21.refs_0_), channel_id=1, source_target_pairs={{0,12},{4,0},{8,4},{12,8},{16,20},{20,24},{24,28},{28,16},{1,13},{... | collective-permute-start | bytes 221192 | tf_op jit(solution)/shard_map/ppermute | solution.py:50
  23.6 6.9 %collective-permute-start.2 = (f32[16,1152]{1,0:T(8,128)S(1)}, f32[16,1152]{1,0:T(8,128)S(1)}, u32[]{:S(2)}, u32[]{:S(2)}) collective-permute-start(f32[16,1152]{1,0:T(8,128)S(1)} %collective-permute-done.refs_1_), channel_id=1, source_target_pairs={{0,4},{4,8},{8,12},{12,0},{16,28},{20,16},{24,20},{28,24},{1,5},{5... | collective-permute-start | bytes 221192 | tf_op jit(solution)/shard_map/ppermute | solution.py:50
  30.5 18.1 %collective-permute-start.6 = (f32[128,1152]{1,0:T(8,128)S(1)}, f32[128,1152]{1,0:T(8,128)S(1)}, u32[]{:S(2)}, u32[]{:S(2)}) collective-permute-start(f32[128,1152]{1,0:T(8,128)S(1)} %shard_map.51.a_ref), channel_id=1, source_target_pairs={{0,44},{32,0},{4,32},{36,4},{8,36},{40,8},{12,40},{44,12},{16,48},... | collective-permute-start | bytes 1769480 | tf_op jit(solution)/shard_map/ppermute | solution.py:59
  34.5 19.7 %collective-permute-start.3 = (f32[64,1152]{1,0:T(8,128)S(1)}, f32[64,1152]{1,0:T(8,128)S(1)}, u32[]{:S(2)}, u32[]{:S(2)}) collective-permute-start(f32[64,1152]{1,0:T(8,128)S(1)} %shard_map.50.refs_1_.i0), channel_id=1, source_target_pairs={{0,1},{1,2},{2,3},{3,0},{16,19},{17,16},{18,17},{19,18},{4,5},{5,6... | collective-permute-start | bytes 884744 | tf_op jit(solution)/shard_map/ppermute | solution.py:50
  38.9 23.9 %collective-permute-start.7 = (f32[128,1152]{1,0:T(8,128)S(1)}, f32[128,1152]{1,0:T(8,128)S(1)}, u32[]{:S(2)}, u32[]{:S(2)}) collective-permute-start(f32[128,1152]{1,0:T(8,128)S(1)} %shard_map.51.a_ref), channel_id=1, source_target_pairs={{0,16},{16,0},{1,17},{17,1},{2,18},{18,2},{3,19},{19,3},{4,20},{20... | collective-permute-start | bytes 1769480 | tf_op jit(solution)/shard_map/ppermute | solution.py:63
  48.6 14.2 %collective-permute-start.8 = (f32[128,1152]{1,0:T(8,128)S(1)}, f32[128,1152]{1,0:T(8,128)S(1)}, u32[]{:S(2)}, u32[]{:S(2)}) collective-permute-start(f32[128,1152]{1,0:T(8,128)S(1)} %collective-permute-done.6.b_ref), channel_id=1, source_target_pairs={{0,16},{16,0},{1,17},{17,1},{2,18},{18,2},{3,19},{19,3},{4,20},{20... | collective-permute-start | bytes 1769480 | tf_op jit(solution)/shard_map/ppermute | solution.py:63
  51.1 8.7 %collective-permute-start.4 = (f32[64,1152]{1,0:T(8,128)S(1)}, f32[64,1152]{1,0:T(8,128)S(1)}, u32[]{:S(2)}, u32[]{:S(2)}) collective-permute-start(f32[64,1152]{1,0:T(8,128)S(1)} %shard_map.50.refs_1_.i0), channel_id=1, source_target_pairs={{0,3},{1,0},{2,1},{3,2},{16,17},{17,18},{18,19},{19,16},{4,7},{5,4... | collective-permute-start | bytes 884744 | tf_op jit(solution)/shard_map/ppermute | solution.py:50
  54.2 8.5 %collective-permute-start.5 = (f32[64,1152]{1,0:T(8,128)S(1)}, f32[64,1152]{1,0:T(8,128)S(1)}, u32[]{:S(2)}, u32[]{:S(2)}) collective-permute-start(f32[64,1152]{1,0:T(8,128)S(1)} %collective-permute-done.3.i1), channel_id=1, source_target_pairs={{0,1},{1,2},{2,3},{3,0},{16,19},{17,16},{18,17},{19,18},{4,5},{5,6... | collective-permute-start | bytes 884744 | tf_op jit(solution)/shard_map/ppermute | solution.py:50
  66.4 8.7 %collective-permute-start.12 = (f32[256,1152]{1,0:T(8,128)S(1)}, f32[256,1152]{1,0:T(8,128)S(1)}, u32[]{:S(2)}, u32[]{:S(2)}) collective-permute-start(f32[256,1152]{1,0:T(8,128)S(1)} %get-tuple-element.28), channel_id=1, source_target_pairs={{0,16},{16,0},{1,17},{17,1},{2,18},{18,2},{3,19},{19,3},{4,20},{20... | collective-permute-start | bytes 3538952 | tf_op jit(solution)/shard_map/ppermute | solution.py:63
  73.1 12.6 %collective-permute-start.9 = (f32[64,1152]{1,0:T(8,128)S(1)}, f32[64,1152]{1,0:T(8,128)S(1)}, u32[]{:S(2)}, u32[]{:S(2)}) collective-permute-start(f32[64,1152]{1,0:T(8,128)S(1)} %get-tuple-element.26), channel_id=1, source_target_pairs={{0,3},{1,0},{2,1},{3,2},{16,17},{17,18},{18,19},{19,16},{4,7},{5,4... | collective-permute-start | bytes 884744 | tf_op jit(solution)/shard_map/ppermute | solution.py:50
  75.8 26.2 %collective-permute-start.13 = (f32[128,1152]{1,0:T(8,128)S(1)}, f32[128,1152]{1,0:T(8,128)S(1)}, u32[]{:S(2)}, u32[]{:S(2)}) collective-permute-start(f32[128,1152]{1,0:T(8,128)S(1)} %get-tuple-element.30), channel_id=1, source_target_pairs={{0,32},{32,4},{4,36},{36,8},{8,40},{40,12},{12,44},{44,0},{16,60},... | collective-permute-start | bytes 1769480 | tf_op jit(solution)/shard_map/ppermute | solution.py:59
  81.2 20.9 %collective-permute-start.11 = (f32[64,1152]{1,0:T(8,128)S(1)}, f32[64,1152]{1,0:T(8,128)S(1)}, u32[]{:S(2)}, u32[]{:S(2)}) collective-permute-start(f32[64,1152]{1,0:T(8,128)S(1)} %get-tuple-element.27), channel_id=1, source_target_pairs={{0,1},{1,2},{2,3},{3,0},{16,19},{17,16},{18,17},{19,18},{4,5},{5,6... | collective-permute-start | bytes 884744 | tf_op jit(solution)/shard_map/ppermute | solution.py:50
  85.8 16.3 %collective-permute-start.10 = (f32[64,1152]{1,0:T(8,128)S(1)}, f32[64,1152]{1,0:T(8,128)S(1)}, u32[]{:S(2)}, u32[]{:S(2)}) collective-permute-start(f32[64,1152]{1,0:T(8,128)S(1)} %shard_map.54), channel_id=1, source_target_pairs={{0,3},{1,0},{2,1},{3,2},{16,17},{17,18},{18,19},{19,16},{4,7},{5,4... | collective-permute-start | bytes 884744 | tf_op jit(solution)/shard_map/ppermute | solution.py:50
  103.1 21.1 %copy-start.1 = (f32[16,1152]{1,0:T(8,128)S(1)}, f32[16,1152]{1,0:T(8,128)}, u32[]{:S(2)}) copy-start(f32[16,1152]{1,0:T(8,128)} %emb_ref.3) | copy-start | bytes 221188
  103.1 26.2 %copy-start.3 = (f32[16,1152]{1,0:T(8,128)S(1)}, f32[16,1152]{1,0:T(8,128)}, u32[]{:S(2)}) copy-start(f32[16,1152]{1,0:T(8,128)} %emb_ref.2) | copy-start | bytes 221188
  103.1 26.2 %all-to-all-start.2 = ((f32[8,152,128]{2,1,0:T(8,128)}), f32[8,152,128]{2,1,0:T(8,128)S(1)}, u32[]{:S(2)}, u32[]{:S(2)}) async-start(f32[8,152,128]{2,1,0:T(8,128)} %get-tuple-element.32), calls=%async_computation.2 | async-start | bytes 1245184 | tf_op jit(solution)/shard_map/all_to_all | solution.py:44
  109.2 7.7 %collective-permute-start.14 = (f32[16,1152]{1,0:T(8,128)S(1)}, f32[16,1152]{1,0:T(8,128)S(1)}, u32[]{:S(2)}, u32[]{:S(2)}) collective-permute-start(f32[16,1152]{1,0:T(8,128)S(1)} %get-tuple-element.36), channel_id=1, source_target_pairs={{0,12},{4,0},{8,4},{12,8},{16,20},{20,24},{24,28},{28,16},{1,13},{... | collective-permute-start | bytes 221192 | tf_op jit(solution)/shard_map/ppermute | solution.py:50
  111.5 7.7 %collective-permute-start.16 = (f32[16,1152]{1,0:T(8,128)S(1)}, f32[16,1152]{1,0:T(8,128)S(1)}, u32[]{:S(2)}, u32[]{:S(2)}) collective-permute-start(f32[16,1152]{1,0:T(8,128)S(1)} %get-tuple-element.37), channel_id=1, source_target_pairs={{0,4},{4,8},{8,12},{12,0},{16,28},{20,16},{24,20},{28,24},{1,5},{5... | collective-permute-start | bytes 221192 | tf_op jit(solution)/shard_map/ppermute | solution.py:50
  116.9 7.2 %collective-permute-start.15 = (f32[16,1152]{1,0:T(8,128)S(1)}, f32[16,1152]{1,0:T(8,128)S(1)}, u32[]{:S(2)}, u32[]{:S(2)}) collective-permute-start(f32[16,1152]{1,0:T(8,128)S(1)} %shard_map.58), channel_id=1, source_target_pairs={{0,12},{4,0},{8,4},{12,8},{16,20},{20,24},{24,28},{28,16},{1,13},{... | collective-permute-start | bytes 221192 | tf_op jit(solution)/shard_map/ppermute | solution.py:50

commit v4 on v3

--- a/solution.py
+++ b/solution.py
@@ -21,6 +21,7 @@
 VMEM = pl.BlockSpec(memory_space=pltpu.VMEM)
 ANY = pl.BlockSpec(memory_space=pl.ANY)
 SMEM = pl.BlockSpec(memory_space=pltpu.SMEM)
+HBM = pl.BlockSpec(memory_space=pltpu.HBM)
 
 
 def shape(*dims):
@@ -91,11 +92,19 @@
     return dot(left[1], right[0]) + dot(left[0], right[1]) + dot(left[0], right[0])
 
 
-def normalize_kernel(image_ref, text_ref, image_out, text_out):
-    image_out[...] = normalize(image_ref[...])[0]
+def normalize_kernel(image_hbm, text_hbm, image_out, text_out, image_ref, text_ref, sems):
+    copies = [
+        pltpu.make_async_copy(text_hbm, text_ref, sems.at[0]),
+        pltpu.make_async_copy(image_hbm, image_ref, sems.at[1]),
+    ]
+    for copy in copies:
+        copy.start()
+    copies[0].wait()
     text_unit = normalize(text_ref[...])[0]
     for y in range(NY):
         text_out[pl.ds(y * ROWS, ROWS), :] = text_unit
+    copies[1].wait()
+    image_out[...] = normalize(image_ref[...])[0]
 
 
 def stack_kernel(*refs):
@@ -107,26 +116,33 @@
     pass
 
 
+def pair_kernel(a_ref, b_ref, x1, x2, out):
+    half = a_ref.shape[0]
+    out[pl.ds(0, half), :] = a_ref[...]
+    out[pl.ds(half, half), :] = b_ref[...]
+
+
 def stacked(*refs):
     return jnp.concatenate([ref[...] for ref in refs], axis=0)
 
 
-def logits_kernel(place, i0, i1, i2, i3, a_ref, b_ref, c_ref, d_ref, slope_out, other_out, loss_out):
+def logits_kernel(place, i0, i1, i2, i3, own_ref, far_ref, slope_out, other_out, loss_out):
     image = halves(stacked(i0, i1, i2, i3))
-    quarter = a_ref.shape[0]
+    quarter = own_ref.shape[0] // 2
     count = NX * i0.shape[0]
     row = lax.broadcasted_iota(jnp.int32, (count, quarter), 0)
     column = lax.broadcasted_iota(jnp.int32, (count, quarter), 1) - place[0]
     matched = (row == column) & (row < ROWS)
     total = jnp.zeros((), F32)
-    for k, ref in enumerate((c_ref, d_ref, a_ref, b_ref)):
-        logits = LOGIT_MULT * dot3(image, halves(ref[...]), ((1,), (1,))) + LOGIT_SHIFT
-        if ref is a_ref:
+    for k, (ref, half) in enumerate(((far_ref, 0), (far_ref, 1), (own_ref, 0), (own_ref, 1))):
+        text = halves(ref[pl.ds(half * quarter, quarter), :])
+        logits = LOGIT_MULT * dot3(image, text, ((1,), (1,))) + LOGIT_SHIFT
+        if k == 2:
             logits = jnp.where(matched, -logits, logits)
         small = jnp.exp(-jnp.abs(logits))
         total += jnp.sum(jnp.maximum(logits, 0.0) + jnp.log1p(small))
         slope = jnp.where(logits >= 0.0, 1.0, small) / (1.0 + small) * (LOGIT_MULT / PAIRS)
-        if ref is a_ref:
+        if k == 2:
             slope = jnp.where(matched, -slope, slope)
         slope_out[:, pl.ds((k + 2) % 4 * quarter, quarter)] = slope
         if k < 2:
@@ -134,11 +150,11 @@
     loss_out[...] = jnp.full(loss_out.shape, total)
 
 
-def image_kernel(slope_ref, a_ref, b_ref, c_ref, d_ref, *outs):
-    quarter = a_ref.shape[0]
+def image_kernel(slope_ref, own_ref, far_ref, *outs):
+    half = own_ref.shape[0]
     total = None
-    for k, ref in enumerate((a_ref, b_ref, c_ref, d_ref)):
-        slope = slope_ref[:, pl.ds(k * quarter, quarter)]
+    for k, ref in enumerate((own_ref, far_ref)):
+        slope = slope_ref[:, pl.ds(k * half, half)]
         term = dot3(halves(slope), halves(ref[...]), ((1,), (0,)))
         total = term if total is None else total + term
     rows = total.shape[0] // NX
@@ -154,8 +170,8 @@
         out[...] = dot3(halves(slope_ref[:, rows]), image, ((0,), (0,))) + other_ref[rows, :]
 
 
-def add_kernel(left, right, out):
-    out[...] = left[...] + right[...]
+def add_kernel(left, right, *refs):
+    refs[-1][...] = left[...] + right[...]
 
 
 def join_kernel(x0, x1, x2, keep_ref, received_ref, losses_ref, packed_out, *zs):
@@ -183,33 +199,41 @@
         total = total + packed_ref[y]
     direction = jnp.concatenate([total[k * ROWS : (k + 1) * ROWS] for k in range(COLS)], axis=1)
     out[...] = project_back(unit, direction, length)
-    loss_out[...] = total[PACK:] / PAIRS
+    loss_out[0, 0] = jnp.max(total[PACK:]) / PAIRS
 
 
 def on_device(image_emb, text_emb):
     rows, features = image_emb.shape
     image_unit, text_tiled = call(
-        normalize_kernel, (image_emb, text_emb), [shape(rows, features), shape(NY * rows, features)]
-    )
-    text_y = exchange(text_tiled, "y")
+        normalize_kernel,
+        (image_emb, text_emb),
+        [shape(rows, features), shape(NY * rows, features)],
+        in_specs=[HBM] * 2,
+        scratch_shapes=[pltpu.VMEM((rows, features), F32)] * 2 + [pltpu.SemaphoreType.DMA((2,))],
+    )
+    text_a = exchange(text_tiled, "y")
     (image_z,) = call(stack_kernel, ring_gather(image_unit, "zh"), [shape(NZH * rows, features)])
     images = ring_gather(image_z, "x")
     (text_a,) = call(
-        tie_kernel, (text_y, image_z), [shape(*text_y.shape)], [ANY] * 2, [ANY], input_output_aliases={0: 0}
-    )
-    text_b = planes(text_a, -1)
-    text_c = other_core(text_a)
-    text_d = other_core(text_b)
-    texts = (text_a, text_b, text_c, text_d)
+        tie_kernel, (text_a, image_z), [shape(*text_a.shape)], [ANY] * 2, [ANY], input_output_aliases={0: 0}
+    )
+    quarter = text_a.shape[0]
+    (own,) = call(
+        pair_kernel,
+        (text_a, planes(text_a, -1), *images[1:3]),
+        [shape(2 * quarter, features)],
+        in_specs=[VMEM] * 2 + [ANY] * 2,
+    )
+    texts = (own, other_core(own))
 
     place = (lax.axis_index("y") * rows).astype(jnp.int32).reshape(1)
-    part, quarter = image_z.shape[0], text_a.shape[0]
+    part = image_z.shape[0]
     product = 2 * NX * part * quarter * features * 3
     slope, other, loss = call(
         logits_kernel,
         (place, *images, *texts),
         [shape(NX * part, 4 * quarter), shape(2 * quarter, features), shape(64, LANES)],
-        in_specs=[SMEM] + [VMEM] * 8,
+        in_specs=[SMEM] + [VMEM] * 6,
         flops=6 * product,
     )
     received = other_core(other)
@@ -220,9 +244,11 @@
         text_kernel, (slope, *images, received), [shape(quarter, features)] * 2, flops=2 * product
     )
     received = planes(send, 1)
-    (relay,) = call(add_kernel, (xs[1], relay), [shape(part, features)])
+    losses = exchange(loss, ("zl", "c", "zh", "x"))
+    (relay,) = call(
+        add_kernel, (xs[1], relay, losses), [shape(part, features)], in_specs=[VMEM] * 2 + [ANY]
+    )
     back = turned(relay, "x", -1)
-    losses = exchange(loss, ("zl", "c", "zh", "x"))
     packed, *zs = call(
         join_kernel,
         (xs[0], back, ahead, keep, received, losses),
@@ -234,8 +260,13 @@
     (relay,) = call(add_kernel, (zs[1], relay), [shape(rows, features)])
     back = turned(relay, "zh", -1)
     (image_grad,) = call(image_grad_kernel, (image_emb, zs[0], back, ahead), [shape(rows, features)])
-    text_grad, loss = call(text_grad_kernel, (text_emb, packed), [shape(rows, features), shape(8, LANES)])
-    return loss[0, 0], image_grad, text_grad
+    text_grad, loss = call(
+        text_grad_kernel,
+        (text_emb, packed),
+        [shape(rows, features), shape(1, 1)],
+        out_specs=[VMEM, SMEM],
+    )
+    return loss.reshape(()), image_grad, text_grad
 
 
 def solution(mesh):

time: 131 us -> 138 us (1.053)
  waiting for transfers between devices: 17.9 us -> 35.6 us
  blocking collectives: 14.3 us -> 0 us
  Pallas kernels: 10 us -> 14 us
    all_to_all x1 -> x0, blocking collectives: 14.3 us -> none  [exchange(): return lax.all_to_all(values, axes, 0, 0, tiled=True)]
    ppermute x12, waiting for transfers between devices: 12.1 us -> 23.7 us  [turned(): return lax.ppermute(values, ('c', axis), pairs)]
    all_to_all x2 -> x3, starting transfers between devices: 13.8 us -> 20.1 us  [exchange(): return lax.all_to_all(values, axes, 0, 0, tiled=True)]
    all_to_all x2 -> x3, waiting for transfers between devices: 4.3 us -> 9.06 us  [exchange(): return lax.all_to_all(values, axes, 0, 0, tiled=True)]
    pallas_call x11 -> x12, Pallas kernels: 10 us -> 14 us  [call(): pl.pallas_call(kernel, out_shape=outs, in_specs=in_specs or [VMEM] * len(...]
    ppermute x2, starting transfers between devices: 9.31 us -> 6.17 us  [planes(): return lax.ppermute(values, ('zl', 'c', 'zh'), pairs)]
    ppermute x12, starting transfers between devices: 46.6 us -> 44.3 us  [turned(): return lax.ppermute(values, ('c', axis), pairs)]
    ppermute x3 -> x2, starting transfers between devices: 15.5 us -> 13.9 us  [other_core(): return lax.ppermute(values, 'c', [(0, 1), (1, 0)])]
  transfers between devices with their start and end apart: 19 -> 19, of which waited for: 9 -> 12; matrix products, arithmetic and copies ran while one was open for 0% -> 0% of each run, Pallas kernels for 3% -> 4%
where the time goes in v4:
time: 138 us; the launch traced here: 137 us
  starting transfers between devices  84.5 us (61%)
  waiting for transfers between devices  35.6 us (26%)
  Pallas kernels  14 us (10%)
  local copies, waits for them, and re-layouts  1.77 us (1%)
    ppermute x12, starting transfers between devices, turned(): return lax.ppermute(values, ('c', axis), pairs)  44.3 us
    ppermute x12, waiting for transfers between devices, turned(): return lax.ppermute(values, ('c', axis), pairs)  23.7 us
    all_to_all x3, starting transfers between devices, exchange(): return lax.all_to_all(values, axes, 0, 0, tiled=True)  20.1 us
    pallas_call x12, Pallas kernels, call(): pl.pallas_call(kernel, out_shape=outs, in_specs=in_specs or [VMEM] * len(...  14 us
    ppermute x2, starting transfers between devices, other_core(): return lax.ppermute(values, 'c', [(0, 1), (1, 0)])  13.9 us
    all_to_all x3, waiting for transfers between devices, exchange(): return lax.all_to_all(values, axes, 0, 0, tiled=True)  9.06 us
    ppermute x2, starting transfers between devices, planes(): return lax.ppermute(values, ('zl', 'c', 'zh'), pairs)  6.17 us
    ppermute x2, waiting for transfers between devices, planes(): return lax.ppermute(values, ('zl', 'c', 'zh'), pairs)  2.88 us
  transfers between devices with their start and end apart: 19, of which 12 were waited for; matrix products, arithmetic and copies ran while one was open for 0% of the time, Pallas kernels for 4%

profile of v4, /device:TPU:1, one launch (start us, length us, event | category | flops | bytes accessed | tf_op | source)
XLA Modules:
  0.0 136.7 jit_solution(3894171042339686540)
XLA Ops:
  3.6 7.7 %all-to-all-start = ((f32[8,16,1152]{2,1,0:T(8,128)}), f32[8,16,1152]{2,1,0:T(8,128)S(1)}, u32[]{:S(2)}, u32[]{:S(2)}) async-start(f32[8,16,1152]{2,1,0:T(8,128)} %bitcast.1), calls=%async_computation | async-start | bytes 1179648 | tf_op jit(solution)/shard_map/all_to_all | solution.py:45
  11.2 10.6 %collective-permute-start = (f32[16,1152]{1,0:T(8,128)S(1)}, f32[16,1152]{1,0:T(8,128)S(1)}, u32[]{:S(2)}, u32[]{:S(2)}) collective-permute-start(f32[16,1152]{1,0:T(8,128)S(1)} %get-tuple-element.21.refs_0_), channel_id=1, source_target_pairs={{0,4},{4,8},{8,12},{12,0},{16,28},{20,16},{24,20},{28,24},{1,5},{5... | collective-permute-start | bytes 221192 | tf_op jit(solution)/shard_map/ppermute | solution.py:51
  23.8 5.5 %collective-permute-start.2 = (f32[16,1152]{1,0:T(8,128)S(1)}, f32[16,1152]{1,0:T(8,128)S(1)}, u32[]{:S(2)}, u32[]{:S(2)}) collective-permute-start(f32[16,1152]{1,0:T(8,128)S(1)} %collective-permute-done.refs_1_), channel_id=1, source_target_pairs={{0,4},{4,8},{8,12},{12,0},{16,28},{20,16},{24,20},{28,24},{1,5},{5... | collective-permute-start | bytes 221192 | tf_op jit(solution)/shard_map/ppermute | solution.py:51
  30.7 4.0 %collective-permute-start.6 = (f32[128,1152]{1,0:T(8,128)S(1)}, f32[128,1152]{1,0:T(8,128)S(1)}, u32[]{:S(2)}, u32[]{:S(2)}) collective-permute-start(f32[128,1152]{1,0:T(8,128)S(1)} %shard_map.51.a_ref), channel_id=1, source_target_pairs={{0,44},{32,0},{4,32},{36,4},{8,36},{40,8},{12,40},{44,12},{16,48},... | collective-permute-start | bytes 1769480 | tf_op jit(solution)/shard_map/ppermute | solution.py:60
  34.7 3.1 %collective-permute-start.4 = (f32[64,1152]{1,0:T(8,128)S(1)}, f32[64,1152]{1,0:T(8,128)S(1)}, u32[]{:S(2)}, u32[]{:S(2)}) collective-permute-start(f32[64,1152]{1,0:T(8,128)S(1)} %shard_map.50.refs_1_.i0), channel_id=1, source_target_pairs={{0,3},{1,0},{2,1},{3,2},{16,17},{17,18},{18,19},{19,16},{4,7},{5,4... | collective-permute-start | bytes 884744 | tf_op jit(solution)/shard_map/ppermute | solution.py:51
  37.9 3.4 %collective-permute-start.3 = (f32[64,1152]{1,0:T(8,128)S(1)}, f32[64,1152]{1,0:T(8,128)S(1)}, u32[]{:S(2)}, u32[]{:S(2)}) collective-permute-start(f32[64,1152]{1,0:T(8,128)S(1)} %shard_map.50.refs_1_.i0), channel_id=1, source_target_pairs={{0,1},{1,2},{2,3},{3,0},{16,19},{17,16},{18,17},{19,18},{4,5},{5,6... | collective-permute-start | bytes 884744 | tf_op jit(solution)/shard_map/ppermute | solution.py:51
  41.2 2.2 %collective-permute-done.4.x2.i2 = f32[64,1152]{1,0:T(8,128)S(1)} collective-permute-done((f32[64,1152]{1,0:T(8,128)S(1)}, f32[64,1152]{1,0:T(8,128)S(1)}, u32[]{:S(2)}, u32[]{:S(2)}) %collective-permute-start.4) | collective-permute-done | bytes 294944 | tf_op jit(solution)/shard_map/ppermute | solution.py:51
  43.4 2.2 %collective-permute-done.3.x1.i1 = f32[64,1152]{1,0:T(8,128)S(1)} collective-permute-done((f32[64,1152]{1,0:T(8,128)S(1)}, f32[64,1152]{1,0:T(8,128)S(1)}, u32[]{:S(2)}, u32[]{:S(2)}) %collective-permute-start.3) | collective-permute-done | bytes 294944 | tf_op jit(solution)/shard_map/ppermute | solution.py:51
  45.6 2.9 %collective-permute-done.6.b_ref = f32[128,1152]{1,0:T(8,128)S(1)} collective-permute-done((f32[128,1152]{1,0:T(8,128)S(1)}, f32[128,1152]{1,0:T(8,128)S(1)}, u32[]{:S(2)}, u32[]{:S(2)}) %collective-permute-start.6) | collective-permute-done | bytes 589856 | tf_op jit(solution)/shard_map/ppermute | solution.py:60
  48.6 9.9 %collective-permute-start.7 = (f32[256,1152]{1,0:T(8,128)S(1)}, f32[256,1152]{1,0:T(8,128)}, u32[]{:S(2)}, u32[]{:S(2)}) collective-permute-start(f32[256,1152]{1,0:T(8,128)S(1)} %shard_map.52.own_ref), channel_id=1, source_target_pairs={{0,16},{16,0},{1,17},{17,1},{2,18},{18,2},{3,19},{19,3},{4,20},{20... | collective-permute-start | bytes 3538952 | tf_op jit(solution)/shard_map/ppermute | solution.py:64
  60.5 5.8 %collective-permute-done.5.i3 = f32[64,1152]{1,0:T(8,128)S(1)} collective-permute-done((f32[64,1152]{1,0:T(8,128)S(1)}, f32[64,1152]{1,0:T(8,128)S(1)}, u32[]{:S(2)}, u32[]{:S(2)}) %collective-permute-start.5) | collective-permute-done | bytes 294944 | tf_op jit(solution)/shard_map/ppermute | solution.py:51
  66.3 5.4 %shard_map.53 = (f32[256,512]{1,0:T(8,128)S(1)}, f32[256,1152]{1,0:T(8,128)S(1)}, f32[64,128]{1,0:T(8,128)}) custom-call(s32[1]{0:T(128)} %bitcast.place, f32[64,1152]{1,0:T(8,128)S(1)} %shard_map.50.refs_1_.i0, f32[64,1152]{1,0:T(8,128)S(1)} %collective-permute-done.3.x1.i1, f32[64,1152]{1,0:T(8,128)S(1)} %collective-permute-done.4.x2.i2, ...), custom_call_target="tpu_custom_call" | custom-call | flops 1358954496 | bytes 5275652 | tf_op jit(solution)/shard_map/pallas_call | solution.py:33
  71.7 4.0 %collective-permute-start.11 = (f32[256,1152]{1,0:T(8,128)S(1)}, f32[256,1152]{1,0:T(8,128)S(1)}, u32[]{:S(2)}, u32[]{:S(2)}) collective-permute-start(f32[256,1152]{1,0:T(8,128)S(1)} %get-tuple-element.29), channel_id=1, source_target_pairs={{0,16},{16,0},{1,17},{17,1},{2,18},{18,2},{3,19},{19,3},{4,20},{20... | collective-permute-start | bytes 3538952 | tf_op jit(solution)/shard_map/ppermute | solution.py:64
  75.7 3.2 %shard_map.54 = (f32[64,1152]{1,0:T(8,128)S(1)}, f32[64,1152]{1,0:T(8,128)S(1)}, f32[64,1152]{1,0:T(8,128)S(1)}, f32[64,1152]{1,0:T(8,128)}) custom-call(f32[256,512]{1,0:T(8,128)S(1)} %get-tuple-element.23.slope_ref, f32[256,1152]{1,0:T(8,128)S(1)} %shard_map.52.own_ref, f32[256,1152]{1,0:T(8,128)} %collective-permute-done.7.far_ref), custom_call_target="tpu_custom_call" | custom-call | flops 905969664 | bytes 4063232 | tf_op jit(solution)/shard_map/pallas_call | solution.py:33
  84.4 6.3 %all-to-all-start.1 = ((f32[64,1,128]{2,1,0:T(1,128)}), f32[64,1,128]{2,1,0:T(1,128)S(1)}, u32[]{:S(2)}, u32[]{:S(2)}) async-start(f32[64,1,128]{2,1,0:T(1,128)} %bitcast.4), calls=%async_computation.1 | async-start | bytes 65536 | tf_op jit(solution)/shard_map/all_to_all | solution.py:45
  90.7 4.5 %collective-permute-start.10 = (f32[64,1152]{1,0:T(8,128)}, f32[64,1152]{1,0:T(8,128)S(1)}, u32[]{:S(2)}, u32[]{:S(2)}) collective-permute-start(f32[64,1152]{1,0:T(8,128)} %copy-done.4), channel_id=1, source_target_pairs={{0,1},{1,2},{2,3},{3,0},{16,19},{17,16},{18,17},{19,18},{4,5},{5,6... | collective-permute-start | bytes 884744 | tf_op jit(solution)/shard_map/ppermute | solution.py:51
  95.2 4.8 %all-to-all-done.1 = f32[64,1,128]{2,1,0:T(1,128)S(1)} async-done(((f32[64,1,128]{2,1,0:T(1,128)}), f32[64,1,128]{2,1,0:T(1,128)S(1)}, u32[]{:S(2)}, u32[]{:S(2)}) %all-to-all-start.1) | async-done | bytes 32800 | tf_op jit(solution)/shard_map/all_to_all | solution.py:45
  100.0 2.2 %collective-permute-start.9 = (f32[64,1152]{1,0:T(8,128)S(1)}, f32[64,1152]{1,0:T(8,128)S(1)}, u32[]{:S(2)}, u32[]{:S(2)}) collective-permute-start(f32[64,1152]{1,0:T(8,128)S(1)} %shard_map.55), channel_id=1, source_target_pairs={{0,3},{1,0},{2,1},{3,2},{16,17},{17,18},{18,19},{19,16},{4,7},{5,4... | collective-permute-start | bytes 884744 | tf_op jit(solution)/shard_map/ppermute | solution.py:51
  102.2 6.5 %collective-permute-done.9.x1 = f32[64,1152]{1,0:T(8,128)S(1)} collective-permute-done((f32[64,1152]{1,0:T(8,128)S(1)}, f32[64,1152]{1,0:T(8,128)S(1)}, u32[]{:S(2)}, u32[]{:S(2)}) %collective-permute-start.9) | collective-permute-done | bytes 294944 | tf_op jit(solution)/shard_map/ppermute | solution.py:51
  109.7 6.1 %all-to-all-start.2 = ((f32[8,152,128]{2,1,0:T(8,128)}), f32[8,152,128]{2,1,0:T(8,128)S(1)}, u32[]{:S(2)}, u32[]{:S(2)}) async-start(f32[8,152,128]{2,1,0:T(8,128)} %get-tuple-element.32), calls=%async_computation.2 | async-start | bytes 1245184 | tf_op jit(solution)/shard_map/all_to_all | solution.py:45
  115.8 2.3 %collective-permute-start.13 = (f32[16,1152]{1,0:T(8,128)S(1)}, f32[16,1152]{1,0:T(8,128)S(1)}, u32[]{:S(2)}, u32[]{:S(2)}) collective-permute-start(f32[16,1152]{1,0:T(8,128)S(1)} %get-tuple-element.36), channel_id=1, source_target_pairs={{0,12},{4,0},{8,4},{12,8},{16,20},{20,24},{24,28},{28,16},{1,13},{... | collective-permute-start | bytes 221192 | tf_op jit(solution)/shard_map/ppermute | solution.py:51
  118.0 5.1 %collective-permute-start.15 = (f32[16,1152]{1,0:T(8,128)S(1)}, f32[16,1152]{1,0:T(8,128)S(1)}, u32[]{:S(2)}, u32[]{:S(2)}) collective-permute-start(f32[16,1152]{1,0:T(8,128)S(1)} %get-tuple-element.37), channel_id=1, source_target_pairs={{0,4},{4,8},{8,12},{12,0},{16,28},{20,16},{24,20},{28,24},{1,5},{5... | collective-permute-start | bytes 221192 | tf_op jit(solution)/shard_map/ppermute | solution.py:51
  125.7 5.0 %collective-permute-done.14.z1 = f32[16,1152]{1,0:T(8,128)S(1)} collective-permute-done((f32[16,1152]{1,0:T(8,128)S(1)}, f32[16,1152]{1,0:T(8,128)S(1)}, u32[]{:S(2)}, u32[]{:S(2)}) %collective-permute-start.14) | collective-permute-done | bytes 73760 | tf_op jit(solution)/shard_map/ppermute | solution.py:51
  131.5 4.3 %all-to-all-done.2.packed_ref = f32[8,152,128]{2,1,0:T(8,128)S(1)} async-done(((f32[8,152,128]{2,1,0:T(8,128)}), f32[8,152,128]{2,1,0:T(8,128)S(1)}, u32[]{:S(2)}, u32[]{:S(2)}) %all-to-all-start.2) | async-done | bytes 622624 | tf_op jit(solution)/shard_map/all_to_all | solution.py:45
  (36 shorter events, 18.9 us)
Async XLA Ops:
  0.6 0.9 copy-start
  1.5 0.9 copy-start.2
  3.6 27.1 %all-to-all-start = ((f32[8,16,1152]{2,1,0:T(8,128)}), f32[8,16,1152]{2,1,0:T(8,128)S(1)}, u32[]{:S(2)}, u32[]{:S(2)}) async-start(f32[8,16,1152]{2,1,0:T(8,128)} %bitcast.1), calls=%async_computation | async-start | bytes 1179648 | tf_op jit(solution)/shard_map/all_to_all | solution.py:45
  11.2 12.6 %collective-permute-start = (f32[16,1152]{1,0:T(8,128)S(1)}, f32[16,1152]{1,0:T(8,128)S(1)}, u32[]{:S(2)}, u32[]{:S(2)}) collective-permute-start(f32[16,1152]{1,0:T(8,128)S(1)} %get-tuple-element.21.refs_0_), channel_id=1, source_target_pairs={{0,4},{4,8},{8,12},{12,0},{16,28},{20,16},{24,20},{28,24},{1,5},{5... | collective-permute-start | bytes 221192 | tf_op jit(solution)/shard_map/ppermute | solution.py:51
  21.9 8.7 %collective-permute-start.1 = (f32[16,1152]{1,0:T(8,128)S(1)}, f32[16,1152]{1,0:T(8,128)S(1)}, u32[]{:S(2)}, u32[]{:S(2)}) collective-permute-start(f32[16,1152]{1,0:T(8,128)S(1)} %get-tuple-element.21.refs_0_), channel_id=1, source_target_pairs={{0,12},{4,0},{8,4},{12,8},{16,20},{20,24},{24,28},{28,16},{1,13},{... | collective-permute-start | bytes 221192 | tf_op jit(solution)/shard_map/ppermute | solution.py:51
  23.8 6.9 %collective-permute-start.2 = (f32[16,1152]{1,0:T(8,128)S(1)}, f32[16,1152]{1,0:T(8,128)S(1)}, u32[]{:S(2)}, u32[]{:S(2)}) collective-permute-start(f32[16,1152]{1,0:T(8,128)S(1)} %collective-permute-done.refs_1_), channel_id=1, source_target_pairs={{0,4},{4,8},{8,12},{12,0},{16,28},{20,16},{24,20},{28,24},{1,5},{5... | collective-permute-start | bytes 221192 | tf_op jit(solution)/shard_map/ppermute | solution.py:51
  30.7 17.8 %collective-permute-start.6 = (f32[128,1152]{1,0:T(8,128)S(1)}, f32[128,1152]{1,0:T(8,128)S(1)}, u32[]{:S(2)}, u32[]{:S(2)}) collective-permute-start(f32[128,1152]{1,0:T(8,128)S(1)} %shard_map.51.a_ref), channel_id=1, source_target_pairs={{0,44},{32,0},{4,32},{36,4},{8,36},{40,8},{12,40},{44,12},{16,48},... | collective-permute-start | bytes 1769480 | tf_op jit(solution)/shard_map/ppermute | solution.py:60
  34.7 8.7 %collective-permute-start.4 = (f32[64,1152]{1,0:T(8,128)S(1)}, f32[64,1152]{1,0:T(8,128)S(1)}, u32[]{:S(2)}, u32[]{:S(2)}) collective-permute-start(f32[64,1152]{1,0:T(8,128)S(1)} %shard_map.50.refs_1_.i0), channel_id=1, source_target_pairs={{0,3},{1,0},{2,1},{3,2},{16,17},{17,18},{18,19},{19,16},{4,7},{5,4... | collective-permute-start | bytes 884744 | tf_op jit(solution)/shard_map/ppermute | solution.py:51
  37.9 7.8 %collective-permute-start.3 = (f32[64,1152]{1,0:T(8,128)S(1)}, f32[64,1152]{1,0:T(8,128)S(1)}, u32[]{:S(2)}, u32[]{:S(2)}) collective-permute-start(f32[64,1152]{1,0:T(8,128)S(1)} %shard_map.50.refs_1_.i0), channel_id=1, source_target_pairs={{0,1},{1,2},{2,3},{3,0},{16,19},{17,16},{18,17},{19,18},{4,5},{5,6... | collective-permute-start | bytes 884744 | tf_op jit(solution)/shard_map/ppermute | solution.py:51
  48.6 17.7 %collective-permute-start.7 = (f32[256,1152]{1,0:T(8,128)S(1)}, f32[256,1152]{1,0:T(8,128)}, u32[]{:S(2)}, u32[]{:S(2)}) collective-permute-start(f32[256,1152]{1,0:T(8,128)S(1)} %shard_map.52.own_ref), channel_id=1, source_target_pairs={{0,16},{16,0},{1,17},{17,1},{2,18},{18,2},{3,19},{19,3},{4,20},{20... | collective-permute-start | bytes 3538952 | tf_op jit(solution)/shard_map/ppermute | solution.py:64
  58.5 7.8 %collective-permute-start.5 = (f32[64,1152]{1,0:T(8,128)S(1)}, f32[64,1152]{1,0:T(8,128)S(1)}, u32[]{:S(2)}, u32[]{:S(2)}) collective-permute-start(f32[64,1152]{1,0:T(8,128)S(1)} %collective-permute-done.3.x1.i1), channel_id=1, source_target_pairs={{0,1},{1,2},{2,3},{3,0},{16,19},{17,16},{18,17},{19,18},{4,5},{5,6... | collective-permute-start | bytes 884744 | tf_op jit(solution)/shard_map/ppermute | solution.py:51
  71.7 9.1 %collective-permute-start.11 = (f32[256,1152]{1,0:T(8,128)S(1)}, f32[256,1152]{1,0:T(8,128)S(1)}, u32[]{:S(2)}, u32[]{:S(2)}) collective-permute-start(f32[256,1152]{1,0:T(8,128)S(1)} %get-tuple-element.29), channel_id=1, source_target_pairs={{0,16},{16,0},{1,17},{17,1},{2,18},{18,2},{3,19},{19,3},{4,20},{20... | collective-permute-start | bytes 3538952 | tf_op jit(solution)/shard_map/ppermute | solution.py:64
  78.9 3.3 %copy-start.4 = (f32[64,1152]{1,0:T(8,128)}, f32[64,1152]{1,0:T(8,128)S(1)}, u32[]{:S(2)}) copy-start(f32[64,1152]{1,0:T(8,128)S(1)} %get-tuple-element.28) | copy-start | bytes 884740
  78.9 21.0 %collective-permute-start.8 = (f32[64,1152]{1,0:T(8,128)}, f32[64,1152]{1,0:T(8,128)S(1)}, u32[]{:S(2)}, u32[]{:S(2)}) collective-permute-start(f32[64,1152]{1,0:T(8,128)} %get-tuple-element.26), channel_id=1, source_target_pairs={{0,3},{1,0},{2,1},{3,2},{16,17},{17,18},{18,19},{19,16},{4,7},{5,4... | collective-permute-start | bytes 884744 | tf_op jit(solution)/shard_map/ppermute | solution.py:51
  82.2 26.4 %collective-permute-start.12 = (f32[128,1152]{1,0:T(8,128)}, f32[128,1152]{1,0:T(8,128)S(1)}, u32[]{:S(2)}, u32[]{:S(2)}) collective-permute-start(f32[128,1152]{1,0:T(8,128)} %get-tuple-element.31), channel_id=1, source_target_pairs={{0,32},{32,4},{4,36},{36,8},{8,40},{40,12},{12,44},{44,0},{16,60},... | collective-permute-start | bytes 1769480 | tf_op jit(solution)/shard_map/ppermute | solution.py:60
  84.4 15.5 %all-to-all-start.1 = ((f32[64,1,128]{2,1,0:T(1,128)}), f32[64,1,128]{2,1,0:T(1,128)S(1)}, u32[]{:S(2)}, u32[]{:S(2)}) async-start(f32[64,1,128]{2,1,0:T(1,128)} %bitcast.4), calls=%async_computation.1 | async-start | bytes 65536 | tf_op jit(solution)/shard_map/all_to_all | solution.py:45
  90.7 11.5 %collective-permute-start.10 = (f32[64,1152]{1,0:T(8,128)}, f32[64,1152]{1,0:T(8,128)S(1)}, u32[]{:S(2)}, u32[]{:S(2)}) collective-permute-start(f32[64,1152]{1,0:T(8,128)} %copy-done.4), channel_id=1, source_target_pairs={{0,1},{1,2},{2,3},{3,0},{16,19},{17,16},{18,17},{19,18},{4,5},{5,6... | collective-permute-start | bytes 884744 | tf_op jit(solution)/shard_map/ppermute | solution.py:51
  100.0 8.7 %collective-permute-start.9 = (f32[64,1152]{1,0:T(8,128)S(1)}, f32[64,1152]{1,0:T(8,128)S(1)}, u32[]{:S(2)}, u32[]{:S(2)}) collective-permute-start(f32[64,1152]{1,0:T(8,128)S(1)} %shard_map.55), channel_id=1, source_target_pairs={{0,3},{1,0},{2,1},{3,2},{16,17},{17,18},{18,19},{19,16},{4,7},{5,4... | collective-permute-start | bytes 884744 | tf_op jit(solution)/shard_map/ppermute | solution.py:51
  109.7 21.1 %copy-start.1 = (f32[16,1152]{1,0:T(8,128)S(1)}, f32[16,1152]{1,0:T(8,128)}, u32[]{:S(2)}) copy-start(f32[16,1152]{1,0:T(8,128)} %emb_ref.3) | copy-start | bytes 221188
  109.7 26.2 %copy-start.3 = (f32[16,1152]{1,0:T(8,128)S(1)}, f32[16,1152]{1,0:T(8,128)}, u32[]{:S(2)}) copy-start(f32[16,1152]{1,0:T(8,128)} %emb_ref.2) | copy-start | bytes 221188
  109.7 26.2 %all-to-all-start.2 = ((f32[8,152,128]{2,1,0:T(8,128)}), f32[8,152,128]{2,1,0:T(8,128)S(1)}, u32[]{:S(2)}, u32[]{:S(2)}) async-start(f32[8,152,128]{2,1,0:T(8,128)} %get-tuple-element.32), calls=%async_computation.2 | async-start | bytes 1245184 | tf_op jit(solution)/shard_map/all_to_all | solution.py:45
  115.8 7.7 %collective-permute-start.13 = (f32[16,1152]{1,0:T(8,128)S(1)}, f32[16,1152]{1,0:T(8,128)S(1)}, u32[]{:S(2)}, u32[]{:S(2)}) collective-permute-start(f32[16,1152]{1,0:T(8,128)S(1)} %get-tuple-element.36), channel_id=1, source_target_pairs={{0,12},{4,0},{8,4},{12,8},{16,20},{20,24},{24,28},{28,16},{1,13},{... | collective-permute-start | bytes 221192 | tf_op jit(solution)/shard_map/ppermute | solution.py:51
  118.0 7.6 %collective-permute-start.15 = (f32[16,1152]{1,0:T(8,128)S(1)}, f32[16,1152]{1,0:T(8,128)S(1)}, u32[]{:S(2)}, u32[]{:S(2)}) collective-permute-start(f32[16,1152]{1,0:T(8,128)S(1)} %get-tuple-element.37), channel_id=1, source_target_pairs={{0,4},{4,8},{8,12},{12,0},{16,28},{20,16},{24,20},{28,24},{1,5},{5... | collective-permute-start | bytes 221192 | tf_op jit(solution)/shard_map/ppermute | solution.py:51
  123.5 7.2 %collective-permute-start.14 = (f32[16,1152]{1,0:T(8,128)S(1)}, f32[16,1152]{1,0:T(8,128)S(1)}, u32[]{:S(2)}, u32[]{:S(2)}) collective-permute-start(f32[16,1152]{1,0:T(8,128)S(1)} %shard_map.59), channel_id=1, source_target_pairs={{0,12},{4,0},{8,4},{12,8},{16,20},{20,24},{24,28},{28,16},{1,13},{... | collective-permute-start | bytes 221192 | tf_op jit(solution)/shard_map/ppermute | solution.py:51

commit v5 on v4

v5 whole, which is shorter than its diff:
```python
import jax
import jax.numpy as jnp
from jax import lax
from jax.experimental import pallas as pl
from jax.experimental.pallas import tpu as pltpu
from jax.sharding import Mesh, PartitionSpec as P

LOGIT_MULT = 16.0
LOGIT_SHIFT = -10.0
EPSILON = 1e-06

AXES = ("y", "zl", "c", "zh", "x")
SIZES = (8, 2, 2, 4, 4)
NY, NZH, NX = 8, 4, 4
ROWS, FEATURES, LANES = 16, 1152, 128
COLS = FEATURES // LANES
PACK = COLS * ROWS
PAIRS = 8192
F32, BF16 = jnp.float32, jnp.bfloat16

VMEM = pl.BlockSpec(memory_space=pltpu.VMEM)
ANY = pl.BlockSpec(memory_space=pl.ANY)
SMEM = pl.BlockSpec(memory_space=pltpu.SMEM)
HBM = pl.BlockSpec(memory_space=pltpu.HBM)


def shape(*dims):
    return jax.ShapeDtypeStruct(dims, F32)


def call(kernel, ins, outs, in_specs=None, out_specs=None, flops=0, vmem=8, **kw):
    moved = 4 * sum(a.size for a in list(ins) + list(outs))
    return pl.pallas_call(
        kernel,
        out_shape=outs,
        in_specs=in_specs or [VMEM] * len(ins),
        out_specs=out_specs or [VMEM] * len(outs),
        cost_estimate=pl.CostEstimate(flops=flops, bytes_accessed=moved, transcendentals=0),
        compiler_params=pltpu.CompilerParams(vmem_limit_bytes=vmem * 2**20),
        **kw,
    )(*ins)


def exchange(values, axes):
    return lax.all_to_all(values, axes, 0, 0, tiled=True)


def turned(values, axis, step):
    count = lax.axis_size(axis)
    pairs = [(c * count + i, c * count + (i + (1 - 2 * c) * step) % count) for c in range(2) for i in range(count)]
    return lax.ppermute(values, ("c", axis), pairs)


def planes(values, step):
    pairs = []
    for c in range(2):
        for z in range(2 * NZH):
            to = (z + (1 - 2 * c) * step) % (2 * NZH)
            pairs.append((((z % 2) * 2 + c) * NZH + z // 2, ((to % 2) * 2 + c) * NZH + to // 2))
    return lax.ppermute(values, ("zl", "c", "zh"), pairs)


def other_core(values):
    return lax.ppermute(values, "c", [(0, 1), (1, 0)])


def ring_gather(values, axis):
    back = turned(values, axis, 1)
    ahead = turned(values, axis, -1)
    return values, back, ahead, turned(back, axis, 1)


def normalize(values):
    length = jnp.sqrt(jnp.sum(values * values, axis=1, keepdims=True) + EPSILON)
    return values / length, length


def project_back(unit, direction, length):
    inner = jnp.sum(unit * direction, axis=1, keepdims=True)
    return (direction - unit * inner) / length


def halves(values):
    high = values.astype(BF16)
    return high, (values - high.astype(F32)).astype(BF16)


def dot3(left, right, dims):
    def dot(a, b):
        return lax.dot_general(a, b, (dims, ((), ())), preferred_element_type=F32)

    return dot(left[1], right[0]) + dot(left[0], right[1]) + dot(left[0], right[0])


def normalize_kernel(image_hbm, text_hbm, image_out, text_out, image_ref, text_ref, sems):
    copies = [
        pltpu.make_async_copy(text_hbm, text_ref, sems.at[0]),
        pltpu.make_async_copy(image_hbm, image_ref, sems.at[1]),
    ]
    for copy in copies:
        copy.start()
    copies[0].wait()
    text_unit = normalize(text_ref[...])[0]
    for y in range(NY):
        text_out[pl.ds(y * ROWS, ROWS), :] = text_unit
    copies[1].wait()
    image_out[...] = normalize(image_ref[...])[0]


def spread_kernel(*refs):
    for x in range(NX):
        for k, part in enumerate(refs[:-1]):
            refs[-1][pl.ds((x * NZH + k) * ROWS, ROWS), :] = part[...]


def tie_kernel(*refs):
    pass


def in_turn(place, image_ref):
    rows = image_ref.shape[0] // NX
    starts = [pl.multiple_of(place[1 + k] * rows, rows) for k in range(NX)]
    return halves(jnp.concatenate([image_ref[pl.ds(start, rows), :] for start in starts], axis=0))


def tile_kernel(place, image_ref, a_ref, b_ref, c_ref, d_ref, other_out, a_out, b_out, loss_out, *x_outs):
    image = in_turn(place, image_ref)
    quarter = a_ref.shape[0]
    count = image_ref.shape[0]
    row = lax.broadcasted_iota(jnp.int32, (count, quarter), 0)
    column = lax.broadcasted_iota(jnp.int32, (count, quarter), 1) - place[0]
    matched = (row == column) & (row < ROWS)
    lower, upper = other_out.at[pl.ds(0, quarter), :], other_out.at[pl.ds(quarter, quarter), :]
    total = jnp.zeros((), F32)
    image_dir = None
    for ref, out in ((c_ref, lower), (d_ref, upper), (a_ref, a_out), (b_ref, b_out)):
        text = halves(ref[...])
        logits = LOGIT_MULT * dot3(image, text, ((1,), (1,))) + LOGIT_SHIFT
        if ref is a_ref:
            logits = jnp.where(matched, -logits, logits)
        small = jnp.exp(-jnp.abs(logits))
        total += jnp.sum(jnp.maximum(logits, 0.0) + jnp.log1p(small))
        slope = jnp.where(logits >= 0.0, 1.0, small) / (1.0 + small) * (LOGIT_MULT / PAIRS)
        if ref is a_ref:
            slope = jnp.where(matched, -slope, slope)
        slope = halves(slope)
        out[...] = dot3(slope, image, ((0,), (0,)))
        term = dot3(slope, text, ((1,), (0,)))
        image_dir = term if image_dir is None else image_dir + term
    rows = count // NX
    for k, out in enumerate(x_outs):
        out[...] = image_dir[k * rows : (k + 1) * rows]
    loss_out[...] = jnp.full(loss_out.shape, total)


def add_kernel(b_ref, received_ref, back_ref, relay_ref, losses_ref, send_out, back_out):
    quarter = b_ref.shape[0]
    send_out[...] = b_ref[...] + received_ref[pl.ds(quarter, quarter), :]
    back_out[...] = back_ref[...] + relay_ref[...]


def relay_kernel(left, right, out):
    out[...] = left[...] + right[...]


def join_kernel(x0, x1, x2, a_ref, core_ref, plane_ref, losses_ref, packed_out, *zs):
    for k, out in enumerate(zs):
        rows = pl.ds(k * ROWS, ROWS)
        out[...] = x0[rows, :] + (x1[rows, :] + x2[rows, :])
    loss = jnp.sum(losses_ref[:, 0:1])
    for y in range(NY):
        rows = pl.ds(y * ROWS, ROWS)
        for k in range(COLS):
            lanes = pl.ds(k * LANES, LANES)
            packed_out[y, pl.ds(k * ROWS, ROWS), :] = (
                a_ref[rows, lanes] + core_ref[rows, lanes] + plane_ref[rows, lanes]
            )
        packed_out[y, pl.ds(PACK, 8), :] = jnp.full((8, LANES), loss)


def image_grad_kernel(emb_ref, z0, z1, z2, out):
    unit, length = normalize(emb_ref[...])
    out[...] = project_back(unit, z0[...] + (z1[...] + z2[...]), length)


def text_grad_kernel(emb_ref, packed_ref, out, loss_out):
    unit, length = normalize(emb_ref[...])
    total = packed_ref[0]
    for y in range(1, NY):
        total = total + packed_ref[y]
    direction = jnp.concatenate([total[k * ROWS : (k + 1) * ROWS] for k in range(COLS)], axis=1)
    out[...] = project_back(unit, direction, length)
    loss_out[0, 0] = jnp.max(total[PACK:]) / PAIRS


def on_device(image_emb, text_emb):
    rows, features = image_emb.shape
    image_unit, text_tiled = call(
        normalize_kernel,
        (image_emb, text_emb),
        [shape(rows, features), shape(NY * rows, features)],
        in_specs=[HBM] * 2,
        scratch_shapes=[pltpu.VMEM((rows, features), F32)] * 2 + [pltpu.SemaphoreType.DMA((2,))],
    )
    text_a = exchange(text_tiled, "y")
    (image_tiled,) = call(spread_kernel, ring_gather(image_unit, "zh"), [shape(NX * NZH * rows, features)])
    (text_a,) = call(
        tie_kernel, (text_a, image_tiled), [shape(*text_a.shape)], [ANY] * 2, [ANY], input_output_aliases={0: 0}
    )
    image = exchange(image_tiled, "x")
    text_b = planes(text_a, -1)
    texts = (text_a, text_b, other_core(text_a), other_core(text_b))

    count, quarter = image.shape[0], text_a.shape[0]
    part = count // NX
    x, turn = lax.axis_index("x"), 1 - 2 * lax.axis_index("c")
    blocks = [x, (x - turn) % NX, (x + turn) % NX, (x + 2) % NX]
    place = jnp.stack([lax.axis_index("y") * rows, *blocks]).astype(jnp.int32)
    product = 2 * count * quarter * features * 3
    other, text_a, text_b, loss, *xs = call(
        tile_kernel,
        (place, image, *texts),
        [shape(2 * quarter, features)]
        + [shape(quarter, features)] * 2
        + [shape(64, LANES)]
        + [shape(part, features)] * NX,
        in_specs=[SMEM] + [VMEM] * 5,
        flops=12 * product,
        vmem=24,
    )
    received = other_core(other)
    relay = turned(xs[3], "x", -1)
    losses = exchange(loss, ("zl", "c", "zh", "x"))
    send, relay = call(
        add_kernel,
        (text_b, received, xs[1], relay, losses),
        [shape(quarter, features), shape(part, features)],
        in_specs=[VMEM] * 4 + [ANY],
    )
    plane = planes(send, 1)
    back = turned(relay, "x", -1)
    ahead = turned(xs[2], "x", 1)
    packed, *zs = call(
        join_kernel,
        (xs[0], back, ahead, text_a, received, plane, losses),
        [shape(NY, PACK + 8, LANES)] + [shape(rows, features)] * NZH,
    )
    packed = exchange(packed, "y")
    relay = turned(zs[3], "zh", -1)
    ahead = turned(zs[2], "zh", 1)
    (relay,) = call(relay_kernel, (zs[1], relay), [shape(rows, features)])
    back = turned(relay, "zh", -1)
    (image_grad,) = call(image_grad_kernel, (image_emb, zs[0], back, ahead), [shape(rows, features)])
    text_grad, loss = call(
        text_grad_kernel,
        (text_emb, packed),
        [shape(rows, features), shape(1, 1)],
        out_specs=[VMEM, SMEM],
    )
    return loss.reshape(()), image_grad, text_grad


def solution(mesh):
    split = Mesh(mesh.devices.reshape(SIZES), AXES)
    return jax.shard_map(
        on_device,
        mesh=split,
        in_specs=(P(AXES, None), P(AXES, None)),
        out_specs=(P(), P(AXES, None), P(AXES, None)),
        check_vma=False,
    )
```

time: 138 us -> 131 us (0.949)
  blocking collectives: 0 us -> 19.5 us
  waiting for transfers between devices: 35.6 us -> 21.1 us
  starting transfers between devices: 84.5 us -> 74.3 us
  Pallas kernels: 14 us -> 12.1 us
    all_to_all x0 -> x1, blocking collectives: none -> 19.5 us  [exchange(): return lax.all_to_all(values, axes, 0, 0, tiled=True)]
    ppermute x12 -> x9, starting transfers between devices: 44.3 us -> 34.8 us  [turned(): return lax.ppermute(values, ('c', axis), pairs)]
    ppermute x12 -> x9, waiting for transfers between devices: 23.7 us -> 15.4 us  [turned(): return lax.ppermute(values, ('c', axis), pairs)]
    all_to_all x3, waiting for transfers between devices: 9.06 us -> 3.98 us  [exchange(): return lax.all_to_all(values, axes, 0, 0, tiled=True)]
    all_to_all x3, starting transfers between devices: 20.1 us -> 15.4 us  [exchange(): return lax.all_to_all(values, axes, 0, 0, tiled=True)]
    ppermute x2 -> x3, starting transfers between devices: 13.9 us -> 18.1 us  [other_core(): return lax.ppermute(values, 'c', [(0, 1), (1, 0)])]
    ppermute x2, waiting for transfers between devices: 2.88 us -> 0.28 us  [planes(): return lax.ppermute(values, ('zl', 'c', 'zh'), pairs)]
    pallas_call x12 -> x9, Pallas kernels: 14 us -> 12.1 us  [call(): pl.pallas_call(kernel, out_shape=outs, in_specs=in_specs or [VMEM] * len(...]
  transfers between devices with their start and end apart: 19 -> 17, of which waited for: 12 -> 9; matrix products, arithmetic and copies ran while one was open for 0% -> 0% of each run, Pallas kernels for 4% -> 2%
where the time goes in v5:
time: 131 us; the launch traced here: 130 us
  starting transfers between devices  74.3 us (57%)
  waiting for transfers between devices  21.1 us (16%)
  blocking collectives  19.5 us (15%)
  Pallas kernels  12.1 us (9%)
  local copies, waits for them, and re-layouts  1.86 us (1%)
    ppermute x9, starting transfers between devices, turned(): return lax.ppermute(values, ('c', axis), pairs)  34.8 us
    all_to_all x1, blocking collectives, exchange(): return lax.all_to_all(values, axes, 0, 0, tiled=True)  19.5 us
    ppermute x3, starting transfers between devices, other_core(): return lax.ppermute(values, 'c', [(0, 1), (1, 0)])  18.1 us
    ppermute x9, waiting for transfers between devices, turned(): return lax.ppermute(values, ('c', axis), pairs)  15.4 us
    all_to_all x3, starting transfers between devices, exchange(): return lax.all_to_all(values, axes, 0, 0, tiled=True)  15.4 us
    pallas_call x9, Pallas kernels, call(): pl.pallas_call(kernel, out_shape=outs, in_specs=in_specs or [VMEM] * len(...  12.1 us
    ppermute x2, starting transfers between devices, planes(): return lax.ppermute(values, ('zl', 'c', 'zh'), pairs)  6.04 us
    all_to_all x3, waiting for transfers between devices, exchange(): return lax.all_to_all(values, axes, 0, 0, tiled=True)  3.98 us
  transfers between devices with their start and end apart: 17, of which 9 were waited for; matrix products, arithmetic and copies ran while one was open for 0% of the time, Pallas kernels for 2%

profile of v5, /device:TPU:1, one launch (start us, length us, event | category | flops | bytes accessed | tf_op | source)
XLA Modules:
  0.0 129.8 jit_solution(10710831999161060535)
XLA Ops:
  3.5 7.7 %all-to-all-start.1 = ((f32[8,16,1152]{2,1,0:T(8,128)}), f32[8,16,1152]{2,1,0:T(8,128)S(1)}, u32[]{:S(2)}, u32[]{:S(2)}) async-start(f32[8,16,1152]{2,1,0:T(8,128)} %bitcast.7), calls=%async_computation.1 | async-start | bytes 1179648 | tf_op jit(solution)/shard_map/all_to_all | solution.py:45
  11.2 10.6 %collective-permute-start = (f32[16,1152]{1,0:T(8,128)S(1)}, f32[16,1152]{1,0:T(8,128)S(1)}, u32[]{:S(2)}, u32[]{:S(2)}) collective-permute-start(f32[16,1152]{1,0:T(8,128)S(1)} %get-tuple-element.22.refs_0_), channel_id=1, source_target_pairs={{0,4},{4,8},{8,12},{12,0},{16,28},{20,16},{24,20},{28,24},{1,5},{5... | collective-permute-start | bytes 221192 | tf_op jit(solution)/shard_map/ppermute | solution.py:51
  21.9 1.9 %collective-permute-start.1 = (f32[16,1152]{1,0:T(8,128)S(1)}, f32[16,1152]{1,0:T(8,128)S(1)}, u32[]{:S(2)}, u32[]{:S(2)}) collective-permute-start(f32[16,1152]{1,0:T(8,128)S(1)} %get-tuple-element.22.refs_0_), channel_id=1, source_target_pairs={{0,12},{4,0},{8,4},{12,8},{16,20},{20,24},{24,28},{28,16},{1,13},{... | collective-permute-start | bytes 221192 | tf_op jit(solution)/shard_map/ppermute | solution.py:51
  23.8 5.5 %collective-permute-start.2 = (f32[16,1152]{1,0:T(8,128)S(1)}, f32[16,1152]{1,0:T(8,128)S(1)}, u32[]{:S(2)}, u32[]{:S(2)}) collective-permute-start(f32[16,1152]{1,0:T(8,128)S(1)} %collective-permute-done.refs_1_), channel_id=1, source_target_pairs={{0,4},{4,8},{8,12},{12,0},{16,28},{20,16},{24,20},{28,24},{1,5},{5... | collective-permute-start | bytes 221192 | tf_op jit(solution)/shard_map/ppermute | solution.py:51
  31.8 4.0 %collective-permute-start.3 = (f32[128,1152]{1,0:T(8,128)S(1)}, f32[128,1152]{1,0:T(8,128)S(1)}, u32[]{:S(2)}, u32[]{:S(2)}) collective-permute-start(f32[128,1152]{1,0:T(8,128)S(1)} %shard_map.51.a_ref), channel_id=1, source_target_pairs={{0,44},{32,0},{4,32},{36,4},{8,36},{40,8},{12,40},{44,12},{16,48},... | collective-permute-start | bytes 1769480 | tf_op jit(solution)/shard_map/ppermute | solution.py:60
  35.8 4.0 %all-to-all-start = ((f32[4,64,1152]{2,1,0:T(8,128)}), f32[4,64,1152]{2,1,0:T(8,128)S(1)}, u32[]{:S(2)}, u32[]{:S(2)}) async-start(f32[4,64,1152]{2,1,0:T(8,128)} %bitcast.5), calls=%async_computation | async-start | bytes 2359296 | tf_op jit(solution)/shard_map/all_to_all | solution.py:45
  39.8 8.4 %collective-permute-start.4 = (f32[128,1152]{1,0:T(8,128)S(1)}, f32[128,1152]{1,0:T(8,128)S(1)}, u32[]{:S(2)}, u32[]{:S(2)}) collective-permute-start(f32[128,1152]{1,0:T(8,128)S(1)} %shard_map.51.a_ref), channel_id=1, source_target_pairs={{0,16},{16,0},{1,17},{17,1},{2,18},{18,2},{3,19},{19,3},{4,20},{20... | collective-permute-start | bytes 1769480 | tf_op jit(solution)/shard_map/ppermute | solution.py:64
  48.5 2.8 %collective-permute-start.5 = (f32[128,1152]{1,0:T(8,128)S(1)}, f32[128,1152]{1,0:T(8,128)S(1)}, u32[]{:S(2)}, u32[]{:S(2)}) collective-permute-start(f32[128,1152]{1,0:T(8,128)S(1)} %collective-permute-done.3.b_ref), channel_id=1, source_target_pairs={{0,16},{16,0},{1,17},{17,1},{2,18},{18,2},{3,19},{19,3},{4,20},{20... | collective-permute-start | bytes 1769480 | tf_op jit(solution)/shard_map/ppermute | solution.py:64
  51.4 1.5 %collective-permute-done.5.d_ref = f32[128,1152]{1,0:T(8,128)S(1)} collective-permute-done((f32[128,1152]{1,0:T(8,128)S(1)}, f32[128,1152]{1,0:T(8,128)S(1)}, u32[]{:S(2)}, u32[]{:S(2)}) %collective-permute-start.5) | collective-permute-done | bytes 589856 | tf_op jit(solution)/shard_map/ppermute | solution.py:64
  52.9 7.1 %shard_map.52 = (f32[256,1152]{1,0:T(8,128)S(1)}, f32[128,1152]{1,0:T(8,128)S(1)}, f32[128,1152]{1,0:T(8,128)S(1)}, f32[64,128]{1,0:T(8,128)S(1)}, f32[64,1152]{...) custom-call(s32[5]{0:T(128)S(1)} %stack.23.place, ...), custom_call_target="tpu_custom_call" | custom-call | flops 2717908992 | bytes 7110676 | tf_op jit(solution)/shard_map/pallas_call | solution.py:33
  60.0 6.9 %collective-permute-start.6 = (f32[256,1152]{1,0:T(8,128)S(1)}, f32[256,1152]{1,0:T(8,128)S(1)}, u32[]{:S(2)}, u32[]{:S(2)}) collective-permute-start(f32[256,1152]{1,0:T(8,128)S(1)} %get-tuple-element.26), channel_id=1, source_target_pairs={{0,16},{16,0},{1,17},{17,1},{2,18},{18,2},{3,19},{19,3},{4,20},{20... | collective-permute-start | bytes 3538952 | tf_op jit(solution)/shard_map/ppermute | solution.py:64
  66.9 2.2 %collective-permute-start.7 = (f32[64,1152]{1,0:T(8,128)S(1)}, f32[64,1152]{1,0:T(8,128)S(1)}, u32[]{:S(2)}, u32[]{:S(2)}) collective-permute-start(f32[64,1152]{1,0:T(8,128)S(1)} %get-tuple-element.28), channel_id=1, source_target_pairs={{0,3},{1,0},{2,1},{3,2},{16,17},{17,18},{18,19},{19,16},{4,7},{5,4... | collective-permute-start | bytes 884744 | tf_op jit(solution)/shard_map/ppermute | solution.py:51
  69.1 19.5 %all_to_all.38 = f32[64,1,128]{2,1,0:T(1,128)S(1)} all-to-all(f32[64,1,128]{2,1,0:T(1,128)S(1)} %bitcast.18), channel_id=1, replica_groups=mesh['y'=8,'zl'=2,'c'=2,'zh'=4,'x'=4] {'zl','c','zh','x'}, dimensions={0} | all-to-all | bytes 65536 | tf_op jit(solution)/shard_map/all_to_all | solution.py:45
  88.7 2.0 %collective-permute-start.10 = (f32[128,1152]{1,0:T(8,128)S(1)}, f32[128,1152]{1,0:T(8,128)S(1)}, u32[]{:S(2)}, u32[]{:S(2)}) collective-permute-start(f32[128,1152]{1,0:T(8,128)S(1)} %get-tuple-element.33), channel_id=1, source_target_pairs={{0,32},{32,4},{4,36},{36,8},{8,40},{40,12},{12,44},{44,0},{16,60},... | collective-permute-start | bytes 1769480 | tf_op jit(solution)/shard_map/ppermute | solution.py:60
  90.7 2.9 %collective-permute-start.9 = (f32[64,1152]{1,0:T(8,128)S(1)}, f32[64,1152]{1,0:T(8,128)S(1)}, u32[]{:S(2)}, u32[]{:S(2)}) collective-permute-start(f32[64,1152]{1,0:T(8,128)S(1)} %get-tuple-element.31), channel_id=1, source_target_pairs={{0,1},{1,2},{2,3},{3,0},{16,19},{17,16},{18,17},{19,18},{4,5},{5,6... | collective-permute-start | bytes 884744 | tf_op jit(solution)/shard_map/ppermute | solution.py:51
  93.6 2.4 %collective-permute-start.8 = (f32[64,1152]{1,0:T(8,128)S(1)}, f32[64,1152]{1,0:T(8,128)S(1)}, u32[]{:S(2)}, u32[]{:S(2)}) collective-permute-start(f32[64,1152]{1,0:T(8,128)S(1)} %get-tuple-element.30), channel_id=1, source_target_pairs={{0,3},{1,0},{2,1},{3,2},{16,17},{17,18},{18,19},{19,16},{4,7},{5,4... | collective-permute-start | bytes 884744 | tf_op jit(solution)/shard_map/ppermute | solution.py:51
  96.0 2.5 %collective-permute-done.9.x2 = f32[64,1152]{1,0:T(8,128)S(1)} collective-permute-done((f32[64,1152]{1,0:T(8,128)S(1)}, f32[64,1152]{1,0:T(8,128)S(1)}, u32[]{:S(2)}, u32[]{:S(2)}) %collective-permute-start.9) | collective-permute-done | bytes 294944 | tf_op jit(solution)/shard_map/ppermute | solution.py:51
  98.5 5.7 %collective-permute-done.8.x1 = f32[64,1152]{1,0:T(8,128)S(1)} collective-permute-done((f32[64,1152]{1,0:T(8,128)S(1)}, f32[64,1152]{1,0:T(8,128)S(1)}, u32[]{:S(2)}, u32[]{:S(2)}) %collective-permute-start.8) | collective-permute-done | bytes 294944 | tf_op jit(solution)/shard_map/ppermute | solution.py:51
  105.2 3.7 %all-to-all-start.3 = ((f32[8,152,128]{2,1,0:T(8,128)}), f32[8,152,128]{2,1,0:T(8,128)S(1)}, u32[]{:S(2)}, u32[]{:S(2)}) async-start(f32[8,152,128]{2,1,0:T(8,128)} %get-tuple-element.34), calls=%async_computation.3 | async-start | bytes 1245184 | tf_op jit(solution)/shard_map/all_to_all | solution.py:45
  108.9 2.2 %collective-permute-start.11 = (f32[16,1152]{1,0:T(8,128)S(1)}, f32[16,1152]{1,0:T(8,128)S(1)}, u32[]{:S(2)}, u32[]{:S(2)}) collective-permute-start(f32[16,1152]{1,0:T(8,128)S(1)} %get-tuple-element.38), channel_id=1, source_target_pairs={{0,12},{4,0},{8,4},{12,8},{16,20},{20,24},{24,28},{28,16},{1,13},{... | collective-permute-start | bytes 221192 | tf_op jit(solution)/shard_map/ppermute | solution.py:51
  111.1 5.2 %collective-permute-start.13 = (f32[16,1152]{1,0:T(8,128)S(1)}, f32[16,1152]{1,0:T(8,128)S(1)}, u32[]{:S(2)}, u32[]{:S(2)}) collective-permute-start(f32[16,1152]{1,0:T(8,128)S(1)} %get-tuple-element.39), channel_id=1, source_target_pairs={{0,4},{4,8},{8,12},{12,0},{16,28},{20,16},{24,20},{28,24},{1,5},{5... | collective-permute-start | bytes 221192 | tf_op jit(solution)/shard_map/ppermute | solution.py:51
  116.9 1.9 %collective-permute-start.12 = (f32[16,1152]{1,0:T(8,128)S(1)}, f32[16,1152]{1,0:T(8,128)S(1)}, u32[]{:S(2)}, u32[]{:S(2)}) collective-permute-start(f32[16,1152]{1,0:T(8,128)S(1)} %shard_map.56), channel_id=1, source_target_pairs={{0,12},{4,0},{8,4},{12,8},{16,20},{20,24},{24,28},{28,16},{1,13},{... | collective-permute-start | bytes 221192 | tf_op jit(solution)/shard_map/ppermute | solution.py:51
  118.8 5.3 %collective-permute-done.12.z1 = f32[16,1152]{1,0:T(8,128)S(1)} collective-permute-done((f32[16,1152]{1,0:T(8,128)S(1)}, f32[16,1152]{1,0:T(8,128)S(1)}, u32[]{:S(2)}, u32[]{:S(2)}) %collective-permute-start.12) | collective-permute-done | bytes 73760 | tf_op jit(solution)/shard_map/ppermute | solution.py:51
  124.9 4.0 %all-to-all-done.3.packed_ref = f32[8,152,128]{2,1,0:T(8,128)S(1)} async-done(((f32[8,152,128]{2,1,0:T(8,128)}), f32[8,152,128]{2,1,0:T(8,128)S(1)}, u32[]{:S(2)}, u32[]{:S(2)}) %all-to-all-start.3) | async-done | bytes 622624 | tf_op jit(solution)/shard_map/all_to_all | solution.py:45
  (29 shorter events, 9.1 us)
Async XLA Ops:
  0.6 0.9 copy-start
  1.5 0.9 copy-start.2
  3.5 28.2 %all-to-all-start.1 = ((f32[8,16,1152]{2,1,0:T(8,128)}), f32[8,16,1152]{2,1,0:T(8,128)S(1)}, u32[]{:S(2)}, u32[]{:S(2)}) async-start(f32[8,16,1152]{2,1,0:T(8,128)} %bitcast.7), calls=%async_computation.1 | async-start | bytes 1179648 | tf_op jit(solution)/shard_map/all_to_all | solution.py:45
  11.2 12.6 %collective-permute-start = (f32[16,1152]{1,0:T(8,128)S(1)}, f32[16,1152]{1,0:T(8,128)S(1)}, u32[]{:S(2)}, u32[]{:S(2)}) collective-permute-start(f32[16,1152]{1,0:T(8,128)S(1)} %get-tuple-element.22.refs_0_), channel_id=1, source_target_pairs={{0,4},{4,8},{8,12},{12,0},{16,28},{20,16},{24,20},{28,24},{1,5},{5... | collective-permute-start | bytes 221192 | tf_op jit(solution)/shard_map/ppermute | solution.py:51
  21.9 8.7 %collective-permute-start.1 = (f32[16,1152]{1,0:T(8,128)S(1)}, f32[16,1152]{1,0:T(8,128)S(1)}, u32[]{:S(2)}, u32[]{:S(2)}) collective-permute-start(f32[16,1152]{1,0:T(8,128)S(1)} %get-tuple-element.22.refs_0_), channel_id=1, source_target_pairs={{0,12},{4,0},{8,4},{12,8},{16,20},{20,24},{24,28},{28,16},{1,13},{... | collective-permute-start | bytes 221192 | tf_op jit(solution)/shard_map/ppermute | solution.py:51
  23.8 6.9 %collective-permute-start.2 = (f32[16,1152]{1,0:T(8,128)S(1)}, f32[16,1152]{1,0:T(8,128)S(1)}, u32[]{:S(2)}, u32[]{:S(2)}) collective-permute-start(f32[16,1152]{1,0:T(8,128)S(1)} %collective-permute-done.refs_1_), channel_id=1, source_target_pairs={{0,4},{4,8},{8,12},{12,0},{16,28},{20,16},{24,20},{28,24},{1,5},{5... | collective-permute-start | bytes 221192 | tf_op jit(solution)/shard_map/ppermute | solution.py:51
  31.8 16.7 %collective-permute-start.3 = (f32[128,1152]{1,0:T(8,128)S(1)}, f32[128,1152]{1,0:T(8,128)S(1)}, u32[]{:S(2)}, u32[]{:S(2)}) collective-permute-start(f32[128,1152]{1,0:T(8,128)S(1)} %shard_map.51.a_ref), channel_id=1, source_target_pairs={{0,44},{32,0},{4,32},{36,4},{8,36},{40,8},{12,40},{44,12},{16,48},... | collective-permute-start | bytes 1769480 | tf_op jit(solution)/shard_map/ppermute | solution.py:60
  35.8 15.6 %all-to-all-start = ((f32[4,64,1152]{2,1,0:T(8,128)}), f32[4,64,1152]{2,1,0:T(8,128)S(1)}, u32[]{:S(2)}, u32[]{:S(2)}) async-start(f32[4,64,1152]{2,1,0:T(8,128)} %bitcast.5), calls=%async_computation | async-start | bytes 2359296 | tf_op jit(solution)/shard_map/all_to_all | solution.py:45
  39.8 11.6 %collective-permute-start.4 = (f32[128,1152]{1,0:T(8,128)S(1)}, f32[128,1152]{1,0:T(8,128)S(1)}, u32[]{:S(2)}, u32[]{:S(2)}) collective-permute-start(f32[128,1152]{1,0:T(8,128)S(1)} %shard_map.51.a_ref), channel_id=1, source_target_pairs={{0,16},{16,0},{1,17},{17,1},{2,18},{18,2},{3,19},{19,3},{4,20},{20... | collective-permute-start | bytes 1769480 | tf_op jit(solution)/shard_map/ppermute | solution.py:64
  48.5 4.4 %collective-permute-start.5 = (f32[128,1152]{1,0:T(8,128)S(1)}, f32[128,1152]{1,0:T(8,128)S(1)}, u32[]{:S(2)}, u32[]{:S(2)}) collective-permute-start(f32[128,1152]{1,0:T(8,128)S(1)} %collective-permute-done.3.b_ref), channel_id=1, source_target_pairs={{0,16},{16,0},{1,17},{17,1},{2,18},{18,2},{3,19},{19,3},{4,20},{20... | collective-permute-start | bytes 1769480 | tf_op jit(solution)/shard_map/ppermute | solution.py:64
  60.0 28.6 %collective-permute-start.6 = (f32[256,1152]{1,0:T(8,128)S(1)}, f32[256,1152]{1,0:T(8,128)S(1)}, u32[]{:S(2)}, u32[]{:S(2)}) collective-permute-start(f32[256,1152]{1,0:T(8,128)S(1)} %get-tuple-element.26), channel_id=1, source_target_pairs={{0,16},{16,0},{1,17},{17,1},{2,18},{18,2},{3,19},{19,3},{4,20},{20... | collective-permute-start | bytes 3538952 | tf_op jit(solution)/shard_map/ppermute | solution.py:64
  66.9 21.7 %collective-permute-start.7 = (f32[64,1152]{1,0:T(8,128)S(1)}, f32[64,1152]{1,0:T(8,128)S(1)}, u32[]{:S(2)}, u32[]{:S(2)}) collective-permute-start(f32[64,1152]{1,0:T(8,128)S(1)} %get-tuple-element.28), channel_id=1, source_target_pairs={{0,3},{1,0},{2,1},{3,2},{16,17},{17,18},{18,19},{19,16},{4,7},{5,4... | collective-permute-start | bytes 884744 | tf_op jit(solution)/shard_map/ppermute | solution.py:51
  88.7 15.5 %collective-permute-start.10 = (f32[128,1152]{1,0:T(8,128)S(1)}, f32[128,1152]{1,0:T(8,128)S(1)}, u32[]{:S(2)}, u32[]{:S(2)}) collective-permute-start(f32[128,1152]{1,0:T(8,128)S(1)} %get-tuple-element.33), channel_id=1, source_target_pairs={{0,32},{32,4},{4,36},{36,8},{8,40},{40,12},{12,44},{44,0},{16,60},... | collective-permute-start | bytes 1769480 | tf_op jit(solution)/shard_map/ppermute | solution.py:60
  90.7 7.8 %collective-permute-start.9 = (f32[64,1152]{1,0:T(8,128)S(1)}, f32[64,1152]{1,0:T(8,128)S(1)}, u32[]{:S(2)}, u32[]{:S(2)}) collective-permute-start(f32[64,1152]{1,0:T(8,128)S(1)} %get-tuple-element.31), channel_id=1, source_target_pairs={{0,1},{1,2},{2,3},{3,0},{16,19},{17,16},{18,17},{19,18},{4,5},{5,6... | collective-permute-start | bytes 884744 | tf_op jit(solution)/shard_map/ppermute | solution.py:51
  93.6 10.6 %collective-permute-start.8 = (f32[64,1152]{1,0:T(8,128)S(1)}, f32[64,1152]{1,0:T(8,128)S(1)}, u32[]{:S(2)}, u32[]{:S(2)}) collective-permute-start(f32[64,1152]{1,0:T(8,128)S(1)} %get-tuple-element.30), channel_id=1, source_target_pairs={{0,3},{1,0},{2,1},{3,2},{16,17},{17,18},{18,19},{19,16},{4,7},{5,4... | collective-permute-start | bytes 884744 | tf_op jit(solution)/shard_map/ppermute | solution.py:51
  105.2 18.9 %copy-start.1 = (f32[16,1152]{1,0:T(8,128)S(1)}, f32[16,1152]{1,0:T(8,128)}, u32[]{:S(2)}) copy-start(f32[16,1152]{1,0:T(8,128)} %emb_ref.3) | copy-start | bytes 221188
  105.2 23.7 %copy-start.3 = (f32[16,1152]{1,0:T(8,128)S(1)}, f32[16,1152]{1,0:T(8,128)}, u32[]{:S(2)}) copy-start(f32[16,1152]{1,0:T(8,128)} %emb_ref.2) | copy-start | bytes 221188
  105.2 23.7 %all-to-all-start.3 = ((f32[8,152,128]{2,1,0:T(8,128)}), f32[8,152,128]{2,1,0:T(8,128)S(1)}, u32[]{:S(2)}, u32[]{:S(2)}) async-start(f32[8,152,128]{2,1,0:T(8,128)} %get-tuple-element.34), calls=%async_computation.3 | async-start | bytes 1245184 | tf_op jit(solution)/shard_map/all_to_all | solution.py:45
  108.9 8.0 %collective-permute-start.11 = (f32[16,1152]{1,0:T(8,128)S(1)}, f32[16,1152]{1,0:T(8,128)S(1)}, u32[]{:S(2)}, u32[]{:S(2)}) collective-permute-start(f32[16,1152]{1,0:T(8,128)S(1)} %get-tuple-element.38), channel_id=1, source_target_pairs={{0,12},{4,0},{8,4},{12,8},{16,20},{20,24},{24,28},{28,16},{1,13},{... | collective-permute-start | bytes 221192 | tf_op jit(solution)/shard_map/ppermute | solution.py:51
  111.1 7.7 %collective-permute-start.13 = (f32[16,1152]{1,0:T(8,128)S(1)}, f32[16,1152]{1,0:T(8,128)S(1)}, u32[]{:S(2)}, u32[]{:S(2)}) collective-permute-start(f32[16,1152]{1,0:T(8,128)S(1)} %get-tuple-element.39), channel_id=1, source_target_pairs={{0,4},{4,8},{8,12},{12,0},{16,28},{20,16},{24,20},{28,24},{1,5},{5... | collective-permute-start | bytes 221192 | tf_op jit(solution)/shard_map/ppermute | solution.py:51
  116.9 7.2 %collective-permute-start.12 = (f32[16,1152]{1,0:T(8,128)S(1)}, f32[16,1152]{1,0:T(8,128)S(1)}, u32[]{:S(2)}, u32[]{:S(2)}) collective-permute-start(f32[16,1152]{1,0:T(8,128)S(1)} %shard_map.56), channel_id=1, source_target_pairs={{0,12},{4,0},{8,4},{12,8},{16,20},{20,24},{24,28},{28,16},{1,13},{... | collective-permute-start | bytes 221192 | tf_op jit(solution)/shard_map/ppermute | solution.py:51

commit v6 on v5

--- a/solution.py
+++ b/solution.py
@@ -117,44 +117,55 @@
     pass
 
 
-def in_turn(place, image_ref):
-    rows = image_ref.shape[0] // NX
-    starts = [pl.multiple_of(place[1 + k] * rows, rows) for k in range(NX)]
-    return halves(jnp.concatenate([image_ref[pl.ds(start, rows), :] for start in starts], axis=0))
-
-
-def tile_kernel(place, image_ref, a_ref, b_ref, c_ref, d_ref, other_out, a_out, b_out, loss_out, *x_outs):
-    image = in_turn(place, image_ref)
-    quarter = a_ref.shape[0]
-    count = image_ref.shape[0]
+def tile_kernel(place, image_hbm, a_hbm, b_hbm, c_hbm, d_hbm, other_out, a_out, b_out, *refs):
+    x_outs, (image_ref, texts_ref, sems) = refs[:NX], refs[NX:]
+    count, quarter = image_ref.shape[0], a_out.shape[0]
+    rows = count // NX
+    copies = []
+    for k in range(NX):
+        start = pl.multiple_of(place[1 + k] * rows, rows)
+        copies.append((image_hbm.at[pl.ds(start, rows), :], image_ref.at[pl.ds(k * rows, rows), :]))
+    for k, ref in enumerate((a_hbm, b_hbm, c_hbm, d_hbm)):
+        copies.append((ref, texts_ref.at[k]))
+    copies = [pltpu.make_async_copy(*ends, sems.at[k]) for k, ends in enumerate(copies)]
+    for copy in copies:
+        copy.start()
+    for copy in copies[:NX]:
+        copy.wait()
+    image = halves(image_ref[...])
     row = lax.broadcasted_iota(jnp.int32, (count, quarter), 0)
     column = lax.broadcasted_iota(jnp.int32, (count, quarter), 1) - place[0]
     matched = (row == column) & (row < ROWS)
     lower, upper = other_out.at[pl.ds(0, quarter), :], other_out.at[pl.ds(quarter, quarter), :]
     total = jnp.zeros((), F32)
     image_dir = None
-    for ref, out in ((c_ref, lower), (d_ref, upper), (a_ref, a_out), (b_ref, b_out)):
-        text = halves(ref[...])
+    for k, out in enumerate((a_out, b_out, lower, upper)):
+        copies[NX + k].wait()
+        text = halves(texts_ref[k])
         logits = LOGIT_MULT * dot3(image, text, ((1,), (1,))) + LOGIT_SHIFT
-        if ref is a_ref:
+        if k == 0:
             logits = jnp.where(matched, -logits, logits)
         small = jnp.exp(-jnp.abs(logits))
         total += jnp.sum(jnp.maximum(logits, 0.0) + jnp.log1p(small))
         slope = jnp.where(logits >= 0.0, 1.0, small) / (1.0 + small) * (LOGIT_MULT / PAIRS)
-        if ref is a_ref:
+        if k == 0:
             slope = jnp.where(matched, -slope, slope)
         slope = halves(slope)
         out[...] = dot3(slope, image, ((0,), (0,)))
         term = dot3(slope, text, ((1,), (0,)))
         image_dir = term if image_dir is None else image_dir + term
-    rows = count // NX
     for k, out in enumerate(x_outs):
         out[...] = image_dir[k * rows : (k + 1) * rows]
-    loss_out[...] = jnp.full(loss_out.shape, total)
-
-
-def add_kernel(b_ref, received_ref, back_ref, relay_ref, losses_ref, send_out, back_out):
+    other_out[pl.ds(2 * quarter, 8), :] = jnp.full((8, FEATURES), total)
+
+
+def add_kernel(a_ref, b_ref, other_ref, received_ref, back_ref, relay_ref, keep_out, send_out, back_out, loss_out):
     quarter = b_ref.shape[0]
+    keep_out[...] = a_ref[...] + received_ref[pl.ds(0, quarter), :]
+    rows, lanes = pl.ds(2 * quarter, 8), pl.ds(0, LANES)
+    loss = other_ref[rows, lanes] + received_ref[rows, lanes]
+    for k in range(loss_out.shape[0] // 8):
+        loss_out[pl.ds(8 * k, 8), :] = loss
     send_out[...] = b_ref[...] + received_ref[pl.ds(quarter, quarter), :]
     back_out[...] = back_ref[...] + relay_ref[...]
 
@@ -163,7 +174,7 @@
     out[...] = left[...] + right[...]
 
 
-def join_kernel(x0, x1, x2, a_ref, core_ref, plane_ref, losses_ref, packed_out, *zs):
+def join_kernel(x0, x1, x2, keep_ref, plane_ref, losses_ref, packed_out, *zs):
     for k, out in enumerate(zs):
         rows = pl.ds(k * ROWS, ROWS)
         out[...] = x0[rows, :] + (x1[rows, :] + x2[rows, :])
@@ -172,9 +183,7 @@
         rows = pl.ds(y * ROWS, ROWS)
         for k in range(COLS):
             lanes = pl.ds(k * LANES, LANES)
-            packed_out[y, pl.ds(k * ROWS, ROWS), :] = (
-                a_ref[rows, lanes] + core_ref[rows, lanes] + plane_ref[rows, lanes]
-            )
+            packed_out[y, pl.ds(k * ROWS, ROWS), :] = keep_ref[rows, lanes] + plane_ref[rows, lanes]
         packed_out[y, pl.ds(PACK, 8), :] = jnp.full((8, LANES), loss)
 
 
@@ -217,32 +226,33 @@
     blocks = [x, (x - turn) % NX, (x + turn) % NX, (x + 2) % NX]
     place = jnp.stack([lax.axis_index("y") * rows, *blocks]).astype(jnp.int32)
     product = 2 * count * quarter * features * 3
-    other, text_a, text_b, loss, *xs = call(
+    other, text_a, text_b, *xs = call(
         tile_kernel,
         (place, image, *texts),
-        [shape(2 * quarter, features)]
-        + [shape(quarter, features)] * 2
-        + [shape(64, LANES)]
-        + [shape(part, features)] * NX,
-        in_specs=[SMEM] + [VMEM] * 5,
+        [shape(2 * quarter + 8, features)] + [shape(quarter, features)] * 2 + [shape(part, features)] * NX,
+        in_specs=[SMEM] + [ANY] * 5,
+        scratch_shapes=[
+            pltpu.VMEM((count, features), F32),
+            pltpu.VMEM((4, quarter, features), F32),
+            pltpu.SemaphoreType.DMA((NX + 4,)),
+        ],
         flops=12 * product,
         vmem=24,
     )
     received = other_core(other)
     relay = turned(xs[3], "x", -1)
-    losses = exchange(loss, ("zl", "c", "zh", "x"))
-    send, relay = call(
+    keep, send, relay, loss = call(
         add_kernel,
-        (text_b, received, xs[1], relay, losses),
-        [shape(quarter, features), shape(part, features)],
-        in_specs=[VMEM] * 4 + [ANY],
-    )
+        (text_a, text_b, other, received, xs[1], relay),
+        [shape(quarter, features)] * 2 + [shape(part, features), shape(32, LANES)],
+    )
+    losses = exchange(loss, ("zl", "zh", "x"))
     plane = planes(send, 1)
     back = turned(relay, "x", -1)
     ahead = turned(xs[2], "x", 1)
     packed, *zs = call(
         join_kernel,
-        (xs[0], back, ahead, text_a, received, plane, losses),
+        (xs[0], back, ahead, keep, plane, losses),
         [shape(NY, PACK + 8, LANES)] + [shape(rows, features)] * NZH,
     )
     packed = exchange(packed, "y")

time: 131 us -> 129 us (0.985); the launches traced: 130 us -> 126 us
  blocking collectives: 19.5 us -> 0 us
  starting transfers between devices: 74.3 us -> 83.7 us
  waiting for transfers between devices: 21.1 us -> 25.2 us
  Pallas kernels: 12.1 us -> 14.8 us
    all_to_all x1 -> x0, blocking collectives: 19.5 us -> none  [exchange(): return lax.all_to_all(values, axes, 0, 0, tiled=True)]
    all_to_all x3 -> x4, waiting for transfers between devices: 3.98 us -> 9.16 us  [exchange(): return lax.all_to_all(values, axes, 0, 0, tiled=True)]
    all_to_all x3 -> x4, starting transfers between devices: 15.4 us -> 20.2 us  [exchange(): return lax.all_to_all(values, axes, 0, 0, tiled=True)]
    ppermute x2, starting transfers between devices: 6.04 us -> 10.7 us  [planes(): return lax.ppermute(values, ('zl', 'c', 'zh'), pairs)]
    pallas_call x9, Pallas kernels: 12.1 us -> 14.8 us  [call(): pl.pallas_call(kernel, out_shape=outs, in_specs=in_specs or [VMEM] * len(...]
  transfers between devices with their start and end apart: 17 -> 18, of which waited for: 9 -> 10; matrix products, arithmetic and copies ran while one was open for 0% -> 0% of each run, Pallas kernels for 2% -> 2%
where the time goes in v6:
time: 129 us; the launch traced here: 126 us
  starting transfers between devices  83.7 us (65%)
  waiting for transfers between devices  25.2 us (20%)
  Pallas kernels  14.8 us (11%)
  local copies, waits for them, and re-layouts  1.86 us (1%)
    ppermute x9, starting transfers between devices, turned(): return lax.ppermute(values, ('c', axis), pairs)  34.8 us
    all_to_all x4, starting transfers between devices, exchange(): return lax.all_to_all(values, axes, 0, 0, tiled=True)  20.2 us
    ppermute x3, starting transfers between devices, other_core(): return lax.ppermute(values, 'c', [(0, 1), (1, 0)])  18 us
    pallas_call x9, Pallas kernels, call(): pl.pallas_call(kernel, out_shape=outs, in_specs=in_specs or [VMEM] * len(...  14.8 us
    ppermute x9, waiting for transfers between devices, turned(): return lax.ppermute(values, ('c', axis), pairs)  14.1 us
    ppermute x2, starting transfers between devices, planes(): return lax.ppermute(values, ('zl', 'c', 'zh'), pairs)  10.7 us
    all_to_all x4, waiting for transfers between devices, exchange(): return lax.all_to_all(values, axes, 0, 0, tiled=True)  9.16 us
  transfers between devices with their start and end apart: 18, of which 10 were waited for; matrix products, arithmetic and copies ran while one was open for 0% of the time, Pallas kernels for 2%

profile of v6, /device:TPU:1, one launch (start us, length us, event | category | flops | bytes accessed | tf_op | source)
XLA Modules:
  0.0 126.4 jit_solution(6532875942788373083)
XLA Ops:
  3.5 7.7 %all-to-all-start.1 = ((f32[8,16,1152]{2,1,0:T(8,128)}), f32[8,16,1152]{2,1,0:T(8,128)S(1)}, u32[]{:S(2)}, u32[]{:S(2)}) async-start(f32[8,16,1152]{2,1,0:T(8,128)} %bitcast.7), calls=%async_computation.1 | async-start | bytes 1179648 | tf_op jit(solution)/shard_map/all_to_all | solution.py:45
  11.2 10.6 %collective-permute-start = (f32[16,1152]{1,0:T(8,128)S(1)}, f32[16,1152]{1,0:T(8,128)S(1)}, u32[]{:S(2)}, u32[]{:S(2)}) collective-permute-start(f32[16,1152]{1,0:T(8,128)S(1)} %get-tuple-element.23.refs_0_), channel_id=1, source_target_pairs={{0,4},{4,8},{8,12},{12,0},{16,28},{20,16},{24,20},{28,24},{1,5},{5... | collective-permute-start | bytes 221192 | tf_op jit(solution)/shard_map/ppermute | solution.py:51
  21.9 1.9 %collective-permute-start.1 = (f32[16,1152]{1,0:T(8,128)S(1)}, f32[16,1152]{1,0:T(8,128)S(1)}, u32[]{:S(2)}, u32[]{:S(2)}) collective-permute-start(f32[16,1152]{1,0:T(8,128)S(1)} %get-tuple-element.23.refs_0_), channel_id=1, source_target_pairs={{0,12},{4,0},{8,4},{12,8},{16,20},{20,24},{24,28},{28,16},{1,13},{... | collective-permute-start | bytes 221192 | tf_op jit(solution)/shard_map/ppermute | solution.py:51
  23.8 5.5 %collective-permute-start.2 = (f32[16,1152]{1,0:T(8,128)S(1)}, f32[16,1152]{1,0:T(8,128)S(1)}, u32[]{:S(2)}, u32[]{:S(2)}) collective-permute-start(f32[16,1152]{1,0:T(8,128)S(1)} %collective-permute-done.refs_1_), channel_id=1, source_target_pairs={{0,4},{4,8},{8,12},{12,0},{16,28},{20,16},{24,20},{28,24},{1,5},{5... | collective-permute-start | bytes 221192 | tf_op jit(solution)/shard_map/ppermute | solution.py:51
  29.3 1.2 collective-permute-done.1.refs_2_
  31.8 4.0 %collective-permute-start.3 = (f32[128,1152]{1,0:T(8,128)S(1)}, f32[128,1152]{1,0:T(8,128)S(1)}, u32[]{:S(2)}, u32[]{:S(2)}) collective-permute-start(f32[128,1152]{1,0:T(8,128)S(1)} %shard_map.51.a_hbm), channel_id=1, source_target_pairs={{0,44},{32,0},{4,32},{36,4},{8,36},{40,8},{12,40},{44,12},{16,48},... | collective-permute-start | bytes 1769480 | tf_op jit(solution)/shard_map/ppermute | solution.py:60
  35.8 4.0 %all-to-all-start = ((f32[4,64,1152]{2,1,0:T(8,128)}), f32[4,64,1152]{2,1,0:T(8,128)S(1)}, u32[]{:S(2)}, u32[]{:S(2)}) async-start(f32[4,64,1152]{2,1,0:T(8,128)} %bitcast.5), calls=%async_computation | async-start | bytes 2359296 | tf_op jit(solution)/shard_map/all_to_all | solution.py:45
  39.8 8.4 %collective-permute-start.4 = (f32[128,1152]{1,0:T(8,128)S(1)}, f32[128,1152]{1,0:T(8,128)S(1)}, u32[]{:S(2)}, u32[]{:S(2)}) collective-permute-start(f32[128,1152]{1,0:T(8,128)S(1)} %shard_map.51.a_hbm), channel_id=1, source_target_pairs={{0,16},{16,0},{1,17},{17,1},{2,18},{18,2},{3,19},{19,3},{4,20},{20... | collective-permute-start | bytes 1769480 | tf_op jit(solution)/shard_map/ppermute | solution.py:64
  48.5 2.8 %collective-permute-start.5 = (f32[128,1152]{1,0:T(8,128)S(1)}, f32[128,1152]{1,0:T(8,128)}, u32[]{:S(2)}, u32[]{:S(2)}) collective-permute-start(f32[128,1152]{1,0:T(8,128)S(1)} %collective-permute-done.3.b_hbm), channel_id=1, source_target_pairs={{0,16},{16,0},{1,17},{17,1},{2,18},{18,2},{3,19},{19,3},{4,20},{20... | collective-permute-start | bytes 1769480 | tf_op jit(solution)/shard_map/ppermute | solution.py:64
  51.4 1.6 %collective-permute-done.5.d_hbm = f32[128,1152]{1,0:T(8,128)} collective-permute-done((f32[128,1152]{1,0:T(8,128)S(1)}, f32[128,1152]{1,0:T(8,128)}, u32[]{:S(2)}, u32[]{:S(2)}) %collective-permute-start.5) | collective-permute-done | bytes 589856 | tf_op jit(solution)/shard_map/ppermute | solution.py:64
  53.0 9.1 %shard_map.52 = (f32[264,1152]{1,0:T(8,128)S(1)}, f32[128,1152]{1,0:T(8,128)S(1)}, f32[128,1152]{1,0:T(8,128)S(1)}, f32[64,1152]{1,0:T(8,128)S(1)}, f32[64,1152]...) custom-call(s32[5]{0:T(128)S(1)} %stack.23.place, f32[256,1152]{1,0:T(8,128)S(1)} %bitcast.15, ...), custom_call_target="tpu_custom_call" | custom-call | flops 2717908992 | bytes 7114772 | tf_op jit(solution)/shard_map/pallas_call | solution.py:33
  62.2 6.8 %collective-permute-start.6 = (f32[264,1152]{1,0:T(8,128)S(1)}, f32[264,1152]{1,0:T(8,128)S(1)}, u32[]{:S(2)}, u32[]{:S(2)}) collective-permute-start(f32[264,1152]{1,0:T(8,128)S(1)} %get-tuple-element.28.other_ref), channel_id=1, source_target_pairs={{0,16},{16,0},{1,17},{17,1},{2,18},{18,2},{3,19},{19,3},{4,20},{20... | collective-permute-start | bytes 3649544 | tf_op jit(solution)/shard_map/ppermute | solution.py:64
  69.0 2.2 %collective-permute-start.7 = (f32[64,1152]{1,0:T(8,128)S(1)}, f32[64,1152]{1,0:T(8,128)S(1)}, u32[]{:S(2)}, u32[]{:S(2)}) collective-permute-start(f32[64,1152]{1,0:T(8,128)S(1)} %get-tuple-element.30), channel_id=1, source_target_pairs={{0,3},{1,0},{2,1},{3,2},{16,17},{17,18},{18,19},{19,16},{4,7},{5,4... | collective-permute-start | bytes 884744 | tf_op jit(solution)/shard_map/ppermute | solution.py:51
  71.2 6.5 %collective-permute-done.7.relay_ref = f32[64,1152]{1,0:T(8,128)S(1)} collective-permute-done((f32[64,1152]{1,0:T(8,128)S(1)}, f32[64,1152]{1,0:T(8,128)S(1)}, u32[]{:S(2)}, u32[]{:S(2)}) %collective-permute-start.7) | collective-permute-done | bytes 294944 | tf_op jit(solution)/shard_map/ppermute | solution.py:51
  78.4 6.7 %collective-permute-start.10 = (f32[128,1152]{1,0:T(8,128)S(1)}, f32[128,1152]{1,0:T(8,128)S(1)}, u32[]{:S(2)}, u32[]{:S(2)}) collective-permute-start(f32[128,1152]{1,0:T(8,128)S(1)} %get-tuple-element.34), channel_id=1, source_target_pairs={{0,32},{32,4},{4,36},{36,8},{8,40},{40,12},{12,44},{44,0},{16,60},... | collective-permute-start | bytes 1769480 | tf_op jit(solution)/shard_map/ppermute | solution.py:60
  85.1 1.9 %collective-permute-start.9 = (f32[64,1152]{1,0:T(8,128)S(1)}, f32[64,1152]{1,0:T(8,128)S(1)}, u32[]{:S(2)}, u32[]{:S(2)}) collective-permute-start(f32[64,1152]{1,0:T(8,128)S(1)} %get-tuple-element.32), channel_id=1, source_target_pairs={{0,1},{1,2},{2,3},{3,0},{16,19},{17,16},{18,17},{19,18},{4,5},{5,6... | collective-permute-start | bytes 884744 | tf_op jit(solution)/shard_map/ppermute | solution.py:51
  87.0 3.4 %collective-permute-start.8 = (f32[64,1152]{1,0:T(8,128)S(1)}, f32[64,1152]{1,0:T(8,128)S(1)}, u32[]{:S(2)}, u32[]{:S(2)}) collective-permute-start(f32[64,1152]{1,0:T(8,128)S(1)} %get-tuple-element.31), channel_id=1, source_target_pairs={{0,3},{1,0},{2,1},{3,2},{16,17},{17,18},{18,19},{19,16},{4,7},{5,4... | collective-permute-start | bytes 884744 | tf_op jit(solution)/shard_map/ppermute | solution.py:51
  90.4 4.1 %all-to-all-start.2 = ((f32[32,1,128]{2,1,0:T(1,128)}), f32[32,1,128]{2,1,0:T(1,128)S(1)}, u32[]{:S(2)}, u32[]{:S(2)}) async-start(f32[32,1,128]{2,1,0:T(1,128)} %bitcast.10), calls=%async_computation.2 | async-start | bytes 32768 | tf_op jit(solution)/shard_map/all_to_all | solution.py:45
  94.6 8.4 %all-to-all-done.2 = f32[32,1,128]{2,1,0:T(1,128)S(1)} async-done(((f32[32,1,128]{2,1,0:T(1,128)}), f32[32,1,128]{2,1,0:T(1,128)S(1)}, u32[]{:S(2)}, u32[]{:S(2)}) %all-to-all-start.2) | async-done | bytes 16416 | tf_op jit(solution)/shard_map/all_to_all | solution.py:45
  104.0 4.5 %all-to-all-start.3 = ((f32[8,152,128]{2,1,0:T(8,128)}), f32[8,152,128]{2,1,0:T(8,128)S(1)}, u32[]{:S(2)}, u32[]{:S(2)}) async-start(f32[8,152,128]{2,1,0:T(8,128)} %get-tuple-element.36), calls=%async_computation.3 | async-start | bytes 1245184 | tf_op jit(solution)/shard_map/all_to_all | solution.py:45
  108.5 2.3 %collective-permute-start.11 = (f32[16,1152]{1,0:T(8,128)S(1)}, f32[16,1152]{1,0:T(8,128)S(1)}, u32[]{:S(2)}, u32[]{:S(2)}) collective-permute-start(f32[16,1152]{1,0:T(8,128)S(1)} %get-tuple-element.40), channel_id=1, source_target_pairs={{0,12},{4,0},{8,4},{12,8},{16,20},{20,24},{24,28},{28,16},{1,13},{... | collective-permute-start | bytes 221192 | tf_op jit(solution)/shard_map/ppermute | solution.py:51
  110.8 5.1 %collective-permute-start.13 = (f32[16,1152]{1,0:T(8,128)S(1)}, f32[16,1152]{1,0:T(8,128)S(1)}, u32[]{:S(2)}, u32[]{:S(2)}) collective-permute-start(f32[16,1152]{1,0:T(8,128)S(1)} %get-tuple-element.41), channel_id=1, source_target_pairs={{0,4},{4,8},{8,12},{12,0},{16,28},{20,16},{24,20},{28,24},{1,5},{5... | collective-permute-start | bytes 221192 | tf_op jit(solution)/shard_map/ppermute | solution.py:51
  116.1 1.9 %collective-permute-start.12 = (f32[16,1152]{1,0:T(8,128)S(1)}, f32[16,1152]{1,0:T(8,128)S(1)}, u32[]{:S(2)}, u32[]{:S(2)}) collective-permute-start(f32[16,1152]{1,0:T(8,128)S(1)} %shard_map.56), channel_id=1, source_target_pairs={{0,12},{4,0},{8,4},{12,8},{16,20},{20,24},{24,28},{28,16},{1,13},{... | collective-permute-start | bytes 221192 | tf_op jit(solution)/shard_map/ppermute | solution.py:51
  118.1 5.9 %collective-permute-done.12.z1 = f32[16,1152]{1,0:T(8,128)S(1)} collective-permute-done((f32[16,1152]{1,0:T(8,128)S(1)}, f32[16,1152]{1,0:T(8,128)S(1)}, u32[]{:S(2)}, u32[]{:S(2)}) %collective-permute-start.12) | collective-permute-done | bytes 73760 | tf_op jit(solution)/shard_map/ppermute | solution.py:51
  (30 shorter events, 9.1 us)
Async XLA Ops:
  0.6 0.9 copy-start
  1.5 0.9 copy-start.2
  3.5 28.2 %all-to-all-start.1 = ((f32[8,16,1152]{2,1,0:T(8,128)}), f32[8,16,1152]{2,1,0:T(8,128)S(1)}, u32[]{:S(2)}, u32[]{:S(2)}) async-start(f32[8,16,1152]{2,1,0:T(8,128)} %bitcast.7), calls=%async_computation.1 | async-start | bytes 1179648 | tf_op jit(solution)/shard_map/all_to_all | solution.py:45
  11.2 12.6 %collective-permute-start = (f32[16,1152]{1,0:T(8,128)S(1)}, f32[16,1152]{1,0:T(8,128)S(1)}, u32[]{:S(2)}, u32[]{:S(2)}) collective-permute-start(f32[16,1152]{1,0:T(8,128)S(1)} %get-tuple-element.23.refs_0_), channel_id=1, source_target_pairs={{0,4},{4,8},{8,12},{12,0},{16,28},{20,16},{24,20},{28,24},{1,5},{5... | collective-permute-start | bytes 221192 | tf_op jit(solution)/shard_map/ppermute | solution.py:51
  21.9 8.7 %collective-permute-start.1 = (f32[16,1152]{1,0:T(8,128)S(1)}, f32[16,1152]{1,0:T(8,128)S(1)}, u32[]{:S(2)}, u32[]{:S(2)}) collective-permute-start(f32[16,1152]{1,0:T(8,128)S(1)} %get-tuple-element.23.refs_0_), channel_id=1, source_target_pairs={{0,12},{4,0},{8,4},{12,8},{16,20},{20,24},{24,28},{28,16},{1,13},{... | collective-permute-start | bytes 221192 | tf_op jit(solution)/shard_map/ppermute | solution.py:51
  23.8 6.9 %collective-permute-start.2 = (f32[16,1152]{1,0:T(8,128)S(1)}, f32[16,1152]{1,0:T(8,128)S(1)}, u32[]{:S(2)}, u32[]{:S(2)}) collective-permute-start(f32[16,1152]{1,0:T(8,128)S(1)} %collective-permute-done.refs_1_), channel_id=1, source_target_pairs={{0,4},{4,8},{8,12},{12,0},{16,28},{20,16},{24,20},{28,24},{1,5},{5... | collective-permute-start | bytes 221192 | tf_op jit(solution)/shard_map/ppermute | solution.py:51
  31.8 16.7 %collective-permute-start.3 = (f32[128,1152]{1,0:T(8,128)S(1)}, f32[128,1152]{1,0:T(8,128)S(1)}, u32[]{:S(2)}, u32[]{:S(2)}) collective-permute-start(f32[128,1152]{1,0:T(8,128)S(1)} %shard_map.51.a_hbm), channel_id=1, source_target_pairs={{0,44},{32,0},{4,32},{36,4},{8,36},{40,8},{12,40},{44,12},{16,48},... | collective-permute-start | bytes 1769480 | tf_op jit(solution)/shard_map/ppermute | solution.py:60
  35.8 15.7 %all-to-all-start = ((f32[4,64,1152]{2,1,0:T(8,128)}), f32[4,64,1152]{2,1,0:T(8,128)S(1)}, u32[]{:S(2)}, u32[]{:S(2)}) async-start(f32[4,64,1152]{2,1,0:T(8,128)} %bitcast.5), calls=%async_computation | async-start | bytes 2359296 | tf_op jit(solution)/shard_map/all_to_all | solution.py:45
  39.8 11.6 %collective-permute-start.4 = (f32[128,1152]{1,0:T(8,128)S(1)}, f32[128,1152]{1,0:T(8,128)S(1)}, u32[]{:S(2)}, u32[]{:S(2)}) collective-permute-start(f32[128,1152]{1,0:T(8,128)S(1)} %shard_map.51.a_hbm), channel_id=1, source_target_pairs={{0,16},{16,0},{1,17},{17,1},{2,18},{18,2},{3,19},{19,3},{4,20},{20... | collective-permute-start | bytes 1769480 | tf_op jit(solution)/shard_map/ppermute | solution.py:64
  48.5 4.5 %collective-permute-start.5 = (f32[128,1152]{1,0:T(8,128)S(1)}, f32[128,1152]{1,0:T(8,128)}, u32[]{:S(2)}, u32[]{:S(2)}) collective-permute-start(f32[128,1152]{1,0:T(8,128)S(1)} %collective-permute-done.3.b_hbm), channel_id=1, source_target_pairs={{0,16},{16,0},{1,17},{17,1},{2,18},{18,2},{3,19},{19,3},{4,20},{20... | collective-permute-start | bytes 1769480 | tf_op jit(solution)/shard_map/ppermute | solution.py:64
  62.2 15.5 %collective-permute-start.6 = (f32[264,1152]{1,0:T(8,128)S(1)}, f32[264,1152]{1,0:T(8,128)S(1)}, u32[]{:S(2)}, u32[]{:S(2)}) collective-permute-start(f32[264,1152]{1,0:T(8,128)S(1)} %get-tuple-element.28.other_ref), channel_id=1, source_target_pairs={{0,16},{16,0},{1,17},{17,1},{2,18},{18,2},{3,19},{19,3},{4,20},{20... | collective-permute-start | bytes 3649544 | tf_op jit(solution)/shard_map/ppermute | solution.py:64
  69.0 8.7 %collective-permute-start.7 = (f32[64,1152]{1,0:T(8,128)S(1)}, f32[64,1152]{1,0:T(8,128)S(1)}, u32[]{:S(2)}, u32[]{:S(2)}) collective-permute-start(f32[64,1152]{1,0:T(8,128)S(1)} %get-tuple-element.30), channel_id=1, source_target_pairs={{0,3},{1,0},{2,1},{3,2},{16,17},{17,18},{18,19},{19,16},{4,7},{5,4... | collective-permute-start | bytes 884744 | tf_op jit(solution)/shard_map/ppermute | solution.py:51
  78.4 24.6 %collective-permute-start.10 = (f32[128,1152]{1,0:T(8,128)S(1)}, f32[128,1152]{1,0:T(8,128)S(1)}, u32[]{:S(2)}, u32[]{:S(2)}) collective-permute-start(f32[128,1152]{1,0:T(8,128)S(1)} %get-tuple-element.34), channel_id=1, source_target_pairs={{0,32},{32,4},{4,36},{36,8},{8,40},{40,12},{12,44},{44,0},{16,60},... | collective-permute-start | bytes 1769480 | tf_op jit(solution)/shard_map/ppermute | solution.py:60
  85.1 9.5 %collective-permute-start.9 = (f32[64,1152]{1,0:T(8,128)S(1)}, f32[64,1152]{1,0:T(8,128)S(1)}, u32[]{:S(2)}, u32[]{:S(2)}) collective-permute-start(f32[64,1152]{1,0:T(8,128)S(1)} %get-tuple-element.32), channel_id=1, source_target_pairs={{0,1},{1,2},{2,3},{3,0},{16,19},{17,16},{18,17},{19,18},{4,5},{5,6... | collective-permute-start | bytes 884744 | tf_op jit(solution)/shard_map/ppermute | solution.py:51
  87.0 16.0 %collective-permute-start.8 = (f32[64,1152]{1,0:T(8,128)S(1)}, f32[64,1152]{1,0:T(8,128)S(1)}, u32[]{:S(2)}, u32[]{:S(2)}) collective-permute-start(f32[64,1152]{1,0:T(8,128)S(1)} %get-tuple-element.31), channel_id=1, source_target_pairs={{0,3},{1,0},{2,1},{3,2},{16,17},{17,18},{18,19},{19,16},{4,7},{5,4... | collective-permute-start | bytes 884744 | tf_op jit(solution)/shard_map/ppermute | solution.py:51
  90.4 12.6 %all-to-all-start.2 = ((f32[32,1,128]{2,1,0:T(1,128)}), f32[32,1,128]{2,1,0:T(1,128)S(1)}, u32[]{:S(2)}, u32[]{:S(2)}) async-start(f32[32,1,128]{2,1,0:T(1,128)} %bitcast.10), calls=%async_computation.2 | async-start | bytes 32768 | tf_op jit(solution)/shard_map/all_to_all | solution.py:45
  104.0 19.9 %copy-start.1 = (f32[16,1152]{1,0:T(8,128)S(1)}, f32[16,1152]{1,0:T(8,128)}, u32[]{:S(2)}) copy-start(f32[16,1152]{1,0:T(8,128)} %emb_ref.3) | copy-start | bytes 221188
  104.0 21.5 %copy-start.3 = (f32[16,1152]{1,0:T(8,128)S(1)}, f32[16,1152]{1,0:T(8,128)}, u32[]{:S(2)}) copy-start(f32[16,1152]{1,0:T(8,128)} %emb_ref.2) | copy-start | bytes 221188
  104.0 21.5 %all-to-all-start.3 = ((f32[8,152,128]{2,1,0:T(8,128)}), f32[8,152,128]{2,1,0:T(8,128)S(1)}, u32[]{:S(2)}, u32[]{:S(2)}) async-start(f32[8,152,128]{2,1,0:T(8,128)} %get-tuple-element.36), calls=%async_computation.3 | async-start | bytes 1245184 | tf_op jit(solution)/shard_map/all_to_all | solution.py:45
  108.5 7.6 %collective-permute-start.11 = (f32[16,1152]{1,0:T(8,128)S(1)}, f32[16,1152]{1,0:T(8,128)S(1)}, u32[]{:S(2)}, u32[]{:S(2)}) collective-permute-start(f32[16,1152]{1,0:T(8,128)S(1)} %get-tuple-element.40), channel_id=1, source_target_pairs={{0,12},{4,0},{8,4},{12,8},{16,20},{20,24},{24,28},{28,16},{1,13},{... | collective-permute-start | bytes 221192 | tf_op jit(solution)/shard_map/ppermute | solution.py:51
  110.8 7.3 %collective-permute-start.13 = (f32[16,1152]{1,0:T(8,128)S(1)}, f32[16,1152]{1,0:T(8,128)S(1)}, u32[]{:S(2)}, u32[]{:S(2)}) collective-permute-start(f32[16,1152]{1,0:T(8,128)S(1)} %get-tuple-element.41), channel_id=1, source_target_pairs={{0,4},{4,8},{8,12},{12,0},{16,28},{20,16},{24,20},{28,24},{1,5},{5... | collective-permute-start | bytes 221192 | tf_op jit(solution)/shard_map/ppermute | solution.py:51
  116.1 7.8 %collective-permute-start.12 = (f32[16,1152]{1,0:T(8,128)S(1)}, f32[16,1152]{1,0:T(8,128)S(1)}, u32[]{:S(2)}, u32[]{:S(2)}) collective-permute-start(f32[16,1152]{1,0:T(8,128)S(1)} %shard_map.56), channel_id=1, source_target_pairs={{0,12},{4,0},{8,4},{12,8},{16,20},{20,24},{24,28},{28,16},{1,13},{... | collective-permute-start | bytes 221192 | tf_op jit(solution)/shard_map/ppermute | solution.py:51

commit v7 on v5

--- a/solution.py
+++ b/solution.py
@@ -123,59 +123,80 @@
     return halves(jnp.concatenate([image_ref[pl.ds(start, rows), :] for start in starts], axis=0))
 
 
-def tile_kernel(place, image_ref, a_ref, b_ref, c_ref, d_ref, other_out, a_out, b_out, loss_out, *x_outs):
+def tile_kernel(place, image_ref, a_ref, b_ref, c_ref, d_ref, slope_out, other_out):
     image = in_turn(place, image_ref)
     quarter = a_ref.shape[0]
     count = image_ref.shape[0]
     row = lax.broadcasted_iota(jnp.int32, (count, quarter), 0)
     column = lax.broadcasted_iota(jnp.int32, (count, quarter), 1) - place[0]
     matched = (row == column) & (row < ROWS)
-    lower, upper = other_out.at[pl.ds(0, quarter), :], other_out.at[pl.ds(quarter, quarter), :]
     total = jnp.zeros((), F32)
-    image_dir = None
-    for ref, out in ((c_ref, lower), (d_ref, upper), (a_ref, a_out), (b_ref, b_out)):
-        text = halves(ref[...])
-        logits = LOGIT_MULT * dot3(image, text, ((1,), (1,))) + LOGIT_SHIFT
-        if ref is a_ref:
+    for k, ref in ((2, c_ref), (3, d_ref), (0, a_ref), (1, b_ref)):
+        logits = LOGIT_MULT * dot3(image, halves(ref[...]), ((1,), (1,))) + LOGIT_SHIFT
+        if k == 0:
             logits = jnp.where(matched, -logits, logits)
         small = jnp.exp(-jnp.abs(logits))
         total += jnp.sum(jnp.maximum(logits, 0.0) + jnp.log1p(small))
         slope = jnp.where(logits >= 0.0, 1.0, small) / (1.0 + small) * (LOGIT_MULT / PAIRS)
-        if ref is a_ref:
+        if k == 0:
             slope = jnp.where(matched, -slope, slope)
-        slope = halves(slope)
-        out[...] = dot3(slope, image, ((0,), (0,)))
-        term = dot3(slope, text, ((1,), (0,)))
-        image_dir = term if image_dir is None else image_dir + term
-    rows = count // NX
-    for k, out in enumerate(x_outs):
-        out[...] = image_dir[k * rows : (k + 1) * rows]
-    loss_out[...] = jnp.full(loss_out.shape, total)
-
-
-def add_kernel(b_ref, received_ref, back_ref, relay_ref, losses_ref, send_out, back_out):
-    quarter = b_ref.shape[0]
-    send_out[...] = b_ref[...] + received_ref[pl.ds(quarter, quarter), :]
-    back_out[...] = back_ref[...] + relay_ref[...]
+        slope_out[:, pl.ds(k * quarter, quarter)] = slope
+        if k >= 2:
+            other_out[pl.ds((k - 2) * quarter, quarter), :] = dot3(halves(slope), image, ((0,), (0,)))
+    other_out[pl.ds(2 * quarter, 8), :] = jnp.full((8, FEATURES), total)
+
+
+def image_kernel(slope_ref, a_ref, b_ref, c_ref, d_ref, *outs):
+    quarter = a_ref.shape[0]
+    total = None
+    for k, ref in enumerate((a_ref, b_ref, c_ref, d_ref)):
+        slope = slope_ref[:, pl.ds(k * quarter, quarter)]
+        term = dot3(halves(slope), halves(ref[...]), ((1,), (0,)))
+        total = term if total is None else total + term
+    rows = total.shape[0] // NX
+    for k, out in enumerate(outs):
+        out[...] = total[k * rows : (k + 1) * rows]
+
+
+def text_kernel(place, slope_ref, image_ref, other_ref, received_ref, x0, keep_out, send_out):
+    image = in_turn(place, image_ref)
+    quarter = keep_out.shape[0] - 8
+    last = pl.ds(2 * quarter, 8)
+    loss = other_ref[last, :] + received_ref[last, :]
+    for k, out in ((1, send_out), (0, keep_out)):
+        rows = pl.ds(k * quarter, quarter)
+        out[pl.ds(0, quarter), :] = dot3(halves(slope_ref[:, rows]), image, ((0,), (0,))) + received_ref[rows, :]
+        out[pl.ds(quarter, 8), :] = loss
 
 
 def relay_kernel(left, right, out):
     out[...] = left[...] + right[...]
 
 
-def join_kernel(x0, x1, x2, a_ref, core_ref, plane_ref, losses_ref, packed_out, *zs):
+def join_kernel(x0, x1, x2, keep_ref, plane_ref, packed_out, *zs):
     for k, out in enumerate(zs):
         rows = pl.ds(k * ROWS, ROWS)
         out[...] = x0[rows, :] + (x1[rows, :] + x2[rows, :])
-    loss = jnp.sum(losses_ref[:, 0:1])
+    last, first = pl.ds(NY * ROWS, 8), pl.ds(0, LANES)
+    loss = keep_ref[last, first] + plane_ref[last, first]
     for y in range(NY):
         rows = pl.ds(y * ROWS, ROWS)
         for k in range(COLS):
             lanes = pl.ds(k * LANES, LANES)
-            packed_out[y, pl.ds(k * ROWS, ROWS), :] = (
-                a_ref[rows, lanes] + core_ref[rows, lanes] + plane_ref[rows, lanes]
-            )
-        packed_out[y, pl.ds(PACK, 8), :] = jnp.full((8, LANES), loss)
+            packed_out[y, pl.ds(k * ROWS, ROWS), :] = keep_ref[rows, lanes] + plane_ref[rows, lanes]
+        packed_out[y, pl.ds(PACK, 8), :] = loss
+
+
+def loss_kernel(packed_ref, out):
+    total = packed_ref[0, pl.ds(PACK, 8), :]
+    for y in range(1, NY):
+        total = total + packed_ref[y, pl.ds(PACK, 8), :]
+    for k in range(out.shape[0] // 8):
+        out[pl.ds(8 * k, 8), :] = total
+
+
+def mean_kernel(losses_ref, out):
+    out[0, 0] = jnp.sum(losses_ref[:, 0:1]) / PAIRS
 
 
 def image_grad_kernel(emb_ref, z0, z1, z2, out):
@@ -183,14 +204,13 @@
     out[...] = project_back(unit, z0[...] + (z1[...] + z2[...]), length)
 
 
-def text_grad_kernel(emb_ref, packed_ref, out, loss_out):
+def text_grad_kernel(emb_ref, packed_ref, out):
     unit, length = normalize(emb_ref[...])
     total = packed_ref[0]
     for y in range(1, NY):
         total = total + packed_ref[y]
     direction = jnp.concatenate([total[k * ROWS : (k + 1) * ROWS] for k in range(COLS)], axis=1)
     out[...] = project_back(unit, direction, length)
-    loss_out[0, 0] = jnp.max(total[PACK:]) / PAIRS
 
 
 def on_device(image_emb, text_emb):
@@ -217,32 +237,32 @@
     blocks = [x, (x - turn) % NX, (x + turn) % NX, (x + 2) % NX]
     place = jnp.stack([lax.axis_index("y") * rows, *blocks]).astype(jnp.int32)
     product = 2 * count * quarter * features * 3
-    other, text_a, text_b, loss, *xs = call(
+    slope, other = call(
         tile_kernel,
         (place, image, *texts),
-        [shape(2 * quarter, features)]
-        + [shape(quarter, features)] * 2
-        + [shape(64, LANES)]
-        + [shape(part, features)] * NX,
+        [shape(count, 4 * quarter), shape(2 * quarter + 8, features)],
         in_specs=[SMEM] + [VMEM] * 5,
-        flops=12 * product,
-        vmem=24,
+        flops=6 * product,
+        vmem=20,
     )
     received = other_core(other)
+    xs = call(image_kernel, (slope, *texts), [shape(part, features)] * NX, flops=4 * product, vmem=20)
     relay = turned(xs[3], "x", -1)
-    losses = exchange(loss, ("zl", "c", "zh", "x"))
-    send, relay = call(
-        add_kernel,
-        (text_b, received, xs[1], relay, losses),
-        [shape(quarter, features), shape(part, features)],
-        in_specs=[VMEM] * 4 + [ANY],
+    ahead = turned(xs[2], "x", 1)
+    keep, send = call(
+        text_kernel,
+        (place, slope, image, other, received, xs[0]),
+        [shape(quarter + 8, features)] * 2,
+        in_specs=[SMEM] + [VMEM] * 4 + [ANY],
+        flops=2 * product,
+        vmem=20,
     )
     plane = planes(send, 1)
+    (relay,) = call(relay_kernel, (xs[1], relay), [shape(part, features)])
     back = turned(relay, "x", -1)
-    ahead = turned(xs[2], "x", 1)
     packed, *zs = call(
         join_kernel,
-        (xs[0], back, ahead, text_a, received, plane, losses),
+        (xs[0], back, ahead, keep, plane),
         [shape(NY, PACK + 8, LANES)] + [shape(rows, features)] * NZH,
     )
     packed = exchange(packed, "y")
@@ -251,12 +271,10 @@
     (relay,) = call(relay_kernel, (zs[1], relay), [shape(rows, features)])
     back = turned(relay, "zh", -1)
     (image_grad,) = call(image_grad_kernel, (image_emb, zs[0], back, ahead), [shape(rows, features)])
-    text_grad, loss = call(
-        text_grad_kernel,
-        (text_emb, packed),
-        [shape(rows, features), shape(1, 1)],
-        out_specs=[VMEM, SMEM],
-    )
+    (loss,) = call(loss_kernel, (packed,), [shape(NZH * NX, LANES)])
+    losses = exchange(loss, ("zh", "x"))
+    (text_grad,) = call(text_grad_kernel, (text_emb, packed), [shape(rows, features)])
+    (loss,) = call(mean_kernel, (losses,), [shape(1, 1)], out_specs=[SMEM])
     return loss.reshape(()), image_grad, text_grad
 
 

time: 131 us -> 132 us (level)
  blocking collectives: 19.5 us -> 0 us
  starting transfers between devices: 74.3 us -> 84.6 us
  waiting for transfers between devices: 21.1 us -> 29.9 us
  Pallas kernels: 12.1 us -> 13.6 us
    all_to_all x1 -> x0, blocking collectives: 19.5 us -> none  [exchange(): return lax.all_to_all(values, axes, 0, 0, tiled=True)]
    all_to_all x3 -> x4, waiting for transfers between devices: 3.98 us -> 14 us  [exchange(): return lax.all_to_all(values, axes, 0, 0, tiled=True)]
    ppermute x2, starting transfers between devices: 6.04 us -> 10.7 us  [planes(): return lax.ppermute(values, ('zl', 'c', 'zh'), pairs)]
    all_to_all x3 -> x4, starting transfers between devices: 15.4 us -> 20 us  [exchange(): return lax.all_to_all(values, axes, 0, 0, tiled=True)]
    ppermute x9, waiting for transfers between devices: 15.4 us -> 13.6 us  [turned(): return lax.ppermute(values, ('c', axis), pairs)]
    pallas_call x9 -> x13, Pallas kernels: 12.1 us -> 13.6 us  [call(): pl.pallas_call(kernel, out_shape=outs, in_specs=in_specs or [VMEM] * len(...]
  transfers between devices with their start and end apart: 17 -> 18, of which waited for: 9 -> 9; matrix products, arithmetic and copies ran while one was open for 0% -> 0% of each run, Pallas kernels for 2% -> 4%
where the time goes in v7:
time: 132 us; the launch traced here: 131 us
  starting transfers between devices  84.6 us (64%)
  waiting for transfers between devices  29.9 us (23%)
  Pallas kernels  13.6 us (10%)
  local copies, waits for them, and re-layouts  1.86 us (1%)
    ppermute x9, starting transfers between devices, turned(): return lax.ppermute(values, ('c', axis), pairs)  35.8 us
    all_to_all x4, starting transfers between devices, exchange(): return lax.all_to_all(values, axes, 0, 0, tiled=True)  20 us
    ppermute x3, starting transfers between devices, other_core(): return lax.ppermute(values, 'c', [(0, 1), (1, 0)])  18.1 us
    all_to_all x4, waiting for transfers between devices, exchange(): return lax.all_to_all(values, axes, 0, 0, tiled=True)  14 us
    ppermute x9, waiting for transfers between devices, turned(): return lax.ppermute(values, ('c', axis), pairs)  13.6 us
    pallas_call x13, Pallas kernels, call(): pl.pallas_call(kernel, out_shape=outs, in_specs=in_specs or [VMEM] * len(...  13.6 us
    ppermute x2, starting transfers between devices, planes(): return lax.ppermute(values, ('zl', 'c', 'zh'), pairs)  10.7 us
  transfers between devices with their start and end apart: 18, of which 9 were waited for; matrix products, arithmetic and copies ran while one was open for 0% of the time, Pallas kernels for 4%

profile of v7, /device:TPU:1, one launch (start us, length us, event | category | flops | bytes accessed | tf_op | source)
XLA Modules:
  0.0 130.8 jit_solution(4137493800776363649)
XLA Ops:
  3.5 7.7 %all-to-all-start.1 = ((f32[8,16,1152]{2,1,0:T(8,128)}), f32[8,16,1152]{2,1,0:T(8,128)S(1)}, u32[]{:S(2)}, u32[]{:S(2)}) async-start(f32[8,16,1152]{2,1,0:T(8,128)} %bitcast.7), calls=%async_computation.1 | async-start | bytes 1179648 | tf_op jit(solution)/shard_map/all_to_all | solution.py:45
  11.2 10.6 %collective-permute-start = (f32[16,1152]{1,0:T(8,128)S(1)}, f32[16,1152]{1,0:T(8,128)S(1)}, u32[]{:S(2)}, u32[]{:S(2)}) collective-permute-start(f32[16,1152]{1,0:T(8,128)S(1)} %get-tuple-element.18.refs_0_), channel_id=1, source_target_pairs={{0,4},{4,8},{8,12},{12,0},{16,28},{20,16},{24,20},{28,24},{1,5},{5... | collective-permute-start | bytes 221192 | tf_op jit(solution)/shard_map/ppermute | solution.py:51
  21.9 1.9 %collective-permute-start.1 = (f32[16,1152]{1,0:T(8,128)S(1)}, f32[16,1152]{1,0:T(8,128)S(1)}, u32[]{:S(2)}, u32[]{:S(2)}) collective-permute-start(f32[16,1152]{1,0:T(8,128)S(1)} %get-tuple-element.18.refs_0_), channel_id=1, source_target_pairs={{0,12},{4,0},{8,4},{12,8},{16,20},{20,24},{24,28},{28,16},{1,13},{... | collective-permute-start | bytes 221192 | tf_op jit(solution)/shard_map/ppermute | solution.py:51
  23.8 5.5 %collective-permute-start.2 = (f32[16,1152]{1,0:T(8,128)S(1)}, f32[16,1152]{1,0:T(8,128)S(1)}, u32[]{:S(2)}, u32[]{:S(2)}) collective-permute-start(f32[16,1152]{1,0:T(8,128)S(1)} %collective-permute-done.refs_1_), channel_id=1, source_target_pairs={{0,4},{4,8},{8,12},{12,0},{16,28},{20,16},{24,20},{28,24},{1,5},{5... | collective-permute-start | bytes 221192 | tf_op jit(solution)/shard_map/ppermute | solution.py:51
  31.8 4.0 %collective-permute-start.3 = (f32[128,1152]{1,0:T(8,128)S(1)}, f32[128,1152]{1,0:T(8,128)S(1)}, u32[]{:S(2)}, u32[]{:S(2)}) collective-permute-start(f32[128,1152]{1,0:T(8,128)S(1)} %shard_map.51.a_ref), channel_id=1, source_target_pairs={{0,44},{32,0},{4,32},{36,4},{8,36},{40,8},{12,40},{44,12},{16,48},... | collective-permute-start | bytes 1769480 | tf_op jit(solution)/shard_map/ppermute | solution.py:60
  35.8 4.0 %all-to-all-start = ((f32[4,64,1152]{2,1,0:T(8,128)}), f32[4,64,1152]{2,1,0:T(8,128)S(1)}, u32[]{:S(2)}, u32[]{:S(2)}) async-start(f32[4,64,1152]{2,1,0:T(8,128)} %bitcast.5), calls=%async_computation | async-start | bytes 2359296 | tf_op jit(solution)/shard_map/all_to_all | solution.py:45
  39.8 8.4 %collective-permute-start.4 = (f32[128,1152]{1,0:T(8,128)S(1)}, f32[128,1152]{1,0:T(8,128)S(1)}, u32[]{:S(2)}, u32[]{:S(2)}) collective-permute-start(f32[128,1152]{1,0:T(8,128)S(1)} %shard_map.51.a_ref), channel_id=1, source_target_pairs={{0,16},{16,0},{1,17},{17,1},{2,18},{18,2},{3,19},{19,3},{4,20},{20... | collective-permute-start | bytes 1769480 | tf_op jit(solution)/shard_map/ppermute | solution.py:64
  48.5 2.8 %collective-permute-start.5 = (f32[128,1152]{1,0:T(8,128)S(1)}, f32[128,1152]{1,0:T(8,128)S(1)}, u32[]{:S(2)}, u32[]{:S(2)}) collective-permute-start(f32[128,1152]{1,0:T(8,128)S(1)} %collective-permute-done.3.b_ref), channel_id=1, source_target_pairs={{0,16},{16,0},{1,17},{17,1},{2,18},{18,2},{3,19},{19,3},{4,20},{20... | collective-permute-start | bytes 1769480 | tf_op jit(solution)/shard_map/ppermute | solution.py:64
  52.9 4.1 %shard_map.52 = (f32[256,512]{1,0:T(8,128)S(1)}, f32[264,1152]{1,0:T(8,128)S(1)}) custom-call(s32[5]{0:T(128)S(1)} %stack.23.place, f32[256,1152]{1,0:T(8,128)S(1)} %bitcast.14, f32[128,1152]{1,0:T(8,128)S(1)} %shard_map.51.a_ref, f32[128,1152]{1,0:T(8,128)S(1)} %collective-permute-done.3.b_ref, f32[128,1152]{1,0:T(8,128)S(1)} %collective-permute-done.4.c_ref, ...), custom_call_target="tpu_custom_call" | custom-call | flops 1358954496 | bytes 5279764 | tf_op jit(solution)/shard_map/pallas_call | solution.py:33
  57.0 6.9 %collective-permute-start.9 = (f32[264,1152]{1,0:T(8,128)S(1)}, f32[264,1152]{1,0:T(8,128)S(1)}, u32[]{:S(2)}, u32[]{:S(2)}) collective-permute-start(f32[264,1152]{1,0:T(8,128)S(1)} %get-tuple-element.25.other_ref), channel_id=1, source_target_pairs={{0,16},{16,0},{1,17},{17,1},{2,18},{18,2},{3,19},{19,3},{4,20},{20... | collective-permute-start | bytes 3649544 | tf_op jit(solution)/shard_map/ppermute | solution.py:64
  64.0 2.0 %shard_map.53 = (f32[64,1152]{1,0:T(8,128)S(1)}, f32[64,1152]{1,0:T(8,128)S(1)}, f32[64,1152]{1,0:T(8,128)S(1)}, f32[64,1152]{1,0:T(8,128)S(1)}) custom-call(f32[256,512]{1,0:T(8,128)S(1)} %get-tuple-element.20.slope_ref, f32[128,1152]{1,0:T(8,128)S(1)} %shard_map.51.a_ref, f32[128,1152]{1,0:T(8,128)S(1)} %collective-permute-done.3.b_ref, ...), custom_call_target="tpu_custom_call" | custom-call | flops 905969664 | bytes 4063232 | tf_op jit(solution)/shard_map/pallas_call | solution.py:33
  67.8 6.7 %collective-permute-start.10 = (f32[136,1152]{1,0:T(8,128)S(1)}, f32[136,1152]{1,0:T(8,128)S(1)}, u32[]{:S(2)}, u32[]{:S(2)}) collective-permute-start(f32[136,1152]{1,0:T(8,128)S(1)} %get-tuple-element.27), channel_id=1, source_target_pairs={{0,32},{32,4},{4,36},{36,8},{8,40},{40,12},{12,44},{44,0},{16,60},... | collective-permute-start | bytes 1880072 | tf_op jit(solution)/shard_map/ppermute | solution.py:60
  74.5 2.2 %collective-permute-start.6 = (f32[64,1152]{1,0:T(8,128)S(1)}, f32[64,1152]{1,0:T(8,128)S(1)}, u32[]{:S(2)}, u32[]{:S(2)}) collective-permute-start(f32[64,1152]{1,0:T(8,128)S(1)} %get-tuple-element.23), channel_id=1, source_target_pairs={{0,3},{1,0},{2,1},{3,2},{16,17},{17,18},{18,19},{19,16},{4,7},{5,4... | collective-permute-start | bytes 884744 | tf_op jit(solution)/shard_map/ppermute | solution.py:51
  76.8 4.3 %collective-permute-start.8 = (f32[64,1152]{1,0:T(8,128)S(1)}, f32[64,1152]{1,0:T(8,128)S(1)}, u32[]{:S(2)}, u32[]{:S(2)}) collective-permute-start(f32[64,1152]{1,0:T(8,128)S(1)} %get-tuple-element.24), channel_id=1, source_target_pairs={{0,1},{1,2},{2,3},{3,0},{16,19},{17,16},{18,17},{19,18},{4,5},{5,6... | collective-permute-start | bytes 884744 | tf_op jit(solution)/shard_map/ppermute | solution.py:51
  81.1 5.5 %collective-permute-done.6.right = f32[64,1152]{1,0:T(8,128)S(1)} collective-permute-done((f32[64,1152]{1,0:T(8,128)S(1)}, f32[64,1152]{1,0:T(8,128)S(1)}, u32[]{:S(2)}, u32[]{:S(2)}) %collective-permute-start.6) | collective-permute-done | bytes 294944 | tf_op jit(solution)/shard_map/ppermute | solution.py:51
  86.6 1.9 %collective-permute-start.7 = (f32[64,1152]{1,0:T(8,128)S(1)}, f32[64,1152]{1,0:T(8,128)S(1)}, u32[]{:S(2)}, u32[]{:S(2)}) collective-permute-start(f32[64,1152]{1,0:T(8,128)S(1)} %shard_map.54), channel_id=1, source_target_pairs={{0,3},{1,0},{2,1},{3,2},{16,17},{17,18},{18,19},{19,16},{4,7},{5,4... | collective-permute-start | bytes 884744 | tf_op jit(solution)/shard_map/ppermute | solution.py:51
  88.5 6.7 %collective-permute-done.7.x1 = f32[64,1152]{1,0:T(8,128)S(1)} collective-permute-done((f32[64,1152]{1,0:T(8,128)S(1)}, f32[64,1152]{1,0:T(8,128)S(1)}, u32[]{:S(2)}, u32[]{:S(2)}) %collective-permute-start.7) | collective-permute-done | bytes 294944 | tf_op jit(solution)/shard_map/ppermute | solution.py:51
  96.2 3.7 %all-to-all-start.2 = ((f32[8,152,128]{2,1,0:T(8,128)}), f32[8,152,128]{2,1,0:T(8,128)S(1)}, u32[]{:S(2)}, u32[]{:S(2)}) async-start(f32[8,152,128]{2,1,0:T(8,128)} %get-tuple-element.28), calls=%async_computation.2 | async-start | bytes 1245184 | tf_op jit(solution)/shard_map/all_to_all | solution.py:45
  99.9 1.9 %collective-permute-start.11 = (f32[16,1152]{1,0:T(8,128)S(1)}, f32[16,1152]{1,0:T(8,128)S(1)}, u32[]{:S(2)}, u32[]{:S(2)}) collective-permute-start(f32[16,1152]{1,0:T(8,128)S(1)} %get-tuple-element.31), channel_id=1, source_target_pairs={{0,12},{4,0},{8,4},{12,8},{16,20},{20,24},{24,28},{28,16},{1,13},{... | collective-permute-start | bytes 221192 | tf_op jit(solution)/shard_map/ppermute | solution.py:51
  101.8 5.5 %collective-permute-start.13 = (f32[16,1152]{1,0:T(8,128)S(1)}, f32[16,1152]{1,0:T(8,128)S(1)}, u32[]{:S(2)}, u32[]{:S(2)}) collective-permute-start(f32[16,1152]{1,0:T(8,128)S(1)} %get-tuple-element.32), channel_id=1, source_target_pairs={{0,4},{4,8},{8,12},{12,0},{16,28},{20,16},{24,20},{28,24},{1,5},{5... | collective-permute-start | bytes 221192 | tf_op jit(solution)/shard_map/ppermute | solution.py:51
  107.3 1.9 %collective-permute-start.12 = (f32[16,1152]{1,0:T(8,128)S(1)}, f32[16,1152]{1,0:T(8,128)S(1)}, u32[]{:S(2)}, u32[]{:S(2)}) collective-permute-start(f32[16,1152]{1,0:T(8,128)S(1)} %shard_map.59), channel_id=1, source_target_pairs={{0,12},{4,0},{8,4},{12,8},{16,20},{20,24},{24,28},{28,16},{1,13},{... | collective-permute-start | bytes 221192 | tf_op jit(solution)/shard_map/ppermute | solution.py:51
  109.3 6.9 %all-to-all-done.2.packed_ref = f32[8,152,128]{2,1,0:T(8,128)S(1)} async-done(((f32[8,152,128]{2,1,0:T(8,128)}), f32[8,152,128]{2,1,0:T(8,128)S(1)}, u32[]{:S(2)}, u32[]{:S(2)}) %all-to-all-start.2) | async-done | bytes 622624 | tf_op jit(solution)/shard_map/all_to_all | solution.py:45
  116.7 4.6 %all-to-all-start.3 = ((f32[16,1,128]{2,1,0:T(1,128)}), f32[16,1,128]{2,1,0:T(1,128)S(1)}, u32[]{:S(2)}, u32[]{:S(2)}) async-start(f32[16,1,128]{2,1,0:T(1,128)} %bitcast.10), calls=%async_computation.3 | async-start | bytes 16384 | tf_op jit(solution)/shard_map/all_to_all | solution.py:45
  123.1 7.1 %all-to-all-done.3 = f32[16,1,128]{2,1,0:T(1,128)S(1)} async-done(((f32[16,1,128]{2,1,0:T(1,128)}), f32[16,1,128]{2,1,0:T(1,128)S(1)}, u32[]{:S(2)}, u32[]{:S(2)}) %all-to-all-start.3) | async-done | bytes 8224 | tf_op jit(solution)/shard_map/all_to_all | solution.py:45
  (34 shorter events, 13.0 us)
Async XLA Ops:
  0.6 0.9 copy-start
  1.5 0.9 copy-start.2
  3.5 28.2 %all-to-all-start.1 = ((f32[8,16,1152]{2,1,0:T(8,128)}), f32[8,16,1152]{2,1,0:T(8,128)S(1)}, u32[]{:S(2)}, u32[]{:S(2)}) async-start(f32[8,16,1152]{2,1,0:T(8,128)} %bitcast.7), calls=%async_computation.1 | async-start | bytes 1179648 | tf_op jit(solution)/shard_map/all_to_all | solution.py:45
  11.2 12.6 %collective-permute-start = (f32[16,1152]{1,0:T(8,128)S(1)}, f32[16,1152]{1,0:T(8,128)S(1)}, u32[]{:S(2)}, u32[]{:S(2)}) collective-permute-start(f32[16,1152]{1,0:T(8,128)S(1)} %get-tuple-element.18.refs_0_), channel_id=1, source_target_pairs={{0,4},{4,8},{8,12},{12,0},{16,28},{20,16},{24,20},{28,24},{1,5},{5... | collective-permute-start | bytes 221192 | tf_op jit(solution)/shard_map/ppermute | solution.py:51
  21.9 8.7 %collective-permute-start.1 = (f32[16,1152]{1,0:T(8,128)S(1)}, f32[16,1152]{1,0:T(8,128)S(1)}, u32[]{:S(2)}, u32[]{:S(2)}) collective-permute-start(f32[16,1152]{1,0:T(8,128)S(1)} %get-tuple-element.18.refs_0_), channel_id=1, source_target_pairs={{0,12},{4,0},{8,4},{12,8},{16,20},{20,24},{24,28},{28,16},{1,13},{... | collective-permute-start | bytes 221192 | tf_op jit(solution)/shard_map/ppermute | solution.py:51
  23.8 6.9 %collective-permute-start.2 = (f32[16,1152]{1,0:T(8,128)S(1)}, f32[16,1152]{1,0:T(8,128)S(1)}, u32[]{:S(2)}, u32[]{:S(2)}) collective-permute-start(f32[16,1152]{1,0:T(8,128)S(1)} %collective-permute-done.refs_1_), channel_id=1, source_target_pairs={{0,4},{4,8},{8,12},{12,0},{16,28},{20,16},{24,20},{28,24},{1,5},{5... | collective-permute-start | bytes 221192 | tf_op jit(solution)/shard_map/ppermute | solution.py:51
  31.8 16.7 %collective-permute-start.3 = (f32[128,1152]{1,0:T(8,128)S(1)}, f32[128,1152]{1,0:T(8,128)S(1)}, u32[]{:S(2)}, u32[]{:S(2)}) collective-permute-start(f32[128,1152]{1,0:T(8,128)S(1)} %shard_map.51.a_ref), channel_id=1, source_target_pairs={{0,44},{32,0},{4,32},{36,4},{8,36},{40,8},{12,40},{44,12},{16,48},... | collective-permute-start | bytes 1769480 | tf_op jit(solution)/shard_map/ppermute | solution.py:60
  35.8 15.7 %all-to-all-start = ((f32[4,64,1152]{2,1,0:T(8,128)}), f32[4,64,1152]{2,1,0:T(8,128)S(1)}, u32[]{:S(2)}, u32[]{:S(2)}) async-start(f32[4,64,1152]{2,1,0:T(8,128)} %bitcast.5), calls=%async_computation | async-start | bytes 2359296 | tf_op jit(solution)/shard_map/all_to_all | solution.py:45
  39.8 11.6 %collective-permute-start.4 = (f32[128,1152]{1,0:T(8,128)S(1)}, f32[128,1152]{1,0:T(8,128)S(1)}, u32[]{:S(2)}, u32[]{:S(2)}) collective-permute-start(f32[128,1152]{1,0:T(8,128)S(1)} %shard_map.51.a_ref), channel_id=1, source_target_pairs={{0,16},{16,0},{1,17},{17,1},{2,18},{18,2},{3,19},{19,3},{4,20},{20... | collective-permute-start | bytes 1769480 | tf_op jit(solution)/shard_map/ppermute | solution.py:64
  48.5 4.4 %collective-permute-start.5 = (f32[128,1152]{1,0:T(8,128)S(1)}, f32[128,1152]{1,0:T(8,128)S(1)}, u32[]{:S(2)}, u32[]{:S(2)}) collective-permute-start(f32[128,1152]{1,0:T(8,128)S(1)} %collective-permute-done.3.b_ref), channel_id=1, source_target_pairs={{0,16},{16,0},{1,17},{17,1},{2,18},{18,2},{3,19},{19,3},{4,20},{20... | collective-permute-start | bytes 1769480 | tf_op jit(solution)/shard_map/ppermute | solution.py:64
  57.0 9.4 %collective-permute-start.9 = (f32[264,1152]{1,0:T(8,128)S(1)}, f32[264,1152]{1,0:T(8,128)S(1)}, u32[]{:S(2)}, u32[]{:S(2)}) collective-permute-start(f32[264,1152]{1,0:T(8,128)S(1)} %get-tuple-element.25.other_ref), channel_id=1, source_target_pairs={{0,16},{16,0},{1,17},{17,1},{2,18},{18,2},{3,19},{19,3},{4,20},{20... | collective-permute-start | bytes 3649544 | tf_op jit(solution)/shard_map/ppermute | solution.py:64
  67.8 27.5 %collective-permute-start.10 = (f32[136,1152]{1,0:T(8,128)S(1)}, f32[136,1152]{1,0:T(8,128)S(1)}, u32[]{:S(2)}, u32[]{:S(2)}) collective-permute-start(f32[136,1152]{1,0:T(8,128)S(1)} %get-tuple-element.27), channel_id=1, source_target_pairs={{0,32},{32,4},{4,36},{36,8},{8,40},{40,12},{12,44},{44,0},{16,60},... | collective-permute-start | bytes 1880072 | tf_op jit(solution)/shard_map/ppermute | solution.py:60
  74.5 12.0 %collective-permute-start.6 = (f32[64,1152]{1,0:T(8,128)S(1)}, f32[64,1152]{1,0:T(8,128)S(1)}, u32[]{:S(2)}, u32[]{:S(2)}) collective-permute-start(f32[64,1152]{1,0:T(8,128)S(1)} %get-tuple-element.23), channel_id=1, source_target_pairs={{0,3},{1,0},{2,1},{3,2},{16,17},{17,18},{18,19},{19,16},{4,7},{5,4... | collective-permute-start | bytes 884744 | tf_op jit(solution)/shard_map/ppermute | solution.py:51
  76.8 11.8 %collective-permute-start.8 = (f32[64,1152]{1,0:T(8,128)S(1)}, f32[64,1152]{1,0:T(8,128)S(1)}, u32[]{:S(2)}, u32[]{:S(2)}) collective-permute-start(f32[64,1152]{1,0:T(8,128)S(1)} %get-tuple-element.24), channel_id=1, source_target_pairs={{0,1},{1,2},{2,3},{3,0},{16,19},{17,16},{18,17},{19,18},{4,5},{5,6... | collective-permute-start | bytes 884744 | tf_op jit(solution)/shard_map/ppermute | solution.py:51
  86.6 8.7 %collective-permute-start.7 = (f32[64,1152]{1,0:T(8,128)S(1)}, f32[64,1152]{1,0:T(8,128)S(1)}, u32[]{:S(2)}, u32[]{:S(2)}) collective-permute-start(f32[64,1152]{1,0:T(8,128)S(1)} %shard_map.54), channel_id=1, source_target_pairs={{0,3},{1,0},{2,1},{3,2},{16,17},{17,18},{18,19},{19,16},{4,7},{5,4... | collective-permute-start | bytes 884744 | tf_op jit(solution)/shard_map/ppermute | solution.py:51
  96.2 25.2 %copy-start.3 = (f32[16,1152]{1,0:T(8,128)S(1)}, f32[16,1152]{1,0:T(8,128)}, u32[]{:S(2)}) copy-start(f32[16,1152]{1,0:T(8,128)} %emb_ref.2) | copy-start | bytes 221188
  96.2 26.0 %copy-start.1 = (f32[16,1152]{1,0:T(8,128)S(1)}, f32[16,1152]{1,0:T(8,128)}, u32[]{:S(2)}) copy-start(f32[16,1152]{1,0:T(8,128)} %emb_ref.3) | copy-start | bytes 221188
  96.2 19.9 %all-to-all-start.2 = ((f32[8,152,128]{2,1,0:T(8,128)}), f32[8,152,128]{2,1,0:T(8,128)S(1)}, u32[]{:S(2)}, u32[]{:S(2)}) async-start(f32[8,152,128]{2,1,0:T(8,128)} %get-tuple-element.28), calls=%async_computation.2 | async-start | bytes 1245184 | tf_op jit(solution)/shard_map/all_to_all | solution.py:45
  99.9 7.4 %collective-permute-start.11 = (f32[16,1152]{1,0:T(8,128)S(1)}, f32[16,1152]{1,0:T(8,128)S(1)}, u32[]{:S(2)}, u32[]{:S(2)}) collective-permute-start(f32[16,1152]{1,0:T(8,128)S(1)} %get-tuple-element.31), channel_id=1, source_target_pairs={{0,12},{4,0},{8,4},{12,8},{16,20},{20,24},{24,28},{28,16},{1,13},{... | collective-permute-start | bytes 221192 | tf_op jit(solution)/shard_map/ppermute | solution.py:51
  101.8 19.5 %collective-permute-start.13 = (f32[16,1152]{1,0:T(8,128)S(1)}, f32[16,1152]{1,0:T(8,128)S(1)}, u32[]{:S(2)}, u32[]{:S(2)}) collective-permute-start(f32[16,1152]{1,0:T(8,128)S(1)} %get-tuple-element.32), channel_id=1, source_target_pairs={{0,4},{4,8},{8,12},{12,0},{16,28},{20,16},{24,20},{28,24},{1,5},{5... | collective-permute-start | bytes 221192 | tf_op jit(solution)/shard_map/ppermute | solution.py:51
  107.3 14.0 %collective-permute-start.12 = (f32[16,1152]{1,0:T(8,128)S(1)}, f32[16,1152]{1,0:T(8,128)S(1)}, u32[]{:S(2)}, u32[]{:S(2)}) collective-permute-start(f32[16,1152]{1,0:T(8,128)S(1)} %shard_map.59), channel_id=1, source_target_pairs={{0,12},{4,0},{8,4},{12,8},{16,20},{20,24},{24,28},{28,16},{1,13},{... | collective-permute-start | bytes 221192 | tf_op jit(solution)/shard_map/ppermute | solution.py:51
  116.7 13.4 %all-to-all-start.3 = ((f32[16,1,128]{2,1,0:T(1,128)}), f32[16,1,128]{2,1,0:T(1,128)S(1)}, u32[]{:S(2)}, u32[]{:S(2)}) async-start(f32[16,1,128]{2,1,0:T(1,128)} %bitcast.10), calls=%async_computation.3 | async-start | bytes 16384 | tf_op jit(solution)/shard_map/all_to_all | solution.py:45

commit v8 on v7

--- a/solution.py
+++ b/solution.py
@@ -62,12 +62,6 @@
 
 def other_core(values):
     return lax.ppermute(values, "c", [(0, 1), (1, 0)])
-
-
-def ring_gather(values, axis):
-    back = turned(values, axis, 1)
-    ahead = turned(values, axis, -1)
-    return values, back, ahead, turned(back, axis, 1)
 
 
 def normalize(values):
@@ -107,29 +101,17 @@
     image_out[...] = normalize(image_ref[...])[0]
 
 
-def spread_kernel(*refs):
-    for x in range(NX):
-        for k, part in enumerate(refs[:-1]):
-            refs[-1][pl.ds((x * NZH + k) * ROWS, ROWS), :] = part[...]
-
-
 def tie_kernel(*refs):
     pass
 
 
-def in_turn(place, image_ref):
-    rows = image_ref.shape[0] // NX
-    starts = [pl.multiple_of(place[1 + k] * rows, rows) for k in range(NX)]
-    return halves(jnp.concatenate([image_ref[pl.ds(start, rows), :] for start in starts], axis=0))
-
-
 def tile_kernel(place, image_ref, a_ref, b_ref, c_ref, d_ref, slope_out, other_out):
-    image = in_turn(place, image_ref)
+    image = halves(image_ref[...])
     quarter = a_ref.shape[0]
     count = image_ref.shape[0]
-    row = lax.broadcasted_iota(jnp.int32, (count, quarter), 0)
-    column = lax.broadcasted_iota(jnp.int32, (count, quarter), 1) - place[0]
-    matched = (row == column) & (row < ROWS)
+    row = lax.broadcasted_iota(jnp.int32, (count, quarter), 0) - place[0]
+    column = lax.broadcasted_iota(jnp.int32, (count, quarter), 1) - place[1]
+    matched = (row == column) & (row >= 0) & (row < ROWS)
     total = jnp.zeros((), F32)
     for k, ref in ((2, c_ref), (3, d_ref), (0, a_ref), (1, b_ref)):
         logits = LOGIT_MULT * dot3(image, halves(ref[...]), ((1,), (1,))) + LOGIT_SHIFT
@@ -146,20 +128,18 @@
     other_out[pl.ds(2 * quarter, 8), :] = jnp.full((8, FEATURES), total)
 
 
-def image_kernel(slope_ref, a_ref, b_ref, c_ref, d_ref, *outs):
+def image_kernel(slope_ref, a_ref, b_ref, c_ref, d_ref, out):
     quarter = a_ref.shape[0]
     total = None
     for k, ref in enumerate((a_ref, b_ref, c_ref, d_ref)):
         slope = slope_ref[:, pl.ds(k * quarter, quarter)]
         term = dot3(halves(slope), halves(ref[...]), ((1,), (0,)))
         total = term if total is None else total + term
-    rows = total.shape[0] // NX
-    for k, out in enumerate(outs):
-        out[...] = total[k * rows : (k + 1) * rows]
-
-
-def text_kernel(place, slope_ref, image_ref, other_ref, received_ref, x0, keep_out, send_out):
-    image = in_turn(place, image_ref)
+    out[...] = total
+
+
+def text_kernel(slope_ref, image_ref, other_ref, received_ref, image_sums, keep_out, send_out):
+    image = halves(image_ref[...])
     quarter = keep_out.shape[0] - 8
     last = pl.ds(2 * quarter, 8)
     loss = other_ref[last, :] + received_ref[last, :]
@@ -173,10 +153,12 @@
     out[...] = left[...] + right[...]
 
 
-def join_kernel(x0, x1, x2, keep_ref, plane_ref, packed_out, *zs):
-    for k, out in enumerate(zs):
-        rows = pl.ds(k * ROWS, ROWS)
-        out[...] = x0[rows, :] + (x1[rows, :] + x2[rows, :])
+def split_kernel(place, image_ref, *outs):
+    for k, out in enumerate(outs):
+        out[...] = image_ref[pl.ds(pl.multiple_of(place[2 + k] * ROWS, ROWS), ROWS), :]
+
+
+def pack_kernel(keep_ref, plane_ref, packed_out):
     last, first = pl.ds(NY * ROWS, 8), pl.ds(0, LANES)
     loss = keep_ref[last, first] + plane_ref[last, first]
     for y in range(NY):
@@ -223,19 +205,19 @@
         scratch_shapes=[pltpu.VMEM((rows, features), F32)] * 2 + [pltpu.SemaphoreType.DMA((2,))],
     )
     text_a = exchange(text_tiled, "y")
-    (image_tiled,) = call(spread_kernel, ring_gather(image_unit, "zh"), [shape(NX * NZH * rows, features)])
+    image_z = lax.all_gather(image_unit, "zh", axis=0, tiled=True)
+    image = lax.all_gather(image_z, "x", axis=0, tiled=True)
     (text_a,) = call(
-        tie_kernel, (text_a, image_tiled), [shape(*text_a.shape)], [ANY] * 2, [ANY], input_output_aliases={0: 0}
-    )
-    image = exchange(image_tiled, "x")
+        tie_kernel, (text_a, image_z), [shape(*text_a.shape)], [ANY] * 2, [ANY], input_output_aliases={0: 0}
+    )
     text_b = planes(text_a, -1)
     texts = (text_a, text_b, other_core(text_a), other_core(text_b))
 
     count, quarter = image.shape[0], text_a.shape[0]
-    part = count // NX
-    x, turn = lax.axis_index("x"), 1 - 2 * lax.axis_index("c")
-    blocks = [x, (x - turn) % NX, (x + turn) % NX, (x + 2) % NX]
-    place = jnp.stack([lax.axis_index("y") * rows, *blocks]).astype(jnp.int32)
+    zh, turn = lax.axis_index("zh"), 1 - 2 * lax.axis_index("c")
+    blocks = [zh, (zh - turn) % NZH, (zh + turn) % NZH, (zh + 2) % NZH]
+    own = (lax.axis_index("x") * NZH + zh) * rows
+    place = jnp.stack([own, lax.axis_index("y") * rows, *blocks]).astype(jnp.int32)
     product = 2 * count * quarter * features * 3
     slope, other = call(
         tile_kernel,
@@ -246,26 +228,20 @@
         vmem=20,
     )
     received = other_core(other)
-    xs = call(image_kernel, (slope, *texts), [shape(part, features)] * NX, flops=4 * product, vmem=20)
-    relay = turned(xs[3], "x", -1)
-    ahead = turned(xs[2], "x", 1)
+    (image_sums,) = call(image_kernel, (slope, *texts), [shape(count, features)], flops=4 * product, vmem=20)
+    image_x = lax.psum_scatter(image_sums, "x", scatter_dimension=0, tiled=True)
     keep, send = call(
         text_kernel,
-        (place, slope, image, other, received, xs[0]),
+        (slope, image, other, received, image_sums),
         [shape(quarter + 8, features)] * 2,
-        in_specs=[SMEM] + [VMEM] * 4 + [ANY],
+        in_specs=[VMEM] * 4 + [ANY],
         flops=2 * product,
         vmem=20,
     )
     plane = planes(send, 1)
-    (relay,) = call(relay_kernel, (xs[1], relay), [shape(part, features)])
-    back = turned(relay, "x", -1)
-    packed, *zs = call(
-        join_kernel,
-        (xs[0], back, ahead, keep, plane),
-        [shape(NY, PACK + 8, LANES)] + [shape(rows, features)] * NZH,
-    )
+    (packed,) = call(pack_kernel, (keep, plane), [shape(NY, PACK + 8, LANES)])
     packed = exchange(packed, "y")
+    zs = call(split_kernel, (place, image_x), [shape(rows, features)] * NZH, in_specs=[SMEM, VMEM])
     relay = turned(zs[3], "zh", -1)
     ahead = turned(zs[2], "zh", 1)
     (relay,) = call(relay_kernel, (zs[1], relay), [shape(rows, features)])

time: 132 us -> 155 us (1.17)
  the two profiles are of different devices: /device:TPU:1 before, /device:TPU:8 now
where the time goes in v8:
time: 155 us; the launch traced here: 154 us
  starting transfers between devices  52.2 us (34%)
  waiting for transfers between devices  43.5 us (28%)
  blocking collectives  18.8 us (12%)
  between operations  14.3 us (9%)
  Pallas kernels  13.4 us (9%)
  local copies, waits for them, and re-layouts  11.4 us (7%)
    all_to_all x3, starting transfers between devices, exchange(): return lax.all_to_all(values, axes, 0, 0, tiled=True)  20.2 us
    all_gather x1, blocking collectives, on_device(): image_z = lax.all_gather(image_unit, 'zh', axis=0, tiled=True)  18.8 us
    ppermute x2, waiting for transfers between devices, planes(): return lax.ppermute(values, ('zl', 'c', 'zh'), pairs)  16 us
    ppermute x3, starting transfers between devices, turned(): return lax.ppermute(values, ('c', axis), pairs)  15 us
    pallas_call x12, Pallas kernels, call(): pl.pallas_call(kernel, out_shape=outs, in_specs=in_specs or [VMEM] * len(...  13.4 us
    all_gather x1, waiting for transfers between devices, on_device(): image = lax.all_gather(image_z, 'x', axis=0, tiled=True)  11.4 us
    ppermute x2, starting transfers between devices, planes(): return lax.ppermute(values, ('zl', 'c', 'zh'), pairs)  11.3 us
    unnamed x30, local copies, waits for them, and re-layouts  11.3 us
  transfers between devices with their start and end apart: 13, of which 6 were waited for; matrix products, arithmetic and copies ran while one was open for 0% of the time, Pallas kernels for 5%

profile of v8, /device:TPU:8, one launch (start us, length us, event | category | flops | bytes accessed | tf_op | source)
XLA Modules:
  0.0 153.6 jit_solution(9394483677281634406)
XLA Ops:
  8.9 1.2 shard_map.49
  10.1 9.3 %all-to-all-start = ((f32[8,16,1152]{2,1,0:T(8,128)}), f32[8,16,1152]{2,1,0:T(8,128)S(1)}, u32[]{:S(2)}, u32[]{:S(2)}) async-start(f32[8,16,1152]{2,1,0:T(8,128)} %bitcast.6), calls=%async_computation | async-start | bytes 1179648 | tf_op jit(solution)/shard_map/all_to_all | solution.py:45
  19.4 18.8 %all_gather.6.refs_1_ = f32[64,1152]{1,0:T(8,128)} all-gather(f32[16,1152]{1,0:T(8,128)S(1)} %get-tuple-element.13), channel_id=1, replica_groups=mesh['y'=8,'zl'=2,'c'=2,'zh'=4,'x'=4] {'zh'}, dimensions={0}, use_global_device_ids=true | all-gather | bytes 368640 | tf_op jit(solution)/shard_map/all_gather | solution.py:208
  39.3 7.8 %collective-permute-start = (f32[128,1152]{1,0:T(8,128)S(1)}, f32[128,1152]{1,0:T(8,128)S(1)}, u32[]{:S(2)}, u32[]{:S(2)}) collective-permute-start(f32[128,1152]{1,0:T(8,128)S(1)} %shard_map.50.a_ref), channel_id=1, source_target_pairs={{0,44},{32,0},{4,32},{36,4},{8,36},{40,8},{12,40},{44,12},{16,48},... | collective-permute-start | bytes 1769480 | tf_op jit(solution)/shard_map/ppermute | solution.py:60
  47.0 1.9 %collective-permute-start.1 = (f32[128,1152]{1,0:T(8,128)S(1)}, f32[128,1152]{1,0:T(8,128)S(1)}, u32[]{:S(2)}, u32[]{:S(2)}) collective-permute-start(f32[128,1152]{1,0:T(8,128)S(1)} %shard_map.50.a_ref), channel_id=1, source_target_pairs={{0,16},{16,0},{1,17},{17,1},{2,18},{18,2},{3,19},{19,3},{4,20},{20... | collective-permute-start | bytes 1769480 | tf_op jit(solution)/shard_map/ppermute | solution.py:64
  48.9 5.5 %collective-permute-done.b_ref = f32[128,1152]{1,0:T(8,128)S(1)} collective-permute-done((f32[128,1152]{1,0:T(8,128)S(1)}, f32[128,1152]{1,0:T(8,128)S(1)}, u32[]{:S(2)}, u32[]{:S(2)}) %collective-permute-start) | collective-permute-done | bytes 589856 | tf_op jit(solution)/shard_map/ppermute | solution.py:60
  54.4 1.9 %collective-permute-start.2 = (f32[128,1152]{1,0:T(8,128)S(1)}, f32[128,1152]{1,0:T(8,128)S(1)}, u32[]{:S(2)}, u32[]{:S(2)}) collective-permute-start(f32[128,1152]{1,0:T(8,128)S(1)} %collective-permute-done.b_ref), channel_id=1, source_target_pairs={{0,16},{16,0},{1,17},{17,1},{2,18},{18,2},{3,19},{19,3},{4,20},{20... | collective-permute-start | bytes 1769480 | tf_op jit(solution)/shard_map/ppermute | solution.py:64
  56.5 11.4 %all-gather.2.cloned.1.call-done.image_ref = f32[256,1152]{1,0:T(8,128)} async-done(((f32[64,1152]{1,0:T(8,128)}), f32[256,1152]{1,0:T(8,128)}) %all-gather.2.cloned.1.call-update) | async-done | bytes 1179664 | tf_op jit(solution)/shard_map/all_gather | solution.py:209
  68.7 1.3 copy-done.1
  71.1 4.1 %shard_map.51 = (f32[256,512]{1,0:T(8,128)S(1)}, f32[264,1152]{1,0:T(8,128)S(1)}) custom-call(s32[6]{0:T(128)S(1)} %stack.27.place, f32[256,1152]{1,0:T(8,128)S(1)} %copy-done.1, f32[128,1152]{1,0:T(8,128)S(1)} %shard_map.50.a_ref, f32[128,1152]{1,0:T(8,128)S(1)} %collective-permute-done.b_ref, f32[128,1152]{1,0:T(8,128)S(1)} %collective-permute-done.1.c_ref, ...), custom_call_target="tpu_custom_call" | custom-call | flops 1358954496 | bytes 5279768 | tf_op jit(solution)/shard_map/pallas_call | solution.py:33
  75.2 1.9 %collective-permute-start.3 = (f32[264,1152]{1,0:T(8,128)S(1)}, f32[264,1152]{1,0:T(8,128)S(1)}, u32[]{:S(2)}, u32[]{:S(2)}) collective-permute-start(f32[264,1152]{1,0:T(8,128)S(1)} %get-tuple-element.16.other_ref), channel_id=1, source_target_pairs={{0,16},{16,0},{1,17},{17,1},{2,18},{18,2},{3,19},{19,3},{4,20},{20... | collective-permute-start | bytes 3649544 | tf_op jit(solution)/shard_map/ppermute | solution.py:64
  79.3 1.1 copy-done.9
  80.3 3.0 %shard_map.52.image_sums = f32[256,1152]{1,0:T(8,128)} custom-call(f32[256,512]{1,0:T(8,128)S(1)} %get-tuple-element.15.slope_ref, f32[128,1152]{1,0:T(8,128)S(1)} %shard_map.50.a_ref, f32[128,1152]{1,0:T(8,128)S(1)} %copy-done.4, f32[128,1152]{1,0:T(8,128)S(1)} %copy-done.6, f32[128,1152]{1,0:T(8,128)S(1)} %copy-done.9), custom_call_target="tpu_custom_call" | custom-call | flops 905969664 | bytes 4063232 | tf_op jit(solution)/shard_map/pallas_call | solution.py:33
  83.4 1.3 copy-done.2
  85.4 3.6 %collective-permute-start.4 = (f32[136,1152]{1,0:T(8,128)S(1)}, f32[136,1152]{1,0:T(8,128)S(1)}, u32[]{:S(2)}, u32[]{:S(2)}) collective-permute-start(f32[136,1152]{1,0:T(8,128)S(1)} %get-tuple-element.18), channel_id=1, source_target_pairs={{0,32},{32,4},{4,36},{36,8},{8,40},{40,12},{12,44},{44,0},{16,60},... | collective-permute-start | bytes 1880072 | tf_op jit(solution)/shard_map/ppermute | solution.py:60
  89.0 10.6 %collective-permute-done.4.plane_ref = f32[136,1152]{1,0:T(8,128)S(1)} collective-permute-done((f32[136,1152]{1,0:T(8,128)S(1)}, f32[136,1152]{1,0:T(8,128)S(1)}, u32[]{:S(2)}, u32[]{:S(2)}) %collective-permute-start.4) | collective-permute-done | bytes 626720 | tf_op jit(solution)/shard_map/ppermute | solution.py:60
  100.5 7.4 %all-to-all-start.1 = ((f32[8,152,128]{2,1,0:T(8,128)}), f32[8,152,128]{2,1,0:T(8,128)S(1)}, u32[]{:S(2)}, u32[]{:S(2)}) async-start(f32[8,152,128]{2,1,0:T(8,128)} %shard_map.54), calls=%async_computation.1 | async-start | bytes 1245184 | tf_op jit(solution)/shard_map/all_to_all | solution.py:45
  107.9 5.8 %reduce-scatter.2.cloned.1.call-done.image_ref = f32[64,1152]{1,0:T(8,128)} async-done(((f32[256,1152]{1,0:T(8,128)}), f32[64,1152]{1,0:T(8,128)}) %reduce-scatter.2.cloned.1.call-update) | async-done | bytes 294928 | tf_op jit(solution)/shard_map/reduce_scatter | solution.py:232
  115.2 6.6 %collective-permute-start.5 = (f32[16,1152]{1,0:T(8,128)S(1)}, f32[16,1152]{1,0:T(8,128)S(1)}, u32[]{:S(2)}, u32[]{:S(2)}) collective-permute-start(f32[16,1152]{1,0:T(8,128)S(1)} %get-tuple-element.21), channel_id=1, source_target_pairs={{0,12},{4,0},{8,4},{12,8},{16,20},{20,24},{24,28},{28,16},{1,13},{... | collective-permute-start | bytes 221192 | tf_op jit(solution)/shard_map/ppermute | solution.py:51
  121.8 1.9 %collective-permute-start.7 = (f32[16,1152]{1,0:T(8,128)S(1)}, f32[16,1152]{1,0:T(8,128)S(1)}, u32[]{:S(2)}, u32[]{:S(2)}) collective-permute-start(f32[16,1152]{1,0:T(8,128)S(1)} %get-tuple-element.22), channel_id=1, source_target_pairs={{0,4},{4,8},{8,12},{12,0},{16,28},{20,16},{24,20},{28,24},{1,5},{5... | collective-permute-start | bytes 221192 | tf_op jit(solution)/shard_map/ppermute | solution.py:51
  123.7 1.9 %collective-permute-done.5.right = f32[16,1152]{1,0:T(8,128)S(1)} collective-permute-done((f32[16,1152]{1,0:T(8,128)S(1)}, f32[16,1152]{1,0:T(8,128)S(1)}, u32[]{:S(2)}, u32[]{:S(2)}) %collective-permute-start.5) | collective-permute-done | bytes 73760 | tf_op jit(solution)/shard_map/ppermute | solution.py:51
  125.7 6.5 %collective-permute-start.6 = (f32[16,1152]{1,0:T(8,128)S(1)}, f32[16,1152]{1,0:T(8,128)S(1)}, u32[]{:S(2)}, u32[]{:S(2)}) collective-permute-start(f32[16,1152]{1,0:T(8,128)S(1)} %shard_map.58), channel_id=1, source_target_pairs={{0,12},{4,0},{8,4},{12,8},{16,20},{20,24},{24,28},{28,16},{1,13},{... | collective-permute-start | bytes 221192 | tf_op jit(solution)/shard_map/ppermute | solution.py:51
  132.8 3.5 %all-to-all-start.2 = ((f32[16,1,128]{2,1,0:T(1,128)}), f32[16,1,128]{2,1,0:T(1,128)S(1)}, u32[]{:S(2)}, u32[]{:S(2)}) async-start(f32[16,1,128]{2,1,0:T(1,128)} %bitcast.9), calls=%async_computation.2 | async-start | bytes 16384 | tf_op jit(solution)/shard_map/all_to_all | solution.py:45
  137.9 8.2 %all-to-all-done.2 = f32[16,1,128]{2,1,0:T(1,128)S(1)} async-done(((f32[16,1,128]{2,1,0:T(1,128)}), f32[16,1,128]{2,1,0:T(1,128)S(1)}, u32[]{:S(2)}, u32[]{:S(2)}) %all-to-all-start.2) | async-done | bytes 8224 | tf_op jit(solution)/shard_map/all_to_all | solution.py:45
  (48 shorter events, 13.0 us)
Async XLA Ops:
  10.1 28.2 %all-to-all-start = ((f32[8,16,1152]{2,1,0:T(8,128)}), f32[8,16,1152]{2,1,0:T(8,128)S(1)}, u32[]{:S(2)}, u32[]{:S(2)}) async-start(f32[8,16,1152]{2,1,0:T(8,128)} %bitcast.6), calls=%async_computation | async-start | bytes 1179648 | tf_op jit(solution)/shard_map/all_to_all | solution.py:45
  19.4 48.5 %all-gather.2.cloned.1.call-start = ((), (), s32[]{:S(2)}) async-start(), calls=%async_computation.4 | async-start | bytes 1474560 | tf_op jit(solution)/shard_map/all_gather | solution.py:209
  38.2 75.4 %reduce-scatter.2.cloned.1.call-start = ((), (), s32[]{:S(2)}) async-start(), calls=%async_computation.5 | async-start | bytes 1474560 | tf_op jit(solution)/shard_map/reduce_scatter | solution.py:232
  38.3 1.0 copy-start
  39.3 15.1 %collective-permute-start = (f32[128,1152]{1,0:T(8,128)S(1)}, f32[128,1152]{1,0:T(8,128)S(1)}, u32[]{:S(2)}, u32[]{:S(2)}) collective-permute-start(f32[128,1152]{1,0:T(8,128)S(1)} %shard_map.50.a_ref), channel_id=1, source_target_pairs={{0,44},{32,0},{4,32},{36,4},{8,36},{40,8},{12,40},{44,12},{16,48},... | collective-permute-start | bytes 1769480 | tf_op jit(solution)/shard_map/ppermute | solution.py:60
  47.0 9.4 %collective-permute-start.1 = (f32[128,1152]{1,0:T(8,128)S(1)}, f32[128,1152]{1,0:T(8,128)S(1)}, u32[]{:S(2)}, u32[]{:S(2)}) collective-permute-start(f32[128,1152]{1,0:T(8,128)S(1)} %shard_map.50.a_ref), channel_id=1, source_target_pairs={{0,16},{16,0},{1,17},{17,1},{2,18},{18,2},{3,19},{19,3},{4,20},{20... | collective-permute-start | bytes 1769480 | tf_op jit(solution)/shard_map/ppermute | solution.py:64
  54.4 20.8 %copy-start.3 = (f32[128,1152]{1,0:T(8,128)}, f32[128,1152]{1,0:T(8,128)S(1)}, u32[]{:S(2)}) copy-start(f32[128,1152]{1,0:T(8,128)S(1)} %collective-permute-done.b_ref) | copy-start | bytes 1769476
  54.4 13.5 %collective-permute-start.2 = (f32[128,1152]{1,0:T(8,128)S(1)}, f32[128,1152]{1,0:T(8,128)S(1)}, u32[]{:S(2)}, u32[]{:S(2)}) collective-permute-start(f32[128,1152]{1,0:T(8,128)S(1)} %collective-permute-done.b_ref), channel_id=1, source_target_pairs={{0,16},{16,0},{1,17},{17,1},{2,18},{18,2},{3,19},{19,3},{4,20},{20... | collective-permute-start | bytes 1769480 | tf_op jit(solution)/shard_map/ppermute | solution.py:64
  56.4 18.8 %copy-start.5 = (f32[128,1152]{1,0:T(8,128)}, f32[128,1152]{1,0:T(8,128)S(1)}, u32[]{:S(2)}) copy-start(f32[128,1152]{1,0:T(8,128)S(1)} %collective-permute-done.1.c_ref) | copy-start | bytes 1769476
  68.7 1.3 copy-start.1
  70.0 1.1 copy-start.8
  75.2 8.2 %collective-permute-start.3 = (f32[264,1152]{1,0:T(8,128)S(1)}, f32[264,1152]{1,0:T(8,128)S(1)}, u32[]{:S(2)}, u32[]{:S(2)}) collective-permute-start(f32[264,1152]{1,0:T(8,128)S(1)} %get-tuple-element.16.other_ref), channel_id=1, source_target_pairs={{0,16},{16,0},{1,17},{17,1},{2,18},{18,2},{3,19},{19,3},{4,20},{20... | collective-permute-start | bytes 3649544 | tf_op jit(solution)/shard_map/ppermute | solution.py:64
  77.1 1.1 copy-start.4
  78.2 1.1 copy-start.6
  79.3 1.1 copy-start.9
  83.4 1.3 copy-start.2
  85.4 14.1 %collective-permute-start.4 = (f32[136,1152]{1,0:T(8,128)S(1)}, f32[136,1152]{1,0:T(8,128)S(1)}, u32[]{:S(2)}, u32[]{:S(2)}) collective-permute-start(f32[136,1152]{1,0:T(8,128)S(1)} %get-tuple-element.18), channel_id=1, source_target_pairs={{0,32},{32,4},{4,36},{36,8},{8,40},{40,12},{12,44},{44,0},{16,60},... | collective-permute-start | bytes 1880072 | tf_op jit(solution)/shard_map/ppermute | solution.py:60
  100.5 35.8 %copy-start.14 = (f32[16,1152]{1,0:T(8,128)S(1)}, f32[16,1152]{1,0:T(8,128)}, u32[]{:S(2)}) copy-start(f32[16,1152]{1,0:T(8,128)} %emb_ref.2) | copy-start | bytes 221188
  100.5 36.6 %copy-start.11 = (f32[16,1152]{1,0:T(8,128)S(1)}, f32[16,1152]{1,0:T(8,128)}, u32[]{:S(2)}) copy-start(f32[16,1152]{1,0:T(8,128)} %emb_ref.3) | copy-start | bytes 221188
  100.5 31.7 %all-to-all-start.1 = ((f32[8,152,128]{2,1,0:T(8,128)}), f32[8,152,128]{2,1,0:T(8,128)S(1)}, u32[]{:S(2)}, u32[]{:S(2)}) async-start(f32[8,152,128]{2,1,0:T(8,128)} %shard_map.54), calls=%async_computation.1 | async-start | bytes 1245184 | tf_op jit(solution)/shard_map/all_to_all | solution.py:45
  115.2 10.4 %collective-permute-start.5 = (f32[16,1152]{1,0:T(8,128)S(1)}, f32[16,1152]{1,0:T(8,128)S(1)}, u32[]{:S(2)}, u32[]{:S(2)}) collective-permute-start(f32[16,1152]{1,0:T(8,128)S(1)} %get-tuple-element.21), channel_id=1, source_target_pairs={{0,12},{4,0},{8,4},{12,8},{16,20},{20,24},{24,28},{28,16},{1,13},{... | collective-permute-start | bytes 221192 | tf_op jit(solution)/shard_map/ppermute | solution.py:51
  121.8 14.4 %collective-permute-start.7 = (f32[16,1152]{1,0:T(8,128)S(1)}, f32[16,1152]{1,0:T(8,128)S(1)}, u32[]{:S(2)}, u32[]{:S(2)}) collective-permute-start(f32[16,1152]{1,0:T(8,128)S(1)} %get-tuple-element.22), channel_id=1, source_target_pairs={{0,4},{4,8},{8,12},{12,0},{16,28},{20,16},{24,20},{28,24},{1,5},{5... | collective-permute-start | bytes 221192 | tf_op jit(solution)/shard_map/ppermute | solution.py:51
  125.7 10.6 %collective-permute-start.6 = (f32[16,1152]{1,0:T(8,128)S(1)}, f32[16,1152]{1,0:T(8,128)S(1)}, u32[]{:S(2)}, u32[]{:S(2)}) collective-permute-start(f32[16,1152]{1,0:T(8,128)S(1)} %shard_map.58), channel_id=1, source_target_pairs={{0,12},{4,0},{8,4},{12,8},{16,20},{20,24},{24,28},{28,16},{1,13},{... | collective-permute-start | bytes 221192 | tf_op jit(solution)/shard_map/ppermute | solution.py:51
  132.8 13.4 %all-to-all-start.2 = ((f32[16,1,128]{2,1,0:T(1,128)}), f32[16,1,128]{2,1,0:T(1,128)S(1)}, u32[]{:S(2)}, u32[]{:S(2)}) async-start(f32[16,1,128]{2,1,0:T(1,128)} %bitcast.9), calls=%async_computation.2 | async-start | bytes 16384 | tf_op jit(solution)/shard_map/all_to_all | solution.py:45
  (4 other events, 3.6 us)
Sparse Core Ops, SparseCore 0:
  38.4 29.5 all-gather.1
  83.5 30.1 reduce-scatter.1

commit v9 on v7

--- a/solution.py
+++ b/solution.py
@@ -64,12 +64,6 @@
     return lax.ppermute(values, "c", [(0, 1), (1, 0)])
 
 
-def ring_gather(values, axis):
-    back = turned(values, axis, 1)
-    ahead = turned(values, axis, -1)
-    return values, back, ahead, turned(back, axis, 1)
-
-
 def normalize(values):
     length = jnp.sqrt(jnp.sum(values * values, axis=1, keepdims=True) + EPSILON)
     return values / length, length
@@ -92,34 +86,19 @@
     return dot(left[1], right[0]) + dot(left[0], right[1]) + dot(left[0], right[0])
 
 
-def normalize_kernel(image_hbm, text_hbm, image_out, text_out, image_ref, text_ref, sems):
-    copies = [
-        pltpu.make_async_copy(text_hbm, text_ref, sems.at[0]),
-        pltpu.make_async_copy(image_hbm, image_ref, sems.at[1]),
-    ]
-    for copy in copies:
-        copy.start()
-    copies[0].wait()
-    text_unit = normalize(text_ref[...])[0]
-    for y in range(NY):
-        text_out[pl.ds(y * ROWS, ROWS), :] = text_unit
-    copies[1].wait()
-    image_out[...] = normalize(image_ref[...])[0]
-
-
-def spread_kernel(*refs):
+def image_unit_kernel(image_ref, out):
+    unit = normalize(image_ref[...])[0]
     for x in range(NX):
-        for k, part in enumerate(refs[:-1]):
-            refs[-1][pl.ds((x * NZH + k) * ROWS, ROWS), :] = part[...]
-
-
-def tie_kernel(*refs):
-    pass
+        out[pl.ds(x * NZH * ROWS, NZH * ROWS), :] = unit
+
+
+def text_unit_kernel(text_ref, image_units, out):
+    out[...] = normalize(text_ref[...])[0]
 
 
 def in_turn(place, image_ref):
     rows = image_ref.shape[0] // NX
-    starts = [pl.multiple_of(place[1 + k] * rows, rows) for k in range(NX)]
+    starts = [pl.multiple_of(place[2 + k] * rows, rows) for k in range(NX)]
     return halves(jnp.concatenate([image_ref[pl.ds(start, rows), :] for start in starts], axis=0))
 
 
@@ -127,9 +106,9 @@
     image = in_turn(place, image_ref)
     quarter = a_ref.shape[0]
     count = image_ref.shape[0]
-    row = lax.broadcasted_iota(jnp.int32, (count, quarter), 0)
-    column = lax.broadcasted_iota(jnp.int32, (count, quarter), 1) - place[0]
-    matched = (row == column) & (row < ROWS)
+    row = lax.broadcasted_iota(jnp.int32, (count, quarter), 0) - place[0]
+    column = lax.broadcasted_iota(jnp.int32, (count, quarter), 1) - place[1]
+    matched = (row == column) & (row >= 0) & (row < ROWS)
     total = jnp.zeros((), F32)
     for k, ref in ((2, c_ref), (3, d_ref), (0, a_ref), (1, b_ref)):
         logits = LOGIT_MULT * dot3(image, halves(ref[...]), ((1,), (1,))) + LOGIT_SHIFT
@@ -173,10 +152,13 @@
     out[...] = left[...] + right[...]
 
 
-def join_kernel(x0, x1, x2, keep_ref, plane_ref, packed_out, *zs):
-    for k, out in enumerate(zs):
-        rows = pl.ds(k * ROWS, ROWS)
+def split_kernel(place, x0, x1, x2, *outs):
+    for k, out in enumerate(outs):
+        rows = pl.ds(pl.multiple_of(place[2 + NX + k] * ROWS, ROWS), ROWS)
         out[...] = x0[rows, :] + (x1[rows, :] + x2[rows, :])
+
+
+def pack_kernel(keep_ref, plane_ref, relay_ref, ahead_ref, packed_out):
     last, first = pl.ds(NY * ROWS, 8), pl.ds(0, LANES)
     loss = keep_ref[last, first] + plane_ref[last, first]
     for y in range(NY):
@@ -215,17 +197,11 @@
 
 def on_device(image_emb, text_emb):
     rows, features = image_emb.shape
-    image_unit, text_tiled = call(
-        normalize_kernel,
-        (image_emb, text_emb),
-        [shape(rows, features), shape(NY * rows, features)],
-        in_specs=[HBM] * 2,
-        scratch_shapes=[pltpu.VMEM((rows, features), F32)] * 2 + [pltpu.SemaphoreType.DMA((2,))],
-    )
-    text_a = exchange(text_tiled, "y")
-    (image_tiled,) = call(spread_kernel, ring_gather(image_unit, "zh"), [shape(NX * NZH * rows, features)])
+    text_y = exchange(jnp.tile(text_emb, (NY, 1)), "y")
+    image_z = lax.all_gather(image_emb, "zh", axis=0, tiled=True)
+    (image_tiled,) = call(image_unit_kernel, (image_z,), [shape(NX * NZH * rows, features)])
     (text_a,) = call(
-        tie_kernel, (text_a, image_tiled), [shape(*text_a.shape)], [ANY] * 2, [ANY], input_output_aliases={0: 0}
+        text_unit_kernel, (text_y, image_tiled), [shape(*text_y.shape)], in_specs=[VMEM, ANY]
     )
     image = exchange(image_tiled, "x")
     text_b = planes(text_a, -1)
@@ -233,9 +209,9 @@
 
     count, quarter = image.shape[0], text_a.shape[0]
     part = count // NX
-    x, turn = lax.axis_index("x"), 1 - 2 * lax.axis_index("c")
-    blocks = [x, (x - turn) % NX, (x + turn) % NX, (x + 2) % NX]
-    place = jnp.stack([lax.axis_index("y") * rows, *blocks]).astype(jnp.int32)
+    x, zh, turn = lax.axis_index("x"), lax.axis_index("zh"), 1 - 2 * lax.axis_index("c")
+    blocks = [(at + step) % NX for at in (x, zh) for step in (0, -turn, turn, 2)]
+    place = jnp.stack([zh * rows, lax.axis_index("y") * rows, *blocks]).astype(jnp.int32)
     product = 2 * count * quarter * features * 3
     slope, other = call(
         tile_kernel,
@@ -260,10 +236,17 @@
     plane = planes(send, 1)
     (relay,) = call(relay_kernel, (xs[1], relay), [shape(part, features)])
     back = turned(relay, "x", -1)
-    packed, *zs = call(
-        join_kernel,
-        (xs[0], back, ahead, keep, plane),
-        [shape(NY, PACK + 8, LANES)] + [shape(rows, features)] * NZH,
+    (packed,) = call(
+        pack_kernel,
+        (keep, plane, relay, ahead),
+        [shape(NY, PACK + 8, LANES)],
+        in_specs=[VMEM] * 2 + [ANY] * 2,
+    )
+    zs = call(
+        split_kernel,
+        (place, xs[0], back, ahead),
+        [shape(rows, features)] * NZH,
+        in_specs=[SMEM] + [VMEM] * 3,
     )
     packed = exchange(packed, "y")
     relay = turned(zs[3], "zh", -1)

time: 132 us -> 130 us (0.985)
  the two profiles are of different devices: /device:TPU:1 before, /device:TPU:72 now
where the time goes in v9:
time: 130 us
  starting transfers between devices  59 us (45%)
  waiting for transfers between devices  33.5 us (26%)
  blocking collectives  19.5 us (15%)
  Pallas kernels  14.9 us (11%)
  local copies, waits for them, and re-layouts  1.86 us (1%)
    all_to_all x4, starting transfers between devices, exchange(): return lax.all_to_all(values, axes, 0, 0, tiled=True)  24.8 us
    ppermute x6, starting transfers between devices, turned(): return lax.ppermute(values, ('c', axis), pairs)  22.6 us
    all_gather x1, blocking collectives, on_device(): image_z = lax.all_gather(image_emb, 'zh', axis=0, tiled=True)  19.5 us
    ppermute x6, waiting for transfers between devices, turned(): return lax.ppermute(values, ('c', axis), pairs)  15.1 us
    all_to_all x4, waiting for transfers between devices, exchange(): return lax.all_to_all(values, axes, 0, 0, tiled=True)  15 us
    pallas_call x13, Pallas kernels, call(): pl.pallas_call(kernel, out_shape=outs, in_specs=in_specs or [VMEM] * len(...  14.9 us
    ppermute x2, starting transfers between devices, planes(): return lax.ppermute(values, ('zl', 'c', 'zh'), pairs)  5.84 us
    ppermute x3, starting transfers between devices, other_core(): return lax.ppermute(values, 'c', [(0, 1), (1, 0)])  5.74 us
  transfers between devices with their start and end apart: 15, of which 7 were waited for; matrix products, arithmetic and copies ran while one was open for 0% of the time, Pallas kernels for 6%

profile of v9, /device:TPU:72, one launch (start us, length us, event | category | flops | bytes accessed | tf_op | source)
XLA Modules:
  0.0 129.7 jit_solution(15653657666117616347)
XLA Ops:
  2.4 7.5 %all-to-all-start.1 = ((f32[8,16,1152]{2,1,0:T(8,128)}), f32[8,16,1152]{2,1,0:T(8,128)S(1)}, u32[]{:S(2)}, u32[]{:S(2)}) async-start(f32[8,16,1152]{2,1,0:T(8,128)} %tile.2), calls=%async_computation.1 | async-start | bytes 1179648 | tf_op jit(solution)/shard_map/all_to_all | solution.py:45
  10.0 19.5 %all_gather.3.image_ref = f32[64,1152]{1,0:T(8,128)S(1)} all-gather(f32[16,1152]{1,0:T(8,128)S(1)} %copy-done.1), channel_id=1, replica_groups=mesh['y'=8,'zl'=2,'c'=2,'zh'=4,'x'=4] {'zh'}, dimensions={0}, use_global_device_ids=true | all-gather | bytes 368640 | tf_op jit(solution)/shard_map/all_gather | solution.py:201
  30.8 2.1 %collective-permute-start = (f32[128,1152]{1,0:T(8,128)S(1)}, f32[128,1152]{1,0:T(8,128)S(1)}, u32[]{:S(2)}, u32[]{:S(2)}) collective-permute-start(f32[128,1152]{1,0:T(8,128)S(1)} %shard_map.50.a_ref), channel_id=1, source_target_pairs={{0,44},{32,0},{4,32},{36,4},{8,36},{40,8},{12,40},{44,12},{16,48},... | collective-permute-start | bytes 1769480 | tf_op jit(solution)/shard_map/ppermute | solution.py:60
  32.9 4.3 %all-to-all-start = ((f32[4,64,1152]{2,1,0:T(8,128)}), f32[4,64,1152]{2,1,0:T(8,128)S(1)}, u32[]{:S(2)}, u32[]{:S(2)}) async-start(f32[4,64,1152]{2,1,0:T(8,128)} %bitcast.10), calls=%async_computation | async-start | bytes 2359296 | tf_op jit(solution)/shard_map/all_to_all | solution.py:45
  37.2 1.9 %collective-permute-start.1 = (f32[128,1152]{1,0:T(8,128)S(1)}, f32[128,1152]{1,0:T(8,128)S(1)}, u32[]{:S(2)}, u32[]{:S(2)}) collective-permute-start(f32[128,1152]{1,0:T(8,128)S(1)} %shard_map.50.a_ref), channel_id=1, source_target_pairs={{0,16},{16,0},{1,17},{17,1},{2,18},{18,2},{3,19},{19,3},{4,20},{20... | collective-permute-start | bytes 1769480 | tf_op jit(solution)/shard_map/ppermute | solution.py:64
  39.1 3.4 %collective-permute-done.b_ref = f32[128,1152]{1,0:T(8,128)S(1)} collective-permute-done((f32[128,1152]{1,0:T(8,128)S(1)}, f32[128,1152]{1,0:T(8,128)S(1)}, u32[]{:S(2)}, u32[]{:S(2)}) %collective-permute-start) | collective-permute-done | bytes 589856 | tf_op jit(solution)/shard_map/ppermute | solution.py:60
  42.6 1.9 %collective-permute-start.2 = (f32[128,1152]{1,0:T(8,128)S(1)}, f32[128,1152]{1,0:T(8,128)}, u32[]{:S(2)}, u32[]{:S(2)}) collective-permute-start(f32[128,1152]{1,0:T(8,128)S(1)} %collective-permute-done.b_ref), channel_id=1, source_target_pairs={{0,16},{16,0},{1,17},{17,1},{2,18},{18,2},{3,19},{19,3},{4,20},{20... | collective-permute-start | bytes 1769480 | tf_op jit(solution)/shard_map/ppermute | solution.py:64
  44.7 6.7 %all-to-all-done = f32[4,64,1152]{2,1,0:T(8,128)S(1)} async-done(((f32[4,64,1152]{2,1,0:T(8,128)}), f32[4,64,1152]{2,1,0:T(8,128)S(1)}, u32[]{:S(2)}, u32[]{:S(2)}) %all-to-all-start) | async-done | bytes 1179680 | tf_op jit(solution)/shard_map/all_to_all | solution.py:45
  51.4 4.7 %shard_map.51 = (f32[256,512]{1,0:T(8,128)S(1)}, f32[264,1152]{1,0:T(8,128)S(1)}) custom-call(s32[10]{0:T(128)S(1)} %stack.43.place, f32[256,1152]{1,0:T(8,128)S(1)} %bitcast.18, f32[128,1152]{1,0:T(8,128)S(1)} %shard_map.50.a_ref, f32[128,1152]{1,0:T(8,128)S(1)} %collective-permute-done.b_ref, f32[128,1152]{1,0:T(8,128)S(1)} %collective-permute-done.1.c_ref, ...), custom_call_target="tpu_custom_call" | custom-call | flops 1358954496 | bytes 5279784 | tf_op jit(solution)/shard_map/pallas_call | solution.py:33
  56.1 1.9 %collective-permute-start.3 = (f32[264,1152]{1,0:T(8,128)S(1)}, f32[264,1152]{1,0:T(8,128)S(1)}, u32[]{:S(2)}, u32[]{:S(2)}) collective-permute-start(f32[264,1152]{1,0:T(8,128)S(1)} %get-tuple-element.16.other_ref), channel_id=1, source_target_pairs={{0,16},{16,0},{1,17},{17,1},{2,18},{18,2},{3,19},{19,3},{4,20},{20... | collective-permute-start | bytes 3649544 | tf_op jit(solution)/shard_map/ppermute | solution.py:64
  58.0 3.1 %shard_map.52 = (f32[64,1152]{1,0:T(8,128)S(1)}, f32[64,1152]{1,0:T(8,128)S(1)}, f32[64,1152]{1,0:T(8,128)S(1)}, f32[64,1152]{1,0:T(8,128)S(1)}) custom-call(f32[256,512]{1,0:T(8,128)S(1)} %get-tuple-element.15.slope_ref, f32[128,1152]{1,0:T(8,128)S(1)} %shard_map.50.a_ref, f32[128,1152]{1,0:T(8,128)S(1)} %collective-permute-done.b_ref, ...), custom_call_target="tpu_custom_call" | custom-call | flops 905969664 | bytes 4063232 | tf_op jit(solution)/shard_map/pallas_call | solution.py:33
  62.4 3.7 %collective-permute-start.4 = (f32[136,1152]{1,0:T(8,128)S(1)}, f32[136,1152]{1,0:T(8,128)S(1)}, u32[]{:S(2)}, u32[]{:S(2)}) collective-permute-start(f32[136,1152]{1,0:T(8,128)S(1)} %get-tuple-element.19), channel_id=1, source_target_pairs={{0,32},{32,4},{4,36},{36,8},{8,40},{40,12},{12,44},{44,0},{16,60},... | collective-permute-start | bytes 1880072 | tf_op jit(solution)/shard_map/ppermute | solution.py:60
  66.2 3.1 %collective-permute-start.5 = (f32[64,1152]{1,0:T(8,128)S(1)}, f32[64,1152]{1,0:T(8,128)S(1)}, u32[]{:S(2)}, u32[]{:S(2)}) collective-permute-start(f32[64,1152]{1,0:T(8,128)S(1)} %get-tuple-element.21), channel_id=1, source_target_pairs={{0,3},{1,0},{2,1},{3,2},{16,17},{17,18},{18,19},{19,16},{4,7},{5,4... | collective-permute-start | bytes 884744 | tf_op jit(solution)/shard_map/ppermute | solution.py:51
  69.3 2.8 %collective-permute-start.6 = (f32[64,1152]{1,0:T(8,128)S(1)}, f32[64,1152]{1,0:T(8,128)S(1)}, u32[]{:S(2)}, u32[]{:S(2)}) collective-permute-start(f32[64,1152]{1,0:T(8,128)S(1)} %get-tuple-element.22), channel_id=1, source_target_pairs={{0,1},{1,2},{2,3},{3,0},{16,19},{17,16},{18,17},{19,18},{4,5},{5,6... | collective-permute-start | bytes 884744 | tf_op jit(solution)/shard_map/ppermute | solution.py:51
  72.0 3.6 %collective-permute-done.5.right = f32[64,1152]{1,0:T(8,128)S(1)} collective-permute-done((f32[64,1152]{1,0:T(8,128)S(1)}, f32[64,1152]{1,0:T(8,128)S(1)}, u32[]{:S(2)}, u32[]{:S(2)}) %collective-permute-start.5) | collective-permute-done | bytes 294944 | tf_op jit(solution)/shard_map/ppermute | solution.py:51
  75.7 3.6 %collective-permute-done.6.ahead_ref.x2 = f32[64,1152]{1,0:T(8,128)S(1)} collective-permute-done((f32[64,1152]{1,0:T(8,128)S(1)}, f32[64,1152]{1,0:T(8,128)S(1)}, u32[]{:S(2)}, u32[]{:S(2)}) %collective-permute-start.6) | collective-permute-done | bytes 294944 | tf_op jit(solution)/shard_map/ppermute | solution.py:51
  80.2 6.8 %all-to-all-start.2 = ((f32[8,152,128]{2,1,0:T(8,128)}), f32[8,152,128]{2,1,0:T(8,128)S(1)}, u32[]{:S(2)}, u32[]{:S(2)}) async-start(f32[8,152,128]{2,1,0:T(8,128)} %shard_map.55), calls=%async_computation.2 | async-start | bytes 1245184 | tf_op jit(solution)/shard_map/all_to_all | solution.py:45
  87.0 2.0 %collective-permute-start.7 = (f32[64,1152]{1,0:T(8,128)S(1)}, f32[64,1152]{1,0:T(8,128)S(1)}, u32[]{:S(2)}, u32[]{:S(2)}) collective-permute-start(f32[64,1152]{1,0:T(8,128)S(1)} %shard_map.54.relay_ref), channel_id=1, source_target_pairs={{0,3},{1,0},{2,1},{3,2},{16,17},{17,18},{18,19},{19,16},{4,7},{5,4... | collective-permute-start | bytes 884744 | tf_op jit(solution)/shard_map/ppermute | solution.py:51
  89.0 6.7 %collective-permute-done.7.x1 = f32[64,1152]{1,0:T(8,128)S(1)} collective-permute-done((f32[64,1152]{1,0:T(8,128)S(1)}, f32[64,1152]{1,0:T(8,128)S(1)}, u32[]{:S(2)}, u32[]{:S(2)}) %collective-permute-start.7) | collective-permute-done | bytes 294944 | tf_op jit(solution)/shard_map/ppermute | solution.py:51
  96.3 6.3 %collective-permute-start.8 = (f32[16,1152]{1,0:T(8,128)S(1)}, f32[16,1152]{1,0:T(8,128)S(1)}, u32[]{:S(2)}, u32[]{:S(2)}) collective-permute-start(f32[16,1152]{1,0:T(8,128)S(1)} %get-tuple-element.25), channel_id=1, source_target_pairs={{0,12},{4,0},{8,4},{12,8},{16,20},{20,24},{24,28},{28,16},{1,13},{... | collective-permute-start | bytes 221192 | tf_op jit(solution)/shard_map/ppermute | solution.py:51
  102.6 1.9 %collective-permute-start.10 = (f32[16,1152]{1,0:T(8,128)S(1)}, f32[16,1152]{1,0:T(8,128)S(1)}, u32[]{:S(2)}, u32[]{:S(2)}) collective-permute-start(f32[16,1152]{1,0:T(8,128)S(1)} %get-tuple-element.26), channel_id=1, source_target_pairs={{0,4},{4,8},{8,12},{12,0},{16,28},{20,16},{24,20},{28,24},{1,5},{5... | collective-permute-start | bytes 221192 | tf_op jit(solution)/shard_map/ppermute | solution.py:51
  105.8 6.5 %collective-permute-start.9 = (f32[16,1152]{1,0:T(8,128)S(1)}, f32[16,1152]{1,0:T(8,128)S(1)}, u32[]{:S(2)}, u32[]{:S(2)}) collective-permute-start(f32[16,1152]{1,0:T(8,128)S(1)} %shard_map.59), channel_id=1, source_target_pairs={{0,12},{4,0},{8,4},{12,8},{16,20},{20,24},{24,28},{28,16},{1,13},{... | collective-permute-start | bytes 221192 | tf_op jit(solution)/shard_map/ppermute | solution.py:51
  112.9 6.2 %all-to-all-start.3 = ((f32[16,1,128]{2,1,0:T(1,128)}), f32[16,1,128]{2,1,0:T(1,128)S(1)}, u32[]{:S(2)}, u32[]{:S(2)}) async-start(f32[16,1,128]{2,1,0:T(1,128)} %bitcast.14), calls=%async_computation.3 | async-start | bytes 16384 | tf_op jit(solution)/shard_map/all_to_all | solution.py:45
  120.7 8.3 %all-to-all-done.3 = f32[16,1,128]{2,1,0:T(1,128)S(1)} async-done(((f32[16,1,128]{2,1,0:T(1,128)}), f32[16,1,128]{2,1,0:T(1,128)S(1)}, u32[]{:S(2)}, u32[]{:S(2)}) %all-to-all-start.3) | async-done | bytes 8224 | tf_op jit(solution)/shard_map/all_to_all | solution.py:45
  (26 shorter events, 10.3 us)
Async XLA Ops:
  0.6 9.3 %copy-start.1 = (f32[16,1152]{1,0:T(8,128)S(1)}, f32[16,1152]{1,0:T(8,128)}, u32[]{:S(2)}) copy-start(f32[16,1152]{1,0:T(8,128)} %emb_ref.2) | copy-start | bytes 221188
  2.4 28.2 %all-to-all-start.1 = ((f32[8,16,1152]{2,1,0:T(8,128)}), f32[8,16,1152]{2,1,0:T(8,128)S(1)}, u32[]{:S(2)}, u32[]{:S(2)}) async-start(f32[8,16,1152]{2,1,0:T(8,128)} %tile.2), calls=%async_computation.1 | async-start | bytes 1179648 | tf_op jit(solution)/shard_map/all_to_all | solution.py:45
  30.8 11.8 %collective-permute-start = (f32[128,1152]{1,0:T(8,128)S(1)}, f32[128,1152]{1,0:T(8,128)S(1)}, u32[]{:S(2)}, u32[]{:S(2)}) collective-permute-start(f32[128,1152]{1,0:T(8,128)S(1)} %shard_map.50.a_ref), channel_id=1, source_target_pairs={{0,44},{32,0},{4,32},{36,4},{8,36},{40,8},{12,40},{44,12},{16,48},... | collective-permute-start | bytes 1769480 | tf_op jit(solution)/shard_map/ppermute | solution.py:60
  32.9 18.5 %all-to-all-start = ((f32[4,64,1152]{2,1,0:T(8,128)}), f32[4,64,1152]{2,1,0:T(8,128)S(1)}, u32[]{:S(2)}, u32[]{:S(2)}) async-start(f32[4,64,1152]{2,1,0:T(8,128)} %bitcast.10), calls=%async_computation | async-start | bytes 2359296 | tf_op jit(solution)/shard_map/all_to_all | solution.py:45
  37.2 14.2 %collective-permute-start.1 = (f32[128,1152]{1,0:T(8,128)S(1)}, f32[128,1152]{1,0:T(8,128)S(1)}, u32[]{:S(2)}, u32[]{:S(2)}) collective-permute-start(f32[128,1152]{1,0:T(8,128)S(1)} %shard_map.50.a_ref), channel_id=1, source_target_pairs={{0,16},{16,0},{1,17},{17,1},{2,18},{18,2},{3,19},{19,3},{4,20},{20... | collective-permute-start | bytes 1769480 | tf_op jit(solution)/shard_map/ppermute | solution.py:64
  42.6 8.8 %collective-permute-start.2 = (f32[128,1152]{1,0:T(8,128)S(1)}, f32[128,1152]{1,0:T(8,128)}, u32[]{:S(2)}, u32[]{:S(2)}) collective-permute-start(f32[128,1152]{1,0:T(8,128)S(1)} %collective-permute-done.b_ref), channel_id=1, source_target_pairs={{0,16},{16,0},{1,17},{17,1},{2,18},{18,2},{3,19},{19,3},{4,20},{20... | collective-permute-start | bytes 1769480 | tf_op jit(solution)/shard_map/ppermute | solution.py:64
  56.1 5.0 %collective-permute-start.3 = (f32[264,1152]{1,0:T(8,128)S(1)}, f32[264,1152]{1,0:T(8,128)S(1)}, u32[]{:S(2)}, u32[]{:S(2)}) collective-permute-start(f32[264,1152]{1,0:T(8,128)S(1)} %get-tuple-element.16.other_ref), channel_id=1, source_target_pairs={{0,16},{16,0},{1,17},{17,1},{2,18},{18,2},{3,19},{19,3},{4,20},{20... | collective-permute-start | bytes 3649544 | tf_op jit(solution)/shard_map/ppermute | solution.py:64
  62.4 16.8 %collective-permute-start.4 = (f32[136,1152]{1,0:T(8,128)S(1)}, f32[136,1152]{1,0:T(8,128)S(1)}, u32[]{:S(2)}, u32[]{:S(2)}) collective-permute-start(f32[136,1152]{1,0:T(8,128)S(1)} %get-tuple-element.19), channel_id=1, source_target_pairs={{0,32},{32,4},{4,36},{36,8},{8,40},{40,12},{12,44},{44,0},{16,60},... | collective-permute-start | bytes 1880072 | tf_op jit(solution)/shard_map/ppermute | solution.py:60
  66.2 9.4 %collective-permute-start.5 = (f32[64,1152]{1,0:T(8,128)S(1)}, f32[64,1152]{1,0:T(8,128)S(1)}, u32[]{:S(2)}, u32[]{:S(2)}) collective-permute-start(f32[64,1152]{1,0:T(8,128)S(1)} %get-tuple-element.21), channel_id=1, source_target_pairs={{0,3},{1,0},{2,1},{3,2},{16,17},{17,18},{18,19},{19,16},{4,7},{5,4... | collective-permute-start | bytes 884744 | tf_op jit(solution)/shard_map/ppermute | solution.py:51
  69.3 10.0 %collective-permute-start.6 = (f32[64,1152]{1,0:T(8,128)S(1)}, f32[64,1152]{1,0:T(8,128)S(1)}, u32[]{:S(2)}, u32[]{:S(2)}) collective-permute-start(f32[64,1152]{1,0:T(8,128)S(1)} %get-tuple-element.22), channel_id=1, source_target_pairs={{0,1},{1,2},{2,3},{3,0},{16,19},{17,16},{18,17},{19,18},{4,5},{5,6... | collective-permute-start | bytes 884744 | tf_op jit(solution)/shard_map/ppermute | solution.py:51
  80.2 32.1 %all-to-all-start.2 = ((f32[8,152,128]{2,1,0:T(8,128)}), f32[8,152,128]{2,1,0:T(8,128)S(1)}, u32[]{:S(2)}, u32[]{:S(2)}) async-start(f32[8,152,128]{2,1,0:T(8,128)} %shard_map.55), calls=%async_computation.2 | async-start | bytes 1245184 | tf_op jit(solution)/shard_map/all_to_all | solution.py:45
  87.0 32.9 %copy-start = (f32[16,1152]{1,0:T(8,128)S(1)}, f32[16,1152]{1,0:T(8,128)}, u32[]{:S(2)}) copy-start(f32[16,1152]{1,0:T(8,128)} %emb_ref.3) | copy-start | bytes 221188
  87.0 8.7 %collective-permute-start.7 = (f32[64,1152]{1,0:T(8,128)S(1)}, f32[64,1152]{1,0:T(8,128)S(1)}, u32[]{:S(2)}, u32[]{:S(2)}) collective-permute-start(f32[64,1152]{1,0:T(8,128)S(1)} %shard_map.54.relay_ref), channel_id=1, source_target_pairs={{0,3},{1,0},{2,1},{3,2},{16,17},{17,18},{18,19},{19,16},{4,7},{5,4... | collective-permute-start | bytes 884744 | tf_op jit(solution)/shard_map/ppermute | solution.py:51
  96.3 9.4 %collective-permute-start.8 = (f32[16,1152]{1,0:T(8,128)S(1)}, f32[16,1152]{1,0:T(8,128)S(1)}, u32[]{:S(2)}, u32[]{:S(2)}) collective-permute-start(f32[16,1152]{1,0:T(8,128)S(1)} %get-tuple-element.25), channel_id=1, source_target_pairs={{0,12},{4,0},{8,4},{12,8},{16,20},{20,24},{24,28},{28,16},{1,13},{... | collective-permute-start | bytes 221192 | tf_op jit(solution)/shard_map/ppermute | solution.py:51
  102.6 16.4 %collective-permute-start.10 = (f32[16,1152]{1,0:T(8,128)S(1)}, f32[16,1152]{1,0:T(8,128)S(1)}, u32[]{:S(2)}, u32[]{:S(2)}) collective-permute-start(f32[16,1152]{1,0:T(8,128)S(1)} %get-tuple-element.26), channel_id=1, source_target_pairs={{0,4},{4,8},{8,12},{12,0},{16,28},{20,16},{24,20},{28,24},{1,5},{5... | collective-permute-start | bytes 221192 | tf_op jit(solution)/shard_map/ppermute | solution.py:51
  105.8 13.3 %collective-permute-start.9 = (f32[16,1152]{1,0:T(8,128)S(1)}, f32[16,1152]{1,0:T(8,128)S(1)}, u32[]{:S(2)}, u32[]{:S(2)}) collective-permute-start(f32[16,1152]{1,0:T(8,128)S(1)} %shard_map.59), channel_id=1, source_target_pairs={{0,12},{4,0},{8,4},{12,8},{16,20},{20,24},{24,28},{28,16},{1,13},{... | collective-permute-start | bytes 221192 | tf_op jit(solution)/shard_map/ppermute | solution.py:51
  112.9 16.2 %all-to-all-start.3 = ((f32[16,1,128]{2,1,0:T(1,128)}), f32[16,1,128]{2,1,0:T(1,128)S(1)}, u32[]{:S(2)}, u32[]{:S(2)}) async-start(f32[16,1,128]{2,1,0:T(1,128)} %bitcast.14), calls=%async_computation.3 | async-start | bytes 16384 | tf_op jit(solution)/shard_map/all_to_all | solution.py:45

commit v10 on v9

--- a/solution.py
+++ b/solution.py
@@ -86,6 +86,15 @@
     return dot(left[1], right[0]) + dot(left[0], right[1]) + dot(left[0], right[0])
 
 
+def tie_kernel(*refs):
+    pass
+
+
+def after(values, other):
+    out = [shape(*values.shape)]
+    return call(tie_kernel, (values, other), out, [ANY] * 2, [ANY], input_output_aliases={0: 0})[0]
+
+
 def image_unit_kernel(image_ref, out):
     unit = normalize(image_ref[...])[0]
     for x in range(NX):
@@ -102,7 +111,7 @@
     return halves(jnp.concatenate([image_ref[pl.ds(start, rows), :] for start in starts], axis=0))
 
 
-def tile_kernel(place, image_ref, a_ref, b_ref, c_ref, d_ref, slope_out, other_out):
+def tile_kernel(place, image_ref, a_ref, b_ref, c_ref, d_ref, slope_out, other_out, loss_out):
     image = in_turn(place, image_ref)
     quarter = a_ref.shape[0]
     count = image_ref.shape[0]
@@ -122,7 +131,7 @@
         slope_out[:, pl.ds(k * quarter, quarter)] = slope
         if k >= 2:
             other_out[pl.ds((k - 2) * quarter, quarter), :] = dot3(halves(slope), image, ((0,), (0,)))
-    other_out[pl.ds(2 * quarter, 8), :] = jnp.full((8, FEATURES), total)
+    loss_out[...] = jnp.full(loss_out.shape, total)
 
 
 def image_kernel(slope_ref, a_ref, b_ref, c_ref, d_ref, *outs):
@@ -137,15 +146,12 @@
         out[...] = total[k * rows : (k + 1) * rows]
 
 
-def text_kernel(place, slope_ref, image_ref, other_ref, received_ref, x0, keep_out, send_out):
+def text_kernel(place, slope_ref, image_ref, received_ref, x0, loss_ref, keep_out, send_out):
     image = in_turn(place, image_ref)
-    quarter = keep_out.shape[0] - 8
-    last = pl.ds(2 * quarter, 8)
-    loss = other_ref[last, :] + received_ref[last, :]
+    quarter = keep_out.shape[0]
     for k, out in ((1, send_out), (0, keep_out)):
         rows = pl.ds(k * quarter, quarter)
-        out[pl.ds(0, quarter), :] = dot3(halves(slope_ref[:, rows]), image, ((0,), (0,))) + received_ref[rows, :]
-        out[pl.ds(quarter, 8), :] = loss
+        out[...] = dot3(halves(slope_ref[:, rows]), image, ((0,), (0,))) + received_ref[rows, :]
 
 
 def relay_kernel(left, right, out):
@@ -158,27 +164,13 @@
         out[...] = x0[rows, :] + (x1[rows, :] + x2[rows, :])
 
 
-def pack_kernel(keep_ref, plane_ref, relay_ref, ahead_ref, packed_out):
-    last, first = pl.ds(NY * ROWS, 8), pl.ds(0, LANES)
-    loss = keep_ref[last, first] + plane_ref[last, first]
+def pack_kernel(keep_ref, plane_ref, loss_ref, relay_ref, ahead_ref, packed_out):
     for y in range(NY):
         rows = pl.ds(y * ROWS, ROWS)
         for k in range(COLS):
             lanes = pl.ds(k * LANES, LANES)
             packed_out[y, pl.ds(k * ROWS, ROWS), :] = keep_ref[rows, lanes] + plane_ref[rows, lanes]
-        packed_out[y, pl.ds(PACK, 8), :] = loss
-
-
-def loss_kernel(packed_ref, out):
-    total = packed_ref[0, pl.ds(PACK, 8), :]
-    for y in range(1, NY):
-        total = total + packed_ref[y, pl.ds(PACK, 8), :]
-    for k in range(out.shape[0] // 8):
-        out[pl.ds(8 * k, 8), :] = total
-
-
-def mean_kernel(losses_ref, out):
-    out[0, 0] = jnp.sum(losses_ref[:, 0:1]) / PAIRS
+        packed_out[y, pl.ds(PACK, 8), :] = loss_ref[...]
 
 
 def image_grad_kernel(emb_ref, z0, z1, z2, out):
@@ -186,13 +178,14 @@
     out[...] = project_back(unit, z0[...] + (z1[...] + z2[...]), length)
 
 
-def text_grad_kernel(emb_ref, packed_ref, out):
+def text_grad_kernel(emb_ref, packed_ref, out, loss_out):
     unit, length = normalize(emb_ref[...])
     total = packed_ref[0]
     for y in range(1, NY):
         total = total + packed_ref[y]
     direction = jnp.concatenate([total[k * ROWS : (k + 1) * ROWS] for k in range(COLS)], axis=1)
     out[...] = project_back(unit, direction, length)
+    loss_out[0, 0] = jnp.max(total[PACK:]) / PAIRS
 
 
 def on_device(image_emb, text_emb):
@@ -213,34 +206,38 @@
     blocks = [(at + step) % NX for at in (x, zh) for step in (0, -turn, turn, 2)]
     place = jnp.stack([zh * rows, lax.axis_index("y") * rows, *blocks]).astype(jnp.int32)
     product = 2 * count * quarter * features * 3
-    slope, other = call(
+    slope, other, loss = call(
         tile_kernel,
         (place, image, *texts),
-        [shape(count, 4 * quarter), shape(2 * quarter + 8, features)],
+        [shape(count, 4 * quarter), shape(2 * quarter, features), shape(8, LANES)],
         in_specs=[SMEM] + [VMEM] * 5,
         flops=6 * product,
         vmem=20,
     )
+    sums = [loss]
+    for axis, step in (("zl", 1), ("zh", 1), ("zh", 2), ("x", 1), ("x", 2), ("c", 1)):
+        pairs = [(i, i ^ step) for i in range(lax.axis_size(axis))]
+        sums.append(sums[-1] + lax.ppermute(sums[-1], axis, pairs))
     received = other_core(other)
     xs = call(image_kernel, (slope, *texts), [shape(part, features)] * NX, flops=4 * product, vmem=20)
-    relay = turned(xs[3], "x", -1)
-    ahead = turned(xs[2], "x", 1)
+    relay = turned(after(xs[3], sums[2]), "x", -1)
+    ahead = turned(after(xs[2], sums[3]), "x", 1)
     keep, send = call(
         text_kernel,
-        (place, slope, image, other, received, xs[0]),
-        [shape(quarter + 8, features)] * 2,
-        in_specs=[SMEM] + [VMEM] * 4 + [ANY],
+        (place, slope, image, received, xs[0], sums[1]),
+        [shape(quarter, features)] * 2,
+        in_specs=[SMEM] + [VMEM] * 3 + [ANY] * 2,
         flops=2 * product,
         vmem=20,
     )
     plane = planes(send, 1)
-    (relay,) = call(relay_kernel, (xs[1], relay), [shape(part, features)])
+    (relay,) = call(relay_kernel, (xs[1], after(relay, sums[4])), [shape(part, features)])
     back = turned(relay, "x", -1)
     (packed,) = call(
         pack_kernel,
-        (keep, plane, relay, ahead),
+        (keep, plane, sums[-1], relay, ahead),
         [shape(NY, PACK + 8, LANES)],
-        in_specs=[VMEM] * 2 + [ANY] * 2,
+        in_specs=[VMEM] * 3 + [ANY] * 2,
     )
     zs = call(
         split_kernel,
@@ -254,10 +251,12 @@
     (relay,) = call(relay_kernel, (zs[1], relay), [shape(rows, features)])
     back = turned(relay, "zh", -1)
     (image_grad,) = call(image_grad_kernel, (image_emb, zs[0], back, ahead), [shape(rows, features)])
-    (loss,) = call(loss_kernel, (packed,), [shape(NZH * NX, LANES)])
-    losses = exchange(loss, ("zh", "x"))
-    (text_grad,) = call(text_grad_kernel, (text_emb, packed), [shape(rows, features)])
-    (loss,) = call(mean_kernel, (losses,), [shape(1, 1)], out_specs=[SMEM])
+    text_grad, loss = call(
+        text_grad_kernel,
+        (text_emb, packed),
+        [shape(rows, features), shape(1, 1)],
+        out_specs=[VMEM, SMEM],
+    )
     return loss.reshape(()), image_grad, text_grad
 
 

time: 130 us -> 146 us (1.12)
  the two profiles are of different devices: /device:TPU:72 before, /device:TPU:14 now
where the time goes in v10:
time: 146 us; the launch traced here: 145 us
  starting transfers between devices  76.7 us (53%)
  waiting for transfers between devices  32.2 us (22%)
  blocking collectives  20 us (14%)
  Pallas kernels  13.6 us (9%)
  local copies, waits for them, and re-layouts  1.86 us (1%)
    ppermute x6, starting transfers between devices, turned(): return lax.ppermute(values, ('c', axis), pairs)  23.6 us
    all_gather x1, blocking collectives, on_device(): image_z = lax.all_gather(image_emb, 'zh', axis=0, tiled=True)  20 us
    all_to_all x3, starting transfers between devices, exchange(): return lax.all_to_all(values, axes, 0, 0, tiled=True)  19.2 us
    ppermute x6, starting transfers between devices, on_device(): sums.append(sums[-1] + lax.ppermute(sums[-1], axis, pairs))  17.5 us
    ppermute x6, waiting for transfers between devices, on_device(): sums.append(sums[-1] + lax.ppermute(sums[-1], axis, pairs))  15.3 us
    pallas_call x14, Pallas kernels, call(): pl.pallas_call(kernel, out_shape=outs, in_specs=in_specs or [VMEM] * len(...  13.6 us
    ppermute x6, waiting for transfers between devices, turned(): return lax.ppermute(values, ('c', axis), pairs)  11.3 us
    ppermute x2, starting transfers between devices, planes(): return lax.ppermute(values, ('zl', 'c', 'zh'), pairs)  10.6 us
  transfers between devices with their start and end apart: 20, of which 11 were waited for; matrix products, arithmetic and copies ran while one was open for 0% of the time, Pallas kernels for 4%

profile of v10, /device:TPU:14, one launch (start us, length us, event | category | flops | bytes accessed | tf_op | source)
XLA Modules:
  0.0 145.4 jit_solution(15377874927458558106)
XLA Ops:
  2.4 7.5 %all-to-all-start.1 = ((f32[8,16,1152]{2,1,0:T(8,128)}), f32[8,16,1152]{2,1,0:T(8,128)S(1)}, u32[]{:S(2)}, u32[]{:S(2)}) async-start(f32[8,16,1152]{2,1,0:T(8,128)} %tile.2), calls=%async_computation.1 | async-start | bytes 1179648 | tf_op jit(solution)/shard_map/all_to_all | solution.py:45
  10.0 20.0 %all_gather.3.image_ref = f32[64,1152]{1,0:T(8,128)S(1)} all-gather(f32[16,1152]{1,0:T(8,128)S(1)} %copy-done), channel_id=1, replica_groups=mesh['y'=8,'zl'=2,'c'=2,'zh'=4,'x'=4] {'zh'}, dimensions={0}, use_global_device_ids=true | all-gather | bytes 368640 | tf_op jit(solution)/shard_map/all_gather | solution.py:194
  31.3 7.2 %collective-permute-start = (f32[128,1152]{1,0:T(8,128)S(1)}, f32[128,1152]{1,0:T(8,128)S(1)}, u32[]{:S(2)}, u32[]{:S(2)}) collective-permute-start(f32[128,1152]{1,0:T(8,128)S(1)} %shard_map.50.a_ref), channel_id=1, source_target_pairs={{0,44},{32,0},{4,32},{36,4},{8,36},{40,8},{12,40},{44,12},{16,48},... | collective-permute-start | bytes 1769480 | tf_op jit(solution)/shard_map/ppermute | solution.py:60
  38.5 4.8 %all-to-all-start = ((f32[4,64,1152]{2,1,0:T(8,128)}), f32[4,64,1152]{2,1,0:T(8,128)S(1)}, u32[]{:S(2)}, u32[]{:S(2)}) async-start(f32[4,64,1152]{2,1,0:T(8,128)} %bitcast.10), calls=%async_computation | async-start | bytes 2359296 | tf_op jit(solution)/shard_map/all_to_all | solution.py:45
  48.0 4.8 %all-to-all-done = f32[4,64,1152]{2,1,0:T(8,128)S(1)} async-done(((f32[4,64,1152]{2,1,0:T(8,128)}), f32[4,64,1152]{2,1,0:T(8,128)S(1)}, u32[]{:S(2)}, u32[]{:S(2)}) %all-to-all-start) | async-done | bytes 1179680 | tf_op jit(solution)/shard_map/all_to_all | solution.py:45
  52.8 4.7 %shard_map.51 = (f32[256,512]{1,0:T(8,128)S(1)}, f32[256,1152]{1,0:T(8,128)S(1)}, f32[8,128]{1,0:T(8,128)S(1)}) custom-call(s32[10]{0:T(128)S(1)} %stack.43.place, f32[256,1152]{1,0:T(8,128)S(1)} %bitcast.14, f32[128,1152]{1,0:T(8,128)S(1)} %shard_map.50.a_ref, f32[128,1152]{1,0:T(8,128)S(1)} %collective-permute-done.b_ref, ...), custom_call_target="tpu_custom_call" | custom-call | flops 1358954496 | bytes 5247016 | tf_op jit(solution)/shard_map/pallas_call | solution.py:33
  61.4 3.1 %shard_map.52 = (f32[64,1152]{1,0:T(8,128)S(1)}, f32[64,1152]{1,0:T(8,128)S(1)}, f32[64,1152]{1,0:T(8,128)S(1)}, f32[64,1152]{1,0:T(8,128)S(1)}) custom-call(f32[256,512]{1,0:T(8,128)S(1)} %get-tuple-element.18.slope_ref, f32[128,1152]{1,0:T(8,128)S(1)} %shard_map.50.a_ref, f32[128,1152]{1,0:T(8,128)S(1)} %collective-permute-done.b_ref, ...), custom_call_target="tpu_custom_call" | custom-call | flops 905969664 | bytes 4063232 | tf_op jit(solution)/shard_map/pallas_call | solution.py:33
  66.3 3.5 %collective-permute-start.5 = (f32[128,1152]{1,0:T(8,128)S(1)}, f32[128,1152]{1,0:T(8,128)S(1)}, u32[]{:S(2)}, u32[]{:S(2)}) collective-permute-start(f32[128,1152]{1,0:T(8,128)S(1)} %get-tuple-element.23), channel_id=1, source_target_pairs={{0,32},{32,4},{4,36},{36,8},{8,40},{40,12},{12,44},{44,0},{16,60},... | collective-permute-start | bytes 1769480 | tf_op jit(solution)/shard_map/ppermute | solution.py:60
  69.7 3.3 %collective-permute-start.6 = (f32[8,128]{1,0:T(8,128)S(1)}, f32[8,128]{1,0:T(8,128)S(1)}, u32[]{:S(2)}, u32[]{:S(2)}) collective-permute-start(f32[8,128]{1,0:T(8,128)S(1)} %add.75.loss_ref), channel_id=1, source_target_pairs={{0,4},{4,0},{8,12},{12,8},{1,5},{5,1},{9,13},{13,9},{2,6},{6,2},{1... | collective-permute-start | bytes 12296 | tf_op jit(solution)/shard_map/ppermute | solution.py:220
  73.1 4.1 %collective-permute-done.6 = f32[8,128]{1,0:T(8,128)S(1)} collective-permute-done((f32[8,128]{1,0:T(8,128)S(1)}, f32[8,128]{1,0:T(8,128)S(1)}, u32[]{:S(2)}, u32[]{:S(2)}) %collective-permute-start.6) | collective-permute-done | bytes 4128 | tf_op jit(solution)/shard_map/ppermute | solution.py:220
  77.2 5.2 %collective-permute-start.7 = (f32[8,128]{1,0:T(8,128)S(1)}, f32[8,128]{1,0:T(8,128)S(1)}, u32[]{:S(2)}, u32[]{:S(2)}) collective-permute-start(f32[8,128]{1,0:T(8,128)S(1)} %add.76.refs_1_), channel_id=1, source_target_pairs={{0,8},{4,12},{8,0},{12,4},{1,9},{5,13},{9,1},{13,5},{2,10},{6,14},... | collective-permute-start | bytes 12296 | tf_op jit(solution)/shard_map/ppermute | solution.py:220
  82.5 1.9 %collective-permute-start.11 = (f32[64,1152]{1,0:T(8,128)S(1)}, f32[64,1152]{1,0:T(8,128)S(1)}, u32[]{:S(2)}, u32[]{:S(2)}) collective-permute-start(f32[64,1152]{1,0:T(8,128)S(1)} %shard_map.54), channel_id=1, source_target_pairs={{0,3},{1,0},{2,1},{3,2},{16,17},{17,18},{18,19},{19,16},{4,7},{5,4... | collective-permute-start | bytes 884744 | tf_op jit(solution)/shard_map/ppermute | solution.py:51
  84.4 2.2 %collective-permute-done.7 = f32[8,128]{1,0:T(8,128)S(1)} collective-permute-done((f32[8,128]{1,0:T(8,128)S(1)}, f32[8,128]{1,0:T(8,128)S(1)}, u32[]{:S(2)}, u32[]{:S(2)}) %collective-permute-start.7) | collective-permute-done | bytes 4128 | tf_op jit(solution)/shard_map/ppermute | solution.py:220
  86.6 4.0 %collective-permute-start.12 = (f32[64,1152]{1,0:T(8,128)S(1)}, f32[64,1152]{1,0:T(8,128)S(1)}, u32[]{:S(2)}, u32[]{:S(2)}) collective-permute-start(f32[64,1152]{1,0:T(8,128)S(1)} %shard_map.57), channel_id=1, source_target_pairs={{0,1},{1,2},{2,3},{3,0},{16,19},{17,16},{18,17},{19,18},{4,5},{5,6... | collective-permute-start | bytes 884744 | tf_op jit(solution)/shard_map/ppermute | solution.py:51
  92.5 3.6 %collective-permute-done.8 = f32[8,128]{1,0:T(8,128)S(1)} collective-permute-done((f32[8,128]{1,0:T(8,128)S(1)}, f32[8,128]{1,0:T(8,128)S(1)}, u32[]{:S(2)}, u32[]{:S(2)}) %collective-permute-start.8) | collective-permute-done | bytes 4128 | tf_op jit(solution)/shard_map/ppermute | solution.py:220
  96.1 3.2 %collective-permute-start.9 = (f32[8,128]{1,0:T(8,128)S(1)}, f32[8,128]{1,0:T(8,128)S(1)}, u32[]{:S(2)}, u32[]{:S(2)}) collective-permute-start(f32[8,128]{1,0:T(8,128)S(1)} %add.78.refs_1_), channel_id=1, source_target_pairs={{0,2},{1,3},{2,0},{3,1},{4,6},{5,7},{6,4},{7,5},{8,10},{9,11},{10,... | collective-permute-start | bytes 12296 | tf_op jit(solution)/shard_map/ppermute | solution.py:220
  99.3 3.8 %collective-permute-done.9 = f32[8,128]{1,0:T(8,128)S(1)} collective-permute-done((f32[8,128]{1,0:T(8,128)S(1)}, f32[8,128]{1,0:T(8,128)S(1)}, u32[]{:S(2)}, u32[]{:S(2)}) %collective-permute-start.9) | collective-permute-done | bytes 4128 | tf_op jit(solution)/shard_map/ppermute | solution.py:220
  107.1 6.9 %all-to-all-start.2 = ((f32[8,152,128]{2,1,0:T(8,128)}), f32[8,152,128]{2,1,0:T(8,128)S(1)}, u32[]{:S(2)}, u32[]{:S(2)}) async-start(f32[8,152,128]{2,1,0:T(8,128)} %shard_map.58), calls=%async_computation.2 | async-start | bytes 1245184 | tf_op jit(solution)/shard_map/all_to_all | solution.py:45
  114.0 2.0 %collective-permute-start.13 = (f32[64,1152]{1,0:T(8,128)S(1)}, f32[64,1152]{1,0:T(8,128)S(1)}, u32[]{:S(2)}, u32[]{:S(2)}) collective-permute-start(f32[64,1152]{1,0:T(8,128)S(1)} %shard_map.56.relay_ref), channel_id=1, source_target_pairs={{0,3},{1,0},{2,1},{3,2},{16,17},{17,18},{18,19},{19,16},{4,7},{5,4... | collective-permute-start | bytes 884744 | tf_op jit(solution)/shard_map/ppermute | solution.py:51
  116.0 7.8 %collective-permute-done.13.x1 = f32[64,1152]{1,0:T(8,128)S(1)} collective-permute-done((f32[64,1152]{1,0:T(8,128)S(1)}, f32[64,1152]{1,0:T(8,128)S(1)}, u32[]{:S(2)}, u32[]{:S(2)}) %collective-permute-start.13) | collective-permute-done | bytes 294944 | tf_op jit(solution)/shard_map/ppermute | solution.py:51
  124.4 7.3 %collective-permute-start.14 = (f32[16,1152]{1,0:T(8,128)S(1)}, f32[16,1152]{1,0:T(8,128)S(1)}, u32[]{:S(2)}, u32[]{:S(2)}) collective-permute-start(f32[16,1152]{1,0:T(8,128)S(1)} %get-tuple-element.30), channel_id=1, source_target_pairs={{0,12},{4,0},{8,4},{12,8},{16,20},{20,24},{24,28},{28,16},{1,13},{... | collective-permute-start | bytes 221192 | tf_op jit(solution)/shard_map/ppermute | solution.py:51
  131.8 1.9 %collective-permute-start.16 = (f32[16,1152]{1,0:T(8,128)S(1)}, f32[16,1152]{1,0:T(8,128)S(1)}, u32[]{:S(2)}, u32[]{:S(2)}) collective-permute-start(f32[16,1152]{1,0:T(8,128)S(1)} %get-tuple-element.31), channel_id=1, source_target_pairs={{0,4},{4,8},{8,12},{12,0},{16,28},{20,16},{24,20},{28,24},{1,5},{5... | collective-permute-start | bytes 221192 | tf_op jit(solution)/shard_map/ppermute | solution.py:51
  135.1 6.5 %collective-permute-start.15 = (f32[16,1152]{1,0:T(8,128)S(1)}, f32[16,1152]{1,0:T(8,128)S(1)}, u32[]{:S(2)}, u32[]{:S(2)}) collective-permute-start(f32[16,1152]{1,0:T(8,128)S(1)} %shard_map.61), channel_id=1, source_target_pairs={{0,12},{4,0},{8,4},{12,8},{16,20},{20,24},{24,28},{28,16},{1,13},{... | collective-permute-start | bytes 221192 | tf_op jit(solution)/shard_map/ppermute | solution.py:51
  141.6 2.1 %collective-permute-done.15.z1 = f32[16,1152]{1,0:T(8,128)S(1)} collective-permute-done((f32[16,1152]{1,0:T(8,128)S(1)}, f32[16,1152]{1,0:T(8,128)S(1)}, u32[]{:S(2)}, u32[]{:S(2)}) %collective-permute-start.15) | collective-permute-done | bytes 73760 | tf_op jit(solution)/shard_map/ppermute | solution.py:51
  (43 shorter events, 23.0 us)
Async XLA Ops:
  0.6 9.3 %copy-start = (f32[16,1152]{1,0:T(8,128)S(1)}, f32[16,1152]{1,0:T(8,128)}, u32[]{:S(2)}) copy-start(f32[16,1152]{1,0:T(8,128)} %emb_ref.3) | copy-start | bytes 221188
  2.4 28.8 %all-to-all-start.1 = ((f32[8,16,1152]{2,1,0:T(8,128)}), f32[8,16,1152]{2,1,0:T(8,128)S(1)}, u32[]{:S(2)}, u32[]{:S(2)}) async-start(f32[8,16,1152]{2,1,0:T(8,128)} %tile.2), calls=%async_computation.1 | async-start | bytes 1179648 | tf_op jit(solution)/shard_map/all_to_all | solution.py:45
  31.3 14.5 %collective-permute-start = (f32[128,1152]{1,0:T(8,128)S(1)}, f32[128,1152]{1,0:T(8,128)S(1)}, u32[]{:S(2)}, u32[]{:S(2)}) collective-permute-start(f32[128,1152]{1,0:T(8,128)S(1)} %shard_map.50.a_ref), channel_id=1, source_target_pairs={{0,44},{32,0},{4,32},{36,4},{8,36},{40,8},{12,40},{44,12},{16,48},... | collective-permute-start | bytes 1769480 | tf_op jit(solution)/shard_map/ppermute | solution.py:60
  38.5 14.3 %all-to-all-start = ((f32[4,64,1152]{2,1,0:T(8,128)}), f32[4,64,1152]{2,1,0:T(8,128)S(1)}, u32[]{:S(2)}, u32[]{:S(2)}) async-start(f32[4,64,1152]{2,1,0:T(8,128)} %bitcast.10), calls=%async_computation | async-start | bytes 2359296 | tf_op jit(solution)/shard_map/all_to_all | solution.py:45
  43.3 9.5 %collective-permute-start.1 = (f32[128,1152]{1,0:T(8,128)S(1)}, f32[128,1152]{1,0:T(8,128)S(1)}, u32[]{:S(2)}, u32[]{:S(2)}) collective-permute-start(f32[128,1152]{1,0:T(8,128)S(1)} %shard_map.50.a_ref), channel_id=1, source_target_pairs={{0,16},{16,0},{1,17},{17,1},{2,18},{18,2},{3,19},{19,3},{4,20},{20... | collective-permute-start | bytes 1769480 | tf_op jit(solution)/shard_map/ppermute | solution.py:64
  45.9 6.9 %collective-permute-start.2 = (f32[128,1152]{1,0:T(8,128)S(1)}, f32[128,1152]{1,0:T(8,128)}, u32[]{:S(2)}, u32[]{:S(2)}) collective-permute-start(f32[128,1152]{1,0:T(8,128)S(1)} %collective-permute-done.b_ref), channel_id=1, source_target_pairs={{0,16},{16,0},{1,17},{17,1},{2,18},{18,2},{3,19},{19,3},{4,20},{20... | collective-permute-start | bytes 1769480 | tf_op jit(solution)/shard_map/ppermute | solution.py:64
  57.5 7.4 %collective-permute-start.3 = (f32[256,1152]{1,0:T(8,128)S(1)}, f32[256,1152]{1,0:T(8,128)S(1)}, u32[]{:S(2)}, u32[]{:S(2)}) collective-permute-start(f32[256,1152]{1,0:T(8,128)S(1)} %get-tuple-element.19), channel_id=1, source_target_pairs={{0,16},{16,0},{1,17},{17,1},{2,18},{18,2},{3,19},{19,3},{4,20},{20... | collective-permute-start | bytes 3538952 | tf_op jit(solution)/shard_map/ppermute | solution.py:64
  59.4 5.5 %collective-permute-start.4 = (f32[8,128]{1,0:T(8,128)S(1)}, f32[8,128]{1,0:T(8,128)S(1)}, u32[]{:S(2)}, u32[]{:S(2)}) collective-permute-start(f32[8,128]{1,0:T(8,128)S(1)} %get-tuple-element.21), channel_id=1, source_target_pairs={{0,32},{32,0},{1,33},{33,1},{2,34},{34,2},{3,35},{35,3},{4,36},{36... | collective-permute-start | bytes 12296 | tf_op jit(solution)/shard_map/ppermute | solution.py:220
  66.3 39.9 %collective-permute-start.5 = (f32[128,1152]{1,0:T(8,128)S(1)}, f32[128,1152]{1,0:T(8,128)S(1)}, u32[]{:S(2)}, u32[]{:S(2)}) collective-permute-start(f32[128,1152]{1,0:T(8,128)S(1)} %get-tuple-element.23), channel_id=1, source_target_pairs={{0,32},{32,4},{4,36},{36,8},{8,40},{40,12},{12,44},{44,0},{16,60},... | collective-permute-start | bytes 1769480 | tf_op jit(solution)/shard_map/ppermute | solution.py:60
  69.7 7.5 %collective-permute-start.6 = (f32[8,128]{1,0:T(8,128)S(1)}, f32[8,128]{1,0:T(8,128)S(1)}, u32[]{:S(2)}, u32[]{:S(2)}) collective-permute-start(f32[8,128]{1,0:T(8,128)S(1)} %add.75.loss_ref), channel_id=1, source_target_pairs={{0,4},{4,0},{8,12},{12,8},{1,5},{5,1},{9,13},{13,9},{2,6},{6,2},{1... | collective-permute-start | bytes 12296 | tf_op jit(solution)/shard_map/ppermute | solution.py:220
  77.2 9.4 %collective-permute-start.7 = (f32[8,128]{1,0:T(8,128)S(1)}, f32[8,128]{1,0:T(8,128)S(1)}, u32[]{:S(2)}, u32[]{:S(2)}) collective-permute-start(f32[8,128]{1,0:T(8,128)S(1)} %add.76.refs_1_), channel_id=1, source_target_pairs={{0,8},{4,12},{8,0},{12,4},{1,9},{5,13},{9,1},{13,5},{2,10},{6,14},... | collective-permute-start | bytes 12296 | tf_op jit(solution)/shard_map/ppermute | solution.py:220
  82.5 23.7 %collective-permute-start.11 = (f32[64,1152]{1,0:T(8,128)S(1)}, f32[64,1152]{1,0:T(8,128)S(1)}, u32[]{:S(2)}, u32[]{:S(2)}) collective-permute-start(f32[64,1152]{1,0:T(8,128)S(1)} %shard_map.54), channel_id=1, source_target_pairs={{0,3},{1,0},{2,1},{3,2},{16,17},{17,18},{18,19},{19,16},{4,7},{5,4... | collective-permute-start | bytes 884744 | tf_op jit(solution)/shard_map/ppermute | solution.py:51
  86.6 19.6 %collective-permute-start.12 = (f32[64,1152]{1,0:T(8,128)S(1)}, f32[64,1152]{1,0:T(8,128)S(1)}, u32[]{:S(2)}, u32[]{:S(2)}) collective-permute-start(f32[64,1152]{1,0:T(8,128)S(1)} %shard_map.57), channel_id=1, source_target_pairs={{0,1},{1,2},{2,3},{3,0},{16,19},{17,16},{18,17},{19,18},{4,5},{5,6... | collective-permute-start | bytes 884744 | tf_op jit(solution)/shard_map/ppermute | solution.py:51
  90.6 5.5 %collective-permute-start.8 = (f32[8,128]{1,0:T(8,128)S(1)}, f32[8,128]{1,0:T(8,128)S(1)}, u32[]{:S(2)}, u32[]{:S(2)}) collective-permute-start(f32[8,128]{1,0:T(8,128)S(1)} %add.77.refs_1_), channel_id=1, source_target_pairs={{0,1},{1,0},{2,3},{3,2},{4,5},{5,4},{6,7},{7,6},{8,9},{9,8},{10,11... | collective-permute-start | bytes 12296 | tf_op jit(solution)/shard_map/ppermute | solution.py:220
  96.1 7.0 %collective-permute-start.9 = (f32[8,128]{1,0:T(8,128)S(1)}, f32[8,128]{1,0:T(8,128)S(1)}, u32[]{:S(2)}, u32[]{:S(2)}) collective-permute-start(f32[8,128]{1,0:T(8,128)S(1)} %add.78.refs_1_), channel_id=1, source_target_pairs={{0,2},{1,3},{2,0},{3,1},{4,6},{5,7},{6,4},{7,5},{8,10},{9,11},{10,... | collective-permute-start | bytes 12296 | tf_op jit(solution)/shard_map/ppermute | solution.py:220
  103.1 3.0 %collective-permute-start.10 = (f32[8,128]{1,0:T(8,128)S(1)}, f32[8,128]{1,0:T(8,128)S(1)}, u32[]{:S(2)}, u32[]{:S(2)}) collective-permute-start(f32[8,128]{1,0:T(8,128)S(1)} %add.79), channel_id=1, source_target_pairs={{0,16},{16,0},{1,17},{17,1},{2,18},{18,2},{3,19},{19,3},{4,20},{20... | collective-permute-start | bytes 12296 | tf_op jit(solution)/shard_map/ppermute | solution.py:220
  107.1 37.4 %copy-start.1 = (f32[16,1152]{1,0:T(8,128)S(1)}, f32[16,1152]{1,0:T(8,128)}, u32[]{:S(2)}) copy-start(f32[16,1152]{1,0:T(8,128)} %emb_ref.2) | copy-start | bytes 221188
  107.1 37.4 %all-to-all-start.2 = ((f32[8,152,128]{2,1,0:T(8,128)}), f32[8,152,128]{2,1,0:T(8,128)S(1)}, u32[]{:S(2)}, u32[]{:S(2)}) async-start(f32[8,152,128]{2,1,0:T(8,128)} %shard_map.58), calls=%async_computation.2 | async-start | bytes 1245184 | tf_op jit(solution)/shard_map/all_to_all | solution.py:45
  114.0 9.8 %collective-permute-start.13 = (f32[64,1152]{1,0:T(8,128)S(1)}, f32[64,1152]{1,0:T(8,128)S(1)}, u32[]{:S(2)}, u32[]{:S(2)}) collective-permute-start(f32[64,1152]{1,0:T(8,128)S(1)} %shard_map.56.relay_ref), channel_id=1, source_target_pairs={{0,3},{1,0},{2,1},{3,2},{16,17},{17,18},{18,19},{19,16},{4,7},{5,4... | collective-permute-start | bytes 884744 | tf_op jit(solution)/shard_map/ppermute | solution.py:51
  124.4 10.6 %collective-permute-start.14 = (f32[16,1152]{1,0:T(8,128)S(1)}, f32[16,1152]{1,0:T(8,128)S(1)}, u32[]{:S(2)}, u32[]{:S(2)}) collective-permute-start(f32[16,1152]{1,0:T(8,128)S(1)} %get-tuple-element.30), channel_id=1, source_target_pairs={{0,12},{4,0},{8,4},{12,8},{16,20},{20,24},{24,28},{28,16},{1,13},{... | collective-permute-start | bytes 221192 | tf_op jit(solution)/shard_map/ppermute | solution.py:51
  131.8 9.8 %collective-permute-start.16 = (f32[16,1152]{1,0:T(8,128)S(1)}, f32[16,1152]{1,0:T(8,128)S(1)}, u32[]{:S(2)}, u32[]{:S(2)}) collective-permute-start(f32[16,1152]{1,0:T(8,128)S(1)} %get-tuple-element.31), channel_id=1, source_target_pairs={{0,4},{4,8},{8,12},{12,0},{16,28},{20,16},{24,20},{28,24},{1,5},{5... | collective-permute-start | bytes 221192 | tf_op jit(solution)/shard_map/ppermute | solution.py:51
  135.1 8.6 %collective-permute-start.15 = (f32[16,1152]{1,0:T(8,128)S(1)}, f32[16,1152]{1,0:T(8,128)S(1)}, u32[]{:S(2)}, u32[]{:S(2)}) collective-permute-start(f32[16,1152]{1,0:T(8,128)S(1)} %shard_map.61), channel_id=1, source_target_pairs={{0,12},{4,0},{8,4},{12,8},{16,20},{20,24},{24,28},{28,16},{1,13},{... | collective-permute-start | bytes 221192 | tf_op jit(solution)/shard_map/ppermute | solution.py:51

commit v11 on v9

--- a/solution.py
+++ b/solution.py
@@ -92,7 +92,7 @@
         out[pl.ds(x * NZH * ROWS, NZH * ROWS), :] = unit
 
 
-def text_unit_kernel(text_ref, image_units, out):
+def text_unit_kernel(text_ref, image_ref, out):
     out[...] = normalize(text_ref[...])[0]
 
 
@@ -158,7 +158,7 @@
         out[...] = x0[rows, :] + (x1[rows, :] + x2[rows, :])
 
 
-def pack_kernel(keep_ref, plane_ref, relay_ref, ahead_ref, packed_out):
+def pack_kernel(keep_ref, plane_ref, relay_ref, packed_out):
     last, first = pl.ds(NY * ROWS, 8), pl.ds(0, LANES)
     loss = keep_ref[last, first] + plane_ref[last, first]
     for y in range(NY):
@@ -201,7 +201,7 @@
     image_z = lax.all_gather(image_emb, "zh", axis=0, tiled=True)
     (image_tiled,) = call(image_unit_kernel, (image_z,), [shape(NX * NZH * rows, features)])
     (text_a,) = call(
-        text_unit_kernel, (text_y, image_tiled), [shape(*text_y.shape)], in_specs=[VMEM, ANY]
+        text_unit_kernel, (text_y, image_z), [shape(*text_y.shape)], in_specs=[VMEM, ANY]
     )
     image = exchange(image_tiled, "x")
     text_b = planes(text_a, -1)
@@ -234,14 +234,14 @@
         vmem=20,
     )
     plane = planes(send, 1)
+    (packed,) = call(
+        pack_kernel,
+        (keep, plane, relay),
+        [shape(NY, PACK + 8, LANES)],
+        in_specs=[VMEM] * 2 + [ANY],
+    )
     (relay,) = call(relay_kernel, (xs[1], relay), [shape(part, features)])
     back = turned(relay, "x", -1)
-    (packed,) = call(
-        pack_kernel,
-        (keep, plane, relay, ahead),
-        [shape(NY, PACK + 8, LANES)],
-        in_specs=[VMEM] * 2 + [ANY] * 2,
-    )
     zs = call(
         split_kernel,
         (place, xs[0], back, ahead),

time: 130 us -> 133 us (1.023)
  the two profiles are of different devices: /device:TPU:72 before, /device:TPU:8 now
where the time goes in v11:
time: 133 us; the launch traced here: 132 us
  starting transfers between devices  66.7 us (50%)
  waiting for transfers between devices  28.7 us (22%)
  blocking collectives  18.3 us (14%)
  Pallas kernels  15.2 us (11%)
  local copies, waits for them, and re-layouts  1.88 us (1%)
    all_to_all x4, starting transfers between devices, exchange(): return lax.all_to_all(values, axes, 0, 0, tiled=True)  26.3 us
    ppermute x6, starting transfers between devices, turned(): return lax.ppermute(values, ('c', axis), pairs)  23.9 us
    all_gather x1, blocking collectives, on_device(): image_z = lax.all_gather(image_emb, 'zh', axis=0, tiled=True)  18.3 us
    all_to_all x4, waiting for transfers between devices, exchange(): return lax.all_to_all(values, axes, 0, 0, tiled=True)  15.3 us
    pallas_call x13, Pallas kernels, call(): pl.pallas_call(kernel, out_shape=outs, in_specs=in_specs or [VMEM] * len(...  15.2 us
    ppermute x6, waiting for transfers between devices, turned(): return lax.ppermute(values, ('c', axis), pairs)  10.5 us
    ppermute x2, starting transfers between devices, planes(): return lax.ppermute(values, ('zl', 'c', 'zh'), pairs)  10.3 us
    ppermute x3, starting transfers between devices, other_core(): return lax.ppermute(values, 'c', [(0, 1), (1, 0)])  6.24 us
  transfers between devices with their start and end apart: 15, of which 7 were waited for; matrix products, arithmetic and copies ran while one was open for 0% of the time, Pallas kernels for 6%

profile of v11, /device:TPU:8, one launch (start us, length us, event | category | flops | bytes accessed | tf_op | source)
XLA Modules:
  0.0 131.7 jit_solution(15201761976576137899)
XLA Ops:
  0.6 1.8 %tile.2 = f32[8,16,1152]{2,1,0:T(8,128)} broadcast(f32[16,1152]{1,0:T(8,128)} %emb_ref.3), dimensions={1,2} | broadcast | bytes 663552 | tf_op jit(solution)/shard_map/tile | solution.py:200
  2.4 9.3 %all-to-all-start.1 = ((f32[8,16,1152]{2,1,0:T(8,128)}), f32[8,16,1152]{2,1,0:T(8,128)S(1)}, u32[]{:S(2)}, u32[]{:S(2)}) async-start(f32[8,16,1152]{2,1,0:T(8,128)} %tile.2), calls=%async_computation.1 | async-start | bytes 1179648 | tf_op jit(solution)/shard_map/all_to_all | solution.py:45
  11.7 18.3 %all_gather.3.image_ref = f32[64,1152]{1,0:T(8,128)S(1)} all-gather(f32[16,1152]{1,0:T(8,128)S(1)} %copy-done.1), channel_id=1, replica_groups=mesh['y'=8,'zl'=2,'c'=2,'zh'=4,'x'=4] {'zh'}, dimensions={0}, use_global_device_ids=true | all-gather | bytes 368640 | tf_op jit(solution)/shard_map/all_gather | solution.py:201
  30.2 8.4 %collective-permute-start = (f32[128,1152]{1,0:T(8,128)S(1)}, f32[128,1152]{1,0:T(8,128)S(1)}, u32[]{:S(2)}, u32[]{:S(2)}) collective-permute-start(f32[128,1152]{1,0:T(8,128)S(1)} %shard_map.50.a_ref), channel_id=1, source_target_pairs={{0,44},{32,0},{4,32},{36,4},{8,36},{40,8},{12,40},{44,12},{16,48},... | collective-permute-start | bytes 1769480 | tf_op jit(solution)/shard_map/ppermute | solution.py:60
  39.7 4.3 %all-to-all-start = ((f32[4,64,1152]{2,1,0:T(8,128)}), f32[4,64,1152]{2,1,0:T(8,128)S(1)}, u32[]{:S(2)}, u32[]{:S(2)}) async-start(f32[4,64,1152]{2,1,0:T(8,128)} %bitcast.10), calls=%async_computation | async-start | bytes 2359296 | tf_op jit(solution)/shard_map/all_to_all | solution.py:45
  44.0 1.9 %collective-permute-start.1 = (f32[128,1152]{1,0:T(8,128)S(1)}, f32[128,1152]{1,0:T(8,128)}, u32[]{:S(2)}, u32[]{:S(2)}) collective-permute-start(f32[128,1152]{1,0:T(8,128)S(1)} %shard_map.50.a_ref), channel_id=1, source_target_pairs={{0,16},{16,0},{1,17},{17,1},{2,18},{18,2},{3,19},{19,3},{4,20},{20... | collective-permute-start | bytes 1769480 | tf_op jit(solution)/shard_map/ppermute | solution.py:64
  45.9 2.4 %collective-permute-start.2 = (f32[128,1152]{1,0:T(8,128)S(1)}, f32[128,1152]{1,0:T(8,128)}, u32[]{:S(2)}, u32[]{:S(2)}) collective-permute-start(f32[128,1152]{1,0:T(8,128)S(1)} %collective-permute-done.b_ref), channel_id=1, source_target_pairs={{0,16},{16,0},{1,17},{17,1},{2,18},{18,2},{3,19},{19,3},{4,20},{20... | collective-permute-start | bytes 1769480 | tf_op jit(solution)/shard_map/ppermute | solution.py:64
  48.5 7.1 %all-to-all-done = f32[4,64,1152]{2,1,0:T(8,128)S(1)} async-done(((f32[4,64,1152]{2,1,0:T(8,128)}), f32[4,64,1152]{2,1,0:T(8,128)S(1)}, u32[]{:S(2)}, u32[]{:S(2)}) %all-to-all-start) | async-done | bytes 1179680 | tf_op jit(solution)/shard_map/all_to_all | solution.py:45
  55.6 4.8 %shard_map.51 = (f32[256,512]{1,0:T(8,128)S(1)}, f32[264,1152]{1,0:T(8,128)S(1)}) custom-call(s32[10]{0:T(128)S(1)} %stack.43.place, f32[256,1152]{1,0:T(8,128)S(1)} %bitcast.18, f32[128,1152]{1,0:T(8,128)S(1)} %shard_map.50.a_ref, f32[128,1152]{1,0:T(8,128)S(1)} %collective-permute-done.b_ref, f32[128,1152]{1,0:T(8,128)} %collective-permute-done.1.c_ref, ...), custom_call_target="tpu_custom_call" | custom-call | flops 1358954496 | bytes 5279784 | tf_op jit(solution)/shard_map/pallas_call | solution.py:33
  60.5 1.9 %collective-permute-start.3 = (f32[264,1152]{1,0:T(8,128)S(1)}, f32[264,1152]{1,0:T(8,128)S(1)}, u32[]{:S(2)}, u32[]{:S(2)}) collective-permute-start(f32[264,1152]{1,0:T(8,128)S(1)} %get-tuple-element.16.other_ref), channel_id=1, source_target_pairs={{0,16},{16,0},{1,17},{17,1},{2,18},{18,2},{3,19},{19,3},{4,20},{20... | collective-permute-start | bytes 3649544 | tf_op jit(solution)/shard_map/ppermute | solution.py:64
  62.4 3.2 %shard_map.52 = (f32[64,1152]{1,0:T(8,128)S(1)}, f32[64,1152]{1,0:T(8,128)S(1)}, f32[64,1152]{1,0:T(8,128)S(1)}, f32[64,1152]{1,0:T(8,128)S(1)}) custom-call(f32[256,512]{1,0:T(8,128)S(1)} %get-tuple-element.15.slope_ref, f32[128,1152]{1,0:T(8,128)S(1)} %shard_map.50.a_ref, f32[128,1152]{1,0:T(8,128)S(1)} %collective-permute-done.b_ref, ...), custom_call_target="tpu_custom_call" | custom-call | flops 905969664 | bytes 4063232 | tf_op jit(solution)/shard_map/pallas_call | solution.py:33
  67.0 1.9 %collective-permute-start.4 = (f32[136,1152]{1,0:T(8,128)S(1)}, f32[136,1152]{1,0:T(8,128)S(1)}, u32[]{:S(2)}, u32[]{:S(2)}) collective-permute-start(f32[136,1152]{1,0:T(8,128)S(1)} %get-tuple-element.19), channel_id=1, source_target_pairs={{0,32},{32,4},{4,36},{36,8},{8,40},{40,12},{12,44},{44,0},{16,60},... | collective-permute-start | bytes 1880072 | tf_op jit(solution)/shard_map/ppermute | solution.py:60
  68.9 3.1 %collective-permute-start.5 = (f32[64,1152]{1,0:T(8,128)S(1)}, f32[64,1152]{1,0:T(8,128)S(1)}, u32[]{:S(2)}, u32[]{:S(2)}) collective-permute-start(f32[64,1152]{1,0:T(8,128)S(1)} %get-tuple-element.20), channel_id=1, source_target_pairs={{0,3},{1,0},{2,1},{3,2},{16,17},{17,18},{18,19},{19,16},{4,7},{5,4... | collective-permute-start | bytes 884744 | tf_op jit(solution)/shard_map/ppermute | solution.py:51
  72.0 5.5 %collective-permute-done.5.relay_ref.right = f32[64,1152]{1,0:T(8,128)S(1)} collective-permute-done((f32[64,1152]{1,0:T(8,128)S(1)}, f32[64,1152]{1,0:T(8,128)S(1)}, u32[]{:S(2)}, u32[]{:S(2)}) %collective-permute-start.5) | collective-permute-done | bytes 294944 | tf_op jit(solution)/shard_map/ppermute | solution.py:51
  77.5 2.8 %collective-permute-done.4.plane_ref = f32[136,1152]{1,0:T(8,128)S(1)} collective-permute-done((f32[136,1152]{1,0:T(8,128)S(1)}, f32[136,1152]{1,0:T(8,128)S(1)}, u32[]{:S(2)}, u32[]{:S(2)}) %collective-permute-start.4) | collective-permute-done | bytes 626720 | tf_op jit(solution)/shard_map/ppermute | solution.py:60
  81.3 6.8 %all-to-all-start.2 = ((f32[8,152,128]{2,1,0:T(8,128)}), f32[8,152,128]{2,1,0:T(8,128)S(1)}, u32[]{:S(2)}, u32[]{:S(2)}) async-start(f32[8,152,128]{2,1,0:T(8,128)} %shard_map.54), calls=%async_computation.2 | async-start | bytes 1245184 | tf_op jit(solution)/shard_map/all_to_all | solution.py:45
  88.1 2.5 %collective-permute-start.7 = (f32[64,1152]{1,0:T(8,128)S(1)}, f32[64,1152]{1,0:T(8,128)S(1)}, u32[]{:S(2)}, u32[]{:S(2)}) collective-permute-start(f32[64,1152]{1,0:T(8,128)S(1)} %get-tuple-element.22), channel_id=1, source_target_pairs={{0,1},{1,2},{2,3},{3,0},{16,19},{17,16},{18,17},{19,18},{4,5},{5,6... | collective-permute-start | bytes 884744 | tf_op jit(solution)/shard_map/ppermute | solution.py:51
  90.6 4.7 %collective-permute-start.6 = (f32[64,1152]{1,0:T(8,128)S(1)}, f32[64,1152]{1,0:T(8,128)S(1)}, u32[]{:S(2)}, u32[]{:S(2)}) collective-permute-start(f32[64,1152]{1,0:T(8,128)S(1)} %shard_map.57), channel_id=1, source_target_pairs={{0,3},{1,0},{2,1},{3,2},{16,17},{17,18},{18,19},{19,16},{4,7},{5,4... | collective-permute-start | bytes 884744 | tf_op jit(solution)/shard_map/ppermute | solution.py:51
  95.3 4.1 %collective-permute-done.7.x2 = f32[64,1152]{1,0:T(8,128)S(1)} collective-permute-done((f32[64,1152]{1,0:T(8,128)S(1)}, f32[64,1152]{1,0:T(8,128)S(1)}, u32[]{:S(2)}, u32[]{:S(2)}) %collective-permute-start.7) | collective-permute-done | bytes 294944 | tf_op jit(solution)/shard_map/ppermute | solution.py:51
  100.2 5.2 %collective-permute-start.8 = (f32[16,1152]{1,0:T(8,128)S(1)}, f32[16,1152]{1,0:T(8,128)S(1)}, u32[]{:S(2)}, u32[]{:S(2)}) collective-permute-start(f32[16,1152]{1,0:T(8,128)S(1)} %get-tuple-element.25), channel_id=1, source_target_pairs={{0,12},{4,0},{8,4},{12,8},{16,20},{20,24},{24,28},{28,16},{1,13},{... | collective-permute-start | bytes 221192 | tf_op jit(solution)/shard_map/ppermute | solution.py:51
  105.3 1.9 %collective-permute-start.10 = (f32[16,1152]{1,0:T(8,128)S(1)}, f32[16,1152]{1,0:T(8,128)S(1)}, u32[]{:S(2)}, u32[]{:S(2)}) collective-permute-start(f32[16,1152]{1,0:T(8,128)S(1)} %get-tuple-element.26), channel_id=1, source_target_pairs={{0,4},{4,8},{8,12},{12,0},{16,28},{20,16},{24,20},{28,24},{1,5},{5... | collective-permute-start | bytes 221192 | tf_op jit(solution)/shard_map/ppermute | solution.py:51
  108.0 6.6 %collective-permute-start.9 = (f32[16,1152]{1,0:T(8,128)S(1)}, f32[16,1152]{1,0:T(8,128)S(1)}, u32[]{:S(2)}, u32[]{:S(2)}) collective-permute-start(f32[16,1152]{1,0:T(8,128)S(1)} %shard_map.59), channel_id=1, source_target_pairs={{0,12},{4,0},{8,4},{12,8},{16,20},{20,24},{24,28},{28,16},{1,13},{... | collective-permute-start | bytes 221192 | tf_op jit(solution)/shard_map/ppermute | solution.py:51
  115.2 5.9 %all-to-all-start.3 = ((f32[16,1,128]{2,1,0:T(1,128)}), f32[16,1,128]{2,1,0:T(1,128)S(1)}, u32[]{:S(2)}, u32[]{:S(2)}) async-start(f32[16,1,128]{2,1,0:T(1,128)} %bitcast.14), calls=%async_computation.3 | async-start | bytes 16384 | tf_op jit(solution)/shard_map/all_to_all | solution.py:45
  122.8 8.3 %all-to-all-done.3 = f32[16,1,128]{2,1,0:T(1,128)S(1)} async-done(((f32[16,1,128]{2,1,0:T(1,128)}), f32[16,1,128]{2,1,0:T(1,128)S(1)}, u32[]{:S(2)}, u32[]{:S(2)}) %all-to-all-start.3) | async-done | bytes 8224 | tf_op jit(solution)/shard_map/all_to_all | solution.py:45
  (26 shorter events, 8.1 us)
Async XLA Ops:
  0.6 11.1 %copy-start.1 = (f32[16,1152]{1,0:T(8,128)S(1)}, f32[16,1152]{1,0:T(8,128)}, u32[]{:S(2)}) copy-start(f32[16,1152]{1,0:T(8,128)} %emb_ref.2) | copy-start | bytes 221188
  2.4 27.6 %all-to-all-start.1 = ((f32[8,16,1152]{2,1,0:T(8,128)}), f32[8,16,1152]{2,1,0:T(8,128)S(1)}, u32[]{:S(2)}, u32[]{:S(2)}) async-start(f32[8,16,1152]{2,1,0:T(8,128)} %tile.2), calls=%async_computation.1 | async-start | bytes 1179648 | tf_op jit(solution)/shard_map/all_to_all | solution.py:45
  30.2 15.8 %collective-permute-start = (f32[128,1152]{1,0:T(8,128)S(1)}, f32[128,1152]{1,0:T(8,128)S(1)}, u32[]{:S(2)}, u32[]{:S(2)}) collective-permute-start(f32[128,1152]{1,0:T(8,128)S(1)} %shard_map.50.a_ref), channel_id=1, source_target_pairs={{0,44},{32,0},{4,32},{36,4},{8,36},{40,8},{12,40},{44,12},{16,48},... | collective-permute-start | bytes 1769480 | tf_op jit(solution)/shard_map/ppermute | solution.py:60
  39.7 15.9 %all-to-all-start = ((f32[4,64,1152]{2,1,0:T(8,128)}), f32[4,64,1152]{2,1,0:T(8,128)S(1)}, u32[]{:S(2)}, u32[]{:S(2)}) async-start(f32[4,64,1152]{2,1,0:T(8,128)} %bitcast.10), calls=%async_computation | async-start | bytes 2359296 | tf_op jit(solution)/shard_map/all_to_all | solution.py:45
  44.0 11.6 %collective-permute-start.1 = (f32[128,1152]{1,0:T(8,128)S(1)}, f32[128,1152]{1,0:T(8,128)}, u32[]{:S(2)}, u32[]{:S(2)}) collective-permute-start(f32[128,1152]{1,0:T(8,128)S(1)} %shard_map.50.a_ref), channel_id=1, source_target_pairs={{0,16},{16,0},{1,17},{17,1},{2,18},{18,2},{3,19},{19,3},{4,20},{20... | collective-permute-start | bytes 1769480 | tf_op jit(solution)/shard_map/ppermute | solution.py:64
  45.9 9.7 %collective-permute-start.2 = (f32[128,1152]{1,0:T(8,128)S(1)}, f32[128,1152]{1,0:T(8,128)}, u32[]{:S(2)}, u32[]{:S(2)}) collective-permute-start(f32[128,1152]{1,0:T(8,128)S(1)} %collective-permute-done.b_ref), channel_id=1, source_target_pairs={{0,16},{16,0},{1,17},{17,1},{2,18},{18,2},{3,19},{19,3},{4,20},{20... | collective-permute-start | bytes 1769480 | tf_op jit(solution)/shard_map/ppermute | solution.py:64
  60.5 5.2 %collective-permute-start.3 = (f32[264,1152]{1,0:T(8,128)S(1)}, f32[264,1152]{1,0:T(8,128)S(1)}, u32[]{:S(2)}, u32[]{:S(2)}) collective-permute-start(f32[264,1152]{1,0:T(8,128)S(1)} %get-tuple-element.16.other_ref), channel_id=1, source_target_pairs={{0,16},{16,0},{1,17},{17,1},{2,18},{18,2},{3,19},{19,3},{4,20},{20... | collective-permute-start | bytes 3649544 | tf_op jit(solution)/shard_map/ppermute | solution.py:64
  67.0 13.4 %collective-permute-start.4 = (f32[136,1152]{1,0:T(8,128)S(1)}, f32[136,1152]{1,0:T(8,128)S(1)}, u32[]{:S(2)}, u32[]{:S(2)}) collective-permute-start(f32[136,1152]{1,0:T(8,128)S(1)} %get-tuple-element.19), channel_id=1, source_target_pairs={{0,32},{32,4},{4,36},{36,8},{8,40},{40,12},{12,44},{44,0},{16,60},... | collective-permute-start | bytes 1880072 | tf_op jit(solution)/shard_map/ppermute | solution.py:60
  68.9 8.6 %collective-permute-start.5 = (f32[64,1152]{1,0:T(8,128)S(1)}, f32[64,1152]{1,0:T(8,128)S(1)}, u32[]{:S(2)}, u32[]{:S(2)}) collective-permute-start(f32[64,1152]{1,0:T(8,128)S(1)} %get-tuple-element.20), channel_id=1, source_target_pairs={{0,3},{1,0},{2,1},{3,2},{16,17},{17,18},{18,19},{19,16},{4,7},{5,4... | collective-permute-start | bytes 884744 | tf_op jit(solution)/shard_map/ppermute | solution.py:51
  81.3 33.3 %all-to-all-start.2 = ((f32[8,152,128]{2,1,0:T(8,128)}), f32[8,152,128]{2,1,0:T(8,128)S(1)}, u32[]{:S(2)}, u32[]{:S(2)}) async-start(f32[8,152,128]{2,1,0:T(8,128)} %shard_map.54), calls=%async_computation.2 | async-start | bytes 1245184 | tf_op jit(solution)/shard_map/all_to_all | solution.py:45
  88.1 11.4 %collective-permute-start.7 = (f32[64,1152]{1,0:T(8,128)S(1)}, f32[64,1152]{1,0:T(8,128)S(1)}, u32[]{:S(2)}, u32[]{:S(2)}) collective-permute-start(f32[64,1152]{1,0:T(8,128)S(1)} %get-tuple-element.22), channel_id=1, source_target_pairs={{0,1},{1,2},{2,3},{3,0},{16,19},{17,16},{18,17},{19,18},{4,5},{5,6... | collective-permute-start | bytes 884744 | tf_op jit(solution)/shard_map/ppermute | solution.py:51
  90.6 31.4 %copy-start = (f32[16,1152]{1,0:T(8,128)S(1)}, f32[16,1152]{1,0:T(8,128)}, u32[]{:S(2)}) copy-start(f32[16,1152]{1,0:T(8,128)} %emb_ref.3) | copy-start | bytes 221188
  90.6 8.9 %collective-permute-start.6 = (f32[64,1152]{1,0:T(8,128)S(1)}, f32[64,1152]{1,0:T(8,128)S(1)}, u32[]{:S(2)}, u32[]{:S(2)}) collective-permute-start(f32[64,1152]{1,0:T(8,128)S(1)} %shard_map.57), channel_id=1, source_target_pairs={{0,3},{1,0},{2,1},{3,2},{16,17},{17,18},{18,19},{19,16},{4,7},{5,4... | collective-permute-start | bytes 884744 | tf_op jit(solution)/shard_map/ppermute | solution.py:51
  100.2 7.8 %collective-permute-start.8 = (f32[16,1152]{1,0:T(8,128)S(1)}, f32[16,1152]{1,0:T(8,128)S(1)}, u32[]{:S(2)}, u32[]{:S(2)}) collective-permute-start(f32[16,1152]{1,0:T(8,128)S(1)} %get-tuple-element.25), channel_id=1, source_target_pairs={{0,12},{4,0},{8,4},{12,8},{16,20},{20,24},{24,28},{28,16},{1,13},{... | collective-permute-start | bytes 221192 | tf_op jit(solution)/shard_map/ppermute | solution.py:51
  105.3 15.8 %collective-permute-start.10 = (f32[16,1152]{1,0:T(8,128)S(1)}, f32[16,1152]{1,0:T(8,128)S(1)}, u32[]{:S(2)}, u32[]{:S(2)}) collective-permute-start(f32[16,1152]{1,0:T(8,128)S(1)} %get-tuple-element.26), channel_id=1, source_target_pairs={{0,4},{4,8},{8,12},{12,0},{16,28},{20,16},{24,20},{28,24},{1,5},{5... | collective-permute-start | bytes 221192 | tf_op jit(solution)/shard_map/ppermute | solution.py:51
  108.0 13.2 %collective-permute-start.9 = (f32[16,1152]{1,0:T(8,128)S(1)}, f32[16,1152]{1,0:T(8,128)S(1)}, u32[]{:S(2)}, u32[]{:S(2)}) collective-permute-start(f32[16,1152]{1,0:T(8,128)S(1)} %shard_map.59), channel_id=1, source_target_pairs={{0,12},{4,0},{8,4},{12,8},{16,20},{20,24},{24,28},{28,16},{1,13},{... | collective-permute-start | bytes 221192 | tf_op jit(solution)/shard_map/ppermute | solution.py:51
  115.2 15.9 %all-to-all-start.3 = ((f32[16,1,128]{2,1,0:T(1,128)}), f32[16,1,128]{2,1,0:T(1,128)S(1)}, u32[]{:S(2)}, u32[]{:S(2)}) async-start(f32[16,1,128]{2,1,0:T(1,128)} %bitcast.14), calls=%async_computation.3 | async-start | bytes 16384 | tf_op jit(solution)/shard_map/all_to_all | solution.py:45

commit v12 on v11

--- a/solution.py
+++ b/solution.py
@@ -45,12 +45,6 @@
     return lax.all_to_all(values, axes, 0, 0, tiled=True)
 
 
-def turned(values, axis, step):
-    count = lax.axis_size(axis)
-    pairs = [(c * count + i, c * count + (i + (1 - 2 * c) * step) % count) for c in range(2) for i in range(count)]
-    return lax.ppermute(values, ("c", axis), pairs)
-
-
 def planes(values, step):
     pairs = []
     for c in range(2):
@@ -96,14 +90,8 @@
     out[...] = normalize(text_ref[...])[0]
 
 
-def in_turn(place, image_ref):
-    rows = image_ref.shape[0] // NX
-    starts = [pl.multiple_of(place[2 + k] * rows, rows) for k in range(NX)]
-    return halves(jnp.concatenate([image_ref[pl.ds(start, rows), :] for start in starts], axis=0))
-
-
 def tile_kernel(place, image_ref, a_ref, b_ref, c_ref, d_ref, slope_out, other_out):
-    image = in_turn(place, image_ref)
+    image = halves(image_ref[...])
     quarter = a_ref.shape[0]
     count = image_ref.shape[0]
     row = lax.broadcasted_iota(jnp.int32, (count, quarter), 0) - place[0]
@@ -125,20 +113,18 @@
     other_out[pl.ds(2 * quarter, 8), :] = jnp.full((8, FEATURES), total)
 
 
-def image_kernel(slope_ref, a_ref, b_ref, c_ref, d_ref, *outs):
+def image_kernel(slope_ref, a_ref, b_ref, c_ref, d_ref, out):
     quarter = a_ref.shape[0]
     total = None
     for k, ref in enumerate((a_ref, b_ref, c_ref, d_ref)):
         slope = slope_ref[:, pl.ds(k * quarter, quarter)]
         term = dot3(halves(slope), halves(ref[...]), ((1,), (0,)))
         total = term if total is None else total + term
-    rows = total.shape[0] // NX
-    for k, out in enumerate(outs):
-        out[...] = total[k * rows : (k + 1) * rows]
-
-
-def text_kernel(place, slope_ref, image_ref, other_ref, received_ref, x0, keep_out, send_out):
-    image = in_turn(place, image_ref)
+    out[...] = total
+
+
+def text_kernel(slope_ref, image_ref, other_ref, received_ref, x0, keep_out, send_out):
+    image = halves(image_ref[...])
     quarter = keep_out.shape[0] - 8
     last = pl.ds(2 * quarter, 8)
     loss = other_ref[last, :] + received_ref[last, :]
@@ -148,17 +134,13 @@
         out[pl.ds(quarter, 8), :] = loss
 
 
-def relay_kernel(left, right, out):
-    out[...] = left[...] + right[...]
-
-
-def split_kernel(place, x0, x1, x2, *outs):
-    for k, out in enumerate(outs):
-        rows = pl.ds(pl.multiple_of(place[2 + NX + k] * ROWS, ROWS), ROWS)
-        out[...] = x0[rows, :] + (x1[rows, :] + x2[rows, :])
-
-
-def pack_kernel(keep_ref, plane_ref, relay_ref, packed_out):
+def sum_kernel(parts_ref, out):
+    rows = out.shape[0]
+    parts = [parts_ref[pl.ds(x * rows, rows), :] for x in range(NX)]
+    out[...] = (parts[0] + parts[1]) + (parts[2] + parts[3])
+
+
+def pack_kernel(keep_ref, plane_ref, image_ref, packed_out):
     last, first = pl.ds(NY * ROWS, 8), pl.ds(0, LANES)
     loss = keep_ref[last, first] + plane_ref[last, first]
     for y in range(NY):
@@ -181,9 +163,9 @@
     out[0, 0] = jnp.sum(losses_ref[:, 0:1]) / PAIRS
 
 
-def image_grad_kernel(emb_ref, z0, z1, z2, out):
+def image_grad_kernel(emb_ref, direction_ref, out):
     unit, length = normalize(emb_ref[...])
-    out[...] = project_back(unit, z0[...] + (z1[...] + z2[...]), length)
+    out[...] = project_back(unit, direction_ref[...], length)
 
 
 def text_grad_kernel(emb_ref, packed_ref, out):
@@ -208,10 +190,8 @@
     texts = (text_a, text_b, other_core(text_a), other_core(text_b))
 
     count, quarter = image.shape[0], text_a.shape[0]
-    part = count // NX
-    x, zh, turn = lax.axis_index("x"), lax.axis_index("zh"), 1 - 2 * lax.axis_index("c")
-    blocks = [(at + step) % NX for at in (x, zh) for step in (0, -turn, turn, 2)]
-    place = jnp.stack([zh * rows, lax.axis_index("y") * rows, *blocks]).astype(jnp.int32)
+    own = (lax.axis_index("x") * NZH + lax.axis_index("zh")) * rows
+    place = jnp.stack([own, lax.axis_index("y") * rows]).astype(jnp.int32)
     product = 2 * count * quarter * features * 3
     slope, other = call(
         tile_kernel,
@@ -222,38 +202,27 @@
         vmem=20,
     )
     received = other_core(other)
-    xs = call(image_kernel, (slope, *texts), [shape(part, features)] * NX, flops=4 * product, vmem=20)
-    relay = turned(xs[3], "x", -1)
-    ahead = turned(xs[2], "x", 1)
+    (image_sums,) = call(image_kernel, (slope, *texts), [shape(count, features)], flops=4 * product, vmem=20)
     keep, send = call(
         text_kernel,
-        (place, slope, image, other, received, xs[0]),
+        (slope, image, other, received, image_sums),
         [shape(quarter + 8, features)] * 2,
-        in_specs=[SMEM] + [VMEM] * 4 + [ANY],
+        in_specs=[VMEM] * 4 + [ANY],
         flops=2 * product,
         vmem=20,
     )
     plane = planes(send, 1)
+    image_parts = exchange(image_sums, "x")
+    (image_x,) = call(sum_kernel, (image_parts,), [shape(count // NX, features)])
+    image_dir = lax.psum_scatter(image_x, "zh", scatter_dimension=0, tiled=True)
     (packed,) = call(
         pack_kernel,
-        (keep, plane, relay),
+        (keep, plane, image_x),
         [shape(NY, PACK + 8, LANES)],
         in_specs=[VMEM] * 2 + [ANY],
     )
-    (relay,) = call(relay_kernel, (xs[1], relay), [shape(part, features)])
-    back = turned(relay, "x", -1)
-    zs = call(
-        split_kernel,
-        (place, xs[0], back, ahead),
-        [shape(rows, features)] * NZH,
-        in_specs=[SMEM] + [VMEM] * 3,
-    )
     packed = exchange(packed, "y")
-    relay = turned(zs[3], "zh", -1)
-    ahead = turned(zs[2], "zh", 1)
-    (relay,) = call(relay_kernel, (zs[1], relay), [shape(rows, features)])
-    back = turned(relay, "zh", -1)
-    (image_grad,) = call(image_grad_kernel, (image_emb, zs[0], back, ahead), [shape(rows, features)])
+    (image_grad,) = call(image_grad_kernel, (image_emb, image_dir), [shape(rows, features)])
     (loss,) = call(loss_kernel, (packed,), [shape(NZH * NX, LANES)])
     losses = exchange(loss, ("zh", "x"))
     (text_grad,) = call(text_grad_kernel, (text_emb, packed), [shape(rows, features)])

time: 133 us -> 150 us (1.13)
  the two profiles are of different devices: /device:TPU:8 before, /device:TPU:1 now
where the time goes in v12:
time: 150 us; the launch traced here: 149 us
  starting transfers between devices  58.4 us (39%)
  waiting for transfers between devices  34.1 us (23%)
  Pallas kernels  18.9 us (13%)
  blocking collectives  18 us (12%)
  between operations  14.2 us (9%)
  local copies, waits for them, and re-layouts  5.46 us (4%)
    all_to_all x5, waiting for transfers between devices, exchange(): return lax.all_to_all(values, axes, 0, 0, tiled=True)  27.6 us
    all_to_all x5, starting transfers between devices, exchange(): return lax.all_to_all(values, axes, 0, 0, tiled=True)  26.2 us
    ppermute x3, starting transfers between devices, other_core(): return lax.ppermute(values, 'c', [(0, 1), (1, 0)])  19.9 us
    pallas_call x11, Pallas kernels, call(): pl.pallas_call(kernel, out_shape=outs, in_specs=in_specs or [VMEM] * len(...  18.9 us
    all_gather x1, blocking collectives, on_device(): image_z = lax.all_gather(image_emb, 'zh', axis=0, tiled=True)  18 us
    ppermute x2, starting transfers between devices, planes(): return lax.ppermute(values, ('zl', 'c', 'zh'), pairs)  12.2 us
    unnamed x16, local copies, waits for them, and re-layouts  3.66 us
    reduce_scatter x1, waiting for transfers between devices, on_device(): image_dir = lax.psum_scatter(image_x, 'zh', scatter_dimension=0, tiled=True)  3.62 us
  transfers between devices with their start and end apart: 11, of which 6 were waited for; matrix products, arithmetic and copies ran while one was open for 0% of the time, Pallas kernels for 8%

profile of v12, /device:TPU:1, one launch (start us, length us, event | category | flops | bytes accessed | tf_op | source)
XLA Modules:
  0.0 149.1 jit_solution(12094711380946950730)
XLA Ops:
  7.2 1.8 %tile.2 = f32[8,16,1152]{2,1,0:T(8,128)} broadcast(f32[16,1152]{1,0:T(8,128)} %emb_ref.3), dimensions={1,2} | broadcast | bytes 663552 | tf_op jit(solution)/shard_map/tile | solution.py:182
  9.0 7.7 %all-to-all-start.1 = ((f32[8,16,1152]{2,1,0:T(8,128)}), f32[8,16,1152]{2,1,0:T(8,128)S(1)}, u32[]{:S(2)}, u32[]{:S(2)}) async-start(f32[8,16,1152]{2,1,0:T(8,128)} %tile.2), calls=%async_computation.1 | async-start | bytes 1179648 | tf_op jit(solution)/shard_map/all_to_all | solution.py:45
  16.6 18.0 %all_gather.3.image_ref = f32[64,1152]{1,0:T(8,128)S(1)} all-gather(f32[16,1152]{1,0:T(8,128)S(1)} %copy-done.5), channel_id=1, replica_groups=mesh['y'=8,'zl'=2,'c'=2,'zh'=4,'x'=4] {'zh'}, dimensions={0}, use_global_device_ids=true | all-gather | bytes 368640 | tf_op jit(solution)/shard_map/all_gather | solution.py:183
  34.7 5.4 %collective-permute-start = (f32[128,1152]{1,0:T(8,128)S(1)}, f32[128,1152]{1,0:T(8,128)S(1)}, u32[]{:S(2)}, u32[]{:S(2)}) collective-permute-start(f32[128,1152]{1,0:T(8,128)S(1)} %shard_map.50.a_ref), channel_id=1, source_target_pairs={{0,44},{32,0},{4,32},{36,4},{8,36},{40,8},{12,40},{44,12},{16,48},... | collective-permute-start | bytes 1769480 | tf_op jit(solution)/shard_map/ppermute | solution.py:54
  40.1 1.2 shard_map.49
  41.4 4.0 %all-to-all-start = ((f32[4,64,1152]{2,1,0:T(8,128)}), f32[4,64,1152]{2,1,0:T(8,128)S(1)}, u32[]{:S(2)}, u32[]{:S(2)}) async-start(f32[4,64,1152]{2,1,0:T(8,128)} %bitcast.2), calls=%async_computation | async-start | bytes 2359296 | tf_op jit(solution)/shard_map/all_to_all | solution.py:45
  45.4 9.6 %collective-permute-start.1 = (f32[128,1152]{1,0:T(8,128)S(1)}, f32[128,1152]{1,0:T(8,128)S(1)}, u32[]{:S(2)}, u32[]{:S(2)}) collective-permute-start(f32[128,1152]{1,0:T(8,128)S(1)} %shard_map.50.a_ref), channel_id=1, source_target_pairs={{0,16},{16,0},{1,17},{17,1},{2,18},{18,2},{3,19},{19,3},{4,20},{20... | collective-permute-start | bytes 1769480 | tf_op jit(solution)/shard_map/ppermute | solution.py:58
  55.0 1.9 %collective-permute-start.2 = (f32[128,1152]{1,0:T(8,128)S(1)}, f32[128,1152]{1,0:T(8,128)}, u32[]{:S(2)}, u32[]{:S(2)}) collective-permute-start(f32[128,1152]{1,0:T(8,128)S(1)} %collective-permute-done.b_ref), channel_id=1, source_target_pairs={{0,16},{16,0},{1,17},{17,1},{2,18},{18,2},{3,19},{19,3},{4,20},{20... | collective-permute-start | bytes 1769480 | tf_op jit(solution)/shard_map/ppermute | solution.py:58
  57.9 1.2 collective-permute-done.2.d_ref
  59.0 1.1 copy-done.3
  60.1 5.7 %shard_map.51 = (f32[256,512]{1,0:T(8,128)S(1)}, f32[264,1152]{1,0:T(8,128)}) custom-call(s32[2]{0:T(128)S(1)} %pad_add_fusion.place, f32[256,1152]{1,0:T(8,128)S(1)} %bitcast.13, f32[128,1152]{1,0:T(8,128)S(1)} %shard_map.50.a_ref, f32[128,1152]{1,0:T(8,128)S(1)} %collective-permute-done.b_ref, f32[128,1152]{1,0:T(8,128)S(1)} %copy-done.3, ...), custom_call_target="tpu_custom_call" | custom-call | flops 1358954496 | bytes 5279752 | tf_op jit(solution)/shard_map/pallas_call | solution.py:33
  65.8 8.4 %collective-permute-start.3 = (f32[264,1152]{1,0:T(8,128)}, f32[264,1152]{1,0:T(8,128)}, u32[]{:S(2)}, u32[]{:S(2)}) collective-permute-start(f32[264,1152]{1,0:T(8,128)} %get-tuple-element.8.other_ref), channel_id=1, source_target_pairs={{0,16},{16,0},{1,17},{17,1},{2,18},{18,2},{3,19},{19,3},{4,20},{20... | collective-permute-start | bytes 3649544 | tf_op jit(solution)/shard_map/ppermute | solution.py:58
  74.2 4.1 %shard_map.52.x0 = f32[256,1152]{1,0:T(8,128)} custom-call(f32[256,512]{1,0:T(8,128)S(1)} %get-tuple-element.7.slope_ref, f32[128,1152]{1,0:T(8,128)S(1)} %shard_map.50.a_ref, f32[128,1152]{1,0:T(8,128)S(1)} %collective-permute-done.b_ref, f32[128,1152]{1,0:T(8,128)S(1)} %copy-done.3, f32[128,1152]{1,0:T(8,128)} %collective-permute-done.2.d_ref), custom_call_target="tpu_custom_call" | custom-call | flops 905969664 | bytes 4063232 | tf_op jit(solution)/shard_map/pallas_call | solution.py:33
  78.3 3.5 %all-to-all-start.2 = ((f32[4,64,1152]{2,1,0:T(8,128)}), f32[4,64,1152]{2,1,0:T(8,128)S(1)}, u32[]{:S(2)}, u32[]{:S(2)}) async-start(f32[4,64,1152]{2,1,0:T(8,128)} %bitcast.5), calls=%async_computation.2 | async-start | bytes 2359296 | tf_op jit(solution)/shard_map/all_to_all | solution.py:45
  81.8 3.2 %shard_map.53 = (f32[136,1152]{1,0:T(8,128)S(1)}, f32[136,1152]{1,0:T(8,128)}) custom-call(f32[256,512]{1,0:T(8,128)S(1)} %get-tuple-element.7.slope_ref, f32[256,1152]{1,0:T(8,128)S(1)} %bitcast.14, f32[264,1152]{1,0:T(8,128)} %get-tuple-element.8.other_ref, f32[264,1152]{1,0:T(8,128)} %collective-permute-done.3.received_ref, f32[256,1152]{1,0:T(8,128)} %shard_map.52.x0), custom_call_target="tpu_custom_call" | custom-call | flops 452984832 | bytes 6569984 | tf_op jit(solution)/shard_map/pallas_call | solution.py:33
  85.9 6.8 %collective-permute-start.4 = (f32[136,1152]{1,0:T(8,128)}, f32[136,1152]{1,0:T(8,128)S(1)}, u32[]{:S(2)}, u32[]{:S(2)}) collective-permute-start(f32[136,1152]{1,0:T(8,128)} %get-tuple-element.10), channel_id=1, source_target_pairs={{0,32},{32,4},{4,36},{36,8},{8,40},{40,12},{12,44},{44,0},{16,60},... | collective-permute-start | bytes 1880072 | tf_op jit(solution)/shard_map/ppermute | solution.py:54
  92.7 5.7 %all-to-all-done.2 = f32[4,64,1152]{2,1,0:T(8,128)S(1)} async-done(((f32[4,64,1152]{2,1,0:T(8,128)}), f32[4,64,1152]{2,1,0:T(8,128)S(1)}, u32[]{:S(2)}, u32[]{:S(2)}) %all-to-all-start.2) | async-done | bytes 1179680 | tf_op jit(solution)/shard_map/all_to_all | solution.py:45
  99.2 1.0 collective-permute-done.4.plane_ref
  100.2 0.9 shard_map.55
  101.2 3.7 %all-to-all-start.3 = ((f32[8,152,128]{2,1,0:T(8,128)}), f32[8,152,128]{2,1,0:T(8,128)S(1)}, u32[]{:S(2)}, u32[]{:S(2)}) async-start(f32[8,152,128]{2,1,0:T(8,128)} %shard_map.55), calls=%async_computation.3 | async-start | bytes 1245184 | tf_op jit(solution)/shard_map/all_to_all | solution.py:45
  105.6 19.2 %all-to-all-done.3.packed_ref = f32[8,152,128]{2,1,0:T(8,128)S(1)} async-done(((f32[8,152,128]{2,1,0:T(8,128)}), f32[8,152,128]{2,1,0:T(8,128)S(1)}, u32[]{:S(2)}, u32[]{:S(2)}) %all-to-all-start.3) | async-done | bytes 622624 | tf_op jit(solution)/shard_map/all_to_all | solution.py:45
  125.5 7.3 %all-to-all-start.4 = ((f32[16,1,128]{2,1,0:T(1,128)}), f32[16,1,128]{2,1,0:T(1,128)S(1)}, u32[]{:S(2)}, u32[]{:S(2)}) async-start(f32[16,1,128]{2,1,0:T(1,128)} %bitcast.8), calls=%async_computation.4 | async-start | bytes 16384 | tf_op jit(solution)/shard_map/all_to_all | solution.py:45
  132.8 3.6 %reduce-scatter.2.cloned.1.call-done.direction_ref = f32[16,1152]{1,0:T(8,128)} async-done(((f32[64,1152]{1,0:T(8,128)}), f32[16,1152]{1,0:T(8,128)}) %reduce-scatter.2.cloned.1.call-update) | async-done | bytes 73744 | tf_op jit(solution)/shard_map/reduce_scatter | solution.py:217
  138.9 2.7 %all-to-all-done.4 = f32[16,1,128]{2,1,0:T(1,128)S(1)} async-done(((f32[16,1,128]{2,1,0:T(1,128)}), f32[16,1,128]{2,1,0:T(1,128)S(1)}, u32[]{:S(2)}, u32[]{:S(2)}) %all-to-all-start.4) | async-done | bytes 8224 | tf_op jit(solution)/shard_map/all_to_all | solution.py:45
  (29 shorter events, 7.2 us)
Async XLA Ops:
  7.2 9.5 %copy-start.5 = (f32[16,1152]{1,0:T(8,128)S(1)}, f32[16,1152]{1,0:T(8,128)}, u32[]{:S(2)}) copy-start(f32[16,1152]{1,0:T(8,128)} %emb_ref.2) | copy-start | bytes 221188
  9.0 25.6 %all-to-all-start.1 = ((f32[8,16,1152]{2,1,0:T(8,128)}), f32[8,16,1152]{2,1,0:T(8,128)S(1)}, u32[]{:S(2)}, u32[]{:S(2)}) async-start(f32[8,16,1152]{2,1,0:T(8,128)} %tile.2), calls=%async_computation.1 | async-start | bytes 1179648 | tf_op jit(solution)/shard_map/all_to_all | solution.py:45
  34.7 20.3 %collective-permute-start = (f32[128,1152]{1,0:T(8,128)S(1)}, f32[128,1152]{1,0:T(8,128)S(1)}, u32[]{:S(2)}, u32[]{:S(2)}) collective-permute-start(f32[128,1152]{1,0:T(8,128)S(1)} %shard_map.50.a_ref), channel_id=1, source_target_pairs={{0,44},{32,0},{4,32},{36,4},{8,36},{40,8},{12,40},{44,12},{16,48},... | collective-permute-start | bytes 1769480 | tf_op jit(solution)/shard_map/ppermute | solution.py:54
  41.4 15.7 %all-to-all-start = ((f32[4,64,1152]{2,1,0:T(8,128)}), f32[4,64,1152]{2,1,0:T(8,128)S(1)}, u32[]{:S(2)}, u32[]{:S(2)}) async-start(f32[4,64,1152]{2,1,0:T(8,128)} %bitcast.2), calls=%async_computation | async-start | bytes 2359296 | tf_op jit(solution)/shard_map/all_to_all | solution.py:45
  45.4 11.7 %collective-permute-start.1 = (f32[128,1152]{1,0:T(8,128)S(1)}, f32[128,1152]{1,0:T(8,128)S(1)}, u32[]{:S(2)}, u32[]{:S(2)}) collective-permute-start(f32[128,1152]{1,0:T(8,128)S(1)} %shard_map.50.a_ref), channel_id=1, source_target_pairs={{0,16},{16,0},{1,17},{17,1},{2,18},{18,2},{3,19},{19,3},{4,20},{20... | collective-permute-start | bytes 1769480 | tf_op jit(solution)/shard_map/ppermute | solution.py:58
  55.0 4.0 %collective-permute-start.2 = (f32[128,1152]{1,0:T(8,128)S(1)}, f32[128,1152]{1,0:T(8,128)}, u32[]{:S(2)}, u32[]{:S(2)}) collective-permute-start(f32[128,1152]{1,0:T(8,128)S(1)} %collective-permute-done.b_ref), channel_id=1, source_target_pairs={{0,16},{16,0},{1,17},{17,1},{2,18},{18,2},{3,19},{19,3},{4,20},{20... | collective-permute-start | bytes 1769480 | tf_op jit(solution)/shard_map/ppermute | solution.py:58
  57.0 0.8 copy-start.2
  59.0 1.1 copy-start.3
  65.8 16.0 %collective-permute-start.3 = (f32[264,1152]{1,0:T(8,128)}, f32[264,1152]{1,0:T(8,128)}, u32[]{:S(2)}, u32[]{:S(2)}) collective-permute-start(f32[264,1152]{1,0:T(8,128)} %get-tuple-element.8.other_ref), channel_id=1, source_target_pairs={{0,16},{16,0},{1,17},{17,1},{2,18},{18,2},{3,19},{19,3},{4,20},{20... | collective-permute-start | bytes 3649544 | tf_op jit(solution)/shard_map/ppermute | solution.py:58
  78.3 20.2 %all-to-all-start.2 = ((f32[4,64,1152]{2,1,0:T(8,128)}), f32[4,64,1152]{2,1,0:T(8,128)S(1)}, u32[]{:S(2)}, u32[]{:S(2)}) async-start(f32[4,64,1152]{2,1,0:T(8,128)} %bitcast.5), calls=%async_computation.2 | async-start | bytes 2359296 | tf_op jit(solution)/shard_map/all_to_all | solution.py:45
  85.0 0.9 copy-start
  85.9 14.4 %copy-start.1 = (f32[136,1152]{1,0:T(8,128)S(1)}, f32[136,1152]{1,0:T(8,128)}, u32[]{:S(2)}) copy-start(f32[136,1152]{1,0:T(8,128)} %copy-done) | copy-start | bytes 1880068
  85.9 14.4 %collective-permute-start.4 = (f32[136,1152]{1,0:T(8,128)}, f32[136,1152]{1,0:T(8,128)S(1)}, u32[]{:S(2)}, u32[]{:S(2)}) collective-permute-start(f32[136,1152]{1,0:T(8,128)} %get-tuple-element.10), channel_id=1, source_target_pairs={{0,32},{32,4},{4,36},{36,8},{8,40},{40,12},{12,44},{44,0},{16,60},... | collective-permute-start | bytes 1880072 | tf_op jit(solution)/shard_map/ppermute | solution.py:54
  101.2 35.2 %copy-start.6 = (f32[16,1152]{1,0:T(8,128)S(1)}, f32[16,1152]{1,0:T(8,128)}, u32[]{:S(2)}) copy-start(f32[16,1152]{1,0:T(8,128)} %emb_ref.2) | copy-start | bytes 221188
  101.2 36.9 %copy-start.4 = (f32[16,1152]{1,0:T(8,128)S(1)}, f32[16,1152]{1,0:T(8,128)}, u32[]{:S(2)}) copy-start(f32[16,1152]{1,0:T(8,128)} %emb_ref.3) | copy-start | bytes 221188
  101.2 23.7 %all-to-all-start.3 = ((f32[8,152,128]{2,1,0:T(8,128)}), f32[8,152,128]{2,1,0:T(8,128)S(1)}, u32[]{:S(2)}, u32[]{:S(2)}) async-start(f32[8,152,128]{2,1,0:T(8,128)} %shard_map.55), calls=%async_computation.3 | async-start | bytes 1245184 | tf_op jit(solution)/shard_map/all_to_all | solution.py:45
  104.9 31.5 %reduce-scatter.2.cloned.1.call-start = ((), (), s32[]{:S(2)}) async-start(), calls=%async_computation.6 | async-start | bytes 368640 | tf_op jit(solution)/shard_map/reduce_scatter | solution.py:217
  125.5 16.1 %all-to-all-start.4 = ((f32[16,1,128]{2,1,0:T(1,128)}), f32[16,1,128]{2,1,0:T(1,128)S(1)}, u32[]{:S(2)}, u32[]{:S(2)}) async-start(f32[16,1,128]{2,1,0:T(1,128)} %bitcast.8), calls=%async_computation.4 | async-start | bytes 16384 | tf_op jit(solution)/shard_map/all_to_all | solution.py:45
  136.4 0.9 copy-start.7
Sparse Core Ops, SparseCore 0:
  108.5 27.8 reduce-scatter.1

commit v13 on v9

--- a/solution.py
+++ b/solution.py
@@ -84,6 +84,15 @@
         return lax.dot_general(a, b, (dims, ((), ())), preferred_element_type=F32)
 
     return dot(left[1], right[0]) + dot(left[0], right[1]) + dot(left[0], right[0])
+
+
+def tie_kernel(*refs):
+    pass
+
+
+def after(values, other):
+    out = [shape(*values.shape)]
+    return call(tie_kernel, (values, other), out, [ANY] * 2, [ANY], input_output_aliases={0: 0})[0]
 
 
 def image_unit_kernel(image_ref, out):
@@ -134,18 +143,27 @@
         total = term if total is None else total + term
     rows = total.shape[0] // NX
     for k, out in enumerate(outs):
-        out[...] = total[k * rows : (k + 1) * rows]
-
-
-def text_kernel(place, slope_ref, image_ref, other_ref, received_ref, x0, keep_out, send_out):
+        out[pl.ds(0, rows), :] = total[k * rows : (k + 1) * rows]
+
+
+def text_kernel(place, slope_ref, image_ref, other_ref, received_ref, *refs):
+    keep_out, send_out = refs[NX : NX + 2]
+    blocks, (loss_ref, sems) = refs[NX + 2 : 2 * NX + 2], refs[2 * NX + 2 :]
     image = in_turn(place, image_ref)
-    quarter = keep_out.shape[0] - 8
+    quarter = keep_out.shape[0]
     last = pl.ds(2 * quarter, 8)
-    loss = other_ref[last, :] + received_ref[last, :]
+    loss_ref[...] = other_ref[last, :] + received_ref[last, :]
+    copies = [
+        pltpu.make_async_copy(loss_ref, block.at[pl.ds(block.shape[0] - 8, 8), :], sems.at[k])
+        for k, block in enumerate(blocks)
+    ]
+    for copy in copies:
+        copy.start()
     for k, out in ((1, send_out), (0, keep_out)):
         rows = pl.ds(k * quarter, quarter)
-        out[pl.ds(0, quarter), :] = dot3(halves(slope_ref[:, rows]), image, ((0,), (0,))) + received_ref[rows, :]
-        out[pl.ds(quarter, 8), :] = loss
+        out[...] = dot3(halves(slope_ref[:, rows]), image, ((0,), (0,))) + received_ref[rows, :]
+    for copy in copies:
+        copy.wait()
 
 
 def relay_kernel(left, right, out):
@@ -153,37 +171,31 @@
 
 
 def split_kernel(place, x0, x1, x2, *outs):
+    last = pl.ds(NZH * ROWS, 8)
+    loss = x0[last, :] + (x1[last, :] + x2[last, :])
     for k, out in enumerate(outs):
         rows = pl.ds(pl.multiple_of(place[2 + NX + k] * ROWS, ROWS), ROWS)
-        out[...] = x0[rows, :] + (x1[rows, :] + x2[rows, :])
-
-
-def pack_kernel(keep_ref, plane_ref, relay_ref, ahead_ref, packed_out):
-    last, first = pl.ds(NY * ROWS, 8), pl.ds(0, LANES)
-    loss = keep_ref[last, first] + plane_ref[last, first]
+        out[pl.ds(0, ROWS), :] = x0[rows, :] + (x1[rows, :] + x2[rows, :])
+        out[pl.ds(ROWS, 8), :] = loss
+
+
+def pack_kernel(keep_ref, plane_ref, image_ref, packed_out):
     for y in range(NY):
         rows = pl.ds(y * ROWS, ROWS)
         for k in range(COLS):
             lanes = pl.ds(k * LANES, LANES)
             packed_out[y, pl.ds(k * ROWS, ROWS), :] = keep_ref[rows, lanes] + plane_ref[rows, lanes]
-        packed_out[y, pl.ds(PACK, 8), :] = loss
-
-
-def loss_kernel(packed_ref, out):
-    total = packed_ref[0, pl.ds(PACK, 8), :]
-    for y in range(1, NY):
-        total = total + packed_ref[y, pl.ds(PACK, 8), :]
-    for k in range(out.shape[0] // 8):
-        out[pl.ds(8 * k, 8), :] = total
 
 
 def mean_kernel(losses_ref, out):
     out[0, 0] = jnp.sum(losses_ref[:, 0:1]) / PAIRS
 
 
-def image_grad_kernel(emb_ref, z0, z1, z2, out):
+def image_grad_kernel(emb_ref, z0, z1, z2, out, loss_out):
     unit, length = normalize(emb_ref[...])
-    out[...] = project_back(unit, z0[...] + (z1[...] + z2[...]), length)
+    total = z0[...] + (z1[...] + z2[...])
+    out[...] = project_back(unit, total[:ROWS], length)
+    loss_out[...] = total[ROWS:, :LANES]
 
 
 def text_grad_kernel(emb_ref, packed_ref, out):
@@ -222,40 +234,40 @@
         vmem=20,
     )
     received = other_core(other)
-    xs = call(image_kernel, (slope, *texts), [shape(part, features)] * NX, flops=4 * product, vmem=20)
+    xs = call(image_kernel, (slope, *texts), [shape(part + 8, features)] * NX, flops=4 * product, vmem=20)
+    keep, send, *xs = call(
+        text_kernel,
+        (place, slope, image, other, received, *xs),
+        [shape(quarter, features)] * 2 + [shape(part + 8, features)] * NX,
+        in_specs=[SMEM] + [VMEM] * 4 + [ANY] * NX,
+        out_specs=[VMEM] * 2 + [ANY] * NX,
+        input_output_aliases={5 + k: 2 + k for k in range(NX)},
+        scratch_shapes=[pltpu.VMEM((8, features), F32), pltpu.SemaphoreType.DMA((NX,))],
+        flops=2 * product,
+        vmem=20,
+    )
     relay = turned(xs[3], "x", -1)
     ahead = turned(xs[2], "x", 1)
-    keep, send = call(
-        text_kernel,
-        (place, slope, image, other, received, xs[0]),
-        [shape(quarter + 8, features)] * 2,
-        in_specs=[SMEM] + [VMEM] * 4 + [ANY],
-        flops=2 * product,
-        vmem=20,
-    )
     plane = planes(send, 1)
-    (relay,) = call(relay_kernel, (xs[1], relay), [shape(part, features)])
+    (relay,) = call(relay_kernel, (xs[1], relay), [shape(part + 8, features)])
     back = turned(relay, "x", -1)
-    (packed,) = call(
-        pack_kernel,
-        (keep, plane, relay, ahead),
-        [shape(NY, PACK + 8, LANES)],
-        in_specs=[VMEM] * 2 + [ANY] * 2,
-    )
     zs = call(
         split_kernel,
         (place, xs[0], back, ahead),
-        [shape(rows, features)] * NZH,
+        [shape(rows + 8, features)] * NZH,
         in_specs=[SMEM] + [VMEM] * 3,
     )
+    (packed,) = call(pack_kernel, (keep, plane, zs[0]), [shape(NY, PACK, LANES)], in_specs=[VMEM] * 2 + [ANY])
     packed = exchange(packed, "y")
     relay = turned(zs[3], "zh", -1)
     ahead = turned(zs[2], "zh", 1)
-    (relay,) = call(relay_kernel, (zs[1], relay), [shape(rows, features)])
+    (relay,) = call(relay_kernel, (zs[1], relay), [shape(rows + 8, features)])
     back = turned(relay, "zh", -1)
-    (image_grad,) = call(image_grad_kernel, (image_emb, zs[0], back, ahead), [shape(rows, features)])
-    (loss,) = call(loss_kernel, (packed,), [shape(NZH * NX, LANES)])
-    losses = exchange(loss, ("zh", "x"))
+    image_grad, loss = call(
+        image_grad_kernel, (image_emb, zs[0], back, ahead), [shape(rows, features), shape(8, LANES)]
+    )
+    loss = loss + lax.ppermute(loss, "zl", [(0, 1), (1, 0)])
+    losses = exchange(after(loss, packed), "y")
     (text_grad,) = call(text_grad_kernel, (text_emb, packed), [shape(rows, features)])
     (loss,) = call(mean_kernel, (losses,), [shape(1, 1)], out_specs=[SMEM])
     return loss.reshape(()), image_grad, text_grad

time: 130 us -> 136 us (1.046)
  the two profiles are of different devices: /device:TPU:72 before, /device:TPU:6 now
where the time goes in v13:
time: 136 us; the launch traced here: 135 us
  starting transfers between devices  61.4 us (45%)
  waiting for transfers between devices  35.2 us (26%)
  blocking collectives  20.1 us (15%)
  Pallas kernels  14.7 us (11%)
  local copies, waits for them, and re-layouts  1.89 us (1%)
    all_to_all x4, starting transfers between devices, exchange(): return lax.all_to_all(values, axes, 0, 0, tiled=True)  22.9 us
    all_gather x1, blocking collectives, on_device(): image_z = lax.all_gather(image_emb, 'zh', axis=0, tiled=True)  20.1 us
    ppermute x6, waiting for transfers between devices, turned(): return lax.ppermute(values, ('c', axis), pairs)  19.9 us
    ppermute x6, starting transfers between devices, turned(): return lax.ppermute(values, ('c', axis), pairs)  19.2 us
    pallas_call x13, Pallas kernels, call(): pl.pallas_call(kernel, out_shape=outs, in_specs=in_specs or [VMEM] * len(...  14.7 us
    all_to_all x4, waiting for transfers between devices, exchange(): return lax.all_to_all(values, axes, 0, 0, tiled=True)  11.7 us
    ppermute x2, starting transfers between devices, planes(): return lax.ppermute(values, ('zl', 'c', 'zh'), pairs)  10.9 us
    ppermute x3, starting transfers between devices, other_core(): return lax.ppermute(values, 'c', [(0, 1), (1, 0)])  5.74 us
  transfers between devices with their start and end apart: 16, of which 9 were waited for; matrix products, arithmetic and copies ran while one was open for 1% of the time, Pallas kernels for 5%

profile of v13, /device:TPU:6, one launch (start us, length us, event | category | flops | bytes accessed | tf_op | source)
XLA Modules:
  0.0 134.8 jit_solution(1654216894193185947)
XLA Ops:
  2.4 7.1 %all-to-all-start.1 = ((f32[8,16,1152]{2,1,0:T(8,128)}), f32[8,16,1152]{2,1,0:T(8,128)S(1)}, u32[]{:S(2)}, u32[]{:S(2)}) async-start(f32[8,16,1152]{2,1,0:T(8,128)} %tile.2), calls=%async_computation.1 | async-start | bytes 1179648 | tf_op jit(solution)/shard_map/all_to_all | solution.py:45
  9.5 20.1 %all_gather.3.image_ref = f32[64,1152]{1,0:T(8,128)S(1)} all-gather(f32[16,1152]{1,0:T(8,128)S(1)} %copy-done.1), channel_id=1, replica_groups=mesh['y'=8,'zl'=2,'c'=2,'zh'=4,'x'=4] {'zh'}, dimensions={0}, use_global_device_ids=true | all-gather | bytes 368640 | tf_op jit(solution)/shard_map/all_gather | solution.py:213
  31.0 8.5 %collective-permute-start = (f32[128,1152]{1,0:T(8,128)S(1)}, f32[128,1152]{1,0:T(8,128)S(1)}, u32[]{:S(2)}, u32[]{:S(2)}) collective-permute-start(f32[128,1152]{1,0:T(8,128)S(1)} %shard_map.50.a_ref), channel_id=1, source_target_pairs={{0,44},{32,0},{4,32},{36,4},{8,36},{40,8},{12,40},{44,12},{16,48},... | collective-permute-start | bytes 1769480 | tf_op jit(solution)/shard_map/ppermute | solution.py:60
  39.5 4.8 %all-to-all-start = ((f32[4,64,1152]{2,1,0:T(8,128)}), f32[4,64,1152]{2,1,0:T(8,128)S(1)}, u32[]{:S(2)}, u32[]{:S(2)}) async-start(f32[4,64,1152]{2,1,0:T(8,128)} %bitcast.10), calls=%async_computation | async-start | bytes 2359296 | tf_op jit(solution)/shard_map/all_to_all | solution.py:45
  49.0 4.8 %all-to-all-done = f32[4,64,1152]{2,1,0:T(8,128)S(1)} async-done(((f32[4,64,1152]{2,1,0:T(8,128)}), f32[4,64,1152]{2,1,0:T(8,128)S(1)}, u32[]{:S(2)}, u32[]{:S(2)}) %all-to-all-start) | async-done | bytes 1179680 | tf_op jit(solution)/shard_map/all_to_all | solution.py:45
  53.9 4.7 %shard_map.51 = (f32[256,512]{1,0:T(8,128)S(1)}, f32[264,1152]{1,0:T(8,128)S(1)}) custom-call(s32[10]{0:T(128)S(1)} %stack.43.place, f32[256,1152]{1,0:T(8,128)S(1)} %bitcast.18, f32[128,1152]{1,0:T(8,128)S(1)} %shard_map.50.a_ref, f32[128,1152]{1,0:T(8,128)S(1)} %collective-permute-done.b_ref, f32[128,1152]{1,0:T(8,128)S(1)} %collective-permute-done.1.c_ref, ...), custom_call_target="tpu_custom_call" | custom-call | flops 1358954496 | bytes 5279784 | tf_op jit(solution)/shard_map/pallas_call | solution.py:33
  58.5 1.9 %collective-permute-start.3 = (f32[264,1152]{1,0:T(8,128)S(1)}, f32[264,1152]{1,0:T(8,128)S(1)}, u32[]{:S(2)}, u32[]{:S(2)}) collective-permute-start(f32[264,1152]{1,0:T(8,128)S(1)} %get-tuple-element.22.other_ref), channel_id=1, source_target_pairs={{0,16},{16,0},{1,17},{17,1},{2,18},{18,2},{3,19},{19,3},{4,20},{20... | collective-permute-start | bytes 3649544 | tf_op jit(solution)/shard_map/ppermute | solution.py:64
  60.5 3.1 %shard_map.52 = (f32[72,1152]{1,0:T(8,128)S(1)}, f32[72,1152]{1,0:T(8,128)S(1)}, f32[72,1152]{1,0:T(8,128)S(1)}, f32[72,1152]{1,0:T(8,128)S(1)}) custom-call(f32[256,512]{1,0:T(8,128)S(1)} %get-tuple-element.21.slope_ref, f32[128,1152]{1,0:T(8,128)S(1)} %shard_map.50.a_ref, f32[128,1152]{1,0:T(8,128)S(1)} %collective-permute-done.b_ref, ...), custom_call_target="tpu_custom_call" | custom-call | flops 905969664 | bytes 4210688 | tf_op jit(solution)/shard_map/pallas_call | solution.py:33
  65.3 1.9 %collective-permute-start.4 = (f32[72,1152]{1,0:T(8,128)S(1)}, f32[72,1152]{1,0:T(8,128)S(1)}, u32[]{:S(2)}, u32[]{:S(2)}) collective-permute-start(f32[72,1152]{1,0:T(8,128)S(1)} %get-tuple-element.29), channel_id=1, source_target_pairs={{0,3},{1,0},{2,1},{3,2},{16,17},{17,18},{18,19},{19,16},{4,7},{5,4... | collective-permute-start | bytes 995336 | tf_op jit(solution)/shard_map/ppermute | solution.py:51
  67.2 2.4 %collective-permute-start.11 = (f32[128,1152]{1,0:T(8,128)S(1)}, f32[128,1152]{1,0:T(8,128)S(1)}, u32[]{:S(2)}, u32[]{:S(2)}) collective-permute-start(f32[128,1152]{1,0:T(8,128)S(1)} %get-tuple-element.37), channel_id=1, source_target_pairs={{0,32},{32,4},{4,36},{36,8},{8,40},{40,12},{12,44},{44,0},{16,60},... | collective-permute-start | bytes 1769480 | tf_op jit(solution)/shard_map/ppermute | solution.py:60
  69.7 5.1 %collective-permute-start.6 = (f32[72,1152]{1,0:T(8,128)S(1)}, f32[72,1152]{1,0:T(8,128)S(1)}, u32[]{:S(2)}, u32[]{:S(2)}) collective-permute-start(f32[72,1152]{1,0:T(8,128)S(1)} %get-tuple-element.30), channel_id=1, source_target_pairs={{0,1},{1,2},{2,3},{3,0},{16,19},{17,16},{18,17},{19,18},{4,5},{5,6... | collective-permute-start | bytes 995336 | tf_op jit(solution)/shard_map/ppermute | solution.py:51
  75.6 1.9 %collective-permute-start.5 = (f32[72,1152]{1,0:T(8,128)S(1)}, f32[72,1152]{1,0:T(8,128)S(1)}, u32[]{:S(2)}, u32[]{:S(2)}) collective-permute-start(f32[72,1152]{1,0:T(8,128)S(1)} %shard_map.54), channel_id=1, source_target_pairs={{0,3},{1,0},{2,1},{3,2},{16,17},{17,18},{18,19},{19,16},{4,7},{5,4... | collective-permute-start | bytes 995336 | tf_op jit(solution)/shard_map/ppermute | solution.py:51
  77.5 1.9 %collective-permute-done.6.x2 = f32[72,1152]{1,0:T(8,128)S(1)} collective-permute-done((f32[72,1152]{1,0:T(8,128)S(1)}, f32[72,1152]{1,0:T(8,128)S(1)}, u32[]{:S(2)}, u32[]{:S(2)}) %collective-permute-start.6) | collective-permute-done | bytes 331808 | tf_op jit(solution)/shard_map/ppermute | solution.py:51
  79.4 9.6 %collective-permute-done.5.x1 = f32[72,1152]{1,0:T(8,128)S(1)} collective-permute-done((f32[72,1152]{1,0:T(8,128)S(1)}, f32[72,1152]{1,0:T(8,128)S(1)}, u32[]{:S(2)}, u32[]{:S(2)}) %collective-permute-start.5) | collective-permute-done | bytes 331808 | tf_op jit(solution)/shard_map/ppermute | solution.py:51
  90.6 3.7 %all-to-all-start.2 = ((f32[8,144,128]{2,1,0:T(8,128)}), f32[8,144,128]{2,1,0:T(8,128)S(1)}, u32[]{:S(2)}, u32[]{:S(2)}) async-start(f32[8,144,128]{2,1,0:T(8,128)} %shard_map.58), calls=%async_computation.2 | async-start | bytes 1179648 | tf_op jit(solution)/shard_map/all_to_all | solution.py:45
  94.3 4.9 %collective-permute-start.7 = (f32[24,1152]{1,0:T(8,128)S(1)}, f32[24,1152]{1,0:T(8,128)S(1)}, u32[]{:S(2)}, u32[]{:S(2)}) collective-permute-start(f32[24,1152]{1,0:T(8,128)S(1)} %get-tuple-element.33), channel_id=1, source_target_pairs={{0,12},{4,0},{8,4},{12,8},{16,20},{20,24},{24,28},{28,16},{1,13},{... | collective-permute-start | bytes 331784 | tf_op jit(solution)/shard_map/ppermute | solution.py:51
  99.2 1.9 %collective-permute-start.9 = (f32[24,1152]{1,0:T(8,128)S(1)}, f32[24,1152]{1,0:T(8,128)S(1)}, u32[]{:S(2)}, u32[]{:S(2)}) collective-permute-start(f32[24,1152]{1,0:T(8,128)S(1)} %get-tuple-element.34), channel_id=1, source_target_pairs={{0,4},{4,8},{8,12},{12,0},{16,28},{20,16},{24,20},{28,24},{1,5},{5... | collective-permute-start | bytes 331784 | tf_op jit(solution)/shard_map/ppermute | solution.py:51
  101.1 3.4 %collective-permute-done.7.right = f32[24,1152]{1,0:T(8,128)S(1)} collective-permute-done((f32[24,1152]{1,0:T(8,128)S(1)}, f32[24,1152]{1,0:T(8,128)S(1)}, u32[]{:S(2)}, u32[]{:S(2)}) %collective-permute-start.7) | collective-permute-done | bytes 110624 | tf_op jit(solution)/shard_map/ppermute | solution.py:51
  104.6 3.4 %collective-permute-start.8 = (f32[24,1152]{1,0:T(8,128)S(1)}, f32[24,1152]{1,0:T(8,128)S(1)}, u32[]{:S(2)}, u32[]{:S(2)}) collective-permute-start(f32[24,1152]{1,0:T(8,128)S(1)} %shard_map.56), channel_id=1, source_target_pairs={{0,12},{4,0},{8,4},{12,8},{16,20},{20,24},{24,28},{28,16},{1,13},{... | collective-permute-start | bytes 331784 | tf_op jit(solution)/shard_map/ppermute | solution.py:51
  108.0 4.2 %collective-permute-done.8.z1 = f32[24,1152]{1,0:T(8,128)S(1)} collective-permute-done((f32[24,1152]{1,0:T(8,128)S(1)}, f32[24,1152]{1,0:T(8,128)S(1)}, u32[]{:S(2)}, u32[]{:S(2)}) %collective-permute-start.8) | collective-permute-done | bytes 110624 | tf_op jit(solution)/shard_map/ppermute | solution.py:51
  113.0 2.5 %collective-permute-start.10 = (f32[8,128]{1,0:T(8,128)S(1)}, f32[8,128]{1,0:T(8,128)S(1)}, u32[]{:S(2)}, u32[]{:S(2)}) collective-permute-start(f32[8,128]{1,0:T(8,128)S(1)} %get-tuple-element.35), channel_id=1, source_target_pairs={{0,32},{32,0},{1,33},{33,1},{2,34},{34,2},{3,35},{35,3},{4,36},{36... | collective-permute-start | bytes 12296 | tf_op jit(solution)/shard_map/ppermute | solution.py:269
  115.6 3.0 %collective-permute-done.10 = f32[8,128]{1,0:T(8,128)S(1)} collective-permute-done((f32[8,128]{1,0:T(8,128)S(1)}, f32[8,128]{1,0:T(8,128)S(1)}, u32[]{:S(2)}, u32[]{:S(2)}) %collective-permute-start.10) | collective-permute-done | bytes 4128 | tf_op jit(solution)/shard_map/ppermute | solution.py:269
  119.1 7.4 %all-to-all-start.3 = ((f32[8,1,128]{2,1,0:T(1,128)}), f32[8,1,128]{2,1,0:T(1,128)S(1)}, u32[]{:S(2)}, u32[]{:S(2)}) async-start(f32[8,1,128]{2,1,0:T(1,128)} %bitcast.14), calls=%async_computation.3 | async-start | bytes 8192 | tf_op jit(solution)/shard_map/all_to_all | solution.py:45
  127.3 6.8 %all-to-all-done.3 = f32[8,1,128]{2,1,0:T(1,128)S(1)} async-done(((f32[8,1,128]{2,1,0:T(1,128)}), f32[8,1,128]{2,1,0:T(1,128)S(1)}, u32[]{:S(2)}, u32[]{:S(2)}) %all-to-all-start.3) | async-done | bytes 4128 | tf_op jit(solution)/shard_map/all_to_all | solution.py:45
  (29 shorter events, 14.7 us)
Async XLA Ops:
  0.6 8.9 %copy-start.1 = (f32[16,1152]{1,0:T(8,128)S(1)}, f32[16,1152]{1,0:T(8,128)}, u32[]{:S(2)}) copy-start(f32[16,1152]{1,0:T(8,128)} %emb_ref.2) | copy-start | bytes 221188
  2.4 28.4 %all-to-all-start.1 = ((f32[8,16,1152]{2,1,0:T(8,128)}), f32[8,16,1152]{2,1,0:T(8,128)S(1)}, u32[]{:S(2)}, u32[]{:S(2)}) async-start(f32[8,16,1152]{2,1,0:T(8,128)} %tile.2), calls=%async_computation.1 | async-start | bytes 1179648 | tf_op jit(solution)/shard_map/all_to_all | solution.py:45
  31.0 15.9 %collective-permute-start = (f32[128,1152]{1,0:T(8,128)S(1)}, f32[128,1152]{1,0:T(8,128)S(1)}, u32[]{:S(2)}, u32[]{:S(2)}) collective-permute-start(f32[128,1152]{1,0:T(8,128)S(1)} %shard_map.50.a_ref), channel_id=1, source_target_pairs={{0,44},{32,0},{4,32},{36,4},{8,36},{40,8},{12,40},{44,12},{16,48},... | collective-permute-start | bytes 1769480 | tf_op jit(solution)/shard_map/ppermute | solution.py:60
  39.5 14.3 %all-to-all-start = ((f32[4,64,1152]{2,1,0:T(8,128)}), f32[4,64,1152]{2,1,0:T(8,128)S(1)}, u32[]{:S(2)}, u32[]{:S(2)}) async-start(f32[4,64,1152]{2,1,0:T(8,128)} %bitcast.10), calls=%async_computation | async-start | bytes 2359296 | tf_op jit(solution)/shard_map/all_to_all | solution.py:45
  44.3 9.5 %collective-permute-start.1 = (f32[128,1152]{1,0:T(8,128)S(1)}, f32[128,1152]{1,0:T(8,128)S(1)}, u32[]{:S(2)}, u32[]{:S(2)}) collective-permute-start(f32[128,1152]{1,0:T(8,128)S(1)} %shard_map.50.a_ref), channel_id=1, source_target_pairs={{0,16},{16,0},{1,17},{17,1},{2,18},{18,2},{3,19},{19,3},{4,20},{20... | collective-permute-start | bytes 1769480 | tf_op jit(solution)/shard_map/ppermute | solution.py:64
  46.9 6.9 %collective-permute-start.2 = (f32[128,1152]{1,0:T(8,128)S(1)}, f32[128,1152]{1,0:T(8,128)}, u32[]{:S(2)}, u32[]{:S(2)}) collective-permute-start(f32[128,1152]{1,0:T(8,128)S(1)} %collective-permute-done.b_ref), channel_id=1, source_target_pairs={{0,16},{16,0},{1,17},{17,1},{2,18},{18,2},{3,19},{19,3},{4,20},{20... | collective-permute-start | bytes 1769480 | tf_op jit(solution)/shard_map/ppermute | solution.py:64
  58.5 5.0 %collective-permute-start.3 = (f32[264,1152]{1,0:T(8,128)S(1)}, f32[264,1152]{1,0:T(8,128)S(1)}, u32[]{:S(2)}, u32[]{:S(2)}) collective-permute-start(f32[264,1152]{1,0:T(8,128)S(1)} %get-tuple-element.22.other_ref), channel_id=1, source_target_pairs={{0,16},{16,0},{1,17},{17,1},{2,18},{18,2},{3,19},{19,3},{4,20},{20... | collective-permute-start | bytes 3649544 | tf_op jit(solution)/shard_map/ppermute | solution.py:64
  65.3 10.2 %collective-permute-start.4 = (f32[72,1152]{1,0:T(8,128)S(1)}, f32[72,1152]{1,0:T(8,128)S(1)}, u32[]{:S(2)}, u32[]{:S(2)}) collective-permute-start(f32[72,1152]{1,0:T(8,128)S(1)} %get-tuple-element.29), channel_id=1, source_target_pairs={{0,3},{1,0},{2,1},{3,2},{16,17},{17,18},{18,19},{19,16},{4,7},{5,4... | collective-permute-start | bytes 995336 | tf_op jit(solution)/shard_map/ppermute | solution.py:51
  67.2 22.4 %collective-permute-start.11 = (f32[128,1152]{1,0:T(8,128)S(1)}, f32[128,1152]{1,0:T(8,128)S(1)}, u32[]{:S(2)}, u32[]{:S(2)}) collective-permute-start(f32[128,1152]{1,0:T(8,128)S(1)} %get-tuple-element.37), channel_id=1, source_target_pairs={{0,32},{32,4},{4,36},{36,8},{8,40},{40,12},{12,44},{44,0},{16,60},... | collective-permute-start | bytes 1769480 | tf_op jit(solution)/shard_map/ppermute | solution.py:60
  69.7 9.8 %collective-permute-start.6 = (f32[72,1152]{1,0:T(8,128)S(1)}, f32[72,1152]{1,0:T(8,128)S(1)}, u32[]{:S(2)}, u32[]{:S(2)}) collective-permute-start(f32[72,1152]{1,0:T(8,128)S(1)} %get-tuple-element.30), channel_id=1, source_target_pairs={{0,1},{1,2},{2,3},{3,0},{16,19},{17,16},{18,17},{19,18},{4,5},{5,6... | collective-permute-start | bytes 995336 | tf_op jit(solution)/shard_map/ppermute | solution.py:51
  75.6 13.5 %collective-permute-start.5 = (f32[72,1152]{1,0:T(8,128)S(1)}, f32[72,1152]{1,0:T(8,128)S(1)}, u32[]{:S(2)}, u32[]{:S(2)}) collective-permute-start(f32[72,1152]{1,0:T(8,128)S(1)} %shard_map.54), channel_id=1, source_target_pairs={{0,3},{1,0},{2,1},{3,2},{16,17},{17,18},{18,19},{19,16},{4,7},{5,4... | collective-permute-start | bytes 995336 | tf_op jit(solution)/shard_map/ppermute | solution.py:51
  90.6 35.9 %copy-start = (f32[16,1152]{1,0:T(8,128)S(1)}, f32[16,1152]{1,0:T(8,128)}, u32[]{:S(2)}) copy-start(f32[16,1152]{1,0:T(8,128)} %emb_ref.3) | copy-start | bytes 221188
  90.6 28.5 %all-to-all-start.2 = ((f32[8,144,128]{2,1,0:T(8,128)}), f32[8,144,128]{2,1,0:T(8,128)S(1)}, u32[]{:S(2)}, u32[]{:S(2)}) async-start(f32[8,144,128]{2,1,0:T(8,128)} %shard_map.58), calls=%async_computation.2 | async-start | bytes 1179648 | tf_op jit(solution)/shard_map/all_to_all | solution.py:45
  94.3 10.3 %collective-permute-start.7 = (f32[24,1152]{1,0:T(8,128)S(1)}, f32[24,1152]{1,0:T(8,128)S(1)}, u32[]{:S(2)}, u32[]{:S(2)}) collective-permute-start(f32[24,1152]{1,0:T(8,128)S(1)} %get-tuple-element.33), channel_id=1, source_target_pairs={{0,12},{4,0},{8,4},{12,8},{16,20},{20,24},{24,28},{28,16},{1,13},{... | collective-permute-start | bytes 331784 | tf_op jit(solution)/shard_map/ppermute | solution.py:51
  99.2 8.8 %collective-permute-start.9 = (f32[24,1152]{1,0:T(8,128)S(1)}, f32[24,1152]{1,0:T(8,128)S(1)}, u32[]{:S(2)}, u32[]{:S(2)}) collective-permute-start(f32[24,1152]{1,0:T(8,128)S(1)} %get-tuple-element.34), channel_id=1, source_target_pairs={{0,4},{4,8},{8,12},{12,0},{16,28},{20,16},{24,20},{28,24},{1,5},{5... | collective-permute-start | bytes 331784 | tf_op jit(solution)/shard_map/ppermute | solution.py:51
  104.6 7.6 %collective-permute-start.8 = (f32[24,1152]{1,0:T(8,128)S(1)}, f32[24,1152]{1,0:T(8,128)S(1)}, u32[]{:S(2)}, u32[]{:S(2)}) collective-permute-start(f32[24,1152]{1,0:T(8,128)S(1)} %shard_map.56), channel_id=1, source_target_pairs={{0,12},{4,0},{8,4},{12,8},{16,20},{20,24},{24,28},{28,16},{1,13},{... | collective-permute-start | bytes 331784 | tf_op jit(solution)/shard_map/ppermute | solution.py:51
  113.0 5.5 %collective-permute-start.10 = (f32[8,128]{1,0:T(8,128)S(1)}, f32[8,128]{1,0:T(8,128)S(1)}, u32[]{:S(2)}, u32[]{:S(2)}) collective-permute-start(f32[8,128]{1,0:T(8,128)S(1)} %get-tuple-element.35), channel_id=1, source_target_pairs={{0,32},{32,0},{1,33},{33,1},{2,34},{34,2},{3,35},{35,3},{4,36},{36... | collective-permute-start | bytes 12296 | tf_op jit(solution)/shard_map/ppermute | solution.py:269
  119.1 15.0 %all-to-all-start.3 = ((f32[8,1,128]{2,1,0:T(1,128)}), f32[8,1,128]{2,1,0:T(1,128)S(1)}, u32[]{:S(2)}, u32[]{:S(2)}) async-start(f32[8,1,128]{2,1,0:T(1,128)} %bitcast.14), calls=%async_computation.3 | async-start | bytes 8192 | tf_op jit(solution)/shard_map/all_to_all | solution.py:45

commit v14 on v10

--- a/solution.py
+++ b/solution.py
@@ -86,15 +86,6 @@
     return dot(left[1], right[0]) + dot(left[0], right[1]) + dot(left[0], right[0])
 
 
-def tie_kernel(*refs):
-    pass
-
-
-def after(values, other):
-    out = [shape(*values.shape)]
-    return call(tie_kernel, (values, other), out, [ANY] * 2, [ANY], input_output_aliases={0: 0})[0]
-
-
 def image_unit_kernel(image_ref, out):
     unit = normalize(image_ref[...])[0]
     for x in range(NX):
@@ -111,7 +102,7 @@
     return halves(jnp.concatenate([image_ref[pl.ds(start, rows), :] for start in starts], axis=0))
 
 
-def tile_kernel(place, image_ref, a_ref, b_ref, c_ref, d_ref, slope_out, other_out, loss_out):
+def tile_kernel(place, image_ref, a_ref, b_ref, c_ref, d_ref, slope_out, other_out):
     image = in_turn(place, image_ref)
     quarter = a_ref.shape[0]
     count = image_ref.shape[0]
@@ -131,7 +122,7 @@
         slope_out[:, pl.ds(k * quarter, quarter)] = slope
         if k >= 2:
             other_out[pl.ds((k - 2) * quarter, quarter), :] = dot3(halves(slope), image, ((0,), (0,)))
-    loss_out[...] = jnp.full(loss_out.shape, total)
+    other_out[pl.ds(2 * quarter, 8), :] = jnp.full((8, FEATURES), total)
 
 
 def image_kernel(slope_ref, a_ref, b_ref, c_ref, d_ref, *outs):
@@ -146,12 +137,15 @@
         out[...] = total[k * rows : (k + 1) * rows]
 
 
-def text_kernel(place, slope_ref, image_ref, received_ref, x0, loss_ref, keep_out, send_out):
+def text_kernel(place, slope_ref, image_ref, other_ref, received_ref, x0, keep_out, send_out, loss_out):
     image = in_turn(place, image_ref)
     quarter = keep_out.shape[0]
     for k, out in ((1, send_out), (0, keep_out)):
         rows = pl.ds(k * quarter, quarter)
         out[...] = dot3(halves(slope_ref[:, rows]), image, ((0,), (0,))) + received_ref[rows, :]
+    last, first = pl.ds(2 * quarter, 8), pl.ds(0, LANES)
+    for k in range(loss_out.shape[0] // 8):
+        loss_out[pl.ds(8 * k, 8), :] = other_ref[last, first] + received_ref[last, first]
 
 
 def relay_kernel(left, right, out):
@@ -164,13 +158,14 @@
         out[...] = x0[rows, :] + (x1[rows, :] + x2[rows, :])
 
 
-def pack_kernel(keep_ref, plane_ref, loss_ref, relay_ref, ahead_ref, packed_out):
+def pack_kernel(keep_ref, plane_ref, losses_ref, back_ref, ahead_ref, packed_out):
+    loss = jnp.full((8, LANES), jnp.sum(losses_ref[:, 0:1]))
     for y in range(NY):
         rows = pl.ds(y * ROWS, ROWS)
         for k in range(COLS):
             lanes = pl.ds(k * LANES, LANES)
             packed_out[y, pl.ds(k * ROWS, ROWS), :] = keep_ref[rows, lanes] + plane_ref[rows, lanes]
-        packed_out[y, pl.ds(PACK, 8), :] = loss_ref[...]
+        packed_out[y, pl.ds(PACK, 8), :] = loss
 
 
 def image_grad_kernel(emb_ref, z0, z1, z2, out):
@@ -206,44 +201,41 @@
     blocks = [(at + step) % NX for at in (x, zh) for step in (0, -turn, turn, 2)]
     place = jnp.stack([zh * rows, lax.axis_index("y") * rows, *blocks]).astype(jnp.int32)
     product = 2 * count * quarter * features * 3
-    slope, other, loss = call(
+    slope, other = call(
         tile_kernel,
         (place, image, *texts),
-        [shape(count, 4 * quarter), shape(2 * quarter, features), shape(8, LANES)],
+        [shape(count, 4 * quarter), shape(2 * quarter + 8, features)],
         in_specs=[SMEM] + [VMEM] * 5,
         flops=6 * product,
         vmem=20,
     )
-    sums = [loss]
-    for axis, step in (("zl", 1), ("zh", 1), ("zh", 2), ("x", 1), ("x", 2), ("c", 1)):
-        pairs = [(i, i ^ step) for i in range(lax.axis_size(axis))]
-        sums.append(sums[-1] + lax.ppermute(sums[-1], axis, pairs))
     received = other_core(other)
     xs = call(image_kernel, (slope, *texts), [shape(part, features)] * NX, flops=4 * product, vmem=20)
-    relay = turned(after(xs[3], sums[2]), "x", -1)
-    ahead = turned(after(xs[2], sums[3]), "x", 1)
-    keep, send = call(
+    keep, send, loss = call(
         text_kernel,
-        (place, slope, image, received, xs[0], sums[1]),
-        [shape(quarter, features)] * 2,
-        in_specs=[SMEM] + [VMEM] * 3 + [ANY] * 2,
+        (place, slope, image, other, received, xs[0]),
+        [shape(quarter, features)] * 2 + [shape(32, LANES)],
+        in_specs=[SMEM] + [VMEM] * 4 + [ANY],
         flops=2 * product,
         vmem=20,
     )
+    losses = exchange(loss, ("zl", "zh", "x"))
+    relay = turned(xs[3], "x", -1)
+    ahead = turned(xs[2], "x", 1)
     plane = planes(send, 1)
-    (relay,) = call(relay_kernel, (xs[1], after(relay, sums[4])), [shape(part, features)])
+    (relay,) = call(relay_kernel, (xs[1], relay), [shape(part, features)])
     back = turned(relay, "x", -1)
-    (packed,) = call(
-        pack_kernel,
-        (keep, plane, sums[-1], relay, ahead),
-        [shape(NY, PACK + 8, LANES)],
-        in_specs=[VMEM] * 3 + [ANY] * 2,
-    )
     zs = call(
         split_kernel,
         (place, xs[0], back, ahead),
         [shape(rows, features)] * NZH,
         in_specs=[SMEM] + [VMEM] * 3,
+    )
+    (packed,) = call(
+        pack_kernel,
+        (keep, plane, losses, back, ahead),
+        [shape(NY, PACK + 8, LANES)],
+        in_specs=[VMEM] * 3 + [ANY] * 2,
     )
     packed = exchange(packed, "y")
     relay = turned(zs[3], "zh", -1)

time: 146 us -> 123 us (0.84)
  the two profiles are of different devices: /device:TPU:14 before, /device:TPU:1 now
where the time goes in v14:
time: 123 us; the launch traced here: 122 us
  starting transfers between devices  68.7 us (56%)
  blocking collectives  18 us (15%)
  waiting for transfers between devices  17.4 us (14%)
  Pallas kernels  14.9 us (12%)
  local copies, waits for them, and re-layouts  1.87 us (2%)
    all_to_all x4, starting transfers between devices, exchange(): return lax.all_to_all(values, axes, 0, 0, tiled=True)  20.9 us
    ppermute x3, starting transfers between devices, other_core(): return lax.ppermute(values, 'c', [(0, 1), (1, 0)])  19.2 us
    all_gather x1, blocking collectives, on_device(): image_z = lax.all_gather(image_emb, 'zh', axis=0, tiled=True)  18 us
    ppermute x6, starting transfers between devices, turned(): return lax.ppermute(values, ('c', axis), pairs)  17.7 us
    pallas_call x11, Pallas kernels, call(): pl.pallas_call(kernel, out_shape=outs, in_specs=in_specs or [VMEM] * len(...  14.9 us
    ppermute x2, starting transfers between devices, planes(): return lax.ppermute(values, ('zl', 'c', 'zh'), pairs)  10.9 us
    all_to_all x4, waiting for transfers between devices, exchange(): return lax.all_to_all(values, axes, 0, 0, tiled=True)  8.61 us
    ppermute x6, waiting for transfers between devices, turned(): return lax.ppermute(values, ('c', axis), pairs)  7.02 us
  transfers between devices with their start and end apart: 15, of which 8 were waited for; matrix products, arithmetic and copies ran while one was open for 0% of the time, Pallas kernels for 7%

profile of v14, /device:TPU:1, one launch (start us, length us, event | category | flops | bytes accessed | tf_op | source)
XLA Modules:
  0.0 121.8 jit_solution(7888662988470121131)
XLA Ops:
  0.6 1.8 %tile.2 = f32[8,16,1152]{2,1,0:T(8,128)} broadcast(f32[16,1152]{1,0:T(8,128)} %emb_ref.2), dimensions={1,2} | broadcast | bytes 663552 | tf_op jit(solution)/shard_map/tile | solution.py:188
  2.4 7.7 %all-to-all-start.1 = ((f32[8,16,1152]{2,1,0:T(8,128)}), f32[8,16,1152]{2,1,0:T(8,128)S(1)}, u32[]{:S(2)}, u32[]{:S(2)}) async-start(f32[8,16,1152]{2,1,0:T(8,128)} %tile.2), calls=%async_computation.1 | async-start | bytes 1179648 | tf_op jit(solution)/shard_map/all_to_all | solution.py:45
  10.1 18.0 %all_gather.3.image_ref = f32[64,1152]{1,0:T(8,128)S(1)} all-gather(f32[16,1152]{1,0:T(8,128)S(1)} %copy-done), channel_id=1, replica_groups=mesh['y'=8,'zl'=2,'c'=2,'zh'=4,'x'=4] {'zh'}, dimensions={0}, use_global_device_ids=true | all-gather | bytes 368640 | tf_op jit(solution)/shard_map/all_gather | solution.py:189
  29.4 4.2 %collective-permute-start = (f32[128,1152]{1,0:T(8,128)S(1)}, f32[128,1152]{1,0:T(8,128)S(1)}, u32[]{:S(2)}, u32[]{:S(2)}) collective-permute-start(f32[128,1152]{1,0:T(8,128)S(1)} %shard_map.50.a_ref), channel_id=1, source_target_pairs={{0,44},{32,0},{4,32},{36,4},{8,36},{40,8},{12,40},{44,12},{16,48},... | collective-permute-start | bytes 1769480 | tf_op jit(solution)/shard_map/ppermute | solution.py:60
  33.6 4.0 %all-to-all-start = ((f32[4,64,1152]{2,1,0:T(8,128)}), f32[4,64,1152]{2,1,0:T(8,128)S(1)}, u32[]{:S(2)}, u32[]{:S(2)}) async-start(f32[4,64,1152]{2,1,0:T(8,128)} %bitcast.10), calls=%async_computation | async-start | bytes 2359296 | tf_op jit(solution)/shard_map/all_to_all | solution.py:45
  37.6 9.6 %collective-permute-start.1 = (f32[128,1152]{1,0:T(8,128)S(1)}, f32[128,1152]{1,0:T(8,128)S(1)}, u32[]{:S(2)}, u32[]{:S(2)}) collective-permute-start(f32[128,1152]{1,0:T(8,128)S(1)} %shard_map.50.a_ref), channel_id=1, source_target_pairs={{0,16},{16,0},{1,17},{17,1},{2,18},{18,2},{3,19},{19,3},{4,20},{20... | collective-permute-start | bytes 1769480 | tf_op jit(solution)/shard_map/ppermute | solution.py:64
  47.5 2.8 %collective-permute-start.2 = (f32[128,1152]{1,0:T(8,128)S(1)}, f32[128,1152]{1,0:T(8,128)}, u32[]{:S(2)}, u32[]{:S(2)}) collective-permute-start(f32[128,1152]{1,0:T(8,128)S(1)} %collective-permute-done.b_ref), channel_id=1, source_target_pairs={{0,16},{16,0},{1,17},{17,1},{2,18},{18,2},{3,19},{19,3},{4,20},{20... | collective-permute-start | bytes 1769480 | tf_op jit(solution)/shard_map/ppermute | solution.py:64
  50.5 1.5 %collective-permute-done.2.d_ref = f32[128,1152]{1,0:T(8,128)} collective-permute-done((f32[128,1152]{1,0:T(8,128)S(1)}, f32[128,1152]{1,0:T(8,128)}, u32[]{:S(2)}, u32[]{:S(2)}) %collective-permute-start.2) | collective-permute-done | bytes 589856 | tf_op jit(solution)/shard_map/ppermute | solution.py:64
  52.1 4.7 %shard_map.51 = (f32[256,512]{1,0:T(8,128)S(1)}, f32[264,1152]{1,0:T(8,128)S(1)}) custom-call(s32[10]{0:T(128)S(1)} %stack.43.place, f32[256,1152]{1,0:T(8,128)S(1)} %bitcast.18, f32[128,1152]{1,0:T(8,128)S(1)} %shard_map.50.a_ref, f32[128,1152]{1,0:T(8,128)S(1)} %collective-permute-done.b_ref, f32[128,1152]{1,0:T(8,128)S(1)} %collective-permute-done.1.c_ref, ...), custom_call_target="tpu_custom_call" | custom-call | flops 1358954496 | bytes 5279784 | tf_op jit(solution)/shard_map/pallas_call | solution.py:33
  56.7 6.8 %collective-permute-start.3 = (f32[264,1152]{1,0:T(8,128)S(1)}, f32[264,1152]{1,0:T(8,128)S(1)}, u32[]{:S(2)}, u32[]{:S(2)}) collective-permute-start(f32[264,1152]{1,0:T(8,128)S(1)} %get-tuple-element.19.other_ref), channel_id=1, source_target_pairs={{0,16},{16,0},{1,17},{17,1},{2,18},{18,2},{3,19},{19,3},{4,20},{20... | collective-permute-start | bytes 3649544 | tf_op jit(solution)/shard_map/ppermute | solution.py:64
  63.5 3.8 %shard_map.52 = (f32[64,1152]{1,0:T(8,128)S(1)}, f32[64,1152]{1,0:T(8,128)S(1)}, f32[64,1152]{1,0:T(8,128)}, f32[64,1152]{1,0:T(8,128)S(1)}) custom-call(f32[256,512]{1,0:T(8,128)S(1)} %get-tuple-element.18.slope_ref, f32[128,1152]{1,0:T(8,128)S(1)} %shard_map.50.a_ref, f32[128,1152]{1,0:T(8,128)S(1)} %collective-permute-done.b_ref, ...), custom_call_target="tpu_custom_call" | custom-call | flops 905969664 | bytes 4063232 | tf_op jit(solution)/shard_map/pallas_call | solution.py:33
  67.3 2.2 %collective-permute-start.5 = (f32[64,1152]{1,0:T(8,128)S(1)}, f32[64,1152]{1,0:T(8,128)S(1)}, u32[]{:S(2)}, u32[]{:S(2)}) collective-permute-start(f32[64,1152]{1,0:T(8,128)S(1)} %get-tuple-element.25), channel_id=1, source_target_pairs={{0,3},{1,0},{2,1},{3,2},{16,17},{17,18},{18,19},{19,16},{4,7},{5,4... | collective-permute-start | bytes 884744 | tf_op jit(solution)/shard_map/ppermute | solution.py:51
  69.5 1.9 %shard_map.53 = (f32[128,1152]{1,0:T(8,128)S(1)}, f32[128,1152]{1,0:T(8,128)S(1)}, f32[32,128]{1,0:T(8,128)}) custom-call(s32[10]{0:T(128)S(1)} %stack.43.place, f32[256,512]{1,0:T(8,128)S(1)} %get-tuple-element.18.slope_ref, f32[256,1152]{1,0:T(8,128)S(1)} %bitcast.19, f32[264,1152]{1,0:T(8,128)S(1)} %get-tuple-element.19.other_ref, ...), custom_call_target="tpu_custom_call" | custom-call | flops 452984832 | bytes 5627944 | tf_op jit(solution)/shard_map/pallas_call | solution.py:33
  71.3 6.7 %collective-permute-start.4 = (f32[128,1152]{1,0:T(8,128)S(1)}, f32[128,1152]{1,0:T(8,128)S(1)}, u32[]{:S(2)}, u32[]{:S(2)}) collective-permute-start(f32[128,1152]{1,0:T(8,128)S(1)} %get-tuple-element.22), channel_id=1, source_target_pairs={{0,32},{32,4},{4,36},{36,8},{8,40},{40,12},{12,44},{44,0},{16,60},... | collective-permute-start | bytes 1769480 | tf_op jit(solution)/shard_map/ppermute | solution.py:60
  78.1 4.3 %collective-permute-start.7 = (f32[64,1152]{1,0:T(8,128)}, f32[64,1152]{1,0:T(8,128)S(1)}, u32[]{:S(2)}, u32[]{:S(2)}) collective-permute-start(f32[64,1152]{1,0:T(8,128)} %get-tuple-element.26), channel_id=1, source_target_pairs={{0,1},{1,2},{2,3},{3,0},{16,19},{17,16},{18,17},{19,18},{4,5},{5,6... | collective-permute-start | bytes 884744 | tf_op jit(solution)/shard_map/ppermute | solution.py:51
  82.4 1.9 %collective-permute-start.6 = (f32[64,1152]{1,0:T(8,128)S(1)}, f32[64,1152]{1,0:T(8,128)S(1)}, u32[]{:S(2)}, u32[]{:S(2)}) collective-permute-start(f32[64,1152]{1,0:T(8,128)S(1)} %shard_map.54), channel_id=1, source_target_pairs={{0,3},{1,0},{2,1},{3,2},{16,17},{17,18},{18,19},{19,16},{4,7},{5,4... | collective-permute-start | bytes 884744 | tf_op jit(solution)/shard_map/ppermute | solution.py:51
  84.4 5.5 %all-to-all-start.2 = ((f32[32,1,128]{2,1,0:T(1,128)}), f32[32,1,128]{2,1,0:T(1,128)S(1)}, u32[]{:S(2)}, u32[]{:S(2)}) async-start(f32[32,1,128]{2,1,0:T(1,128)} %bitcast.14), calls=%async_computation.2 | async-start | bytes 32768 | tf_op jit(solution)/shard_map/all_to_all | solution.py:45
  91.1 7.3 %all-to-all-done.2 = f32[32,1,128]{2,1,0:T(1,128)S(1)} async-done(((f32[32,1,128]{2,1,0:T(1,128)}), f32[32,1,128]{2,1,0:T(1,128)S(1)}, u32[]{:S(2)}, u32[]{:S(2)}) %all-to-all-start.2) | async-done | bytes 16416 | tf_op jit(solution)/shard_map/all_to_all | solution.py:45
  99.4 3.7 %all-to-all-start.3 = ((f32[8,152,128]{2,1,0:T(8,128)}), f32[8,152,128]{2,1,0:T(8,128)S(1)}, u32[]{:S(2)}, u32[]{:S(2)}) async-start(f32[8,152,128]{2,1,0:T(8,128)} %shard_map.55), calls=%async_computation.3 | async-start | bytes 1245184 | tf_op jit(solution)/shard_map/all_to_all | solution.py:45
  103.7 2.3 %collective-permute-start.8 = (f32[16,1152]{1,0:T(8,128)S(1)}, f32[16,1152]{1,0:T(8,128)S(1)}, u32[]{:S(2)}, u32[]{:S(2)}) collective-permute-start(f32[16,1152]{1,0:T(8,128)S(1)} %get-tuple-element.30), channel_id=1, source_target_pairs={{0,12},{4,0},{8,4},{12,8},{16,20},{20,24},{24,28},{28,16},{1,13},{... | collective-permute-start | bytes 221192 | tf_op jit(solution)/shard_map/ppermute | solution.py:51
  106.0 5.1 %collective-permute-start.10 = (f32[16,1152]{1,0:T(8,128)S(1)}, f32[16,1152]{1,0:T(8,128)S(1)}, u32[]{:S(2)}, u32[]{:S(2)}) collective-permute-start(f32[16,1152]{1,0:T(8,128)S(1)} %get-tuple-element.31), channel_id=1, source_target_pairs={{0,4},{4,8},{8,12},{12,0},{16,28},{20,16},{24,20},{28,24},{1,5},{5... | collective-permute-start | bytes 221192 | tf_op jit(solution)/shard_map/ppermute | solution.py:51
  111.6 1.9 %collective-permute-start.9 = (f32[16,1152]{1,0:T(8,128)S(1)}, f32[16,1152]{1,0:T(8,128)S(1)}, u32[]{:S(2)}, u32[]{:S(2)}) collective-permute-start(f32[16,1152]{1,0:T(8,128)S(1)} %shard_map.58), channel_id=1, source_target_pairs={{0,12},{4,0},{8,4},{12,8},{16,20},{20,24},{24,28},{28,16},{1,13},{... | collective-permute-start | bytes 221192 | tf_op jit(solution)/shard_map/ppermute | solution.py:51
  114.5 4.3 %collective-permute-done.9.z1 = f32[16,1152]{1,0:T(8,128)S(1)} collective-permute-done((f32[16,1152]{1,0:T(8,128)S(1)}, f32[16,1152]{1,0:T(8,128)S(1)}, u32[]{:S(2)}, u32[]{:S(2)}) %collective-permute-start.9) | collective-permute-done | bytes 73760 | tf_op jit(solution)/shard_map/ppermute | solution.py:51
  119.6 1.3 %all-to-all-done.3.packed_ref = f32[8,152,128]{2,1,0:T(8,128)S(1)} async-done(((f32[8,152,128]{2,1,0:T(8,128)}), f32[8,152,128]{2,1,0:T(8,128)S(1)}, u32[]{:S(2)}, u32[]{:S(2)}) %all-to-all-start.3) | async-done | bytes 622624 | tf_op jit(solution)/shard_map/all_to_all | solution.py:45
  (24 shorter events, 7.8 us)
Async XLA Ops:
  0.6 9.4 %copy-start = (f32[16,1152]{1,0:T(8,128)S(1)}, f32[16,1152]{1,0:T(8,128)}, u32[]{:S(2)}) copy-start(f32[16,1152]{1,0:T(8,128)} %emb_ref.3) | copy-start | bytes 221188
  2.4 26.8 %all-to-all-start.1 = ((f32[8,16,1152]{2,1,0:T(8,128)}), f32[8,16,1152]{2,1,0:T(8,128)S(1)}, u32[]{:S(2)}, u32[]{:S(2)}) async-start(f32[8,16,1152]{2,1,0:T(8,128)} %tile.2), calls=%async_computation.1 | async-start | bytes 1179648 | tf_op jit(solution)/shard_map/all_to_all | solution.py:45
  29.4 18.1 %collective-permute-start = (f32[128,1152]{1,0:T(8,128)S(1)}, f32[128,1152]{1,0:T(8,128)S(1)}, u32[]{:S(2)}, u32[]{:S(2)}) collective-permute-start(f32[128,1152]{1,0:T(8,128)S(1)} %shard_map.50.a_ref), channel_id=1, source_target_pairs={{0,44},{32,0},{4,32},{36,4},{8,36},{40,8},{12,40},{44,12},{16,48},... | collective-permute-start | bytes 1769480 | tf_op jit(solution)/shard_map/ppermute | solution.py:60
  33.6 16.9 %all-to-all-start = ((f32[4,64,1152]{2,1,0:T(8,128)}), f32[4,64,1152]{2,1,0:T(8,128)S(1)}, u32[]{:S(2)}, u32[]{:S(2)}) async-start(f32[4,64,1152]{2,1,0:T(8,128)} %bitcast.10), calls=%async_computation | async-start | bytes 2359296 | tf_op jit(solution)/shard_map/all_to_all | solution.py:45
  37.6 12.9 %collective-permute-start.1 = (f32[128,1152]{1,0:T(8,128)S(1)}, f32[128,1152]{1,0:T(8,128)S(1)}, u32[]{:S(2)}, u32[]{:S(2)}) collective-permute-start(f32[128,1152]{1,0:T(8,128)S(1)} %shard_map.50.a_ref), channel_id=1, source_target_pairs={{0,16},{16,0},{1,17},{17,1},{2,18},{18,2},{3,19},{19,3},{4,20},{20... | collective-permute-start | bytes 1769480 | tf_op jit(solution)/shard_map/ppermute | solution.py:64
  47.5 4.5 %collective-permute-start.2 = (f32[128,1152]{1,0:T(8,128)S(1)}, f32[128,1152]{1,0:T(8,128)}, u32[]{:S(2)}, u32[]{:S(2)}) collective-permute-start(f32[128,1152]{1,0:T(8,128)S(1)} %collective-permute-done.b_ref), channel_id=1, source_target_pairs={{0,16},{16,0},{1,17},{17,1},{2,18},{18,2},{3,19},{19,3},{4,20},{20... | collective-permute-start | bytes 1769480 | tf_op jit(solution)/shard_map/ppermute | solution.py:64
  56.7 12.8 %collective-permute-start.3 = (f32[264,1152]{1,0:T(8,128)S(1)}, f32[264,1152]{1,0:T(8,128)S(1)}, u32[]{:S(2)}, u32[]{:S(2)}) collective-permute-start(f32[264,1152]{1,0:T(8,128)S(1)} %get-tuple-element.19.other_ref), channel_id=1, source_target_pairs={{0,16},{16,0},{1,17},{17,1},{2,18},{18,2},{3,19},{19,3},{4,20},{20... | collective-permute-start | bytes 3649544 | tf_op jit(solution)/shard_map/ppermute | solution.py:64
  67.3 15.1 %collective-permute-start.5 = (f32[64,1152]{1,0:T(8,128)S(1)}, f32[64,1152]{1,0:T(8,128)S(1)}, u32[]{:S(2)}, u32[]{:S(2)}) collective-permute-start(f32[64,1152]{1,0:T(8,128)S(1)} %get-tuple-element.25), channel_id=1, source_target_pairs={{0,3},{1,0},{2,1},{3,2},{16,17},{17,18},{18,19},{19,16},{4,7},{5,4... | collective-permute-start | bytes 884744 | tf_op jit(solution)/shard_map/ppermute | solution.py:51
  71.3 27.0 %collective-permute-start.4 = (f32[128,1152]{1,0:T(8,128)S(1)}, f32[128,1152]{1,0:T(8,128)S(1)}, u32[]{:S(2)}, u32[]{:S(2)}) collective-permute-start(f32[128,1152]{1,0:T(8,128)S(1)} %get-tuple-element.22), channel_id=1, source_target_pairs={{0,32},{32,4},{4,36},{36,8},{8,40},{40,12},{12,44},{44,0},{16,60},... | collective-permute-start | bytes 1769480 | tf_op jit(solution)/shard_map/ppermute | solution.py:60
  78.1 11.8 %collective-permute-start.7 = (f32[64,1152]{1,0:T(8,128)}, f32[64,1152]{1,0:T(8,128)S(1)}, u32[]{:S(2)}, u32[]{:S(2)}) collective-permute-start(f32[64,1152]{1,0:T(8,128)} %get-tuple-element.26), channel_id=1, source_target_pairs={{0,1},{1,2},{2,3},{3,0},{16,19},{17,16},{18,17},{19,18},{4,5},{5,6... | collective-permute-start | bytes 884744 | tf_op jit(solution)/shard_map/ppermute | solution.py:51
  82.4 8.7 %collective-permute-start.6 = (f32[64,1152]{1,0:T(8,128)S(1)}, f32[64,1152]{1,0:T(8,128)S(1)}, u32[]{:S(2)}, u32[]{:S(2)}) collective-permute-start(f32[64,1152]{1,0:T(8,128)S(1)} %shard_map.54), channel_id=1, source_target_pairs={{0,3},{1,0},{2,1},{3,2},{16,17},{17,18},{18,19},{19,16},{4,7},{5,4... | collective-permute-start | bytes 884744 | tf_op jit(solution)/shard_map/ppermute | solution.py:51
  84.4 14.0 %all-to-all-start.2 = ((f32[32,1,128]{2,1,0:T(1,128)}), f32[32,1,128]{2,1,0:T(1,128)S(1)}, u32[]{:S(2)}, u32[]{:S(2)}) async-start(f32[32,1,128]{2,1,0:T(1,128)} %bitcast.14), calls=%async_computation.2 | async-start | bytes 32768 | tf_op jit(solution)/shard_map/all_to_all | solution.py:45
  99.4 21.6 %copy-start.1 = (f32[16,1152]{1,0:T(8,128)S(1)}, f32[16,1152]{1,0:T(8,128)}, u32[]{:S(2)}) copy-start(f32[16,1152]{1,0:T(8,128)} %emb_ref.2) | copy-start | bytes 221188
  99.4 21.6 %all-to-all-start.3 = ((f32[8,152,128]{2,1,0:T(8,128)}), f32[8,152,128]{2,1,0:T(8,128)S(1)}, u32[]{:S(2)}, u32[]{:S(2)}) async-start(f32[8,152,128]{2,1,0:T(8,128)} %shard_map.55), calls=%async_computation.3 | async-start | bytes 1245184 | tf_op jit(solution)/shard_map/all_to_all | solution.py:45
  103.7 7.9 %collective-permute-start.8 = (f32[16,1152]{1,0:T(8,128)S(1)}, f32[16,1152]{1,0:T(8,128)S(1)}, u32[]{:S(2)}, u32[]{:S(2)}) collective-permute-start(f32[16,1152]{1,0:T(8,128)S(1)} %get-tuple-element.30), channel_id=1, source_target_pairs={{0,12},{4,0},{8,4},{12,8},{16,20},{20,24},{24,28},{28,16},{1,13},{... | collective-permute-start | bytes 221192 | tf_op jit(solution)/shard_map/ppermute | solution.py:51
  106.0 8.6 %collective-permute-start.10 = (f32[16,1152]{1,0:T(8,128)S(1)}, f32[16,1152]{1,0:T(8,128)S(1)}, u32[]{:S(2)}, u32[]{:S(2)}) collective-permute-start(f32[16,1152]{1,0:T(8,128)S(1)} %get-tuple-element.31), channel_id=1, source_target_pairs={{0,4},{4,8},{8,12},{12,0},{16,28},{20,16},{24,20},{28,24},{1,5},{5... | collective-permute-start | bytes 221192 | tf_op jit(solution)/shard_map/ppermute | solution.py:51
  111.6 7.2 %collective-permute-start.9 = (f32[16,1152]{1,0:T(8,128)S(1)}, f32[16,1152]{1,0:T(8,128)S(1)}, u32[]{:S(2)}, u32[]{:S(2)}) collective-permute-start(f32[16,1152]{1,0:T(8,128)S(1)} %shard_map.58), channel_id=1, source_target_pairs={{0,12},{4,0},{8,4},{12,8},{16,20},{20,24},{24,28},{28,16},{1,13},{... | collective-permute-start | bytes 221192 | tf_op jit(solution)/shard_map/ppermute | solution.py:51

commit v15 on v14

--- a/solution.py
+++ b/solution.py
@@ -168,9 +168,9 @@
         packed_out[y, pl.ds(PACK, 8), :] = loss
 
 
-def image_grad_kernel(emb_ref, z0, z1, z2, out):
+def image_grad_kernel(emb_ref, z0, z1, z2, z3, out):
     unit, length = normalize(emb_ref[...])
-    out[...] = project_back(unit, z0[...] + (z1[...] + z2[...]), length)
+    out[...] = project_back(unit, (z0[...] + z1[...]) + (z2[...] + z3[...]), length)
 
 
 def text_grad_kernel(emb_ref, packed_ref, out, loss_out):
@@ -238,11 +238,8 @@
         in_specs=[VMEM] * 3 + [ANY] * 2,
     )
     packed = exchange(packed, "y")
-    relay = turned(zs[3], "zh", -1)
-    ahead = turned(zs[2], "zh", 1)
-    (relay,) = call(relay_kernel, (zs[1], relay), [shape(rows, features)])
-    back = turned(relay, "zh", -1)
-    (image_grad,) = call(image_grad_kernel, (image_emb, zs[0], back, ahead), [shape(rows, features)])
+    zs = [zs[0], turned(zs[3], "zh", 2), turned(zs[1], "zh", -1), turned(zs[2], "zh", 1)]
+    (image_grad,) = call(image_grad_kernel, (image_emb, *zs), [shape(rows, features)])
     text_grad, loss = call(
         text_grad_kernel,
         (text_emb, packed),

time: 123 us -> 124 us (level)
    ppermute x6, waiting for transfers between devices: 7.02 us -> 5.61 us  [turned(): return lax.ppermute(values, ('c', axis), pairs)]
    pallas_call x11 -> x10, Pallas kernels: 14.9 us -> 14.9 us  [call(): pl.pallas_call(kernel, out_shape=outs, in_specs=in_specs or [VMEM] * len(...]
  transfers between devices with their start and end apart: 15 -> 15, of which waited for: 8 -> 7; matrix products, arithmetic and copies ran while one was open for 0% -> 0% of each run, Pallas kernels for 7% -> 7%
where the time goes in v15:
time: 124 us; the launch traced here: 122 us
  starting transfers between devices  69.1 us (56%)
  blocking collectives  18 us (15%)
  waiting for transfers between devices  17 us (14%)
  Pallas kernels  14.9 us (12%)
  local copies, waits for them, and re-layouts  1.87 us (2%)
    all_to_all x4, starting transfers between devices, exchange(): return lax.all_to_all(values, axes, 0, 0, tiled=True)  20.9 us
    ppermute x3, starting transfers between devices, other_core(): return lax.ppermute(values, 'c', [(0, 1), (1, 0)])  19.2 us
    ppermute x6, starting transfers between devices, turned(): return lax.ppermute(values, ('c', axis), pairs)  18.1 us
    all_gather x1, blocking collectives, on_device(): image_z = lax.all_gather(image_emb, 'zh', axis=0, tiled=True)  18 us
    pallas_call x10, Pallas kernels, call(): pl.pallas_call(kernel, out_shape=outs, in_specs=in_specs or [VMEM] * len(...  14.9 us
    ppermute x2, starting transfers between devices, planes(): return lax.ppermute(values, ('zl', 'c', 'zh'), pairs)  10.9 us
    all_to_all x4, waiting for transfers between devices, exchange(): return lax.all_to_all(values, axes, 0, 0, tiled=True)  9.59 us
    ppermute x6, waiting for transfers between devices, turned(): return lax.ppermute(values, ('c', axis), pairs)  5.61 us
  transfers between devices with their start and end apart: 15, of which 7 were waited for; matrix products, arithmetic and copies ran while one was open for 0% of the time, Pallas kernels for 7%

profile of v15, /device:TPU:1, one launch (start us, length us, event | category | flops | bytes accessed | tf_op | source)
XLA Modules:
  0.0 121.8 jit_solution(17026817171342366868)
XLA Ops:
  0.6 1.8 %tile.2 = f32[8,16,1152]{2,1,0:T(8,128)} broadcast(f32[16,1152]{1,0:T(8,128)} %emb_ref.2), dimensions={1,2} | broadcast | bytes 663552 | tf_op jit(solution)/shard_map/tile | solution.py:188
  2.4 7.7 %all-to-all-start.1 = ((f32[8,16,1152]{2,1,0:T(8,128)}), f32[8,16,1152]{2,1,0:T(8,128)S(1)}, u32[]{:S(2)}, u32[]{:S(2)}) async-start(f32[8,16,1152]{2,1,0:T(8,128)} %tile.2), calls=%async_computation.1 | async-start | bytes 1179648 | tf_op jit(solution)/shard_map/all_to_all | solution.py:45
  10.1 18.0 %all_gather.3.image_ref = f32[64,1152]{1,0:T(8,128)S(1)} all-gather(f32[16,1152]{1,0:T(8,128)S(1)} %copy-done), channel_id=1, replica_groups=mesh['y'=8,'zl'=2,'c'=2,'zh'=4,'x'=4] {'zh'}, dimensions={0}, use_global_device_ids=true | all-gather | bytes 368640 | tf_op jit(solution)/shard_map/all_gather | solution.py:189
  29.4 4.2 %collective-permute-start = (f32[128,1152]{1,0:T(8,128)S(1)}, f32[128,1152]{1,0:T(8,128)S(1)}, u32[]{:S(2)}, u32[]{:S(2)}) collective-permute-start(f32[128,1152]{1,0:T(8,128)S(1)} %shard_map.50.a_ref), channel_id=1, source_target_pairs={{0,44},{32,0},{4,32},{36,4},{8,36},{40,8},{12,40},{44,12},{16,48},... | collective-permute-start | bytes 1769480 | tf_op jit(solution)/shard_map/ppermute | solution.py:60
  33.6 4.0 %all-to-all-start = ((f32[4,64,1152]{2,1,0:T(8,128)}), f32[4,64,1152]{2,1,0:T(8,128)S(1)}, u32[]{:S(2)}, u32[]{:S(2)}) async-start(f32[4,64,1152]{2,1,0:T(8,128)} %bitcast.10), calls=%async_computation | async-start | bytes 2359296 | tf_op jit(solution)/shard_map/all_to_all | solution.py:45
  37.6 9.6 %collective-permute-start.1 = (f32[128,1152]{1,0:T(8,128)S(1)}, f32[128,1152]{1,0:T(8,128)S(1)}, u32[]{:S(2)}, u32[]{:S(2)}) collective-permute-start(f32[128,1152]{1,0:T(8,128)S(1)} %shard_map.50.a_ref), channel_id=1, source_target_pairs={{0,16},{16,0},{1,17},{17,1},{2,18},{18,2},{3,19},{19,3},{4,20},{20... | collective-permute-start | bytes 1769480 | tf_op jit(solution)/shard_map/ppermute | solution.py:64
  47.5 2.8 %collective-permute-start.2 = (f32[128,1152]{1,0:T(8,128)S(1)}, f32[128,1152]{1,0:T(8,128)}, u32[]{:S(2)}, u32[]{:S(2)}) collective-permute-start(f32[128,1152]{1,0:T(8,128)S(1)} %collective-permute-done.b_ref), channel_id=1, source_target_pairs={{0,16},{16,0},{1,17},{17,1},{2,18},{18,2},{3,19},{19,3},{4,20},{20... | collective-permute-start | bytes 1769480 | tf_op jit(solution)/shard_map/ppermute | solution.py:64
  52.1 4.7 %shard_map.51 = (f32[256,512]{1,0:T(8,128)S(1)}, f32[264,1152]{1,0:T(8,128)S(1)}) custom-call(s32[10]{0:T(128)S(1)} %stack.43.place, f32[256,1152]{1,0:T(8,128)S(1)} %bitcast.18, f32[128,1152]{1,0:T(8,128)S(1)} %shard_map.50.a_ref, f32[128,1152]{1,0:T(8,128)S(1)} %collective-permute-done.b_ref, f32[128,1152]{1,0:T(8,128)S(1)} %collective-permute-done.1.c_ref, ...), custom_call_target="tpu_custom_call" | custom-call | flops 1358954496 | bytes 5279784 | tf_op jit(solution)/shard_map/pallas_call | solution.py:33
  56.7 6.8 %collective-permute-start.3 = (f32[264,1152]{1,0:T(8,128)S(1)}, f32[264,1152]{1,0:T(8,128)S(1)}, u32[]{:S(2)}, u32[]{:S(2)}) collective-permute-start(f32[264,1152]{1,0:T(8,128)S(1)} %get-tuple-element.19.other_ref), channel_id=1, source_target_pairs={{0,16},{16,0},{1,17},{17,1},{2,18},{18,2},{3,19},{19,3},{4,20},{20... | collective-permute-start | bytes 3649544 | tf_op jit(solution)/shard_map/ppermute | solution.py:64
  63.5 3.8 %shard_map.52 = (f32[64,1152]{1,0:T(8,128)S(1)}, f32[64,1152]{1,0:T(8,128)S(1)}, f32[64,1152]{1,0:T(8,128)}, f32[64,1152]{1,0:T(8,128)S(1)}) custom-call(f32[256,512]{1,0:T(8,128)S(1)} %get-tuple-element.18.slope_ref, f32[128,1152]{1,0:T(8,128)S(1)} %shard_map.50.a_ref, f32[128,1152]{1,0:T(8,128)S(1)} %collective-permute-done.b_ref, ...), custom_call_target="tpu_custom_call" | custom-call | flops 905969664 | bytes 4063232 | tf_op jit(solution)/shard_map/pallas_call | solution.py:33
  67.3 2.2 %collective-permute-start.5 = (f32[64,1152]{1,0:T(8,128)S(1)}, f32[64,1152]{1,0:T(8,128)S(1)}, u32[]{:S(2)}, u32[]{:S(2)}) collective-permute-start(f32[64,1152]{1,0:T(8,128)S(1)} %get-tuple-element.25), channel_id=1, source_target_pairs={{0,3},{1,0},{2,1},{3,2},{16,17},{17,18},{18,19},{19,16},{4,7},{5,4... | collective-permute-start | bytes 884744 | tf_op jit(solution)/shard_map/ppermute | solution.py:51
  69.5 1.9 %shard_map.53 = (f32[128,1152]{1,0:T(8,128)S(1)}, f32[128,1152]{1,0:T(8,128)S(1)}, f32[32,128]{1,0:T(8,128)}) custom-call(s32[10]{0:T(128)S(1)} %stack.43.place, f32[256,512]{1,0:T(8,128)S(1)} %get-tuple-element.18.slope_ref, f32[256,1152]{1,0:T(8,128)S(1)} %bitcast.19, f32[264,1152]{1,0:T(8,128)S(1)} %get-tuple-element.19.other_ref, ...), custom_call_target="tpu_custom_call" | custom-call | flops 452984832 | bytes 5627944 | tf_op jit(solution)/shard_map/pallas_call | solution.py:33
  71.3 6.7 %collective-permute-start.4 = (f32[128,1152]{1,0:T(8,128)S(1)}, f32[128,1152]{1,0:T(8,128)S(1)}, u32[]{:S(2)}, u32[]{:S(2)}) collective-permute-start(f32[128,1152]{1,0:T(8,128)S(1)} %get-tuple-element.22), channel_id=1, source_target_pairs={{0,32},{32,4},{4,36},{36,8},{8,40},{40,12},{12,44},{44,0},{16,60},... | collective-permute-start | bytes 1769480 | tf_op jit(solution)/shard_map/ppermute | solution.py:60
  78.1 4.3 %collective-permute-start.7 = (f32[64,1152]{1,0:T(8,128)}, f32[64,1152]{1,0:T(8,128)S(1)}, u32[]{:S(2)}, u32[]{:S(2)}) collective-permute-start(f32[64,1152]{1,0:T(8,128)} %get-tuple-element.26), channel_id=1, source_target_pairs={{0,1},{1,2},{2,3},{3,0},{16,19},{17,16},{18,17},{19,18},{4,5},{5,6... | collective-permute-start | bytes 884744 | tf_op jit(solution)/shard_map/ppermute | solution.py:51
  82.4 1.9 %collective-permute-start.6 = (f32[64,1152]{1,0:T(8,128)S(1)}, f32[64,1152]{1,0:T(8,128)S(1)}, u32[]{:S(2)}, u32[]{:S(2)}) collective-permute-start(f32[64,1152]{1,0:T(8,128)S(1)} %shard_map.54), channel_id=1, source_target_pairs={{0,3},{1,0},{2,1},{3,2},{16,17},{17,18},{18,19},{19,16},{4,7},{5,4... | collective-permute-start | bytes 884744 | tf_op jit(solution)/shard_map/ppermute | solution.py:51
  84.4 5.5 %all-to-all-start.2 = ((f32[32,1,128]{2,1,0:T(1,128)}), f32[32,1,128]{2,1,0:T(1,128)S(1)}, u32[]{:S(2)}, u32[]{:S(2)}) async-start(f32[32,1,128]{2,1,0:T(1,128)} %bitcast.14), calls=%async_computation.2 | async-start | bytes 32768 | tf_op jit(solution)/shard_map/all_to_all | solution.py:45
  91.1 7.3 %all-to-all-done.2 = f32[32,1,128]{2,1,0:T(1,128)S(1)} async-done(((f32[32,1,128]{2,1,0:T(1,128)}), f32[32,1,128]{2,1,0:T(1,128)S(1)}, u32[]{:S(2)}, u32[]{:S(2)}) %all-to-all-start.2) | async-done | bytes 16416 | tf_op jit(solution)/shard_map/all_to_all | solution.py:45
  99.4 3.7 %all-to-all-start.3 = ((f32[8,152,128]{2,1,0:T(8,128)}), f32[8,152,128]{2,1,0:T(8,128)S(1)}, u32[]{:S(2)}, u32[]{:S(2)}) async-start(f32[8,152,128]{2,1,0:T(8,128)} %shard_map.55), calls=%async_computation.3 | async-start | bytes 1245184 | tf_op jit(solution)/shard_map/all_to_all | solution.py:45
  103.7 2.4 %collective-permute-start.8 = (f32[16,1152]{1,0:T(8,128)S(1)}, f32[16,1152]{1,0:T(8,128)S(1)}, u32[]{:S(2)}, u32[]{:S(2)}) collective-permute-start(f32[16,1152]{1,0:T(8,128)S(1)} %get-tuple-element.29), channel_id=1, source_target_pairs={{0,8},{4,12},{8,0},{12,4},{16,24},{20,28},{24,16},{28,20},{1,9},{5... | collective-permute-start | bytes 221192 | tf_op jit(solution)/shard_map/ppermute | solution.py:51
  106.0 3.9 %collective-permute-start.9 = (f32[16,1152]{1,0:T(8,128)S(1)}, f32[16,1152]{1,0:T(8,128)S(1)}, u32[]{:S(2)}, u32[]{:S(2)}) collective-permute-start(f32[16,1152]{1,0:T(8,128)S(1)} %get-tuple-element.30), channel_id=1, source_target_pairs={{0,12},{4,0},{8,4},{12,8},{16,20},{20,24},{24,28},{28,16},{1,13},{... | collective-permute-start | bytes 221192 | tf_op jit(solution)/shard_map/ppermute | solution.py:51
  109.9 3.5 %collective-permute-start.10 = (f32[16,1152]{1,0:T(8,128)S(1)}, f32[16,1152]{1,0:T(8,128)S(1)}, u32[]{:S(2)}, u32[]{:S(2)}) collective-permute-start(f32[16,1152]{1,0:T(8,128)S(1)} %get-tuple-element.31), channel_id=1, source_target_pairs={{0,4},{4,8},{8,12},{12,0},{16,28},{20,16},{24,20},{28,24},{1,5},{5... | collective-permute-start | bytes 221192 | tf_op jit(solution)/shard_map/ppermute | solution.py:51
  113.4 2.4 %collective-permute-done.9.z2 = f32[16,1152]{1,0:T(8,128)S(1)} collective-permute-done((f32[16,1152]{1,0:T(8,128)S(1)}, f32[16,1152]{1,0:T(8,128)S(1)}, u32[]{:S(2)}, u32[]{:S(2)}) %collective-permute-start.9) | collective-permute-done | bytes 73760 | tf_op jit(solution)/shard_map/ppermute | solution.py:51
  115.9 1.9 %collective-permute-done.10.z3 = f32[16,1152]{1,0:T(8,128)S(1)} collective-permute-done((f32[16,1152]{1,0:T(8,128)S(1)}, f32[16,1152]{1,0:T(8,128)S(1)}, u32[]{:S(2)}, u32[]{:S(2)}) %collective-permute-start.10) | collective-permute-done | bytes 73760 | tf_op jit(solution)/shard_map/ppermute | solution.py:51
  118.7 2.3 %all-to-all-done.3.packed_ref = f32[8,152,128]{2,1,0:T(8,128)S(1)} async-done(((f32[8,152,128]{2,1,0:T(8,128)}), f32[8,152,128]{2,1,0:T(8,128)S(1)}, u32[]{:S(2)}, u32[]{:S(2)}) %all-to-all-start.3) | async-done | bytes 622624 | tf_op jit(solution)/shard_map/all_to_all | solution.py:45
  (23 shorter events, 7.8 us)
Async XLA Ops:
  0.6 9.4 %copy-start = (f32[16,1152]{1,0:T(8,128)S(1)}, f32[16,1152]{1,0:T(8,128)}, u32[]{:S(2)}) copy-start(f32[16,1152]{1,0:T(8,128)} %emb_ref.3) | copy-start | bytes 221188
  2.4 26.8 %all-to-all-start.1 = ((f32[8,16,1152]{2,1,0:T(8,128)}), f32[8,16,1152]{2,1,0:T(8,128)S(1)}, u32[]{:S(2)}, u32[]{:S(2)}) async-start(f32[8,16,1152]{2,1,0:T(8,128)} %tile.2), calls=%async_computation.1 | async-start | bytes 1179648 | tf_op jit(solution)/shard_map/all_to_all | solution.py:45
  29.4 18.1 %collective-permute-start = (f32[128,1152]{1,0:T(8,128)S(1)}, f32[128,1152]{1,0:T(8,128)S(1)}, u32[]{:S(2)}, u32[]{:S(2)}) collective-permute-start(f32[128,1152]{1,0:T(8,128)S(1)} %shard_map.50.a_ref), channel_id=1, source_target_pairs={{0,44},{32,0},{4,32},{36,4},{8,36},{40,8},{12,40},{44,12},{16,48},... | collective-permute-start | bytes 1769480 | tf_op jit(solution)/shard_map/ppermute | solution.py:60
  33.6 16.9 %all-to-all-start = ((f32[4,64,1152]{2,1,0:T(8,128)}), f32[4,64,1152]{2,1,0:T(8,128)S(1)}, u32[]{:S(2)}, u32[]{:S(2)}) async-start(f32[4,64,1152]{2,1,0:T(8,128)} %bitcast.10), calls=%async_computation | async-start | bytes 2359296 | tf_op jit(solution)/shard_map/all_to_all | solution.py:45
  37.6 12.9 %collective-permute-start.1 = (f32[128,1152]{1,0:T(8,128)S(1)}, f32[128,1152]{1,0:T(8,128)S(1)}, u32[]{:S(2)}, u32[]{:S(2)}) collective-permute-start(f32[128,1152]{1,0:T(8,128)S(1)} %shard_map.50.a_ref), channel_id=1, source_target_pairs={{0,16},{16,0},{1,17},{17,1},{2,18},{18,2},{3,19},{19,3},{4,20},{20... | collective-permute-start | bytes 1769480 | tf_op jit(solution)/shard_map/ppermute | solution.py:64
  47.5 4.5 %collective-permute-start.2 = (f32[128,1152]{1,0:T(8,128)S(1)}, f32[128,1152]{1,0:T(8,128)}, u32[]{:S(2)}, u32[]{:S(2)}) collective-permute-start(f32[128,1152]{1,0:T(8,128)S(1)} %collective-permute-done.b_ref), channel_id=1, source_target_pairs={{0,16},{16,0},{1,17},{17,1},{2,18},{18,2},{3,19},{19,3},{4,20},{20... | collective-permute-start | bytes 1769480 | tf_op jit(solution)/shard_map/ppermute | solution.py:64
  56.7 12.8 %collective-permute-start.3 = (f32[264,1152]{1,0:T(8,128)S(1)}, f32[264,1152]{1,0:T(8,128)S(1)}, u32[]{:S(2)}, u32[]{:S(2)}) collective-permute-start(f32[264,1152]{1,0:T(8,128)S(1)} %get-tuple-element.19.other_ref), channel_id=1, source_target_pairs={{0,16},{16,0},{1,17},{17,1},{2,18},{18,2},{3,19},{19,3},{4,20},{20... | collective-permute-start | bytes 3649544 | tf_op jit(solution)/shard_map/ppermute | solution.py:64
  67.3 15.1 %collective-permute-start.5 = (f32[64,1152]{1,0:T(8,128)S(1)}, f32[64,1152]{1,0:T(8,128)S(1)}, u32[]{:S(2)}, u32[]{:S(2)}) collective-permute-start(f32[64,1152]{1,0:T(8,128)S(1)} %get-tuple-element.25), channel_id=1, source_target_pairs={{0,3},{1,0},{2,1},{3,2},{16,17},{17,18},{18,19},{19,16},{4,7},{5,4... | collective-permute-start | bytes 884744 | tf_op jit(solution)/shard_map/ppermute | solution.py:51
  71.3 27.0 %collective-permute-start.4 = (f32[128,1152]{1,0:T(8,128)S(1)}, f32[128,1152]{1,0:T(8,128)S(1)}, u32[]{:S(2)}, u32[]{:S(2)}) collective-permute-start(f32[128,1152]{1,0:T(8,128)S(1)} %get-tuple-element.22), channel_id=1, source_target_pairs={{0,32},{32,4},{4,36},{36,8},{8,40},{40,12},{12,44},{44,0},{16,60},... | collective-permute-start | bytes 1769480 | tf_op jit(solution)/shard_map/ppermute | solution.py:60
  78.1 11.8 %collective-permute-start.7 = (f32[64,1152]{1,0:T(8,128)}, f32[64,1152]{1,0:T(8,128)S(1)}, u32[]{:S(2)}, u32[]{:S(2)}) collective-permute-start(f32[64,1152]{1,0:T(8,128)} %get-tuple-element.26), channel_id=1, source_target_pairs={{0,1},{1,2},{2,3},{3,0},{16,19},{17,16},{18,17},{19,18},{4,5},{5,6... | collective-permute-start | bytes 884744 | tf_op jit(solution)/shard_map/ppermute | solution.py:51
  82.4 8.7 %collective-permute-start.6 = (f32[64,1152]{1,0:T(8,128)S(1)}, f32[64,1152]{1,0:T(8,128)S(1)}, u32[]{:S(2)}, u32[]{:S(2)}) collective-permute-start(f32[64,1152]{1,0:T(8,128)S(1)} %shard_map.54), channel_id=1, source_target_pairs={{0,3},{1,0},{2,1},{3,2},{16,17},{17,18},{18,19},{19,16},{4,7},{5,4... | collective-permute-start | bytes 884744 | tf_op jit(solution)/shard_map/ppermute | solution.py:51
  84.4 14.0 %all-to-all-start.2 = ((f32[32,1,128]{2,1,0:T(1,128)}), f32[32,1,128]{2,1,0:T(1,128)S(1)}, u32[]{:S(2)}, u32[]{:S(2)}) async-start(f32[32,1,128]{2,1,0:T(1,128)} %bitcast.14), calls=%async_computation.2 | async-start | bytes 32768 | tf_op jit(solution)/shard_map/all_to_all | solution.py:45
  99.4 21.6 %copy-start.1 = (f32[16,1152]{1,0:T(8,128)S(1)}, f32[16,1152]{1,0:T(8,128)}, u32[]{:S(2)}) copy-start(f32[16,1152]{1,0:T(8,128)} %emb_ref.2) | copy-start | bytes 221188
  99.4 21.6 %all-to-all-start.3 = ((f32[8,152,128]{2,1,0:T(8,128)}), f32[8,152,128]{2,1,0:T(8,128)S(1)}, u32[]{:S(2)}, u32[]{:S(2)}) async-start(f32[8,152,128]{2,1,0:T(8,128)} %shard_map.55), calls=%async_computation.3 | async-start | bytes 1245184 | tf_op jit(solution)/shard_map/all_to_all | solution.py:45
  103.7 9.8 %collective-permute-start.8 = (f32[16,1152]{1,0:T(8,128)S(1)}, f32[16,1152]{1,0:T(8,128)S(1)}, u32[]{:S(2)}, u32[]{:S(2)}) collective-permute-start(f32[16,1152]{1,0:T(8,128)S(1)} %get-tuple-element.29), channel_id=1, source_target_pairs={{0,8},{4,12},{8,0},{12,4},{16,24},{20,28},{24,16},{28,20},{1,9},{5... | collective-permute-start | bytes 221192 | tf_op jit(solution)/shard_map/ppermute | solution.py:51
  106.0 9.9 %collective-permute-start.9 = (f32[16,1152]{1,0:T(8,128)S(1)}, f32[16,1152]{1,0:T(8,128)S(1)}, u32[]{:S(2)}, u32[]{:S(2)}) collective-permute-start(f32[16,1152]{1,0:T(8,128)S(1)} %get-tuple-element.30), channel_id=1, source_target_pairs={{0,12},{4,0},{8,4},{12,8},{16,20},{20,24},{24,28},{28,16},{1,13},{... | collective-permute-start | bytes 221192 | tf_op jit(solution)/shard_map/ppermute | solution.py:51
  109.9 7.9 %collective-permute-start.10 = (f32[16,1152]{1,0:T(8,128)S(1)}, f32[16,1152]{1,0:T(8,128)S(1)}, u32[]{:S(2)}, u32[]{:S(2)}) collective-permute-start(f32[16,1152]{1,0:T(8,128)S(1)} %get-tuple-element.31), channel_id=1, source_target_pairs={{0,4},{4,8},{8,12},{12,0},{16,28},{20,16},{24,20},{28,24},{1,5},{5... | collective-permute-start | bytes 221192 | tf_op jit(solution)/shard_map/ppermute | solution.py:51

commit v16 on v15

--- a/solution.py
+++ b/solution.py
@@ -158,7 +158,7 @@
         out[...] = x0[rows, :] + (x1[rows, :] + x2[rows, :])
 
 
-def pack_kernel(keep_ref, plane_ref, losses_ref, back_ref, ahead_ref, packed_out):
+def pack_kernel(keep_ref, plane_ref, losses_ref, first_ref, ahead_ref, packed_out):
     loss = jnp.full((8, LANES), jnp.sum(losses_ref[:, 0:1]))
     for y in range(NY):
         rows = pl.ds(y * ROWS, ROWS)
@@ -220,10 +220,10 @@
         vmem=20,
     )
     losses = exchange(loss, ("zl", "zh", "x"))
-    relay = turned(xs[3], "x", -1)
+    first = turned(xs[3], "x", -1)
     ahead = turned(xs[2], "x", 1)
     plane = planes(send, 1)
-    (relay,) = call(relay_kernel, (xs[1], relay), [shape(part, features)])
+    (relay,) = call(relay_kernel, (xs[1], first), [shape(part, features)])
     back = turned(relay, "x", -1)
     zs = call(
         split_kernel,
@@ -233,7 +233,7 @@
     )
     (packed,) = call(
         pack_kernel,
-        (keep, plane, losses, back, ahead),
+        (keep, plane, losses, first, ahead),
         [shape(NY, PACK + 8, LANES)],
         in_specs=[VMEM] * 3 + [ANY] * 2,
     )

time: 124 us -> 131 us (1.056)
  the two profiles are of different devices: /device:TPU:1 before, /device:TPU:8 now
where the time goes in v16:
time: 131 us; the launch traced here: 130 us
  starting transfers between devices  63.4 us (48%)
  waiting for transfers between devices  29.6 us (23%)
  blocking collectives  18.3 us (14%)
  Pallas kernels  15.3 us (12%)
  local copies, waits for them, and re-layouts  2.93 us (2%)
    all_to_all x4, starting transfers between devices, exchange(): return lax.all_to_all(values, axes, 0, 0, tiled=True)  29.7 us
    ppermute x6, starting transfers between devices, turned(): return lax.ppermute(values, ('c', axis), pairs)  19 us
    all_gather x1, blocking collectives, on_device(): image_z = lax.all_gather(image_emb, 'zh', axis=0, tiled=True)  18.3 us
    all_to_all x4, waiting for transfers between devices, exchange(): return lax.all_to_all(values, axes, 0, 0, tiled=True)  15.6 us
    pallas_call x10, Pallas kernels, call(): pl.pallas_call(kernel, out_shape=outs, in_specs=in_specs or [VMEM] * len(...  15.3 us
    ppermute x6, waiting for transfers between devices, turned(): return lax.ppermute(values, ('c', axis), pairs)  12.8 us
    ppermute x2, starting transfers between devices, planes(): return lax.ppermute(values, ('zl', 'c', 'zh'), pairs)  9.04 us
    ppermute x3, starting transfers between devices, other_core(): return lax.ppermute(values, 'c', [(0, 1), (1, 0)])  5.74 us
  transfers between devices with their start and end apart: 15, of which 8 were waited for; matrix products, arithmetic and copies ran while one was open for 0% of the time, Pallas kernels for 5%

profile of v16, /device:TPU:8, one launch (start us, length us, event | category | flops | bytes accessed | tf_op | source)
XLA Modules:
  0.0 130.4 jit_solution(1452689029853486865)
XLA Ops:
  0.6 1.8 %tile.2 = f32[8,16,1152]{2,1,0:T(8,128)} broadcast(f32[16,1152]{1,0:T(8,128)} %emb_ref.2), dimensions={1,2} | broadcast | bytes 663552 | tf_op jit(solution)/shard_map/tile | solution.py:188
  2.4 9.3 %all-to-all-start.1 = ((f32[8,16,1152]{2,1,0:T(8,128)}), f32[8,16,1152]{2,1,0:T(8,128)S(1)}, u32[]{:S(2)}, u32[]{:S(2)}) async-start(f32[8,16,1152]{2,1,0:T(8,128)} %tile.2), calls=%async_computation.1 | async-start | bytes 1179648 | tf_op jit(solution)/shard_map/all_to_all | solution.py:45
  11.7 18.3 %all_gather.3.image_ref = f32[64,1152]{1,0:T(8,128)S(1)} all-gather(f32[16,1152]{1,0:T(8,128)S(1)} %copy-done), channel_id=1, replica_groups=mesh['y'=8,'zl'=2,'c'=2,'zh'=4,'x'=4] {'zh'}, dimensions={0}, use_global_device_ids=true | all-gather | bytes 368640 | tf_op jit(solution)/shard_map/all_gather | solution.py:189
  31.4 7.1 %collective-permute-start = (f32[128,1152]{1,0:T(8,128)S(1)}, f32[128,1152]{1,0:T(8,128)S(1)}, u32[]{:S(2)}, u32[]{:S(2)}) collective-permute-start(f32[128,1152]{1,0:T(8,128)S(1)} %shard_map.50.a_ref), channel_id=1, source_target_pairs={{0,44},{32,0},{4,32},{36,4},{8,36},{40,8},{12,40},{44,12},{16,48},... | collective-permute-start | bytes 1769480 | tf_op jit(solution)/shard_map/ppermute | solution.py:60
  38.5 4.3 %all-to-all-start = ((f32[4,64,1152]{2,1,0:T(8,128)}), f32[4,64,1152]{2,1,0:T(8,128)S(1)}, u32[]{:S(2)}, u32[]{:S(2)}) async-start(f32[4,64,1152]{2,1,0:T(8,128)} %bitcast.10), calls=%async_computation | async-start | bytes 2359296 | tf_op jit(solution)/shard_map/all_to_all | solution.py:45
  42.8 1.9 %collective-permute-start.1 = (f32[128,1152]{1,0:T(8,128)S(1)}, f32[128,1152]{1,0:T(8,128)S(1)}, u32[]{:S(2)}, u32[]{:S(2)}) collective-permute-start(f32[128,1152]{1,0:T(8,128)S(1)} %shard_map.50.a_ref), channel_id=1, source_target_pairs={{0,16},{16,0},{1,17},{17,1},{2,18},{18,2},{3,19},{19,3},{4,20},{20... | collective-permute-start | bytes 1769480 | tf_op jit(solution)/shard_map/ppermute | solution.py:64
  45.9 1.9 %collective-permute-start.2 = (f32[128,1152]{1,0:T(8,128)S(1)}, f32[128,1152]{1,0:T(8,128)}, u32[]{:S(2)}, u32[]{:S(2)}) collective-permute-start(f32[128,1152]{1,0:T(8,128)S(1)} %collective-permute-done.b_ref), channel_id=1, source_target_pairs={{0,16},{16,0},{1,17},{17,1},{2,18},{18,2},{3,19},{19,3},{4,20},{20... | collective-permute-start | bytes 1769480 | tf_op jit(solution)/shard_map/ppermute | solution.py:64
  48.0 6.4 %all-to-all-done = f32[4,64,1152]{2,1,0:T(8,128)S(1)} async-done(((f32[4,64,1152]{2,1,0:T(8,128)}), f32[4,64,1152]{2,1,0:T(8,128)S(1)}, u32[]{:S(2)}, u32[]{:S(2)}) %all-to-all-start) | async-done | bytes 1179680 | tf_op jit(solution)/shard_map/all_to_all | solution.py:45
  54.4 4.9 %shard_map.51 = (f32[256,512]{1,0:T(8,128)S(1)}, f32[264,1152]{1,0:T(8,128)S(1)}) custom-call(s32[10]{0:T(128)S(1)} %stack.43.place, f32[256,1152]{1,0:T(8,128)S(1)} %bitcast.18, f32[128,1152]{1,0:T(8,128)S(1)} %shard_map.50.a_ref, f32[128,1152]{1,0:T(8,128)S(1)} %collective-permute-done.b_ref, f32[128,1152]{1,0:T(8,128)S(1)} %collective-permute-done.1.c_ref, ...), custom_call_target="tpu_custom_call" | custom-call | flops 1358954496 | bytes 5279784 | tf_op jit(solution)/shard_map/pallas_call | solution.py:33
  59.3 1.9 %collective-permute-start.3 = (f32[264,1152]{1,0:T(8,128)S(1)}, f32[264,1152]{1,0:T(8,128)S(1)}, u32[]{:S(2)}, u32[]{:S(2)}) collective-permute-start(f32[264,1152]{1,0:T(8,128)S(1)} %get-tuple-element.19.other_ref), channel_id=1, source_target_pairs={{0,16},{16,0},{1,17},{17,1},{2,18},{18,2},{3,19},{19,3},{4,20},{20... | collective-permute-start | bytes 3649544 | tf_op jit(solution)/shard_map/ppermute | solution.py:64
  62.3 3.9 %shard_map.52 = (f32[64,1152]{1,0:T(8,128)S(1)}, f32[64,1152]{1,0:T(8,128)S(1)}, f32[64,1152]{1,0:T(8,128)}, f32[64,1152]{1,0:T(8,128)}) custom-call(f32[256,512]{1,0:T(8,128)S(1)} %get-tuple-element.18.slope_ref, f32[128,1152]{1,0:T(8,128)S(1)} %shard_map.50.a_ref, f32[128,1152]{1,0:T(8,128)S(1)} %collective-permute-done.b_ref, f32[128,1152]{1,0:T(8,128)S(1)} %copy-done.3, ...), custom_call_target="tpu_custom_call" | custom-call | flops 905969664 | bytes 4063232 | tf_op jit(solution)/shard_map/pallas_call | solution.py:33
  66.2 1.9 %shard_map.53 = (f32[128,1152]{1,0:T(8,128)S(1)}, f32[128,1152]{1,0:T(8,128)S(1)}, f32[32,128]{1,0:T(8,128)}) custom-call(s32[10]{0:T(128)S(1)} %stack.43.place, f32[256,512]{1,0:T(8,128)S(1)} %get-tuple-element.18.slope_ref, f32[256,1152]{1,0:T(8,128)S(1)} %bitcast.19, f32[264,1152]{1,0:T(8,128)S(1)} %get-tuple-element.19.other_ref, ...), custom_call_target="tpu_custom_call" | custom-call | flops 452984832 | bytes 5627944 | tf_op jit(solution)/shard_map/pallas_call | solution.py:33
  68.1 1.9 %collective-permute-start.4 = (f32[128,1152]{1,0:T(8,128)S(1)}, f32[128,1152]{1,0:T(8,128)S(1)}, u32[]{:S(2)}, u32[]{:S(2)}) collective-permute-start(f32[128,1152]{1,0:T(8,128)S(1)} %get-tuple-element.22), channel_id=1, source_target_pairs={{0,32},{32,4},{4,36},{36,8},{8,40},{40,12},{12,44},{44,0},{16,60},... | collective-permute-start | bytes 1769480 | tf_op jit(solution)/shard_map/ppermute | solution.py:60
  70.0 3.1 %collective-permute-start.5 = (f32[64,1152]{1,0:T(8,128)}, f32[64,1152]{1,0:T(8,128)S(1)}, u32[]{:S(2)}, u32[]{:S(2)}) collective-permute-start(f32[64,1152]{1,0:T(8,128)} %get-tuple-element.24), channel_id=1, source_target_pairs={{0,3},{1,0},{2,1},{3,2},{16,17},{17,18},{18,19},{19,16},{4,7},{5,4... | collective-permute-start | bytes 884744 | tf_op jit(solution)/shard_map/ppermute | solution.py:51
  73.1 2.8 %collective-permute-start.6 = (f32[64,1152]{1,0:T(8,128)}, f32[64,1152]{1,0:T(8,128)S(1)}, u32[]{:S(2)}, u32[]{:S(2)}) collective-permute-start(f32[64,1152]{1,0:T(8,128)} %get-tuple-element.25), channel_id=1, source_target_pairs={{0,1},{1,2},{2,3},{3,0},{16,19},{17,16},{18,17},{19,18},{4,5},{5,6... | collective-permute-start | bytes 884744 | tf_op jit(solution)/shard_map/ppermute | solution.py:51
  75.9 8.3 %all-to-all-start.2 = ((f32[32,1,128]{2,1,0:T(1,128)}), f32[32,1,128]{2,1,0:T(1,128)S(1)}, u32[]{:S(2)}, u32[]{:S(2)}) async-start(f32[32,1,128]{2,1,0:T(1,128)} %bitcast.14), calls=%async_computation.2 | async-start | bytes 32768 | tf_op jit(solution)/shard_map/all_to_all | solution.py:45
  84.6 9.2 %all-to-all-done.2 = f32[32,1,128]{2,1,0:T(1,128)S(1)} async-done(((f32[32,1,128]{2,1,0:T(1,128)}), f32[32,1,128]{2,1,0:T(1,128)S(1)}, u32[]{:S(2)}, u32[]{:S(2)}) %all-to-all-start.2) | async-done | bytes 16416 | tf_op jit(solution)/shard_map/all_to_all | solution.py:45
  94.8 7.8 %all-to-all-start.3 = ((f32[8,152,128]{2,1,0:T(8,128)}), f32[8,152,128]{2,1,0:T(8,128)S(1)}, u32[]{:S(2)}, u32[]{:S(2)}) async-start(f32[8,152,128]{2,1,0:T(8,128)} %shard_map.54), calls=%async_computation.3 | async-start | bytes 1245184 | tf_op jit(solution)/shard_map/all_to_all | solution.py:45
  102.7 3.1 %collective-permute-start.7 = (f32[64,1152]{1,0:T(8,128)S(1)}, f32[64,1152]{1,0:T(8,128)S(1)}, u32[]{:S(2)}, u32[]{:S(2)}) collective-permute-start(f32[64,1152]{1,0:T(8,128)S(1)} %shard_map.56), channel_id=1, source_target_pairs={{0,3},{1,0},{2,1},{3,2},{16,17},{17,18},{18,19},{19,16},{4,7},{5,4... | collective-permute-start | bytes 884744 | tf_op jit(solution)/shard_map/ppermute | solution.py:51
  105.8 5.5 %collective-permute-done.7.x1 = f32[64,1152]{1,0:T(8,128)S(1)} collective-permute-done((f32[64,1152]{1,0:T(8,128)S(1)}, f32[64,1152]{1,0:T(8,128)S(1)}, u32[]{:S(2)}, u32[]{:S(2)}) %collective-permute-start.7) | collective-permute-done | bytes 294944 | tf_op jit(solution)/shard_map/ppermute | solution.py:51
  111.9 2.6 %collective-permute-start.8 = (f32[16,1152]{1,0:T(8,128)S(1)}, f32[16,1152]{1,0:T(8,128)S(1)}, u32[]{:S(2)}, u32[]{:S(2)}) collective-permute-start(f32[16,1152]{1,0:T(8,128)S(1)} %get-tuple-element.29), channel_id=1, source_target_pairs={{0,8},{4,12},{8,0},{12,4},{16,24},{20,28},{24,16},{28,20},{1,9},{5... | collective-permute-start | bytes 221192 | tf_op jit(solution)/shard_map/ppermute | solution.py:51
  114.5 5.4 %collective-permute-start.9 = (f32[16,1152]{1,0:T(8,128)S(1)}, f32[16,1152]{1,0:T(8,128)S(1)}, u32[]{:S(2)}, u32[]{:S(2)}) collective-permute-start(f32[16,1152]{1,0:T(8,128)S(1)} %get-tuple-element.30), channel_id=1, source_target_pairs={{0,12},{4,0},{8,4},{12,8},{16,20},{20,24},{24,28},{28,16},{1,13},{... | collective-permute-start | bytes 221192 | tf_op jit(solution)/shard_map/ppermute | solution.py:51
  120.0 1.9 %collective-permute-start.10 = (f32[16,1152]{1,0:T(8,128)S(1)}, f32[16,1152]{1,0:T(8,128)S(1)}, u32[]{:S(2)}, u32[]{:S(2)}) collective-permute-start(f32[16,1152]{1,0:T(8,128)S(1)} %get-tuple-element.31), channel_id=1, source_target_pairs={{0,4},{4,8},{8,12},{12,0},{16,28},{20,16},{24,20},{28,24},{1,5},{5... | collective-permute-start | bytes 221192 | tf_op jit(solution)/shard_map/ppermute | solution.py:51
  124.1 4.7 %collective-permute-done.10.z3 = f32[16,1152]{1,0:T(8,128)S(1)} collective-permute-done((f32[16,1152]{1,0:T(8,128)S(1)}, f32[16,1152]{1,0:T(8,128)S(1)}, u32[]{:S(2)}, u32[]{:S(2)}) %collective-permute-start.10) | collective-permute-done | bytes 73760 | tf_op jit(solution)/shard_map/ppermute | solution.py:51
  (27 shorter events, 9.6 us)
Async XLA Ops:
  0.6 11.1 %copy-start = (f32[16,1152]{1,0:T(8,128)S(1)}, f32[16,1152]{1,0:T(8,128)}, u32[]{:S(2)}) copy-start(f32[16,1152]{1,0:T(8,128)} %emb_ref.3) | copy-start | bytes 221188
  2.4 28.8 %all-to-all-start.1 = ((f32[8,16,1152]{2,1,0:T(8,128)}), f32[8,16,1152]{2,1,0:T(8,128)S(1)}, u32[]{:S(2)}, u32[]{:S(2)}) async-start(f32[8,16,1152]{2,1,0:T(8,128)} %tile.2), calls=%async_computation.1 | async-start | bytes 1179648 | tf_op jit(solution)/shard_map/all_to_all | solution.py:45
  31.4 14.5 %collective-permute-start = (f32[128,1152]{1,0:T(8,128)S(1)}, f32[128,1152]{1,0:T(8,128)S(1)}, u32[]{:S(2)}, u32[]{:S(2)}) collective-permute-start(f32[128,1152]{1,0:T(8,128)S(1)} %shard_map.50.a_ref), channel_id=1, source_target_pairs={{0,44},{32,0},{4,32},{36,4},{8,36},{40,8},{12,40},{44,12},{16,48},... | collective-permute-start | bytes 1769480 | tf_op jit(solution)/shard_map/ppermute | solution.py:60
  38.5 15.9 %all-to-all-start = ((f32[4,64,1152]{2,1,0:T(8,128)}), f32[4,64,1152]{2,1,0:T(8,128)S(1)}, u32[]{:S(2)}, u32[]{:S(2)}) async-start(f32[4,64,1152]{2,1,0:T(8,128)} %bitcast.10), calls=%async_computation | async-start | bytes 2359296 | tf_op jit(solution)/shard_map/all_to_all | solution.py:45
  42.8 11.6 %collective-permute-start.1 = (f32[128,1152]{1,0:T(8,128)S(1)}, f32[128,1152]{1,0:T(8,128)S(1)}, u32[]{:S(2)}, u32[]{:S(2)}) collective-permute-start(f32[128,1152]{1,0:T(8,128)S(1)} %shard_map.50.a_ref), channel_id=1, source_target_pairs={{0,16},{16,0},{1,17},{17,1},{2,18},{18,2},{3,19},{19,3},{4,20},{20... | collective-permute-start | bytes 1769480 | tf_op jit(solution)/shard_map/ppermute | solution.py:64
  45.9 8.5 %collective-permute-start.2 = (f32[128,1152]{1,0:T(8,128)S(1)}, f32[128,1152]{1,0:T(8,128)}, u32[]{:S(2)}, u32[]{:S(2)}) collective-permute-start(f32[128,1152]{1,0:T(8,128)S(1)} %collective-permute-done.b_ref), channel_id=1, source_target_pairs={{0,16},{16,0},{1,17},{17,1},{2,18},{18,2},{3,19},{19,3},{4,20},{20... | collective-permute-start | bytes 1769480 | tf_op jit(solution)/shard_map/ppermute | solution.py:64
  54.4 4.9 %copy-start.2 = (f32[128,1152]{1,0:T(8,128)}, f32[128,1152]{1,0:T(8,128)S(1)}, u32[]{:S(2)}) copy-start(f32[128,1152]{1,0:T(8,128)S(1)} %collective-permute-done.1.c_ref) | copy-start | bytes 1769476
  59.3 6.9 %collective-permute-start.3 = (f32[264,1152]{1,0:T(8,128)S(1)}, f32[264,1152]{1,0:T(8,128)S(1)}, u32[]{:S(2)}, u32[]{:S(2)}) collective-permute-start(f32[264,1152]{1,0:T(8,128)S(1)} %get-tuple-element.19.other_ref), channel_id=1, source_target_pairs={{0,16},{16,0},{1,17},{17,1},{2,18},{18,2},{3,19},{19,3},{4,20},{20... | collective-permute-start | bytes 3649544 | tf_op jit(solution)/shard_map/ppermute | solution.py:64
  61.3 1.1 copy-start.3
  68.1 25.7 %collective-permute-start.4 = (f32[128,1152]{1,0:T(8,128)S(1)}, f32[128,1152]{1,0:T(8,128)S(1)}, u32[]{:S(2)}, u32[]{:S(2)}) collective-permute-start(f32[128,1152]{1,0:T(8,128)S(1)} %get-tuple-element.22), channel_id=1, source_target_pairs={{0,32},{32,4},{4,36},{36,8},{8,40},{40,12},{12,44},{44,0},{16,60},... | collective-permute-start | bytes 1769480 | tf_op jit(solution)/shard_map/ppermute | solution.py:60
  70.0 14.2 %collective-permute-start.5 = (f32[64,1152]{1,0:T(8,128)}, f32[64,1152]{1,0:T(8,128)S(1)}, u32[]{:S(2)}, u32[]{:S(2)}) collective-permute-start(f32[64,1152]{1,0:T(8,128)} %get-tuple-element.24), channel_id=1, source_target_pairs={{0,3},{1,0},{2,1},{3,2},{16,17},{17,18},{18,19},{19,16},{4,7},{5,4... | collective-permute-start | bytes 884744 | tf_op jit(solution)/shard_map/ppermute | solution.py:51
  73.1 11.5 %collective-permute-start.6 = (f32[64,1152]{1,0:T(8,128)}, f32[64,1152]{1,0:T(8,128)S(1)}, u32[]{:S(2)}, u32[]{:S(2)}) collective-permute-start(f32[64,1152]{1,0:T(8,128)} %get-tuple-element.25), channel_id=1, source_target_pairs={{0,1},{1,2},{2,3},{3,0},{16,19},{17,16},{18,17},{19,18},{4,5},{5,6... | collective-permute-start | bytes 884744 | tf_op jit(solution)/shard_map/ppermute | solution.py:51
  75.9 18.0 %all-to-all-start.2 = ((f32[32,1,128]{2,1,0:T(1,128)}), f32[32,1,128]{2,1,0:T(1,128)S(1)}, u32[]{:S(2)}, u32[]{:S(2)}) async-start(f32[32,1,128]{2,1,0:T(1,128)} %bitcast.14), calls=%async_computation.2 | async-start | bytes 32768 | tf_op jit(solution)/shard_map/all_to_all | solution.py:45
  94.8 34.8 %all-to-all-start.3 = ((f32[8,152,128]{2,1,0:T(8,128)}), f32[8,152,128]{2,1,0:T(8,128)S(1)}, u32[]{:S(2)}, u32[]{:S(2)}) async-start(f32[8,152,128]{2,1,0:T(8,128)} %shard_map.54), calls=%async_computation.3 | async-start | bytes 1245184 | tf_op jit(solution)/shard_map/all_to_all | solution.py:45
  102.6 27.0 %copy-start.1 = (f32[16,1152]{1,0:T(8,128)S(1)}, f32[16,1152]{1,0:T(8,128)}, u32[]{:S(2)}) copy-start(f32[16,1152]{1,0:T(8,128)} %emb_ref.2) | copy-start | bytes 221188
  102.7 8.6 %collective-permute-start.7 = (f32[64,1152]{1,0:T(8,128)S(1)}, f32[64,1152]{1,0:T(8,128)S(1)}, u32[]{:S(2)}, u32[]{:S(2)}) collective-permute-start(f32[64,1152]{1,0:T(8,128)S(1)} %shard_map.56), channel_id=1, source_target_pairs={{0,3},{1,0},{2,1},{3,2},{16,17},{17,18},{18,19},{19,16},{4,7},{5,4... | collective-permute-start | bytes 884744 | tf_op jit(solution)/shard_map/ppermute | solution.py:51
  111.9 11.1 %collective-permute-start.8 = (f32[16,1152]{1,0:T(8,128)S(1)}, f32[16,1152]{1,0:T(8,128)S(1)}, u32[]{:S(2)}, u32[]{:S(2)}) collective-permute-start(f32[16,1152]{1,0:T(8,128)S(1)} %get-tuple-element.29), channel_id=1, source_target_pairs={{0,8},{4,12},{8,0},{12,4},{16,24},{20,28},{24,16},{28,20},{1,9},{5... | collective-permute-start | bytes 221192 | tf_op jit(solution)/shard_map/ppermute | solution.py:51
  114.5 9.6 %collective-permute-start.9 = (f32[16,1152]{1,0:T(8,128)S(1)}, f32[16,1152]{1,0:T(8,128)S(1)}, u32[]{:S(2)}, u32[]{:S(2)}) collective-permute-start(f32[16,1152]{1,0:T(8,128)S(1)} %get-tuple-element.30), channel_id=1, source_target_pairs={{0,12},{4,0},{8,4},{12,8},{16,20},{20,24},{24,28},{28,16},{1,13},{... | collective-permute-start | bytes 221192 | tf_op jit(solution)/shard_map/ppermute | solution.py:51
  120.0 8.8 %collective-permute-start.10 = (f32[16,1152]{1,0:T(8,128)S(1)}, f32[16,1152]{1,0:T(8,128)S(1)}, u32[]{:S(2)}, u32[]{:S(2)}) collective-permute-start(f32[16,1152]{1,0:T(8,128)S(1)} %get-tuple-element.31), channel_id=1, source_target_pairs={{0,4},{4,8},{8,12},{12,0},{16,28},{20,16},{24,20},{28,24},{1,5},{5... | collective-permute-start | bytes 221192 | tf_op jit(solution)/shard_map/ppermute | solution.py:51

commit v17 on v14

--- a/solution.py
+++ b/solution.py
@@ -148,8 +148,8 @@
         loss_out[pl.ds(8 * k, 8), :] = other_ref[last, first] + received_ref[last, first]
 
 
-def relay_kernel(left, right, out):
-    out[...] = left[...] + right[...]
+def relay_kernel(left, right, *refs):
+    refs[-1][...] = left[...] + right[...]
 
 
 def split_kernel(place, x0, x1, x2, *outs):
@@ -223,7 +223,9 @@
     relay = turned(xs[3], "x", -1)
     ahead = turned(xs[2], "x", 1)
     plane = planes(send, 1)
-    (relay,) = call(relay_kernel, (xs[1], relay), [shape(part, features)])
+    (relay,) = call(
+        relay_kernel, (xs[1], relay, losses), [shape(part, features)], in_specs=[VMEM] * 2 + [ANY]
+    )
     back = turned(relay, "x", -1)
     zs = call(
         split_kernel,

time: 123 us -> 127 us (1.033)
  waiting for transfers between devices: 17.4 us -> 19.3 us
    ppermute x6, waiting for transfers between devices: 7.02 us -> 12 us  [turned(): return lax.ppermute(values, ('c', axis), pairs)]
    all_to_all x4, waiting for transfers between devices: 8.61 us -> 5.56 us  [exchange(): return lax.all_to_all(values, axes, 0, 0, tiled=True)]
where the time goes in v17:
time: 127 us; the launch traced here: 125 us
  starting transfers between devices  68.9 us (54%)
  waiting for transfers between devices  19.3 us (15%)
  blocking collectives  18 us (14%)
  Pallas kernels  15 us (12%)
  local copies, waits for them, and re-layouts  2.93 us (2%)
    all_to_all x4, starting transfers between devices, exchange(): return lax.all_to_all(values, axes, 0, 0, tiled=True)  20.6 us
    ppermute x3, starting transfers between devices, other_core(): return lax.ppermute(values, 'c', [(0, 1), (1, 0)])  19.4 us
    ppermute x6, starting transfers between devices, turned(): return lax.ppermute(values, ('c', axis), pairs)  18.1 us
    all_gather x1, blocking collectives, on_device(): image_z = lax.all_gather(image_emb, 'zh', axis=0, tiled=True)  18 us
    pallas_call x11, Pallas kernels, call(): pl.pallas_call(kernel, out_shape=outs, in_specs=in_specs or [VMEM] * len(...  15 us
    ppermute x6, waiting for transfers between devices, turned(): return lax.ppermute(values, ('c', axis), pairs)  12 us
    ppermute x2, starting transfers between devices, planes(): return lax.ppermute(values, ('zl', 'c', 'zh'), pairs)  10.9 us
    all_to_all x4, waiting for transfers between devices, exchange(): return lax.all_to_all(values, axes, 0, 0, tiled=True)  5.56 us
  transfers between devices with their start and end apart: 15, of which 8 were waited for; matrix products, arithmetic and copies ran while one was open for 0% of the time, Pallas kernels for 7%

profile of v17, /device:TPU:1, one launch (start us, length us, event | category | flops | bytes accessed | tf_op | source)
XLA Modules:
  0.0 125.1 jit_solution(16037726595741345587)
XLA Ops:
  0.6 1.8 %tile.2 = f32[8,16,1152]{2,1,0:T(8,128)} broadcast(f32[16,1152]{1,0:T(8,128)} %emb_ref.2), dimensions={1,2} | broadcast | bytes 663552 | tf_op jit(solution)/shard_map/tile | solution.py:188
  2.4 7.7 %all-to-all-start.1 = ((f32[8,16,1152]{2,1,0:T(8,128)}), f32[8,16,1152]{2,1,0:T(8,128)S(1)}, u32[]{:S(2)}, u32[]{:S(2)}) async-start(f32[8,16,1152]{2,1,0:T(8,128)} %tile.2), calls=%async_computation.1 | async-start | bytes 1179648 | tf_op jit(solution)/shard_map/all_to_all | solution.py:45
  10.1 18.0 %all_gather.3.image_ref = f32[64,1152]{1,0:T(8,128)S(1)} all-gather(f32[16,1152]{1,0:T(8,128)S(1)} %copy-done), channel_id=1, replica_groups=mesh['y'=8,'zl'=2,'c'=2,'zh'=4,'x'=4] {'zh'}, dimensions={0}, use_global_device_ids=true | all-gather | bytes 368640 | tf_op jit(solution)/shard_map/all_gather | solution.py:189
  29.4 4.2 %collective-permute-start = (f32[128,1152]{1,0:T(8,128)S(1)}, f32[128,1152]{1,0:T(8,128)S(1)}, u32[]{:S(2)}, u32[]{:S(2)}) collective-permute-start(f32[128,1152]{1,0:T(8,128)S(1)} %shard_map.50.a_ref), channel_id=1, source_target_pairs={{0,44},{32,0},{4,32},{36,4},{8,36},{40,8},{12,40},{44,12},{16,48},... | collective-permute-start | bytes 1769480 | tf_op jit(solution)/shard_map/ppermute | solution.py:60
  33.6 4.0 %all-to-all-start = ((f32[4,64,1152]{2,1,0:T(8,128)}), f32[4,64,1152]{2,1,0:T(8,128)S(1)}, u32[]{:S(2)}, u32[]{:S(2)}) async-start(f32[4,64,1152]{2,1,0:T(8,128)} %bitcast.10), calls=%async_computation | async-start | bytes 2359296 | tf_op jit(solution)/shard_map/all_to_all | solution.py:45
  37.6 9.6 %collective-permute-start.1 = (f32[128,1152]{1,0:T(8,128)S(1)}, f32[128,1152]{1,0:T(8,128)S(1)}, u32[]{:S(2)}, u32[]{:S(2)}) collective-permute-start(f32[128,1152]{1,0:T(8,128)S(1)} %shard_map.50.a_ref), channel_id=1, source_target_pairs={{0,16},{16,0},{1,17},{17,1},{2,18},{18,2},{3,19},{19,3},{4,20},{20... | collective-permute-start | bytes 1769480 | tf_op jit(solution)/shard_map/ppermute | solution.py:64
  47.5 2.8 %collective-permute-start.2 = (f32[128,1152]{1,0:T(8,128)S(1)}, f32[128,1152]{1,0:T(8,128)}, u32[]{:S(2)}, u32[]{:S(2)}) collective-permute-start(f32[128,1152]{1,0:T(8,128)S(1)} %collective-permute-done.b_ref), channel_id=1, source_target_pairs={{0,16},{16,0},{1,17},{17,1},{2,18},{18,2},{3,19},{19,3},{4,20},{20... | collective-permute-start | bytes 1769480 | tf_op jit(solution)/shard_map/ppermute | solution.py:64
  50.5 1.5 %collective-permute-done.2.d_ref = f32[128,1152]{1,0:T(8,128)} collective-permute-done((f32[128,1152]{1,0:T(8,128)S(1)}, f32[128,1152]{1,0:T(8,128)}, u32[]{:S(2)}, u32[]{:S(2)}) %collective-permute-start.2) | collective-permute-done | bytes 589856 | tf_op jit(solution)/shard_map/ppermute | solution.py:64
  52.0 4.7 %shard_map.51 = (f32[256,512]{1,0:T(8,128)S(1)}, f32[264,1152]{1,0:T(8,128)S(1)}) custom-call(s32[10]{0:T(128)S(1)} %stack.43.place, f32[256,1152]{1,0:T(8,128)S(1)} %bitcast.18, f32[128,1152]{1,0:T(8,128)S(1)} %shard_map.50.a_ref, f32[128,1152]{1,0:T(8,128)S(1)} %collective-permute-done.b_ref, f32[128,1152]{1,0:T(8,128)S(1)} %collective-permute-done.1.c_ref, ...), custom_call_target="tpu_custom_call" | custom-call | flops 1358954496 | bytes 5279784 | tf_op jit(solution)/shard_map/pallas_call | solution.py:33
  56.7 7.0 %collective-permute-start.3 = (f32[264,1152]{1,0:T(8,128)S(1)}, f32[264,1152]{1,0:T(8,128)S(1)}, u32[]{:S(2)}, u32[]{:S(2)}) collective-permute-start(f32[264,1152]{1,0:T(8,128)S(1)} %get-tuple-element.19.other_ref), channel_id=1, source_target_pairs={{0,16},{16,0},{1,17},{17,1},{2,18},{18,2},{3,19},{19,3},{4,20},{20... | collective-permute-start | bytes 3649544 | tf_op jit(solution)/shard_map/ppermute | solution.py:64
  64.8 3.8 %shard_map.52 = (f32[64,1152]{1,0:T(8,128)S(1)}, f32[64,1152]{1,0:T(8,128)S(1)}, f32[64,1152]{1,0:T(8,128)S(1)}, f32[64,1152]{1,0:T(8,128)}) custom-call(f32[256,512]{1,0:T(8,128)S(1)} %get-tuple-element.18.slope_ref, f32[128,1152]{1,0:T(8,128)S(1)} %shard_map.50.a_ref, f32[128,1152]{1,0:T(8,128)S(1)} %collective-permute-done.b_ref, ...), custom_call_target="tpu_custom_call" | custom-call | flops 905969664 | bytes 4063232 | tf_op jit(solution)/shard_map/pallas_call | solution.py:33
  68.6 2.2 %collective-permute-start.5 = (f32[64,1152]{1,0:T(8,128)}, f32[64,1152]{1,0:T(8,128)S(1)}, u32[]{:S(2)}, u32[]{:S(2)}) collective-permute-start(f32[64,1152]{1,0:T(8,128)} %get-tuple-element.25), channel_id=1, source_target_pairs={{0,3},{1,0},{2,1},{3,2},{16,17},{17,18},{18,19},{19,16},{4,7},{5,4... | collective-permute-start | bytes 884744 | tf_op jit(solution)/shard_map/ppermute | solution.py:51
  70.8 1.9 %shard_map.53 = (f32[128,1152]{1,0:T(8,128)S(1)}, f32[128,1152]{1,0:T(8,128)S(1)}, f32[32,128]{1,0:T(8,128)}) custom-call(s32[10]{0:T(128)S(1)} %stack.43.place, f32[256,512]{1,0:T(8,128)S(1)} %get-tuple-element.18.slope_ref, f32[256,1152]{1,0:T(8,128)S(1)} %bitcast.19, f32[264,1152]{1,0:T(8,128)S(1)} %get-tuple-element.19.other_ref, ...), custom_call_target="tpu_custom_call" | custom-call | flops 452984832 | bytes 5627944 | tf_op jit(solution)/shard_map/pallas_call | solution.py:33
  72.7 6.7 %collective-permute-start.4 = (f32[128,1152]{1,0:T(8,128)S(1)}, f32[128,1152]{1,0:T(8,128)S(1)}, u32[]{:S(2)}, u32[]{:S(2)}) collective-permute-start(f32[128,1152]{1,0:T(8,128)S(1)} %get-tuple-element.22), channel_id=1, source_target_pairs={{0,32},{32,4},{4,36},{36,8},{8,40},{40,12},{12,44},{44,0},{16,60},... | collective-permute-start | bytes 1769480 | tf_op jit(solution)/shard_map/ppermute | solution.py:60
  79.4 5.3 %all-to-all-start.2 = ((f32[32,1,128]{2,1,0:T(1,128)}), f32[32,1,128]{2,1,0:T(1,128)S(1)}, u32[]{:S(2)}, u32[]{:S(2)}) async-start(f32[32,1,128]{2,1,0:T(1,128)} %bitcast.14), calls=%async_computation.2 | async-start | bytes 32768 | tf_op jit(solution)/shard_map/all_to_all | solution.py:45
  84.7 4.3 %collective-permute-start.7 = (f32[64,1152]{1,0:T(8,128)}, f32[64,1152]{1,0:T(8,128)S(1)}, u32[]{:S(2)}, u32[]{:S(2)}) collective-permute-start(f32[64,1152]{1,0:T(8,128)} %copy-done.4), channel_id=1, source_target_pairs={{0,1},{1,2},{2,3},{3,0},{16,19},{17,16},{18,17},{19,18},{4,5},{5,6... | collective-permute-start | bytes 884744 | tf_op jit(solution)/shard_map/ppermute | solution.py:51
  89.0 4.1 %all-to-all-done.2 = f32[32,1,128]{2,1,0:T(1,128)S(1)} async-done(((f32[32,1,128]{2,1,0:T(1,128)}), f32[32,1,128]{2,1,0:T(1,128)S(1)}, u32[]{:S(2)}, u32[]{:S(2)}) %all-to-all-start.2) | async-done | bytes 16416 | tf_op jit(solution)/shard_map/all_to_all | solution.py:45
  93.2 2.2 %collective-permute-start.6 = (f32[64,1152]{1,0:T(8,128)S(1)}, f32[64,1152]{1,0:T(8,128)S(1)}, u32[]{:S(2)}, u32[]{:S(2)}) collective-permute-start(f32[64,1152]{1,0:T(8,128)S(1)} %shard_map.54), channel_id=1, source_target_pairs={{0,3},{1,0},{2,1},{3,2},{16,17},{17,18},{18,19},{19,16},{4,7},{5,4... | collective-permute-start | bytes 884744 | tf_op jit(solution)/shard_map/ppermute | solution.py:51
  95.4 6.4 %collective-permute-done.6.back_ref.x1 = f32[64,1152]{1,0:T(8,128)S(1)} collective-permute-done((f32[64,1152]{1,0:T(8,128)S(1)}, f32[64,1152]{1,0:T(8,128)S(1)}, u32[]{:S(2)}, u32[]{:S(2)}) %collective-permute-start.6) | collective-permute-done | bytes 294944 | tf_op jit(solution)/shard_map/ppermute | solution.py:51
  102.8 3.7 %all-to-all-start.3 = ((f32[8,152,128]{2,1,0:T(8,128)}), f32[8,152,128]{2,1,0:T(8,128)S(1)}, u32[]{:S(2)}, u32[]{:S(2)}) async-start(f32[8,152,128]{2,1,0:T(8,128)} %shard_map.55), calls=%async_computation.3 | async-start | bytes 1245184 | tf_op jit(solution)/shard_map/all_to_all | solution.py:45
  107.1 2.3 %collective-permute-start.8 = (f32[16,1152]{1,0:T(8,128)S(1)}, f32[16,1152]{1,0:T(8,128)S(1)}, u32[]{:S(2)}, u32[]{:S(2)}) collective-permute-start(f32[16,1152]{1,0:T(8,128)S(1)} %get-tuple-element.30), channel_id=1, source_target_pairs={{0,12},{4,0},{8,4},{12,8},{16,20},{20,24},{24,28},{28,16},{1,13},{... | collective-permute-start | bytes 221192 | tf_op jit(solution)/shard_map/ppermute | solution.py:51
  109.4 5.1 %collective-permute-start.10 = (f32[16,1152]{1,0:T(8,128)S(1)}, f32[16,1152]{1,0:T(8,128)S(1)}, u32[]{:S(2)}, u32[]{:S(2)}) collective-permute-start(f32[16,1152]{1,0:T(8,128)S(1)} %get-tuple-element.31), channel_id=1, source_target_pairs={{0,4},{4,8},{8,12},{12,0},{16,28},{20,16},{24,20},{28,24},{1,5},{5... | collective-permute-start | bytes 221192 | tf_op jit(solution)/shard_map/ppermute | solution.py:51
  114.8 1.9 %collective-permute-start.9 = (f32[16,1152]{1,0:T(8,128)S(1)}, f32[16,1152]{1,0:T(8,128)S(1)}, u32[]{:S(2)}, u32[]{:S(2)}) collective-permute-start(f32[16,1152]{1,0:T(8,128)S(1)} %shard_map.58), channel_id=1, source_target_pairs={{0,12},{4,0},{8,4},{12,8},{16,20},{20,24},{24,28},{28,16},{1,13},{... | collective-permute-start | bytes 221192 | tf_op jit(solution)/shard_map/ppermute | solution.py:51
  118.0 4.0 %collective-permute-done.9.z1 = f32[16,1152]{1,0:T(8,128)S(1)} collective-permute-done((f32[16,1152]{1,0:T(8,128)S(1)}, f32[16,1152]{1,0:T(8,128)S(1)}, u32[]{:S(2)}, u32[]{:S(2)}) %collective-permute-start.9) | collective-permute-done | bytes 73760 | tf_op jit(solution)/shard_map/ppermute | solution.py:51
  (30 shorter events, 9.0 us)
Async XLA Ops:
  0.6 9.4 %copy-start = (f32[16,1152]{1,0:T(8,128)S(1)}, f32[16,1152]{1,0:T(8,128)}, u32[]{:S(2)}) copy-start(f32[16,1152]{1,0:T(8,128)} %emb_ref.3) | copy-start | bytes 221188
  2.4 26.9 %all-to-all-start.1 = ((f32[8,16,1152]{2,1,0:T(8,128)}), f32[8,16,1152]{2,1,0:T(8,128)S(1)}, u32[]{:S(2)}, u32[]{:S(2)}) async-start(f32[8,16,1152]{2,1,0:T(8,128)} %tile.2), calls=%async_computation.1 | async-start | bytes 1179648 | tf_op jit(solution)/shard_map/all_to_all | solution.py:45
  29.4 18.1 %collective-permute-start = (f32[128,1152]{1,0:T(8,128)S(1)}, f32[128,1152]{1,0:T(8,128)S(1)}, u32[]{:S(2)}, u32[]{:S(2)}) collective-permute-start(f32[128,1152]{1,0:T(8,128)S(1)} %shard_map.50.a_ref), channel_id=1, source_target_pairs={{0,44},{32,0},{4,32},{36,4},{8,36},{40,8},{12,40},{44,12},{16,48},... | collective-permute-start | bytes 1769480 | tf_op jit(solution)/shard_map/ppermute | solution.py:60
  33.6 16.9 %all-to-all-start = ((f32[4,64,1152]{2,1,0:T(8,128)}), f32[4,64,1152]{2,1,0:T(8,128)S(1)}, u32[]{:S(2)}, u32[]{:S(2)}) async-start(f32[4,64,1152]{2,1,0:T(8,128)} %bitcast.10), calls=%async_computation | async-start | bytes 2359296 | tf_op jit(solution)/shard_map/all_to_all | solution.py:45
  37.6 12.9 %collective-permute-start.1 = (f32[128,1152]{1,0:T(8,128)S(1)}, f32[128,1152]{1,0:T(8,128)S(1)}, u32[]{:S(2)}, u32[]{:S(2)}) collective-permute-start(f32[128,1152]{1,0:T(8,128)S(1)} %shard_map.50.a_ref), channel_id=1, source_target_pairs={{0,16},{16,0},{1,17},{17,1},{2,18},{18,2},{3,19},{19,3},{4,20},{20... | collective-permute-start | bytes 1769480 | tf_op jit(solution)/shard_map/ppermute | solution.py:64
  47.5 4.5 %collective-permute-start.2 = (f32[128,1152]{1,0:T(8,128)S(1)}, f32[128,1152]{1,0:T(8,128)}, u32[]{:S(2)}, u32[]{:S(2)}) collective-permute-start(f32[128,1152]{1,0:T(8,128)S(1)} %collective-permute-done.b_ref), channel_id=1, source_target_pairs={{0,16},{16,0},{1,17},{17,1},{2,18},{18,2},{3,19},{19,3},{4,20},{20... | collective-permute-start | bytes 1769480 | tf_op jit(solution)/shard_map/ppermute | solution.py:64
  50.5 6.2 %copy-start.2 = (f32[128,1152]{1,0:T(8,128)}, f32[128,1152]{1,0:T(8,128)S(1)}, u32[]{:S(2)}) copy-start(f32[128,1152]{1,0:T(8,128)S(1)} %collective-permute-done.1.c_ref) | copy-start | bytes 1769476
  56.7 14.1 %collective-permute-start.3 = (f32[264,1152]{1,0:T(8,128)S(1)}, f32[264,1152]{1,0:T(8,128)S(1)}, u32[]{:S(2)}, u32[]{:S(2)}) collective-permute-start(f32[264,1152]{1,0:T(8,128)S(1)} %get-tuple-element.19.other_ref), channel_id=1, source_target_pairs={{0,16},{16,0},{1,17},{17,1},{2,18},{18,2},{3,19},{19,3},{4,20},{20... | collective-permute-start | bytes 3649544 | tf_op jit(solution)/shard_map/ppermute | solution.py:64
  63.7 1.1 copy-start.3
  68.6 2.2 %copy-start.4 = (f32[64,1152]{1,0:T(8,128)}, f32[64,1152]{1,0:T(8,128)S(1)}, u32[]{:S(2)}) copy-start(f32[64,1152]{1,0:T(8,128)S(1)} %get-tuple-element.26) | copy-start | bytes 884740
  68.6 20.4 %collective-permute-start.5 = (f32[64,1152]{1,0:T(8,128)}, f32[64,1152]{1,0:T(8,128)S(1)}, u32[]{:S(2)}, u32[]{:S(2)}) collective-permute-start(f32[64,1152]{1,0:T(8,128)} %get-tuple-element.25), channel_id=1, source_target_pairs={{0,3},{1,0},{2,1},{3,2},{16,17},{17,18},{18,19},{19,16},{4,7},{5,4... | collective-permute-start | bytes 884744 | tf_op jit(solution)/shard_map/ppermute | solution.py:51
  72.7 29.2 %collective-permute-start.4 = (f32[128,1152]{1,0:T(8,128)S(1)}, f32[128,1152]{1,0:T(8,128)S(1)}, u32[]{:S(2)}, u32[]{:S(2)}) collective-permute-start(f32[128,1152]{1,0:T(8,128)S(1)} %get-tuple-element.22), channel_id=1, source_target_pairs={{0,32},{32,4},{4,36},{36,8},{8,40},{40,12},{12,44},{44,0},{16,60},... | collective-permute-start | bytes 1769480 | tf_op jit(solution)/shard_map/ppermute | solution.py:60
  79.4 13.8 %all-to-all-start.2 = ((f32[32,1,128]{2,1,0:T(1,128)}), f32[32,1,128]{2,1,0:T(1,128)S(1)}, u32[]{:S(2)}, u32[]{:S(2)}) async-start(f32[32,1,128]{2,1,0:T(1,128)} %bitcast.14), calls=%async_computation.2 | async-start | bytes 32768 | tf_op jit(solution)/shard_map/all_to_all | solution.py:45
  84.7 10.8 %collective-permute-start.7 = (f32[64,1152]{1,0:T(8,128)}, f32[64,1152]{1,0:T(8,128)S(1)}, u32[]{:S(2)}, u32[]{:S(2)}) collective-permute-start(f32[64,1152]{1,0:T(8,128)} %copy-done.4), channel_id=1, source_target_pairs={{0,1},{1,2},{2,3},{3,0},{16,19},{17,16},{18,17},{19,18},{4,5},{5,6... | collective-permute-start | bytes 884744 | tf_op jit(solution)/shard_map/ppermute | solution.py:51
  93.2 8.7 %collective-permute-start.6 = (f32[64,1152]{1,0:T(8,128)S(1)}, f32[64,1152]{1,0:T(8,128)S(1)}, u32[]{:S(2)}, u32[]{:S(2)}) collective-permute-start(f32[64,1152]{1,0:T(8,128)S(1)} %shard_map.54), channel_id=1, source_target_pairs={{0,3},{1,0},{2,1},{3,2},{16,17},{17,18},{18,19},{19,16},{4,7},{5,4... | collective-permute-start | bytes 884744 | tf_op jit(solution)/shard_map/ppermute | solution.py:51
  102.8 21.4 %copy-start.1 = (f32[16,1152]{1,0:T(8,128)S(1)}, f32[16,1152]{1,0:T(8,128)}, u32[]{:S(2)}) copy-start(f32[16,1152]{1,0:T(8,128)} %emb_ref.2) | copy-start | bytes 221188
  102.8 21.4 %all-to-all-start.3 = ((f32[8,152,128]{2,1,0:T(8,128)}), f32[8,152,128]{2,1,0:T(8,128)S(1)}, u32[]{:S(2)}, u32[]{:S(2)}) async-start(f32[8,152,128]{2,1,0:T(8,128)} %shard_map.55), calls=%async_computation.3 | async-start | bytes 1245184 | tf_op jit(solution)/shard_map/all_to_all | solution.py:45
  107.1 7.6 %collective-permute-start.8 = (f32[16,1152]{1,0:T(8,128)S(1)}, f32[16,1152]{1,0:T(8,128)S(1)}, u32[]{:S(2)}, u32[]{:S(2)}) collective-permute-start(f32[16,1152]{1,0:T(8,128)S(1)} %get-tuple-element.30), channel_id=1, source_target_pairs={{0,12},{4,0},{8,4},{12,8},{16,20},{20,24},{24,28},{28,16},{1,13},{... | collective-permute-start | bytes 221192 | tf_op jit(solution)/shard_map/ppermute | solution.py:51
  109.4 8.6 %collective-permute-start.10 = (f32[16,1152]{1,0:T(8,128)S(1)}, f32[16,1152]{1,0:T(8,128)S(1)}, u32[]{:S(2)}, u32[]{:S(2)}) collective-permute-start(f32[16,1152]{1,0:T(8,128)S(1)} %get-tuple-element.31), channel_id=1, source_target_pairs={{0,4},{4,8},{8,12},{12,0},{16,28},{20,16},{24,20},{28,24},{1,5},{5... | collective-permute-start | bytes 221192 | tf_op jit(solution)/shard_map/ppermute | solution.py:51
  114.8 7.2 %collective-permute-start.9 = (f32[16,1152]{1,0:T(8,128)S(1)}, f32[16,1152]{1,0:T(8,128)S(1)}, u32[]{:S(2)}, u32[]{:S(2)}) collective-permute-start(f32[16,1152]{1,0:T(8,128)S(1)} %shard_map.58), channel_id=1, source_target_pairs={{0,12},{4,0},{8,4},{12,8},{16,20},{20,24},{24,28},{28,16},{1,13},{... | collective-permute-start | bytes 221192 | tf_op jit(solution)/shard_map/ppermute | solution.py:51

commit v18 on v14

--- a/solution.py
+++ b/solution.py
@@ -158,7 +158,7 @@
         out[...] = x0[rows, :] + (x1[rows, :] + x2[rows, :])
 
 
-def pack_kernel(keep_ref, plane_ref, losses_ref, back_ref, ahead_ref, packed_out):
+def pack_kernel(keep_ref, plane_ref, losses_ref, image_ref, packed_out):
     loss = jnp.full((8, LANES), jnp.sum(losses_ref[:, 0:1]))
     for y in range(NY):
         rows = pl.ds(y * ROWS, ROWS)
@@ -233,9 +233,9 @@
     )
     (packed,) = call(
         pack_kernel,
-        (keep, plane, losses, back, ahead),
+        (keep, plane, losses, zs[0]),
         [shape(NY, PACK + 8, LANES)],
-        in_specs=[VMEM] * 3 + [ANY] * 2,
+        in_specs=[VMEM] * 3 + [ANY],
     )
     packed = exchange(packed, "y")
     relay = turned(zs[3], "zh", -1)

time: 123 us -> 122 us (level)
  transfers between devices with their start and end apart: 15 -> 15, of which waited for: 8 -> 8; matrix products, arithmetic and copies ran while one was open for 0% -> 0% of each run, Pallas kernels for 7% -> 6%
where the time goes in v18:
time: 122 us; the launch traced here: 121 us
  starting transfers between devices  68.7 us (56%)
  blocking collectives  18 us (15%)
  waiting for transfers between devices  17.4 us (14%)
  Pallas kernels  14.6 us (12%)
  local copies, waits for them, and re-layouts  1.87 us (2%)
    all_to_all x4, starting transfers between devices, exchange(): return lax.all_to_all(values, axes, 0, 0, tiled=True)  20.9 us
    ppermute x3, starting transfers between devices, other_core(): return lax.ppermute(values, 'c', [(0, 1), (1, 0)])  19.2 us
    all_gather x1, blocking collectives, on_device(): image_z = lax.all_gather(image_emb, 'zh', axis=0, tiled=True)  18 us
    ppermute x6, starting transfers between devices, turned(): return lax.ppermute(values, ('c', axis), pairs)  17.7 us
    pallas_call x11, Pallas kernels, call(): pl.pallas_call(kernel, out_shape=outs, in_specs=in_specs or [VMEM] * len(...  14.6 us
    ppermute x2, starting transfers between devices, planes(): return lax.ppermute(values, ('zl', 'c', 'zh'), pairs)  10.9 us
    all_to_all x4, waiting for transfers between devices, exchange(): return lax.all_to_all(values, axes, 0, 0, tiled=True)  8.83 us
    ppermute x6, waiting for transfers between devices, turned(): return lax.ppermute(values, ('c', axis), pairs)  6.72 us
  transfers between devices with their start and end apart: 15, of which 8 were waited for; matrix products, arithmetic and copies ran while one was open for 0% of the time, Pallas kernels for 6%

profile of v18, /device:TPU:1, one launch (start us, length us, event | category | flops | bytes accessed | tf_op | source)
XLA Modules:
  0.0 121.4 jit_solution(584472517438240541)
XLA Ops:
  0.6 1.8 %tile.2 = f32[8,16,1152]{2,1,0:T(8,128)} broadcast(f32[16,1152]{1,0:T(8,128)} %emb_ref.2), dimensions={1,2} | broadcast | bytes 663552 | tf_op jit(solution)/shard_map/tile | solution.py:188
  2.4 7.7 %all-to-all-start.1 = ((f32[8,16,1152]{2,1,0:T(8,128)}), f32[8,16,1152]{2,1,0:T(8,128)S(1)}, u32[]{:S(2)}, u32[]{:S(2)}) async-start(f32[8,16,1152]{2,1,0:T(8,128)} %tile.2), calls=%async_computation.1 | async-start | bytes 1179648 | tf_op jit(solution)/shard_map/all_to_all | solution.py:45
  10.1 18.0 %all_gather.3.image_ref = f32[64,1152]{1,0:T(8,128)S(1)} all-gather(f32[16,1152]{1,0:T(8,128)S(1)} %copy-done), channel_id=1, replica_groups=mesh['y'=8,'zl'=2,'c'=2,'zh'=4,'x'=4] {'zh'}, dimensions={0}, use_global_device_ids=true | all-gather | bytes 368640 | tf_op jit(solution)/shard_map/all_gather | solution.py:189
  29.4 4.2 %collective-permute-start = (f32[128,1152]{1,0:T(8,128)S(1)}, f32[128,1152]{1,0:T(8,128)S(1)}, u32[]{:S(2)}, u32[]{:S(2)}) collective-permute-start(f32[128,1152]{1,0:T(8,128)S(1)} %shard_map.50.a_ref), channel_id=1, source_target_pairs={{0,44},{32,0},{4,32},{36,4},{8,36},{40,8},{12,40},{44,12},{16,48},... | collective-permute-start | bytes 1769480 | tf_op jit(solution)/shard_map/ppermute | solution.py:60
  33.6 4.0 %all-to-all-start = ((f32[4,64,1152]{2,1,0:T(8,128)}), f32[4,64,1152]{2,1,0:T(8,128)S(1)}, u32[]{:S(2)}, u32[]{:S(2)}) async-start(f32[4,64,1152]{2,1,0:T(8,128)} %bitcast.10), calls=%async_computation | async-start | bytes 2359296 | tf_op jit(solution)/shard_map/all_to_all | solution.py:45
  37.6 9.6 %collective-permute-start.1 = (f32[128,1152]{1,0:T(8,128)S(1)}, f32[128,1152]{1,0:T(8,128)}, u32[]{:S(2)}, u32[]{:S(2)}) collective-permute-start(f32[128,1152]{1,0:T(8,128)S(1)} %shard_map.50.a_ref), channel_id=1, source_target_pairs={{0,16},{16,0},{1,17},{17,1},{2,18},{18,2},{3,19},{19,3},{4,20},{20... | collective-permute-start | bytes 1769480 | tf_op jit(solution)/shard_map/ppermute | solution.py:64
  47.5 2.8 %collective-permute-start.2 = (f32[128,1152]{1,0:T(8,128)S(1)}, f32[128,1152]{1,0:T(8,128)}, u32[]{:S(2)}, u32[]{:S(2)}) collective-permute-start(f32[128,1152]{1,0:T(8,128)S(1)} %collective-permute-done.b_ref), channel_id=1, source_target_pairs={{0,16},{16,0},{1,17},{17,1},{2,18},{18,2},{3,19},{19,3},{4,20},{20... | collective-permute-start | bytes 1769480 | tf_op jit(solution)/shard_map/ppermute | solution.py:64
  50.5 1.5 %collective-permute-done.2.d_ref = f32[128,1152]{1,0:T(8,128)} collective-permute-done((f32[128,1152]{1,0:T(8,128)S(1)}, f32[128,1152]{1,0:T(8,128)}, u32[]{:S(2)}, u32[]{:S(2)}) %collective-permute-start.2) | collective-permute-done | bytes 589856 | tf_op jit(solution)/shard_map/ppermute | solution.py:64
  52.1 4.8 %shard_map.51 = (f32[256,512]{1,0:T(8,128)S(1)}, f32[264,1152]{1,0:T(8,128)S(1)}) custom-call(s32[10]{0:T(128)S(1)} %stack.43.place, f32[256,1152]{1,0:T(8,128)S(1)} %bitcast.18, f32[128,1152]{1,0:T(8,128)S(1)} %shard_map.50.a_ref, f32[128,1152]{1,0:T(8,128)S(1)} %collective-permute-done.b_ref, f32[128,1152]{1,0:T(8,128)} %collective-permute-done.1.c_ref, ...), custom_call_target="tpu_custom_call" | custom-call | flops 1358954496 | bytes 5279784 | tf_op jit(solution)/shard_map/pallas_call | solution.py:33
  56.9 6.8 %collective-permute-start.3 = (f32[264,1152]{1,0:T(8,128)S(1)}, f32[264,1152]{1,0:T(8,128)S(1)}, u32[]{:S(2)}, u32[]{:S(2)}) collective-permute-start(f32[264,1152]{1,0:T(8,128)S(1)} %get-tuple-element.19.other_ref), channel_id=1, source_target_pairs={{0,16},{16,0},{1,17},{17,1},{2,18},{18,2},{3,19},{19,3},{4,20},{20... | collective-permute-start | bytes 3649544 | tf_op jit(solution)/shard_map/ppermute | solution.py:64
  63.7 3.2 %shard_map.52 = (f32[64,1152]{1,0:T(8,128)S(1)}, f32[64,1152]{1,0:T(8,128)S(1)}, f32[64,1152]{1,0:T(8,128)S(1)}, f32[64,1152]{1,0:T(8,128)S(1)}) custom-call(f32[256,512]{1,0:T(8,128)S(1)} %get-tuple-element.18.slope_ref, f32[128,1152]{1,0:T(8,128)S(1)} %shard_map.50.a_ref, f32[128,1152]{1,0:T(8,128)S(1)} %collective-permute-done.b_ref, ...), custom_call_target="tpu_custom_call" | custom-call | flops 905969664 | bytes 4063232 | tf_op jit(solution)/shard_map/pallas_call | solution.py:33
  67.0 2.2 %collective-permute-start.5 = (f32[64,1152]{1,0:T(8,128)S(1)}, f32[64,1152]{1,0:T(8,128)S(1)}, u32[]{:S(2)}, u32[]{:S(2)}) collective-permute-start(f32[64,1152]{1,0:T(8,128)S(1)} %get-tuple-element.25), channel_id=1, source_target_pairs={{0,3},{1,0},{2,1},{3,2},{16,17},{17,18},{18,19},{19,16},{4,7},{5,4... | collective-permute-start | bytes 884744 | tf_op jit(solution)/shard_map/ppermute | solution.py:51
  69.2 1.9 %shard_map.53 = (f32[128,1152]{1,0:T(8,128)S(1)}, f32[128,1152]{1,0:T(8,128)S(1)}, f32[32,128]{1,0:T(8,128)}) custom-call(s32[10]{0:T(128)S(1)} %stack.43.place, f32[256,512]{1,0:T(8,128)S(1)} %get-tuple-element.18.slope_ref, f32[256,1152]{1,0:T(8,128)S(1)} %bitcast.19, f32[264,1152]{1,0:T(8,128)S(1)} %get-tuple-element.19.other_ref, ...), custom_call_target="tpu_custom_call" | custom-call | flops 452984832 | bytes 5627944 | tf_op jit(solution)/shard_map/pallas_call | solution.py:33
  71.0 6.7 %collective-permute-start.4 = (f32[128,1152]{1,0:T(8,128)S(1)}, f32[128,1152]{1,0:T(8,128)S(1)}, u32[]{:S(2)}, u32[]{:S(2)}) collective-permute-start(f32[128,1152]{1,0:T(8,128)S(1)} %get-tuple-element.22), channel_id=1, source_target_pairs={{0,32},{32,4},{4,36},{36,8},{8,40},{40,12},{12,44},{44,0},{16,60},... | collective-permute-start | bytes 1769480 | tf_op jit(solution)/shard_map/ppermute | solution.py:60
  77.8 4.3 %collective-permute-start.7 = (f32[64,1152]{1,0:T(8,128)S(1)}, f32[64,1152]{1,0:T(8,128)S(1)}, u32[]{:S(2)}, u32[]{:S(2)}) collective-permute-start(f32[64,1152]{1,0:T(8,128)S(1)} %get-tuple-element.26), channel_id=1, source_target_pairs={{0,1},{1,2},{2,3},{3,0},{16,19},{17,16},{18,17},{19,18},{4,5},{5,6... | collective-permute-start | bytes 884744 | tf_op jit(solution)/shard_map/ppermute | solution.py:51
  82.1 1.9 %collective-permute-start.6 = (f32[64,1152]{1,0:T(8,128)S(1)}, f32[64,1152]{1,0:T(8,128)S(1)}, u32[]{:S(2)}, u32[]{:S(2)}) collective-permute-start(f32[64,1152]{1,0:T(8,128)S(1)} %shard_map.54), channel_id=1, source_target_pairs={{0,3},{1,0},{2,1},{3,2},{16,17},{17,18},{18,19},{19,16},{4,7},{5,4... | collective-permute-start | bytes 884744 | tf_op jit(solution)/shard_map/ppermute | solution.py:51
  84.0 5.5 %all-to-all-start.2 = ((f32[32,1,128]{2,1,0:T(1,128)}), f32[32,1,128]{2,1,0:T(1,128)S(1)}, u32[]{:S(2)}, u32[]{:S(2)}) async-start(f32[32,1,128]{2,1,0:T(1,128)} %bitcast.14), calls=%async_computation.2 | async-start | bytes 32768 | tf_op jit(solution)/shard_map/all_to_all | solution.py:45
  91.4 6.7 %all-to-all-done.2 = f32[32,1,128]{2,1,0:T(1,128)S(1)} async-done(((f32[32,1,128]{2,1,0:T(1,128)}), f32[32,1,128]{2,1,0:T(1,128)S(1)}, u32[]{:S(2)}, u32[]{:S(2)}) %all-to-all-start.2) | async-done | bytes 16416 | tf_op jit(solution)/shard_map/all_to_all | solution.py:45
  99.1 3.7 %all-to-all-start.3 = ((f32[8,152,128]{2,1,0:T(8,128)}), f32[8,152,128]{2,1,0:T(8,128)S(1)}, u32[]{:S(2)}, u32[]{:S(2)}) async-start(f32[8,152,128]{2,1,0:T(8,128)} %shard_map.56), calls=%async_computation.3 | async-start | bytes 1245184 | tf_op jit(solution)/shard_map/all_to_all | solution.py:45
  102.7 2.3 %collective-permute-start.8 = (f32[16,1152]{1,0:T(8,128)S(1)}, f32[16,1152]{1,0:T(8,128)S(1)}, u32[]{:S(2)}, u32[]{:S(2)}) collective-permute-start(f32[16,1152]{1,0:T(8,128)S(1)} %get-tuple-element.30), channel_id=1, source_target_pairs={{0,12},{4,0},{8,4},{12,8},{16,20},{20,24},{24,28},{28,16},{1,13},{... | collective-permute-start | bytes 221192 | tf_op jit(solution)/shard_map/ppermute | solution.py:51
  105.0 5.1 %collective-permute-start.10 = (f32[16,1152]{1,0:T(8,128)S(1)}, f32[16,1152]{1,0:T(8,128)S(1)}, u32[]{:S(2)}, u32[]{:S(2)}) collective-permute-start(f32[16,1152]{1,0:T(8,128)S(1)} %get-tuple-element.31), channel_id=1, source_target_pairs={{0,4},{4,8},{8,12},{12,0},{16,28},{20,16},{24,20},{28,24},{1,5},{5... | collective-permute-start | bytes 221192 | tf_op jit(solution)/shard_map/ppermute | solution.py:51
  110.4 1.9 %collective-permute-start.9 = (f32[16,1152]{1,0:T(8,128)S(1)}, f32[16,1152]{1,0:T(8,128)S(1)}, u32[]{:S(2)}, u32[]{:S(2)}) collective-permute-start(f32[16,1152]{1,0:T(8,128)S(1)} %shard_map.58), channel_id=1, source_target_pairs={{0,12},{4,0},{8,4},{12,8},{16,20},{20,24},{24,28},{28,16},{1,13},{... | collective-permute-start | bytes 221192 | tf_op jit(solution)/shard_map/ppermute | solution.py:51
  113.6 4.0 %collective-permute-done.9.z1 = f32[16,1152]{1,0:T(8,128)S(1)} collective-permute-done((f32[16,1152]{1,0:T(8,128)S(1)}, f32[16,1152]{1,0:T(8,128)S(1)}, u32[]{:S(2)}, u32[]{:S(2)}) %collective-permute-start.9) | collective-permute-done | bytes 73760 | tf_op jit(solution)/shard_map/ppermute | solution.py:51
  118.4 2.1 %all-to-all-done.3.packed_ref = f32[8,152,128]{2,1,0:T(8,128)S(1)} async-done(((f32[8,152,128]{2,1,0:T(8,128)}), f32[8,152,128]{2,1,0:T(8,128)S(1)}, u32[]{:S(2)}, u32[]{:S(2)}) %all-to-all-start.3) | async-done | bytes 622624 | tf_op jit(solution)/shard_map/all_to_all | solution.py:45
  (24 shorter events, 7.7 us)
Async XLA Ops:
  0.6 9.4 %copy-start = (f32[16,1152]{1,0:T(8,128)S(1)}, f32[16,1152]{1,0:T(8,128)}, u32[]{:S(2)}) copy-start(f32[16,1152]{1,0:T(8,128)} %emb_ref.3) | copy-start | bytes 221188
  2.4 26.8 %all-to-all-start.1 = ((f32[8,16,1152]{2,1,0:T(8,128)}), f32[8,16,1152]{2,1,0:T(8,128)S(1)}, u32[]{:S(2)}, u32[]{:S(2)}) async-start(f32[8,16,1152]{2,1,0:T(8,128)} %tile.2), calls=%async_computation.1 | async-start | bytes 1179648 | tf_op jit(solution)/shard_map/all_to_all | solution.py:45
  29.4 18.1 %collective-permute-start = (f32[128,1152]{1,0:T(8,128)S(1)}, f32[128,1152]{1,0:T(8,128)S(1)}, u32[]{:S(2)}, u32[]{:S(2)}) collective-permute-start(f32[128,1152]{1,0:T(8,128)S(1)} %shard_map.50.a_ref), channel_id=1, source_target_pairs={{0,44},{32,0},{4,32},{36,4},{8,36},{40,8},{12,40},{44,12},{16,48},... | collective-permute-start | bytes 1769480 | tf_op jit(solution)/shard_map/ppermute | solution.py:60
  33.6 16.9 %all-to-all-start = ((f32[4,64,1152]{2,1,0:T(8,128)}), f32[4,64,1152]{2,1,0:T(8,128)S(1)}, u32[]{:S(2)}, u32[]{:S(2)}) async-start(f32[4,64,1152]{2,1,0:T(8,128)} %bitcast.10), calls=%async_computation | async-start | bytes 2359296 | tf_op jit(solution)/shard_map/all_to_all | solution.py:45
  37.6 12.9 %collective-permute-start.1 = (f32[128,1152]{1,0:T(8,128)S(1)}, f32[128,1152]{1,0:T(8,128)}, u32[]{:S(2)}, u32[]{:S(2)}) collective-permute-start(f32[128,1152]{1,0:T(8,128)S(1)} %shard_map.50.a_ref), channel_id=1, source_target_pairs={{0,16},{16,0},{1,17},{17,1},{2,18},{18,2},{3,19},{19,3},{4,20},{20... | collective-permute-start | bytes 1769480 | tf_op jit(solution)/shard_map/ppermute | solution.py:64
  47.5 4.5 %collective-permute-start.2 = (f32[128,1152]{1,0:T(8,128)S(1)}, f32[128,1152]{1,0:T(8,128)}, u32[]{:S(2)}, u32[]{:S(2)}) collective-permute-start(f32[128,1152]{1,0:T(8,128)S(1)} %collective-permute-done.b_ref), channel_id=1, source_target_pairs={{0,16},{16,0},{1,17},{17,1},{2,18},{18,2},{3,19},{19,3},{4,20},{20... | collective-permute-start | bytes 1769480 | tf_op jit(solution)/shard_map/ppermute | solution.py:64
  56.9 12.3 %collective-permute-start.3 = (f32[264,1152]{1,0:T(8,128)S(1)}, f32[264,1152]{1,0:T(8,128)S(1)}, u32[]{:S(2)}, u32[]{:S(2)}) collective-permute-start(f32[264,1152]{1,0:T(8,128)S(1)} %get-tuple-element.19.other_ref), channel_id=1, source_target_pairs={{0,16},{16,0},{1,17},{17,1},{2,18},{18,2},{3,19},{19,3},{4,20},{20... | collective-permute-start | bytes 3649544 | tf_op jit(solution)/shard_map/ppermute | solution.py:64
  67.0 15.1 %collective-permute-start.5 = (f32[64,1152]{1,0:T(8,128)S(1)}, f32[64,1152]{1,0:T(8,128)S(1)}, u32[]{:S(2)}, u32[]{:S(2)}) collective-permute-start(f32[64,1152]{1,0:T(8,128)S(1)} %get-tuple-element.25), channel_id=1, source_target_pairs={{0,3},{1,0},{2,1},{3,2},{16,17},{17,18},{18,19},{19,16},{4,7},{5,4... | collective-permute-start | bytes 884744 | tf_op jit(solution)/shard_map/ppermute | solution.py:51
  71.0 27.1 %collective-permute-start.4 = (f32[128,1152]{1,0:T(8,128)S(1)}, f32[128,1152]{1,0:T(8,128)S(1)}, u32[]{:S(2)}, u32[]{:S(2)}) collective-permute-start(f32[128,1152]{1,0:T(8,128)S(1)} %get-tuple-element.22), channel_id=1, source_target_pairs={{0,32},{32,4},{4,36},{36,8},{8,40},{40,12},{12,44},{44,0},{16,60},... | collective-permute-start | bytes 1769480 | tf_op jit(solution)/shard_map/ppermute | solution.py:60
  77.8 11.8 %collective-permute-start.7 = (f32[64,1152]{1,0:T(8,128)S(1)}, f32[64,1152]{1,0:T(8,128)S(1)}, u32[]{:S(2)}, u32[]{:S(2)}) collective-permute-start(f32[64,1152]{1,0:T(8,128)S(1)} %get-tuple-element.26), channel_id=1, source_target_pairs={{0,1},{1,2},{2,3},{3,0},{16,19},{17,16},{18,17},{19,18},{4,5},{5,6... | collective-permute-start | bytes 884744 | tf_op jit(solution)/shard_map/ppermute | solution.py:51
  82.1 8.7 %collective-permute-start.6 = (f32[64,1152]{1,0:T(8,128)S(1)}, f32[64,1152]{1,0:T(8,128)S(1)}, u32[]{:S(2)}, u32[]{:S(2)}) collective-permute-start(f32[64,1152]{1,0:T(8,128)S(1)} %shard_map.54), channel_id=1, source_target_pairs={{0,3},{1,0},{2,1},{3,2},{16,17},{17,18},{18,19},{19,16},{4,7},{5,4... | collective-permute-start | bytes 884744 | tf_op jit(solution)/shard_map/ppermute | solution.py:51
  84.0 14.0 %all-to-all-start.2 = ((f32[32,1,128]{2,1,0:T(1,128)}), f32[32,1,128]{2,1,0:T(1,128)S(1)}, u32[]{:S(2)}, u32[]{:S(2)}) async-start(f32[32,1,128]{2,1,0:T(1,128)} %bitcast.14), calls=%async_computation.2 | async-start | bytes 32768 | tf_op jit(solution)/shard_map/all_to_all | solution.py:45
  99.1 21.5 %copy-start.1 = (f32[16,1152]{1,0:T(8,128)S(1)}, f32[16,1152]{1,0:T(8,128)}, u32[]{:S(2)}) copy-start(f32[16,1152]{1,0:T(8,128)} %emb_ref.2) | copy-start | bytes 221188
  99.1 21.5 %all-to-all-start.3 = ((f32[8,152,128]{2,1,0:T(8,128)}), f32[8,152,128]{2,1,0:T(8,128)S(1)}, u32[]{:S(2)}, u32[]{:S(2)}) async-start(f32[8,152,128]{2,1,0:T(8,128)} %shard_map.56), calls=%async_computation.3 | async-start | bytes 1245184 | tf_op jit(solution)/shard_map/all_to_all | solution.py:45
  102.7 7.6 %collective-permute-start.8 = (f32[16,1152]{1,0:T(8,128)S(1)}, f32[16,1152]{1,0:T(8,128)S(1)}, u32[]{:S(2)}, u32[]{:S(2)}) collective-permute-start(f32[16,1152]{1,0:T(8,128)S(1)} %get-tuple-element.30), channel_id=1, source_target_pairs={{0,12},{4,0},{8,4},{12,8},{16,20},{20,24},{24,28},{28,16},{1,13},{... | collective-permute-start | bytes 221192 | tf_op jit(solution)/shard_map/ppermute | solution.py:51
  105.0 8.6 %collective-permute-start.10 = (f32[16,1152]{1,0:T(8,128)S(1)}, f32[16,1152]{1,0:T(8,128)S(1)}, u32[]{:S(2)}, u32[]{:S(2)}) collective-permute-start(f32[16,1152]{1,0:T(8,128)S(1)} %get-tuple-element.31), channel_id=1, source_target_pairs={{0,4},{4,8},{8,12},{12,0},{16,28},{20,16},{24,20},{28,24},{1,5},{5... | collective-permute-start | bytes 221192 | tf_op jit(solution)/shard_map/ppermute | solution.py:51
  110.4 7.2 %collective-permute-start.9 = (f32[16,1152]{1,0:T(8,128)S(1)}, f32[16,1152]{1,0:T(8,128)S(1)}, u32[]{:S(2)}, u32[]{:S(2)}) collective-permute-start(f32[16,1152]{1,0:T(8,128)S(1)} %shard_map.58), channel_id=1, source_target_pairs={{0,12},{4,0},{8,4},{12,8},{16,20},{20,24},{24,28},{28,16},{1,13},{... | collective-permute-start | bytes 221192 | tf_op jit(solution)/shard_map/ppermute | solution.py:51

commit v19 on v18

--- a/solution.py
+++ b/solution.py
@@ -231,16 +231,16 @@
         [shape(rows, features)] * NZH,
         in_specs=[SMEM] + [VMEM] * 3,
     )
+    first = turned(zs[3], "zh", -1)
     (packed,) = call(
         pack_kernel,
-        (keep, plane, losses, zs[0]),
+        (keep, plane, losses, first),
         [shape(NY, PACK + 8, LANES)],
         in_specs=[VMEM] * 3 + [ANY],
     )
     packed = exchange(packed, "y")
-    relay = turned(zs[3], "zh", -1)
     ahead = turned(zs[2], "zh", 1)
-    (relay,) = call(relay_kernel, (zs[1], relay), [shape(rows, features)])
+    (relay,) = call(relay_kernel, (zs[1], first), [shape(rows, features)])
     back = turned(relay, "zh", -1)
     (image_grad,) = call(image_grad_kernel, (image_emb, zs[0], back, ahead), [shape(rows, features)])
     text_grad, loss = call(

time: 122 us -> 132 us (1.082); the launches traced: 121 us -> 129 us
  waiting for transfers between devices: 17.4 us -> 26.8 us
    all_to_all x4, waiting for transfers between devices: 8.83 us -> 14.8 us  [exchange(): return lax.all_to_all(values, axes, 0, 0, tiled=True)]
    ppermute x6, waiting for transfers between devices: 6.72 us -> 10.1 us  [turned(): return lax.ppermute(values, ('c', axis), pairs)]
where the time goes in v19:
time: 132 us; the launch traced here: 129 us
  starting transfers between devices  67.7 us (51%)
  waiting for transfers between devices  26.8 us (20%)
  blocking collectives  18 us (14%)
  Pallas kernels  14.3 us (11%)
  local copies, waits for them, and re-layouts  1.87 us (1%)
    all_to_all x4, starting transfers between devices, exchange(): return lax.all_to_all(values, axes, 0, 0, tiled=True)  21.1 us
    ppermute x3, starting transfers between devices, other_core(): return lax.ppermute(values, 'c', [(0, 1), (1, 0)])  19.2 us
    all_gather x1, blocking collectives, on_device(): image_z = lax.all_gather(image_emb, 'zh', axis=0, tiled=True)  18 us
    ppermute x6, starting transfers between devices, turned(): return lax.ppermute(values, ('c', axis), pairs)  16.5 us
    all_to_all x4, waiting for transfers between devices, exchange(): return lax.all_to_all(values, axes, 0, 0, tiled=True)  14.8 us
    pallas_call x11, Pallas kernels, call(): pl.pallas_call(kernel, out_shape=outs, in_specs=in_specs or [VMEM] * len(...  14.3 us
    ppermute x2, starting transfers between devices, planes(): return lax.ppermute(values, ('zl', 'c', 'zh'), pairs)  10.9 us
    ppermute x6, waiting for transfers between devices, turned(): return lax.ppermute(values, ('c', axis), pairs)  10.1 us
  transfers between devices with their start and end apart: 15, of which 8 were waited for; matrix products, arithmetic and copies ran while one was open for 0% of the time, Pallas kernels for 6%

profile of v19, /device:TPU:1, one launch (start us, length us, event | category | flops | bytes accessed | tf_op | source)
XLA Modules:
  0.0 129.5 jit_solution(11981275581073884354)
XLA Ops:
  2.4 7.7 %all-to-all-start.1 = ((f32[8,16,1152]{2,1,0:T(8,128)}), f32[8,16,1152]{2,1,0:T(8,128)S(1)}, u32[]{:S(2)}, u32[]{:S(2)}) async-start(f32[8,16,1152]{2,1,0:T(8,128)} %tile.2), calls=%async_computation.1 | async-start | bytes 1179648 | tf_op jit(solution)/shard_map/all_to_all | solution.py:45
  10.1 18.0 %all_gather.3.image_ref = f32[64,1152]{1,0:T(8,128)S(1)} all-gather(f32[16,1152]{1,0:T(8,128)S(1)} %copy-done), channel_id=1, replica_groups=mesh['y'=8,'zl'=2,'c'=2,'zh'=4,'x'=4] {'zh'}, dimensions={0}, use_global_device_ids=true | all-gather | bytes 368640 | tf_op jit(solution)/shard_map/all_gather | solution.py:189
  29.4 4.2 %collective-permute-start = (f32[128,1152]{1,0:T(8,128)S(1)}, f32[128,1152]{1,0:T(8,128)S(1)}, u32[]{:S(2)}, u32[]{:S(2)}) collective-permute-start(f32[128,1152]{1,0:T(8,128)S(1)} %shard_map.50.a_ref), channel_id=1, source_target_pairs={{0,44},{32,0},{4,32},{36,4},{8,36},{40,8},{12,40},{44,12},{16,48},... | collective-permute-start | bytes 1769480 | tf_op jit(solution)/shard_map/ppermute | solution.py:60
  33.6 4.0 %all-to-all-start = ((f32[4,64,1152]{2,1,0:T(8,128)}), f32[4,64,1152]{2,1,0:T(8,128)S(1)}, u32[]{:S(2)}, u32[]{:S(2)}) async-start(f32[4,64,1152]{2,1,0:T(8,128)} %bitcast.10), calls=%async_computation | async-start | bytes 2359296 | tf_op jit(solution)/shard_map/all_to_all | solution.py:45
  37.6 9.6 %collective-permute-start.1 = (f32[128,1152]{1,0:T(8,128)S(1)}, f32[128,1152]{1,0:T(8,128)S(1)}, u32[]{:S(2)}, u32[]{:S(2)}) collective-permute-start(f32[128,1152]{1,0:T(8,128)S(1)} %shard_map.50.a_ref), channel_id=1, source_target_pairs={{0,16},{16,0},{1,17},{17,1},{2,18},{18,2},{3,19},{19,3},{4,20},{20... | collective-permute-start | bytes 1769480 | tf_op jit(solution)/shard_map/ppermute | solution.py:64
  47.5 2.8 %collective-permute-start.2 = (f32[128,1152]{1,0:T(8,128)S(1)}, f32[128,1152]{1,0:T(8,128)}, u32[]{:S(2)}, u32[]{:S(2)}) collective-permute-start(f32[128,1152]{1,0:T(8,128)S(1)} %collective-permute-done.b_ref), channel_id=1, source_target_pairs={{0,16},{16,0},{1,17},{17,1},{2,18},{18,2},{3,19},{19,3},{4,20},{20... | collective-permute-start | bytes 1769480 | tf_op jit(solution)/shard_map/ppermute | solution.py:64
  52.1 4.7 %shard_map.51 = (f32[256,512]{1,0:T(8,128)S(1)}, f32[264,1152]{1,0:T(8,128)S(1)}) custom-call(s32[10]{0:T(128)S(1)} %stack.43.place, f32[256,1152]{1,0:T(8,128)S(1)} %bitcast.18, f32[128,1152]{1,0:T(8,128)S(1)} %shard_map.50.a_ref, f32[128,1152]{1,0:T(8,128)S(1)} %collective-permute-done.b_ref, f32[128,1152]{1,0:T(8,128)S(1)} %collective-permute-done.1.c_ref, ...), custom_call_target="tpu_custom_call" | custom-call | flops 1358954496 | bytes 5279784 | tf_op jit(solution)/shard_map/pallas_call | solution.py:33
  56.7 6.8 %collective-permute-start.3 = (f32[264,1152]{1,0:T(8,128)S(1)}, f32[264,1152]{1,0:T(8,128)S(1)}, u32[]{:S(2)}, u32[]{:S(2)}) collective-permute-start(f32[264,1152]{1,0:T(8,128)S(1)} %get-tuple-element.19.other_ref), channel_id=1, source_target_pairs={{0,16},{16,0},{1,17},{17,1},{2,18},{18,2},{3,19},{19,3},{4,20},{20... | collective-permute-start | bytes 3649544 | tf_op jit(solution)/shard_map/ppermute | solution.py:64
  63.5 3.1 %shard_map.52 = (f32[64,1152]{1,0:T(8,128)S(1)}, f32[64,1152]{1,0:T(8,128)S(1)}, f32[64,1152]{1,0:T(8,128)S(1)}, f32[64,1152]{1,0:T(8,128)S(1)}) custom-call(f32[256,512]{1,0:T(8,128)S(1)} %get-tuple-element.18.slope_ref, f32[128,1152]{1,0:T(8,128)S(1)} %shard_map.50.a_ref, f32[128,1152]{1,0:T(8,128)S(1)} %collective-permute-done.b_ref, ...), custom_call_target="tpu_custom_call" | custom-call | flops 905969664 | bytes 4063232 | tf_op jit(solution)/shard_map/pallas_call | solution.py:33
  66.6 2.2 %collective-permute-start.5 = (f32[64,1152]{1,0:T(8,128)S(1)}, f32[64,1152]{1,0:T(8,128)S(1)}, u32[]{:S(2)}, u32[]{:S(2)}) collective-permute-start(f32[64,1152]{1,0:T(8,128)S(1)} %get-tuple-element.25), channel_id=1, source_target_pairs={{0,3},{1,0},{2,1},{3,2},{16,17},{17,18},{18,19},{19,16},{4,7},{5,4... | collective-permute-start | bytes 884744 | tf_op jit(solution)/shard_map/ppermute | solution.py:51
  68.8 1.9 %shard_map.53 = (f32[128,1152]{1,0:T(8,128)S(1)}, f32[128,1152]{1,0:T(8,128)S(1)}, f32[32,128]{1,0:T(8,128)}) custom-call(s32[10]{0:T(128)S(1)} %stack.43.place, f32[256,512]{1,0:T(8,128)S(1)} %get-tuple-element.18.slope_ref, f32[256,1152]{1,0:T(8,128)S(1)} %bitcast.19, f32[264,1152]{1,0:T(8,128)S(1)} %get-tuple-element.19.other_ref, ...), custom_call_target="tpu_custom_call" | custom-call | flops 452984832 | bytes 5627944 | tf_op jit(solution)/shard_map/pallas_call | solution.py:33
  70.7 6.7 %collective-permute-start.4 = (f32[128,1152]{1,0:T(8,128)S(1)}, f32[128,1152]{1,0:T(8,128)S(1)}, u32[]{:S(2)}, u32[]{:S(2)}) collective-permute-start(f32[128,1152]{1,0:T(8,128)S(1)} %get-tuple-element.22), channel_id=1, source_target_pairs={{0,32},{32,4},{4,36},{36,8},{8,40},{40,12},{12,44},{44,0},{16,60},... | collective-permute-start | bytes 1769480 | tf_op jit(solution)/shard_map/ppermute | solution.py:60
  77.4 4.3 %collective-permute-start.7 = (f32[64,1152]{1,0:T(8,128)S(1)}, f32[64,1152]{1,0:T(8,128)S(1)}, u32[]{:S(2)}, u32[]{:S(2)}) collective-permute-start(f32[64,1152]{1,0:T(8,128)S(1)} %get-tuple-element.26), channel_id=1, source_target_pairs={{0,1},{1,2},{2,3},{3,0},{16,19},{17,16},{18,17},{19,18},{4,5},{5,6... | collective-permute-start | bytes 884744 | tf_op jit(solution)/shard_map/ppermute | solution.py:51
  81.8 1.9 %collective-permute-start.6 = (f32[64,1152]{1,0:T(8,128)S(1)}, f32[64,1152]{1,0:T(8,128)S(1)}, u32[]{:S(2)}, u32[]{:S(2)}) collective-permute-start(f32[64,1152]{1,0:T(8,128)S(1)} %shard_map.54), channel_id=1, source_target_pairs={{0,3},{1,0},{2,1},{3,2},{16,17},{17,18},{18,19},{19,16},{4,7},{5,4... | collective-permute-start | bytes 884744 | tf_op jit(solution)/shard_map/ppermute | solution.py:51
  83.7 4.4 %collective-permute-done.7.x2 = f32[64,1152]{1,0:T(8,128)S(1)} collective-permute-done((f32[64,1152]{1,0:T(8,128)S(1)}, f32[64,1152]{1,0:T(8,128)S(1)}, u32[]{:S(2)}, u32[]{:S(2)}) %collective-permute-start.7) | collective-permute-done | bytes 294944 | tf_op jit(solution)/shard_map/ppermute | solution.py:51
  88.1 2.3 %collective-permute-done.6.x1 = f32[64,1152]{1,0:T(8,128)S(1)} collective-permute-done((f32[64,1152]{1,0:T(8,128)S(1)}, f32[64,1152]{1,0:T(8,128)S(1)}, u32[]{:S(2)}, u32[]{:S(2)}) %collective-permute-start.6) | collective-permute-done | bytes 294944 | tf_op jit(solution)/shard_map/ppermute | solution.py:51
  91.0 1.9 %collective-permute-start.8 = (f32[16,1152]{1,0:T(8,128)S(1)}, f32[16,1152]{1,0:T(8,128)S(1)}, u32[]{:S(2)}, u32[]{:S(2)}) collective-permute-start(f32[16,1152]{1,0:T(8,128)S(1)} %get-tuple-element.27), channel_id=1, source_target_pairs={{0,12},{4,0},{8,4},{12,8},{16,20},{20,24},{24,28},{28,16},{1,13},{... | collective-permute-start | bytes 221192 | tf_op jit(solution)/shard_map/ppermute | solution.py:51
  93.0 5.7 %all-to-all-start.2 = ((f32[32,1,128]{2,1,0:T(1,128)}), f32[32,1,128]{2,1,0:T(1,128)S(1)}, u32[]{:S(2)}, u32[]{:S(2)}) async-start(f32[32,1,128]{2,1,0:T(1,128)} %bitcast.14), calls=%async_computation.2 | async-start | bytes 32768 | tf_op jit(solution)/shard_map/all_to_all | solution.py:45
  98.7 8.5 %all-to-all-done.2 = f32[32,1,128]{2,1,0:T(1,128)S(1)} async-done(((f32[32,1,128]{2,1,0:T(1,128)}), f32[32,1,128]{2,1,0:T(1,128)S(1)}, u32[]{:S(2)}, u32[]{:S(2)}) %all-to-all-start.2) | async-done | bytes 16416 | tf_op jit(solution)/shard_map/all_to_all | solution.py:45
  108.2 3.7 %all-to-all-start.3 = ((f32[8,152,128]{2,1,0:T(8,128)}), f32[8,152,128]{2,1,0:T(8,128)S(1)}, u32[]{:S(2)}, u32[]{:S(2)}) async-start(f32[8,152,128]{2,1,0:T(8,128)} %shard_map.56), calls=%async_computation.3 | async-start | bytes 1245184 | tf_op jit(solution)/shard_map/all_to_all | solution.py:45
  111.9 2.3 %collective-permute-start.10 = (f32[16,1152]{1,0:T(8,128)S(1)}, f32[16,1152]{1,0:T(8,128)S(1)}, u32[]{:S(2)}, u32[]{:S(2)}) collective-permute-start(f32[16,1152]{1,0:T(8,128)S(1)} %get-tuple-element.31), channel_id=1, source_target_pairs={{0,4},{4,8},{8,12},{12,0},{16,28},{20,16},{24,20},{28,24},{1,5},{5... | collective-permute-start | bytes 221192 | tf_op jit(solution)/shard_map/ppermute | solution.py:51
  114.2 3.9 %collective-permute-start.9 = (f32[16,1152]{1,0:T(8,128)S(1)}, f32[16,1152]{1,0:T(8,128)S(1)}, u32[]{:S(2)}, u32[]{:S(2)}) collective-permute-start(f32[16,1152]{1,0:T(8,128)S(1)} %shard_map.58), channel_id=1, source_target_pairs={{0,12},{4,0},{8,4},{12,8},{16,20},{20,24},{24,28},{28,16},{1,13},{... | collective-permute-start | bytes 221192 | tf_op jit(solution)/shard_map/ppermute | solution.py:51
  118.7 2.8 %collective-permute-done.9.z1 = f32[16,1152]{1,0:T(8,128)S(1)} collective-permute-done((f32[16,1152]{1,0:T(8,128)S(1)}, f32[16,1152]{1,0:T(8,128)S(1)}, u32[]{:S(2)}, u32[]{:S(2)}) %collective-permute-start.9) | collective-permute-done | bytes 73760 | tf_op jit(solution)/shard_map/ppermute | solution.py:51
  122.3 6.3 %all-to-all-done.3.packed_ref = f32[8,152,128]{2,1,0:T(8,128)S(1)} async-done(((f32[8,152,128]{2,1,0:T(8,128)}), f32[8,152,128]{2,1,0:T(8,128)S(1)}, u32[]{:S(2)}, u32[]{:S(2)}) %all-to-all-start.3) | async-done | bytes 622624 | tf_op jit(solution)/shard_map/all_to_all | solution.py:45
  (24 shorter events, 8.9 us)
Async XLA Ops:
  0.6 9.4 %copy-start = (f32[16,1152]{1,0:T(8,128)S(1)}, f32[16,1152]{1,0:T(8,128)}, u32[]{:S(2)}) copy-start(f32[16,1152]{1,0:T(8,128)} %emb_ref.3) | copy-start | bytes 221188
  2.4 26.8 %all-to-all-start.1 = ((f32[8,16,1152]{2,1,0:T(8,128)}), f32[8,16,1152]{2,1,0:T(8,128)S(1)}, u32[]{:S(2)}, u32[]{:S(2)}) async-start(f32[8,16,1152]{2,1,0:T(8,128)} %tile.2), calls=%async_computation.1 | async-start | bytes 1179648 | tf_op jit(solution)/shard_map/all_to_all | solution.py:45
  29.4 18.1 %collective-permute-start = (f32[128,1152]{1,0:T(8,128)S(1)}, f32[128,1152]{1,0:T(8,128)S(1)}, u32[]{:S(2)}, u32[]{:S(2)}) collective-permute-start(f32[128,1152]{1,0:T(8,128)S(1)} %shard_map.50.a_ref), channel_id=1, source_target_pairs={{0,44},{32,0},{4,32},{36,4},{8,36},{40,8},{12,40},{44,12},{16,48},... | collective-permute-start | bytes 1769480 | tf_op jit(solution)/shard_map/ppermute | solution.py:60
  33.6 16.9 %all-to-all-start = ((f32[4,64,1152]{2,1,0:T(8,128)}), f32[4,64,1152]{2,1,0:T(8,128)S(1)}, u32[]{:S(2)}, u32[]{:S(2)}) async-start(f32[4,64,1152]{2,1,0:T(8,128)} %bitcast.10), calls=%async_computation | async-start | bytes 2359296 | tf_op jit(solution)/shard_map/all_to_all | solution.py:45
  37.6 12.9 %collective-permute-start.1 = (f32[128,1152]{1,0:T(8,128)S(1)}, f32[128,1152]{1,0:T(8,128)S(1)}, u32[]{:S(2)}, u32[]{:S(2)}) collective-permute-start(f32[128,1152]{1,0:T(8,128)S(1)} %shard_map.50.a_ref), channel_id=1, source_target_pairs={{0,16},{16,0},{1,17},{17,1},{2,18},{18,2},{3,19},{19,3},{4,20},{20... | collective-permute-start | bytes 1769480 | tf_op jit(solution)/shard_map/ppermute | solution.py:64
  47.5 4.5 %collective-permute-start.2 = (f32[128,1152]{1,0:T(8,128)S(1)}, f32[128,1152]{1,0:T(8,128)}, u32[]{:S(2)}, u32[]{:S(2)}) collective-permute-start(f32[128,1152]{1,0:T(8,128)S(1)} %collective-permute-done.b_ref), channel_id=1, source_target_pairs={{0,16},{16,0},{1,17},{17,1},{2,18},{18,2},{3,19},{19,3},{4,20},{20... | collective-permute-start | bytes 1769480 | tf_op jit(solution)/shard_map/ppermute | solution.py:64
  56.7 12.1 %collective-permute-start.3 = (f32[264,1152]{1,0:T(8,128)S(1)}, f32[264,1152]{1,0:T(8,128)S(1)}, u32[]{:S(2)}, u32[]{:S(2)}) collective-permute-start(f32[264,1152]{1,0:T(8,128)S(1)} %get-tuple-element.19.other_ref), channel_id=1, source_target_pairs={{0,16},{16,0},{1,17},{17,1},{2,18},{18,2},{3,19},{19,3},{4,20},{20... | collective-permute-start | bytes 3649544 | tf_op jit(solution)/shard_map/ppermute | solution.py:64
  66.6 15.1 %collective-permute-start.5 = (f32[64,1152]{1,0:T(8,128)S(1)}, f32[64,1152]{1,0:T(8,128)S(1)}, u32[]{:S(2)}, u32[]{:S(2)}) collective-permute-start(f32[64,1152]{1,0:T(8,128)S(1)} %get-tuple-element.25), channel_id=1, source_target_pairs={{0,3},{1,0},{2,1},{3,2},{16,17},{17,18},{18,19},{19,16},{4,7},{5,4... | collective-permute-start | bytes 884744 | tf_op jit(solution)/shard_map/ppermute | solution.py:51
  70.7 36.6 %collective-permute-start.4 = (f32[128,1152]{1,0:T(8,128)S(1)}, f32[128,1152]{1,0:T(8,128)S(1)}, u32[]{:S(2)}, u32[]{:S(2)}) collective-permute-start(f32[128,1152]{1,0:T(8,128)S(1)} %get-tuple-element.22), channel_id=1, source_target_pairs={{0,32},{32,4},{4,36},{36,8},{8,40},{40,12},{12,44},{44,0},{16,60},... | collective-permute-start | bytes 1769480 | tf_op jit(solution)/shard_map/ppermute | solution.py:60
  77.4 10.7 %collective-permute-start.7 = (f32[64,1152]{1,0:T(8,128)S(1)}, f32[64,1152]{1,0:T(8,128)S(1)}, u32[]{:S(2)}, u32[]{:S(2)}) collective-permute-start(f32[64,1152]{1,0:T(8,128)S(1)} %get-tuple-element.26), channel_id=1, source_target_pairs={{0,1},{1,2},{2,3},{3,0},{16,19},{17,16},{18,17},{19,18},{4,5},{5,6... | collective-permute-start | bytes 884744 | tf_op jit(solution)/shard_map/ppermute | solution.py:51
  81.8 8.7 %collective-permute-start.6 = (f32[64,1152]{1,0:T(8,128)S(1)}, f32[64,1152]{1,0:T(8,128)S(1)}, u32[]{:S(2)}, u32[]{:S(2)}) collective-permute-start(f32[64,1152]{1,0:T(8,128)S(1)} %shard_map.54), channel_id=1, source_target_pairs={{0,3},{1,0},{2,1},{3,2},{16,17},{17,18},{18,19},{19,16},{4,7},{5,4... | collective-permute-start | bytes 884744 | tf_op jit(solution)/shard_map/ppermute | solution.py:51
  91.0 7.7 %collective-permute-start.8 = (f32[16,1152]{1,0:T(8,128)S(1)}, f32[16,1152]{1,0:T(8,128)S(1)}, u32[]{:S(2)}, u32[]{:S(2)}) collective-permute-start(f32[16,1152]{1,0:T(8,128)S(1)} %get-tuple-element.27), channel_id=1, source_target_pairs={{0,12},{4,0},{8,4},{12,8},{16,20},{20,24},{24,28},{28,16},{1,13},{... | collective-permute-start | bytes 221192 | tf_op jit(solution)/shard_map/ppermute | solution.py:51
  93.0 14.3 %all-to-all-start.2 = ((f32[32,1,128]{2,1,0:T(1,128)}), f32[32,1,128]{2,1,0:T(1,128)S(1)}, u32[]{:S(2)}, u32[]{:S(2)}) async-start(f32[32,1,128]{2,1,0:T(1,128)} %bitcast.14), calls=%async_computation.2 | async-start | bytes 32768 | tf_op jit(solution)/shard_map/all_to_all | solution.py:45
  108.2 20.4 %copy-start.1 = (f32[16,1152]{1,0:T(8,128)S(1)}, f32[16,1152]{1,0:T(8,128)}, u32[]{:S(2)}) copy-start(f32[16,1152]{1,0:T(8,128)} %emb_ref.2) | copy-start | bytes 221188
  108.2 20.4 %all-to-all-start.3 = ((f32[8,152,128]{2,1,0:T(8,128)}), f32[8,152,128]{2,1,0:T(8,128)S(1)}, u32[]{:S(2)}, u32[]{:S(2)}) async-start(f32[8,152,128]{2,1,0:T(8,128)} %shard_map.56), calls=%async_computation.3 | async-start | bytes 1245184 | tf_op jit(solution)/shard_map/all_to_all | solution.py:45
  111.9 6.8 %collective-permute-start.10 = (f32[16,1152]{1,0:T(8,128)S(1)}, f32[16,1152]{1,0:T(8,128)S(1)}, u32[]{:S(2)}, u32[]{:S(2)}) collective-permute-start(f32[16,1152]{1,0:T(8,128)S(1)} %get-tuple-element.31), channel_id=1, source_target_pairs={{0,4},{4,8},{8,12},{12,0},{16,28},{20,16},{24,20},{28,24},{1,5},{5... | collective-permute-start | bytes 221192 | tf_op jit(solution)/shard_map/ppermute | solution.py:51
  114.2 7.3 %collective-permute-start.9 = (f32[16,1152]{1,0:T(8,128)S(1)}, f32[16,1152]{1,0:T(8,128)S(1)}, u32[]{:S(2)}, u32[]{:S(2)}) collective-permute-start(f32[16,1152]{1,0:T(8,128)S(1)} %shard_map.58), channel_id=1, source_target_pairs={{0,12},{4,0},{8,4},{12,8},{16,20},{20,24},{24,28},{28,16},{1,13},{... | collective-permute-start | bytes 221192 | tf_op jit(solution)/shard_map/ppermute | solution.py:51
